TPU v7x, 32 devices: a whole 2x2x4 slice. The times are simulated.
32 devices in a mesh: wide: 8 (over y, x, core), narrow: 4 (over z).
Axes of the slice: x: 2, y: 2, z: 4, core: 2. Of those that a mesh axis runs over, the one named last changes fastest.
Arguments:
- activations: bfloat16 [1024, 16384], P('wide', 'narrow'), may hold values from -30 to 30, as said below
- weight_tile: bfloat16 [16384, 16384], P('wide', 'narrow'), may hold values from -3 to 3
- codes: int32 [16384, 16384], P('wide', 'narrow'), may hold values from -8 to 7
- group_scales: float32 [16384, 128], P('wide', 'narrow'), may hold values from 0.02 to 0.2
- right_factor: bfloat16 [16384, 256], replicated, may hold values from -0.046875 to 0.046875
Outputs:
- residual_product: float32 [16384, 256], P(('wide', 'narrow'))
- gram: float32 [256, 256], replicated
- hessian_tiles: bfloat16 [16384, 16384], P('wide', 'narrow')
Inputs may be any that keep to these rules, and one draw needn't show every extreme that they name: `activations`: each token's features are a product of a token scale, a feature scale and a value.
All inputs are finite; a program needn't handle non-finite values.
Results may differ from a plain program's by a relative error of at most 0.0049.
Values may be sent and summed in bfloat16 or wider, within the bound.
No kernel may reach another device: no remote copies, remote signals or barrier semaphores. Data moves between devices by JAX's collectives and lax.ppermute only.
A program may use at most 192 MiB of HBM per device.

v0:
```python
import jax
import jax.numpy as jnp
from jax import lax
from jax.sharding import PartitionSpec as P


def body(activations, weight_tile, codes, group_scales, right_factor):
    rows_local = weight_tile.shape[0]
    cols_local = weight_tile.shape[1]
    wide_count = lax.axis_size("wide")
    wide_index = lax.axis_index("wide")
    narrow_index = lax.axis_index("narrow")
    total_tokens = activations.shape[0] * wide_count
    contract_first = (((0,), (0,)), ((), ()))
    full_features = lax.all_gather(activations, "narrow", axis=1, tiled=True)
    row_operand = lax.all_to_all(full_features, "wide", split_axis=1, concat_axis=0, tiled=True)
    hess_sum = lax.dot_general(
        row_operand,
        lax.all_gather(activations, "wide", axis=0, tiled=True),
        contract_first,
        preferred_element_type=jnp.float32,
    )
    hessian = hess_sum / total_tokens
    hessian_tiles = hessian.astype(jnp.bfloat16)
    groups = group_scales.shape[1]
    width = cols_local // groups
    quantized = (
        codes.reshape(rows_local, groups, width).astype(jnp.float32) * group_scales[:, :, None]
    ).reshape(rows_local, cols_local)
    residual = (weight_tile.astype(jnp.float32) - quantized).astype(jnp.bfloat16)
    right_rows = lax.dynamic_slice_in_dim(right_factor, wide_index * rows_local, rows_local, 0)
    partial_value = lax.dot_general(
        hessian, right_rows.astype(jnp.float32), contract_first, precision=lax.Precision.HIGHEST
    )
    product_cols = lax.psum(partial_value, "wide").astype(jnp.bfloat16)
    share = cols_local // wide_count
    gram_start = narrow_index * cols_local + wide_index * share
    product_share = lax.dynamic_slice_in_dim(product_cols, wide_index * share, share, 0)
    right_share = lax.dynamic_slice_in_dim(right_factor, gram_start, share, 0)
    gram_part = lax.dot_general(
        right_share, product_share, contract_first, preferred_element_type=jnp.float32
    )
    gram = lax.psum(gram_part, ("wide", "narrow"))
    residual_product = lax.psum_scatter(
        jnp.dot(residual, product_cols, preferred_element_type=jnp.float32),
        "narrow",
        scatter_dimension=0,
        tiled=True,
    )
    return (residual_product, gram, hessian_tiles)


def solution(mesh):
    in_specs = (
        P("wide", "narrow"),
        P("wide", "narrow"),
        P("wide", "narrow"),
        P("wide", "narrow"),
        P(),
    )
    out_specs = (P(("wide", "narrow"), None), P(), P("wide", "narrow"))
    return jax.shard_map(body, mesh=mesh, in_specs=in_specs, out_specs=out_specs, check_vma=False)
```

profile of v0, /device:TPU:0, one launch (start us, length us, event | category | flops | bytes accessed | tf_op | source)
XLA Modules:
  0.0 509.8 jit_solution(13493302869377331191)
XLA Ops:
  7.2 0.0 all-gather.3.cloned.1.call-start
  7.2 2.3 copy.11
  9.5 0.0 all-gather.3.cloned.1.call-update
  9.5 0.0 all-gather.5.cloned.1.call-start
  9.5 0.7 all-gather.5.cloned.1.call-update
  10.3 83.4 %all-gather.3.cloned.1.call-done = bf16[128,16384]{0,1:T(8,128)(2,1)} async-done(((bf16[128,4096]{0,1:T(8,128)(2,1)}), bf16[128,16384]{0,1:T(8,128)(2,1)}) %all-gather.3.cloned.1.call-update) | async-done | bytes 4194320 | tf_op jit(solution)/shard_map/all_gather | solution.py:15
  93.6 4.5 all-to-all-start
  98.2 0.0 all-reduce.3.cloned.1.call-start
  98.2 1.3 copy.10
  99.5 65.3 %all-to-all-done = bf16[128,8,2048]{0,2,1:T(8,128)(2,1)} async-done(((bf16[128,8,2048]{0,2,1:T(8,128)(2,1)}), bf16[128,8,2048]{0,2,1:T(8,128)(2,1)}, u32[]{:S(2)}, u32[]{:S(2)}) %all-to-all-start) | async-done | bytes 4194336 | tf_op jit(solution)/shard_map/all_to_all | solution.py:16
  164.9 6.5 %copy.12 = bf16[8,128,2048]{2,1,0:T(8,128)(2,1)} copy(bf16[8,128,2048]{1,2,0:T(8,128)(2,1)} %bitcast.1) | data formatting | bytes 8388608 | tf_op jit(solution)/shard_map/all_to_all | solution.py:16
  171.4 11.5 %all-gather.5.cloned.1.call-done = bf16[1024,4096]{1,0:T(8,128)(2,1)} async-done(((bf16[128,4096]{1,0:T(8,128)(2,1)}), bf16[1024,4096]{1,0:T(8,128)(2,1)}) %all-gather.5.cloned.1.call-update) | async-done | bytes 8388624 | tf_op jit(solution)/shard_map/all_gather | solution.py:19
  182.9 26.9 %multiply_convert_fusion = (bf16[2048,4096]{1,0:T(8,128)(2,1)}, f32[2048,4096]{1,0:T(8,128)}) fusion(bf16[1024,2048]{1,0:T(8,128)(2,1)} %bitcast.16, bf16[1024,4096]{1,0:T(8,128)(2,1)} %all-gather.5.cloned.1.call-done), kind=kOutput, calls=%fused_computation.3 | convolution fusion | flops 17196646400 | bytes 62914560 | tf_op jit(solution)/shard_map/dot_general | solution.py:17
  209.8 33.9 %fusion.2 = f32[4096,256]{1,0:T(8,128)} fusion(f32[2048,4096]{1,0:T(8,128)} %get-tuple-element.4, bf16[16384,256]{1,0:T(8,128)(2,1)} %param.9, s32[]{:T(128)S(6)} %select_n.9), kind=kOutput, calls=%fused_computation.4 | convolution fusion | flops 25778192384 | bytes 38797316 | tf_op jit(solution)/shard_map/dot_general | solution.py:32
  243.7 86.7 %all-reduce.4 = bf16[4096,256]{1,0:T(8,128)(2,1)S(1)} all-reduce(f32[4096,256]{1,0:T(8,128)} %fusion.2), channel_id=1, replica_groups=mesh['wide'=8,'narrow'=4] {'wide'}, use_global_device_ids=true, to_apply=%region_0.0 | all-reduce | flops 1048576 | bytes 6291456 | tf_op jit(solution)/shard_map/psum | solution.py:35
  330.5 1.9 fusion.8
  332.4 0.0 all-reduce.3.cloned.1.call-update
  332.4 0.0 reduce-scatter.2.cloned.1.call-start
  332.5 22.4 %mul.21 = f32[2048,32,128]{2,1,0:T(8,128)} broadcast(f32[2048,32]{1,0:T(8,128)S(1)} %copy.10), dimensions={0,1} | broadcast | bytes 33816576 | tf_op jit(solution)/shard_map/mul | solution.py:28
  354.9 30.2 %fusion.5 = f32[2048,256]{1,0:T(8,128)} fusion(bf16[4096,256]{1,0:T(8,128)(2,1)S(1)} %all-reduce.4, f32[256,8,32,128]{3,2,1,0:T(8,128)} %bitcast.14, s32[2048,4096]{1,0:T(8,128)} %param.7, bf16[2048,4096]{1,0:T(8,128)(2,1)} %param.6), kind=kOutput, calls=%fused_computation.7 | convolution fusion | flops 4336910336 | bytes 88080384 | tf_op jit(solution)/shard_map/dot_general | solution.py:45
  385.1 0.0 reduce-scatter.2.cloned.1.call-update
  385.1 70.8 %all-reduce.3.cloned.1.call-done = f32[256,256]{1,0:T(8,128)} async-done(((f32[256,256]{1,0:T(8,128)}), f32[256,256]{1,0:T(8,128)}) %all-reduce.3.cloned.1.call-update) | async-done | bytes 262160 | tf_op jit(solution)/shard_map/psum | solution.py:43
  455.9 45.6 %reduce-scatter.2.cloned.1.call-done = f32[512,256]{1,0:T(8,128)} async-done(((f32[2048,256]{1,0:T(8,128)}), f32[512,256]{1,0:T(8,128)}) %reduce-scatter.2.cloned.1.call-update) | async-done | bytes 524304 | tf_op jit(solution)/shard_map/reduce_scatter | solution.py:44
  501.5 1.7 copy.19
Async XLA Ops:
  7.2 86.5 %all-gather.3.cloned.1.call-start = ((), (), s32[]{:S(2)}) async-start(), calls=%async_computation.2 | async-start | bytes 5242880 | tf_op jit(solution)/shard_map/all_gather | solution.py:15
  9.5 173.4 %all-gather.5.cloned.1.call-start = ((), (), s32[]{:S(2)}) async-start(), calls=%async_computation.3 | async-start | bytes 9437184 | tf_op jit(solution)/shard_map/all_gather | solution.py:19
  93.6 71.2 %all-to-all-start = ((bf16[128,8,2048]{0,2,1:T(8,128)(2,1)}), bf16[128,8,2048]{0,2,1:T(8,128)(2,1)}, u32[]{:S(2)}, u32[]{:S(2)}) async-start(bf16[128,8,2048]{0,2,1:T(8,128)(2,1)} %bitcast.15), calls=%async_computation | async-start | bytes 8388608 | tf_op jit(solution)/shard_map/all_to_all | solution.py:16
  98.2 357.7 %all-reduce.3.cloned.1.call-start = ((), (), s32[]{:S(2)}) async-start(), calls=%async_computation.5 | async-start | bytes 524288 | tf_op jit(solution)/shard_map/psum | solution.py:43
  332.4 169.1 %reduce-scatter.2.cloned.1.call-start = ((), (), s32[]{:S(2)}) async-start(), calls=%async_computation.4 | async-start | bytes 2621440 | tf_op jit(solution)/shard_map/reduce_scatter | solution.py:44
Sparse Core Ops, SparseCore 0:
  10.1 83.4 all-gather.2
  95.5 87.3 all-gather.4
  332.5 123.3 all-reduce.2
  458.6 42.8 reduce-scatter.1
where the time goes:
time: 510 us
  waiting for transfers between devices  277 us (54%)
  matrix products  93 us (18%)
  blocking collectives  86.7 us (17%)
  local copies, waits for them, and re-layouts  34.1 us (7%)
  between operations  13.8 us (3%)
    psum x1, blocking collectives, body(): product_cols = lax.psum(partial_value, 'wide').astype(jnp.bfloat16)  86.7 us
    all_gather x1, waiting for transfers between devices, body(): full_features = lax.all_gather(activations, 'narrow', axis=1, tiled=True)  83.4 us
    psum x1, waiting for transfers between devices, body(): gram = lax.psum(gram_part, ('wide', 'narrow'))  70.8 us
    all_to_all x1, waiting for transfers between devices, body(): lax.all_to_all(full_features, 'wide', split_axis=1, concat_axis=0, tiled=...  65.3 us
    reduce_scatter x1, waiting for transfers between devices, body(): lax.psum_scatter(jnp.dot(residual, product_cols, preferred_element_type=j...  45.6 us
    dot_general x1, matrix products, body(): lax.dot_general(hessian, right_rows.astype(jnp.float32), contract_first,...  33.9 us
    dot_general x1, matrix products, body(): jnp.dot(residual, product_cols, preferred_element_type=jnp.float32)  30.2 us
    dot_general x1, matrix products, body(): lax.dot_general(row_operand, lax.all_gather(activations, 'wide', axis=0,...  26.9 us
  transfers between devices with their start and end apart: 5, of which 5 were waited for; matrix products, arithmetic and copies ran while one was open for 12% of the time, Pallas kernels for 0%

commit v1 on v0

v1 whole, which is shorter than its diff:
```python
import functools

import jax
import jax.numpy as jnp
from jax import lax
from jax.experimental import pallas as pl
from jax.experimental.pallas import tpu as pltpu
from jax.sharding import PartitionSpec as P

CHUNKS = 4
MIB = 1024 * 1024
BF16 = jnp.bfloat16
F32 = jnp.float32


def flip(value, axis, mask):
    count = lax.axis_size(axis)
    return lax.ppermute(value, axis, [(i, i ^ mask) for i in range(count)])


def split_float(value):
    high = value.astype(BF16)
    low = (value - high.astype(F32)).astype(BF16)
    return high, low


def gather_kernel(scale, pieces, where_ref, y_ref, *refs):
    piece_refs = refs[:pieces]
    cols_ref, hr_ref, gram_ref, order_ref, sems = refs[pieces:]
    tokens = y_ref.shape[1]
    halves = pieces // y_ref.shape[0]
    width = piece_refs[0].shape[1]
    me = where_ref[0]
    copies = []
    for half in range(halves):
        for mask in range(y_ref.shape[0]):
            at = pl.multiple_of((me ^ mask) * tokens, tokens)
            index = half * y_ref.shape[0] + mask
            copy = pltpu.make_async_copy(
                piece_refs[index],
                cols_ref.at[pl.ds(at, tokens), pl.ds(half * width, width)],
                sems.at[index],
            )
            copy.start()
            copies.append(copy)
    for mask in range(y_ref.shape[0]):
        at = pl.multiple_of((me ^ mask) * tokens, tokens)
        order_ref[pl.ds(at, tokens), :] = y_ref[mask]
    y_high, y_low = split_float(order_ref[...].T)
    across = (((1,), (1,)), ((), ()))
    gram = lax.dot_general(y_high, y_high, across, preferred_element_type=F32)
    gram += lax.dot_general(y_high, y_low, across, preferred_element_type=F32)
    gram += lax.dot_general(y_low, y_high, across, preferred_element_type=F32)
    gram_ref[...] = gram * scale
    for copy in copies:
        copy.wait()
    step = min(512, cols_ref.shape[1])
    for start in range(0, cols_ref.shape[1], step):
        block = cols_ref[:, start : start + step]
        total = jnp.dot(y_high, block, preferred_element_type=F32)
        total += jnp.dot(y_low, block, preferred_element_type=F32)
        hr_ref[:, start : start + step] = (total * scale).astype(BF16)


def gather_columns(pieces, y_blocks, where, scale):
    count, tokens, rank = y_blocks.shape
    halves = len(pieces) // count
    features = halves * pieces[0].shape[1]
    return pl.pallas_call(
        functools.partial(gather_kernel, scale, len(pieces)),
        out_shape=(
            jax.ShapeDtypeStruct((count * tokens, features), BF16),
            jax.ShapeDtypeStruct((rank, features), BF16),
            jax.ShapeDtypeStruct((rank, rank), F32),
        ),
        in_specs=[
            pl.BlockSpec(memory_space=pltpu.SMEM),
            pl.BlockSpec(memory_space=pltpu.VMEM),
        ]
        + [pl.BlockSpec(memory_space=pl.ANY)] * len(pieces),
        out_specs=(pl.BlockSpec(memory_space=pltpu.VMEM),) * 3,
        scratch_shapes=[
            pltpu.VMEM((count * tokens, rank), F32),
            pltpu.SemaphoreType.DMA((len(pieces),)),
        ],
        compiler_params=pltpu.CompilerParams(vmem_limit_bytes=48 * MIB),
        name="columns_hr_gram",
    )(where, y_blocks, *pieces)


def residual_kernel(weight_ref, codes_ref, scales_ref, hr_ref, out_ref):
    groups = scales_ref.shape[1]
    width = weight_ref.shape[1] // groups
    scales = scales_ref[...]
    parts = []
    for group in range(groups):
        at = slice(group * width, (group + 1) * width)
        quantized = codes_ref[:, at].astype(F32) * scales[:, group : group + 1]
        parts.append((weight_ref[:, at].astype(F32) - quantized).astype(BF16))
    residual = jnp.concatenate(parts, axis=1)
    out_ref[...] = lax.dot_general(
        residual, hr_ref[...], (((1,), (1,)), ((), ())), preferred_element_type=F32
    ).astype(BF16)


def residual_partial(weight, codes, scales, hr):
    rows, features = weight.shape
    rank = hr.shape[0]
    block = min(256, rows)
    return pl.pallas_call(
        residual_kernel,
        out_shape=jax.ShapeDtypeStruct((rows, rank), BF16),
        grid=(rows // block,),
        in_specs=[
            pl.BlockSpec((block, features), lambda i: (i, 0)),
            pl.BlockSpec((block, features), lambda i: (i, 0)),
            pl.BlockSpec((block, scales.shape[1]), lambda i: (i, 0)),
            pl.BlockSpec((rank, features), lambda i: (0, 0)),
        ],
        out_specs=pl.BlockSpec((block, rank), lambda i: (i, 0)),
        compiler_params=pltpu.CompilerParams(vmem_limit_bytes=48 * MIB),
        name="residual_product",
    )(weight, codes, scales, hr)


def hessian_kernel(scale, rows_ref, cols_ref, *refs):
    out_ref, turned_ref = refs[-2:]

    @pl.when(pl.program_id(0) == 0)
    def _():
        turned_ref[...] = rows_ref[...].T

    total = jnp.dot(turned_ref[...], cols_ref[...], preferred_element_type=F32)
    out_ref[...] = (total * scale).astype(BF16)


def hessian_rows(rows, cols, earlier, index, shape, scale):
    tokens, height = rows.shape
    tile = min(1024, cols.shape[1])
    ins = [rows, cols]
    specs = [
        pl.BlockSpec((tokens, height), lambda j: (0, 0)),
        pl.BlockSpec((tokens, tile), lambda j: (0, j)),
    ]
    aliases = {}
    if earlier is not None:
        ins.append(earlier)
        specs.append(pl.BlockSpec(memory_space=pl.ANY))
        aliases = {2: 0}
    return pl.pallas_call(
        functools.partial(hessian_kernel, scale),
        out_shape=jax.ShapeDtypeStruct(shape, BF16),
        grid=(cols.shape[1] // tile,),
        in_specs=specs,
        out_specs=pl.BlockSpec((height, tile), lambda j: (index, j)),
        scratch_shapes=[pltpu.VMEM((height, tokens), BF16)],
        input_output_aliases=aliases,
        compiler_params=pltpu.CompilerParams(vmem_limit_bytes=48 * MIB),
        name="hessian_rows",
    )(*ins)


def body(activations, weight_tile, codes, group_scales, right_factor):
    wide_count = lax.axis_size("wide")
    narrow_count = lax.axis_size("narrow")
    wide_index = lax.axis_index("wide")
    narrow_index = lax.axis_index("narrow")
    tokens, features = activations.shape
    rows = weight_tile.shape[0]
    rank = right_factor.shape[1]
    split = features // rows
    scale = 1.0 / (tokens * wide_count)
    bits = [1 << b for b in range(1, wide_count.bit_length() - 1)]

    right_block = lax.dynamic_slice_in_dim(right_factor, narrow_index * features, features, 0)
    product = jnp.dot(activations, right_block, preferred_element_type=F32)
    mask = 1
    while mask < narrow_count:
        product = product + flip(product, "narrow", mask)
        mask *= 2
    y_blocks = product[None]
    mask = 1
    while mask < wide_count:
        y_blocks = jnp.concatenate([y_blocks, flip(y_blocks, "wide", mask)], axis=0)
        mask *= 2

    middle = features // 2
    pieces = []
    for half, order in enumerate((bits[::-1], bits)):
        held = {0: activations[:, half * middle : (half + 1) * middle]}
        for bit in order + [1]:
            held.update({m | bit: flip(held[m], "wide", bit) for m in list(held)})
        pieces += [held[m] for m in range(wide_count)]

    height = rows // CHUNKS
    row_chunks = []
    for chunk in range(CHUNKS):
        mine = jnp.stack(
            [
                activations[:, s * rows + chunk * height : s * rows + (chunk + 1) * height]
                for s in range(split)
            ]
        )
        every = lax.all_gather(mine, "narrow", axis=0, tiled=True)
        chunk_rows = lax.all_to_all(every, "wide", split_axis=0, concat_axis=0, tiled=True)
        row_chunks.append(chunk_rows.reshape(tokens * wide_count, height))

    where = wide_index.astype(jnp.int32).reshape(1)
    cols, hr, gram = gather_columns(pieces, y_blocks, where, scale)
    partial_product = residual_partial(weight_tile, codes, group_scales, hr)
    shares = partial_product.reshape(narrow_count, rows // narrow_count, rank)
    shares = lax.all_to_all(shares, "narrow", split_axis=0, concat_axis=0, tiled=True)
    residual_product = jnp.sum(shares.astype(F32), axis=0)

    hessian = None
    for chunk in range(CHUNKS):
        hessian = hessian_rows(row_chunks[chunk], cols, hessian, chunk, (rows, features), scale)
    return residual_product, gram, hessian


def solution(mesh):
    in_specs = (
        P("wide", "narrow"),
        P("wide", "narrow"),
        P("wide", "narrow"),
        P("wide", "narrow"),
        P(),
    )
    out_specs = (P(("wide", "narrow"), None), P(), P("wide", "narrow"))
    return jax.shard_map(body, mesh=mesh, in_specs=in_specs, out_specs=out_specs, check_vma=False)
```

time: 510 us -> 262 us (0.51)
  waiting for transfers between devices: 277 us -> 128 us
  matrix products: 93 us -> 2.04 us
  blocking collectives: 86.7 us -> 0 us
  Pallas kernels: 0 us -> 65.7 us
  starting transfers between devices: 4.71 us -> 31.3 us
  local copies, waits for them, and re-layouts: 34.1 us -> 11.1 us
  other arithmetic: 0 us -> 8.61 us
    dot_general x4 -> x1, matrix products: 93 us -> 2.04 us  [body(): product = jnp.dot(activations, right_block, preferred_element_type=F32)]
    psum x1 -> x0, blocking collectives: 86.7 us -> none  [body(): product_cols = lax.psum(partial_value, 'wide').astype(jnp.bfloat16)]
    psum x1 -> x0, waiting for transfers between devices: 70.8 us -> none  [body(): gram = lax.psum(gram_part, ('wide', 'narrow'))]
    ppermute x0 -> x19, waiting for transfers between devices: none -> 70.1 us  [flip(): return lax.ppermute(value, axis, [(i, i ^ mask) for i in range(count)])]
    pallas_call x0 -> x6, Pallas kernels: none -> 65.7 us  [the longest x4 35.7 us: hessian_rows(): pl.pallas_call(functools.partial(hessian_kernel, scale), out_shape=jax.Sh...]
    all_to_all x1 -> x5, waiting for transfers between devices: 65.3 us -> 0.01 us  [the longest x4 0.01 us: body(): lax.all_to_all(every, 'wide', split_axis=0, concat_axis=0, tiled=True)]
    reduce_scatter x1 -> x0, waiting for transfers between devices: 45.6 us -> none  [body(): lax.psum_scatter(jnp.dot(residual, product_cols, preferred_element_type=j...]
    all_gather x2 -> x4, waiting for transfers between devices: 94.9 us -> 57.8 us  [body(): every = lax.all_gather(mine, 'narrow', axis=0, tiled=True)]
  transfers between devices with their start and end apart: 5 -> 28, of which waited for: 5 -> 12; matrix products, arithmetic and copies ran while one was open for 12% -> 5% of each run, Pallas kernels for 0% -> 25%
where the time goes in v1:
time: 262 us; the launch traced here: 261 us
  waiting for transfers between devices  128 us (49%)
  Pallas kernels  65.7 us (25%)
  starting transfers between devices  31.3 us (12%)
  between operations  13.9 us (5%)
  local copies, waits for them, and re-layouts  11.1 us (4%)
  other arithmetic  8.61 us (3%)
    ppermute x19, waiting for transfers between devices, flip(): return lax.ppermute(value, axis, [(i, i ^ mask) for i in range(count)])  70.1 us
    all_gather x4, waiting for transfers between devices, body(): every = lax.all_gather(mine, 'narrow', axis=0, tiled=True)  57.8 us
    pallas_call x4, Pallas kernels, hessian_rows(): pl.pallas_call(functools.partial(hessian_kernel, scale), out_shape=jax.Sh...  35.7 us
    pallas_call x1, Pallas kernels, residual_partial(): pl.pallas_call(residual_kernel, out_shape=jax.ShapeDtypeStruct((rows, ran...  19.3 us
    all_to_all x4, starting transfers between devices, body(): lax.all_to_all(every, 'wide', split_axis=0, concat_axis=0, tiled=True)  15.2 us
    ppermute x19, starting transfers between devices, flip(): return lax.ppermute(value, axis, [(i, i ^ mask) for i in range(count)])  12.3 us
    pallas_call x1, Pallas kernels, gather_columns(): pl.pallas_call(functools.partial(gather_kernel, scale, len(pieces)), out_...  10.8 us
    unnamed x19, local copies, waits for them, and re-layouts  7.6 us
  transfers between devices with their start and end apart: 28, of which 12 were waited for; matrix products, arithmetic and copies ran while one was open for 5% of the time, Pallas kernels for 25%

profile of v1, /device:TPU:0, one launch (start us, length us, event | category | flops | bytes accessed | tf_op | source)
XLA Modules:
  0.0 260.7 jit_solution(14786741045713873562)
XLA Ops:
  7.2 0.0 copy-start.8
  7.2 0.0 all-gather.11.cloned.1.call-start
  7.2 1.4 slice_bitcast_fusion.1
  8.7 0.7 pad_maximum_fusion.6
  9.4 0.0 all-gather.11.cloned.1.call-update
  9.4 0.0 all-gather.9.cloned.1.call-start
  9.5 0.7 pad_maximum_fusion.5
  10.2 0.0 all-gather.9.cloned.1.call-update
  10.2 0.0 all-gather.7.cloned.1.call-start
  10.3 0.7 pad_maximum_fusion.4
  11.0 0.0 all-gather.7.cloned.1.call-update
  11.0 29.8 %all-gather.11.cloned.1.call-done = bf16[8,128,512]{2,1,0:T(8,128)(2,1)} async-done(((bf16[2,128,512]{2,1,0:T(8,128)(2,1)}), bf16[8,128,512]{2,1,0:T(8,128)(2,1)}) %all-gather.11.cloned.1.call-update) | async-done | bytes 1048592 | tf_op jit(solution)/shard_map/all_gather | solution.py:204
  40.8 3.7 %all-to-all-start.4 = ((bf16[8,128,512]{2,1,0:T(8,128)(2,1)}), bf16[8,128,512]{2,1,0:T(8,128)(2,1)S(1)}, u32[]{:S(2)}, u32[]{:S(2)}) async-start(bf16[8,128,512]{2,1,0:T(8,128)(2,1)} %all-gather.11.cloned.1.call-done), calls=%async_computation.4 | async-start | bytes 2097152 | tf_op jit(solution)/shard_map/all_to_all | solution.py:205
  44.5 25.9 %all-gather.9.cloned.1.call-done = bf16[8,128,512]{2,1,0:T(8,128)(2,1)} async-done(((bf16[2,128,512]{2,1,0:T(8,128)(2,1)}), bf16[8,128,512]{2,1,0:T(8,128)(2,1)}) %all-gather.9.cloned.1.call-update) | async-done | bytes 1048592 | tf_op jit(solution)/shard_map/all_gather | solution.py:204
  70.4 3.7 %all-to-all-start.3 = ((bf16[8,128,512]{2,1,0:T(8,128)(2,1)}), bf16[8,128,512]{2,1,0:T(8,128)(2,1)S(1)}, u32[]{:S(2)}, u32[]{:S(2)}) async-start(bf16[8,128,512]{2,1,0:T(8,128)(2,1)} %all-gather.9.cloned.1.call-done), calls=%async_computation.3 | async-start | bytes 2097152 | tf_op jit(solution)/shard_map/all_to_all | solution.py:205
  74.1 0.0 all-gather.5.cloned.1.call-start
  74.1 2.0 fusion.2
  76.2 1.5 collective-permute-start
  77.7 4.7 %collective-permute-done = f32[128,256]{1,0:T(8,128)S(1)} collective-permute-done((f32[128,256]{1,0:T(8,128)S(1)}, f32[128,256]{1,0:T(8,128)S(1)}, u32[]{:S(2)}, u32[]{:S(2)}) %collective-permute-start) | collective-permute-done | bytes 131104 | tf_op jit(solution)/shard_map/ppermute | solution.py:18
  82.4 1.7 collective-permute-start.1
  84.1 0.7 pad_maximum_fusion.3
  84.8 0.0 all-gather.5.cloned.1.call-update
  84.8 15.7 %collective-permute-done.1 = f32[128,256]{1,0:T(8,128)S(1)} collective-permute-done((f32[128,256]{1,0:T(8,128)S(1)}, f32[128,256]{1,0:T(8,128)S(1)}, u32[]{:S(2)}, u32[]{:S(2)}) %collective-permute-start.1) | collective-permute-done | bytes 131104 | tf_op jit(solution)/shard_map/ppermute | solution.py:18
  100.6 0.1 collective-permute-start.2
  100.6 1.3 collective-permute-done.2
  102.0 0.7 pad_maximum_fusion.2
  102.7 1.5 collective-permute-start.3
  104.2 2.0 all-gather.7.cloned.1.call-done
  106.2 3.7 %all-to-all-start.2 = ((bf16[8,128,512]{2,1,0:T(8,128)(2,1)}), bf16[8,128,512]{2,1,0:T(8,128)(2,1)S(1)}, u32[]{:S(2)}, u32[]{:S(2)}) async-start(bf16[8,128,512]{2,1,0:T(8,128)(2,1)} %all-gather.7.cloned.1.call-done), calls=%async_computation.2 | async-start | bytes 2097152 | tf_op jit(solution)/shard_map/all_to_all | solution.py:205
  109.9 2.1 fusion.6
  112.0 2.0 collective-permute-start.15
  114.0 1.5 collective-permute-start.13
  115.5 0.8 copy-done.3
  116.3 0.6 collective-permute-start.8
  116.8 0.0 collective-permute-start.6
  116.8 1.8 pad_maximum_fusion.1
  118.6 17.5 %collective-permute-done.15.refs_12_ = bf16[128,2048]{1,0:T(8,128)(2,1)} collective-permute-done((bf16[128,2048]{1,0:T(8,128)(2,1)S(1)}, bf16[128,2048]{1,0:T(8,128)(2,1)}, u32[]{:S(2)}, u32[]{:S(2)}) %collective-permute-start.15) | collective-permute-done | bytes 524320 | tf_op jit(solution)/shard_map/ppermute | solution.py:18
  136.1 0.1 collective-permute-done.13.refs_10_
  136.2 0.4 collective-permute-start.16
  136.7 0.8 copy-done.6
  137.5 1.0 collective-permute-start.17
  138.5 8.9 %collective-permute-done.8.refs_4_ = bf16[128,2048]{1,0:T(8,128)(2,1)} collective-permute-done((bf16[128,2048]{1,0:T(8,128)(2,1)}, bf16[128,2048]{1,0:T(8,128)(2,1)}, u32[]{:S(2)}, u32[]{:S(2)}) %collective-permute-start.8) | collective-permute-done | bytes 524320 | tf_op jit(solution)/shard_map/ppermute | solution.py:18
  147.4 1.0 collective-permute-start.10
  148.4 0.4 collective-permute-start.4
  148.8 4.2 %all-to-all-start.1 = ((bf16[8,128,512]{2,1,0:T(8,128)(2,1)}), bf16[8,128,512]{2,1,0:T(8,128)(2,1)}, u32[]{:S(2)}, u32[]{:S(2)}) async-start(bf16[8,128,512]{2,1,0:T(8,128)(2,1)} %all-gather.5.cloned.1.call-done), calls=%async_computation.1 | async-start | bytes 2097152 | tf_op jit(solution)/shard_map/all_to_all | solution.py:205
  153.1 0.4 collective-permute-start.14
  153.4 0.2 collective-permute-start.9
  153.6 5.0 %collective-permute-done.17.refs_14_ = bf16[128,2048]{1,0:T(8,128)(2,1)} collective-permute-done((bf16[128,2048]{1,0:T(8,128)(2,1)}, bf16[128,2048]{1,0:T(8,128)(2,1)}, u32[]{:S(2)}, u32[]{:S(2)}) %collective-permute-start.17) | collective-permute-done | bytes 524320 | tf_op jit(solution)/shard_map/ppermute | solution.py:18
  158.6 3.9 %collective-permute-done.10.refs_6_ = bf16[128,2048]{1,0:T(8,128)(2,1)} collective-permute-done((bf16[128,2048]{1,0:T(8,128)(2,1)}, bf16[128,2048]{1,0:T(8,128)(2,1)}, u32[]{:S(2)}, u32[]{:S(2)}) %collective-permute-start.10) | collective-permute-done | bytes 524320 | tf_op jit(solution)/shard_map/ppermute | solution.py:18
  162.6 12.9 %collective-permute-done.4 = f32[4,128,256]{2,1,0:T(8,128)} collective-permute-done((f32[4,128,256]{2,1,0:T(8,128)}, f32[4,128,256]{2,1,0:T(8,128)}, u32[]{:S(2)}, u32[]{:S(2)}) %collective-permute-start.4) | collective-permute-done | bytes 524320 | tf_op jit(solution)/shard_map/ppermute | solution.py:18
  175.5 1.3 copy.14.scales_ref
  176.8 2.2 pad_maximum_fusion.y_ref
  179.0 1.0 copy-done.4
  180.1 1.0 copy-done.7
  181.1 10.8 %columns_hr_gram.1 = (bf16[1024,4096]{1,0:T(8,128)(2,1)}, bf16[256,4096]{1,0:T(8,128)(2,1)}, f32[256,256]{1,0:T(8,128)}) custom-call(s32[1]{0:T(128)} %bitcast.where_ref, f32[8,128,256]{2,1,0:T(8,128)} %pad_maximum_fusion.y_ref, bf16[128,2048]{1,0:T(8,128)(2,1)} %get-tuple-element.18.refs_0_, bf16[128,2048]{1,0:T(8,128)(2,1)} %collective-permute-done.5.refs_1_, ...), custom_call_target="tpu_custom_call" | custom-call | tf_op jit(solution)/shard_map/columns_hr_gram/pallas_call | solution.py:69
  191.9 1.6 copy-done.5
  193.5 19.3 %residual_product.1 = bf16[2048,256]{1,0:T(8,128)(2,1)S(1)} custom-call(bf16[2048,4096]{1,0:T(8,128)(2,1)} %weight_ref.1, s32[2048,4096]{1,0:T(8,128)} %codes_ref.1, f32[2048,32]{1,0:T(8,128)S(1)} %copy.14.scales_ref, bf16[256,4096]{1,0:T(8,128)(2,1)S(1)} %copy-done.5), custom_call_target="tpu_custom_call" | custom-call | tf_op jit(solution)/shard_map/residual_product/pallas_call | solution.py:110
  212.8 1.0 copy-done.2
  213.9 3.7 %all-to-all-start = ((bf16[4,512,256]{2,1,0:T(8,128)(2,1)}), bf16[4,512,256]{2,1,0:T(8,128)(2,1)S(1)}, u32[]{:S(2)}, u32[]{:S(2)}) async-start(bf16[4,512,256]{2,1,0:T(8,128)(2,1)} %bitcast.30), calls=%async_computation | async-start | bytes 2097152 | tf_op jit(solution)/shard_map/all_to_all | solution.py:212
  217.6 8.8 %hessian_rows.4.refs_0_ = bf16[2048,4096]{1,0:T(8,128)(2,1)} custom-call(bf16[1024,512]{1,0:T(8,128)(2,1)S(1)} %bitcast.27, bf16[1024,4096]{1,0:T(8,128)(2,1)} %get-tuple-element.8.cols_ref), custom_call_target="tpu_custom_call" | custom-call | tf_op jit(solution)/shard_map/hessian_rows/pallas_call | solution.py:150
  226.4 8.9 %hessian_rows.5.refs_0_ = bf16[2048,4096]{1,0:T(8,128)(2,1)} custom-call(bf16[1024,512]{1,0:T(8,128)(2,1)S(1)} %bitcast.28, bf16[1024,4096]{1,0:T(8,128)(2,1)} %get-tuple-element.8.cols_ref, bf16[2048,4096]{1,0:T(8,128)(2,1)} %hessian_rows.4.refs_0_), custom_call_target="tpu_custom_call", output_to_operand_aliasing={{}: (2, {})} | custom-call | tf_op jit(solution)/shard_map/hessian_rows/pallas_call | solution.py:150
  235.3 8.8 %hessian_rows.6.refs_0_ = bf16[2048,4096]{1,0:T(8,128)(2,1)} custom-call(bf16[1024,512]{1,0:T(8,128)(2,1)S(1)} %bitcast.29, bf16[1024,4096]{1,0:T(8,128)(2,1)} %get-tuple-element.8.cols_ref, bf16[2048,4096]{1,0:T(8,128)(2,1)} %hessian_rows.5.refs_0_), custom_call_target="tpu_custom_call", output_to_operand_aliasing={{}: (2, {})} | custom-call | tf_op jit(solution)/shard_map/hessian_rows/pallas_call | solution.py:150
  244.1 9.1 %hessian_rows.7 = bf16[2048,4096]{1,0:T(8,128)(2,1)} custom-call(bf16[1024,512]{1,0:T(8,128)(2,1)} %bitcast.6.rows_ref, bf16[1024,4096]{1,0:T(8,128)(2,1)} %get-tuple-element.8.cols_ref, bf16[2048,4096]{1,0:T(8,128)(2,1)} %hessian_rows.6.refs_0_), custom_call_target="tpu_custom_call", output_to_operand_aliasing={{}: (2, {})} | custom-call | tf_op jit(solution)/shard_map/hessian_rows/pallas_call | solution.py:150
  253.2 0.9 convert_reduce_fusion
  (34 shorter events, 0.1 us)
Async XLA Ops:
  7.2 67.0 %copy-start.8 = (bf16[128,4096]{1,0:T(8,128)(2,1)S(1)}, bf16[128,4096]{1,0:T(8,128)(2,1)}, u32[]{:S(2)}) copy-start(bf16[128,4096]{1,0:T(8,128)(2,1)} %param.5) | copy-start | bytes 3145732
  7.2 33.6 %all-gather.11.cloned.1.call-start = ((), (), s32[]{:S(2)}) async-start(), calls=%async_computation.8 | async-start | bytes 1310720 | tf_op jit(solution)/shard_map/all_gather | solution.py:204
  9.4 61.0 %all-gather.9.cloned.1.call-start = ((), (), s32[]{:S(2)}) async-start(), calls=%async_computation.7 | async-start | bytes 1310720 | tf_op jit(solution)/shard_map/all_gather | solution.py:204
  10.2 96.0 %all-gather.7.cloned.1.call-start = ((), (), s32[]{:S(2)}) async-start(), calls=%async_computation.6 | async-start | bytes 1310720 | tf_op jit(solution)/shard_map/all_gather | solution.py:204
  40.8 29.6 %all-to-all-start.4 = ((bf16[8,128,512]{2,1,0:T(8,128)(2,1)}), bf16[8,128,512]{2,1,0:T(8,128)(2,1)S(1)}, u32[]{:S(2)}, u32[]{:S(2)}) async-start(bf16[8,128,512]{2,1,0:T(8,128)(2,1)} %all-gather.11.cloned.1.call-done), calls=%async_computation.4 | async-start | bytes 2097152 | tf_op jit(solution)/shard_map/all_to_all | solution.py:205
  70.4 35.8 %all-to-all-start.3 = ((bf16[8,128,512]{2,1,0:T(8,128)(2,1)}), bf16[8,128,512]{2,1,0:T(8,128)(2,1)S(1)}, u32[]{:S(2)}, u32[]{:S(2)}) async-start(bf16[8,128,512]{2,1,0:T(8,128)(2,1)} %all-gather.9.cloned.1.call-done), calls=%async_computation.3 | async-start | bytes 2097152 | tf_op jit(solution)/shard_map/all_to_all | solution.py:205
  74.1 74.7 %all-gather.5.cloned.1.call-start = ((), (), s32[]{:S(2)}) async-start(), calls=%async_computation.5 | async-start | bytes 1310720 | tf_op jit(solution)/shard_map/all_gather | solution.py:204
  76.2 6.2 %collective-permute-start = (f32[128,256]{1,0:T(8,128)S(1)}, f32[128,256]{1,0:T(8,128)S(1)}, u32[]{:S(2)}, u32[]{:S(2)}) collective-permute-start(f32[128,256]{1,0:T(8,128)S(1)} %fusion.2), channel_id=1, source_target_pairs={{0,1},{1,0},{2,3},{3,2},{4,5},{5,4},{6,7},{7,6},{8,9},{9,8},{10,11... | collective-permute-start | bytes 393224 | tf_op jit(solution)/shard_map/ppermute | solution.py:18
  82.4 18.1 %collective-permute-start.1 = (f32[128,256]{1,0:T(8,128)S(1)}, f32[128,256]{1,0:T(8,128)S(1)}, u32[]{:S(2)}, u32[]{:S(2)}) collective-permute-start(f32[128,256]{1,0:T(8,128)S(1)} %add.10), channel_id=1, source_target_pairs={{0,2},{1,3},{2,0},{3,1},{4,6},{5,7},{6,4},{7,5},{8,10},{9,11},{10,... | collective-permute-start | bytes 393224 | tf_op jit(solution)/shard_map/ppermute | solution.py:18
  100.6 1.4 collective-permute-start.2
  102.7 14.1 %collective-permute-start.3 = (f32[2,128,256]{2,1,0:T(8,128)}, f32[2,128,256]{2,1,0:T(8,128)}, u32[]{:S(2)}, u32[]{:S(2)}) collective-permute-start(f32[2,128,256]{2,1,0:T(8,128)} %pad_maximum_fusion.2), channel_id=1, source_target_pairs={{0,8},{4,12},{8,0},{12,4},{16,24},{20,28},{24,16},{28,20},{1,9},{5... | collective-permute-start | bytes 786440 | tf_op jit(solution)/shard_map/ppermute | solution.py:18
  106.2 42.6 %all-to-all-start.2 = ((bf16[8,128,512]{2,1,0:T(8,128)(2,1)}), bf16[8,128,512]{2,1,0:T(8,128)(2,1)S(1)}, u32[]{:S(2)}, u32[]{:S(2)}) async-start(bf16[8,128,512]{2,1,0:T(8,128)(2,1)} %all-gather.7.cloned.1.call-done), calls=%async_computation.2 | async-start | bytes 2097152 | tf_op jit(solution)/shard_map/all_to_all | solution.py:205
  112.0 24.2 %collective-permute-start.15 = (bf16[128,2048]{1,0:T(8,128)(2,1)S(1)}, bf16[128,2048]{1,0:T(8,128)(2,1)}, u32[]{:S(2)}, u32[]{:S(2)}) collective-permute-start(bf16[128,2048]{1,0:T(8,128)(2,1)S(1)} %get-tuple-element.17.refs_8_), channel_id=1, source_target_pairs={{0,16},{4,20},{8,24},{12,28},{16,0},{20,4},{24,8},{28,12},{1,17},{... | collective-permute-start | bytes 1572872 | tf_op jit(solution)/shard_map/ppermute | solution.py:18
  114.0 22.2 %collective-permute-start.13 = (bf16[128,2048]{1,0:T(8,128)(2,1)S(1)}, bf16[128,2048]{1,0:T(8,128)(2,1)}, u32[]{:S(2)}, u32[]{:S(2)}) collective-permute-start(bf16[128,2048]{1,0:T(8,128)(2,1)S(1)} %get-tuple-element.17.refs_8_), channel_id=1, source_target_pairs={{0,8},{4,12},{8,0},{12,4},{16,24},{20,28},{24,16},{28,20},{1,9},{5... | collective-permute-start | bytes 1572872 | tf_op jit(solution)/shard_map/ppermute | solution.py:18
  115.5 21.2 %collective-permute-start.12 = (bf16[128,2048]{1,0:T(8,128)(2,1)S(1)}, bf16[128,2048]{1,0:T(8,128)(2,1)S(1)}, u32[]{:S(2)}, u32[]{:S(2)}) collective-permute-start(bf16[128,2048]{1,0:T(8,128)(2,1)S(1)} %get-tuple-element.17.refs_8_), channel_id=1, source_target_pairs={{0,4},{4,0},{8,12},{12,8},{16,20},{20,16},{24,28},{28,24},{1,5},{5... | collective-permute-start | bytes 1572872 | tf_op jit(solution)/shard_map/ppermute | solution.py:18
  115.5 0.8 copy-start.3
  116.3 31.1 %collective-permute-start.8 = (bf16[128,2048]{1,0:T(8,128)(2,1)}, bf16[128,2048]{1,0:T(8,128)(2,1)}, u32[]{:S(2)}, u32[]{:S(2)}) collective-permute-start(bf16[128,2048]{1,0:T(8,128)(2,1)} %get-tuple-element.18.refs_0_), channel_id=1, source_target_pairs={{0,16},{4,20},{8,24},{12,28},{16,0},{20,4},{24,8},{28,12},{1,17},{... | collective-permute-start | bytes 1572872 | tf_op jit(solution)/shard_map/ppermute | solution.py:18
  116.8 31.6 %collective-permute-start.6 = (bf16[128,2048]{1,0:T(8,128)(2,1)}, bf16[128,2048]{1,0:T(8,128)(2,1)}, u32[]{:S(2)}, u32[]{:S(2)}) collective-permute-start(bf16[128,2048]{1,0:T(8,128)(2,1)} %get-tuple-element.18.refs_0_), channel_id=1, source_target_pairs={{0,8},{4,12},{8,0},{12,4},{16,24},{20,28},{24,16},{28,20},{1,9},{5... | collective-permute-start | bytes 1572872 | tf_op jit(solution)/shard_map/ppermute | solution.py:18
  136.1 16.9 %collective-permute-start.5 = (bf16[128,2048]{1,0:T(8,128)(2,1)}, bf16[128,2048]{1,0:T(8,128)(2,1)}, u32[]{:S(2)}, u32[]{:S(2)}) collective-permute-start(bf16[128,2048]{1,0:T(8,128)(2,1)} %get-tuple-element.18.refs_0_), channel_id=1, source_target_pairs={{0,4},{4,0},{8,12},{12,8},{16,20},{20,16},{24,28},{28,24},{1,5},{5... | collective-permute-start | bytes 1572872 | tf_op jit(solution)/shard_map/ppermute | solution.py:18
  136.2 17.2 %collective-permute-start.16 = (bf16[128,2048]{1,0:T(8,128)(2,1)}, bf16[128,2048]{1,0:T(8,128)(2,1)}, u32[]{:S(2)}, u32[]{:S(2)}) collective-permute-start(bf16[128,2048]{1,0:T(8,128)(2,1)} %collective-permute-done.15.refs_12_), channel_id=1, source_target_pairs={{0,4},{4,0},{8,12},{12,8},{16,20},{20,16},{24,28},{28,24},{1,5},{5... | collective-permute-start | bytes 1572872 | tf_op jit(solution)/shard_map/ppermute | solution.py:18
  136.7 0.8 copy-start.6
  137.5 21.1 %collective-permute-start.17 = (bf16[128,2048]{1,0:T(8,128)(2,1)}, bf16[128,2048]{1,0:T(8,128)(2,1)}, u32[]{:S(2)}, u32[]{:S(2)}) collective-permute-start(bf16[128,2048]{1,0:T(8,128)(2,1)} %collective-permute-done.13.refs_10_), channel_id=1, source_target_pairs={{0,16},{4,20},{8,24},{12,28},{16,0},{20,4},{24,8},{28,12},{1,17},{... | collective-permute-start | bytes 1572872 | tf_op jit(solution)/shard_map/ppermute | solution.py:18
  147.4 15.2 %collective-permute-start.10 = (bf16[128,2048]{1,0:T(8,128)(2,1)}, bf16[128,2048]{1,0:T(8,128)(2,1)}, u32[]{:S(2)}, u32[]{:S(2)}) collective-permute-start(bf16[128,2048]{1,0:T(8,128)(2,1)} %collective-permute-done.8.refs_4_), channel_id=1, source_target_pairs={{0,8},{4,12},{8,0},{12,4},{16,24},{20,28},{24,16},{28,20},{1,9},{5... | collective-permute-start | bytes 1572872 | tf_op jit(solution)/shard_map/ppermute | solution.py:18
  148.4 27.0 %collective-permute-start.4 = (f32[4,128,256]{2,1,0:T(8,128)}, f32[4,128,256]{2,1,0:T(8,128)}, u32[]{:S(2)}, u32[]{:S(2)}) collective-permute-start(f32[4,128,256]{2,1,0:T(8,128)} %pad_maximum_fusion.1), channel_id=1, source_target_pairs={{0,16},{4,20},{8,24},{12,28},{16,0},{20,4},{24,8},{28,12},{1,17},{... | collective-permute-start | bytes 1572872 | tf_op jit(solution)/shard_map/ppermute | solution.py:18
  148.8 26.7 %copy-start = (bf16[8,128,512]{2,1,0:T(8,128)(2,1)}, bf16[8,128,512]{2,1,0:T(8,128)(2,1)S(1)}, u32[]{:S(2)}) copy-start(bf16[8,128,512]{2,1,0:T(8,128)(2,1)S(1)} %all-to-all-done.2) | copy-start | bytes 3145732
  148.8 65.1 %all-to-all-start.1 = ((bf16[8,128,512]{2,1,0:T(8,128)(2,1)}), bf16[8,128,512]{2,1,0:T(8,128)(2,1)}, u32[]{:S(2)}, u32[]{:S(2)}) async-start(bf16[8,128,512]{2,1,0:T(8,128)(2,1)} %all-gather.5.cloned.1.call-done), calls=%async_computation.1 | async-start | bytes 2097152 | tf_op jit(solution)/shard_map/all_to_all | solution.py:205
  153.1 25.9 %collective-permute-start.14 = (bf16[128,2048]{1,0:T(8,128)(2,1)}, bf16[128,2048]{1,0:T(8,128)(2,1)}, u32[]{:S(2)}, u32[]{:S(2)}) collective-permute-start(bf16[128,2048]{1,0:T(8,128)(2,1)} %collective-permute-done.13.refs_10_), channel_id=1, source_target_pairs={{0,4},{4,0},{8,12},{12,8},{16,20},{20,16},{24,28},{28,24},{1,5},{5... | collective-permute-start | bytes 1572872 | tf_op jit(solution)/shard_map/ppermute | solution.py:18
  153.4 25.6 %collective-permute-start.9 = (bf16[128,2048]{1,0:T(8,128)(2,1)}, bf16[128,2048]{1,0:T(8,128)(2,1)}, u32[]{:S(2)}, u32[]{:S(2)}) collective-permute-start(bf16[128,2048]{1,0:T(8,128)(2,1)} %collective-permute-done.8.refs_4_), channel_id=1, source_target_pairs={{0,4},{4,0},{8,12},{12,8},{16,20},{20,16},{24,28},{28,24},{1,5},{5... | collective-permute-start | bytes 1572872 | tf_op jit(solution)/shard_map/ppermute | solution.py:18
  158.6 20.4 %collective-permute-start.7 = (bf16[128,2048]{1,0:T(8,128)(2,1)}, bf16[128,2048]{1,0:T(8,128)(2,1)}, u32[]{:S(2)}, u32[]{:S(2)}) collective-permute-start(bf16[128,2048]{1,0:T(8,128)(2,1)} %collective-permute-done.6.refs_2_), channel_id=1, source_target_pairs={{0,4},{4,0},{8,12},{12,8},{16,20},{20,16},{24,28},{28,24},{1,5},{5... | collective-permute-start | bytes 1572872 | tf_op jit(solution)/shard_map/ppermute | solution.py:18
  162.6 16.5 %collective-permute-start.18 = (bf16[128,2048]{1,0:T(8,128)(2,1)}, bf16[128,2048]{1,0:T(8,128)(2,1)}, u32[]{:S(2)}, u32[]{:S(2)}) collective-permute-start(bf16[128,2048]{1,0:T(8,128)(2,1)} %collective-permute-done.17.refs_14_), channel_id=1, source_target_pairs={{0,4},{4,0},{8,12},{12,8},{16,20},{20,16},{24,28},{28,24},{1,5},{5... | collective-permute-start | bytes 1572872 | tf_op jit(solution)/shard_map/ppermute | solution.py:18
  175.5 3.6 %collective-permute-start.11 = (bf16[128,2048]{1,0:T(8,128)(2,1)}, bf16[128,2048]{1,0:T(8,128)(2,1)}, u32[]{:S(2)}, u32[]{:S(2)}) collective-permute-start(bf16[128,2048]{1,0:T(8,128)(2,1)} %collective-permute-done.10.refs_6_), channel_id=1, source_target_pairs={{0,4},{4,0},{8,12},{12,8},{16,20},{20,16},{24,28},{28,24},{1,5},{5... | collective-permute-start | bytes 1572872 | tf_op jit(solution)/shard_map/ppermute | solution.py:18
  179.0 1.0 copy-start.4
  180.1 1.0 copy-start.7
  191.9 1.6 copy-start.5
  212.8 1.0 copy-start.2
  213.9 39.4 %all-to-all-start = ((bf16[4,512,256]{2,1,0:T(8,128)(2,1)}), bf16[4,512,256]{2,1,0:T(8,128)(2,1)S(1)}, u32[]{:S(2)}, u32[]{:S(2)}) async-start(bf16[4,512,256]{2,1,0:T(8,128)(2,1)} %bitcast.30), calls=%async_computation | async-start | bytes 2097152 | tf_op jit(solution)/shard_map/all_to_all | solution.py:212
  226.4 8.9 %copy-start.1 = (bf16[8,128,512]{2,1,0:T(8,128)(2,1)S(1)}, bf16[8,128,512]{2,1,0:T(8,128)(2,1)}, u32[]{:S(2)}) copy-start(bf16[8,128,512]{2,1,0:T(8,128)(2,1)} %copy-done) | copy-start | bytes 3145732
Sparse Core Ops, SparseCore 0:
  10.2 30.6 all-gather.10
  43.0 27.4 all-gather.8
  72.6 33.5 all-gather.6
  107.6 26.9 all-gather.4

commit v2 on v1

v2 whole, which is shorter than its diff:
```python
import functools

import jax
import jax.numpy as jnp
from jax import lax
from jax.experimental import pallas as pl
from jax.experimental.pallas import tpu as pltpu
from jax.sharding import PartitionSpec as P

CHUNKS = 4
PARTS = 4
MIB = 1024 * 1024
BF16 = jnp.bfloat16
F32 = jnp.float32


def flip(value, axis, mask):
    count = lax.axis_size(axis)
    return lax.ppermute(value, axis, [(i, i ^ mask) for i in range(count)])


def split_float(value):
    high = value.astype(BF16)
    low = (value - high.astype(F32)).astype(BF16)
    return high, low


def hr_kernel(scale, where_ref, cols_ref, y_ref, hr_ref, gram_ref, order_ref, high_ref, low_ref):
    @pl.when(pl.program_id(0) == 0)
    def _():
        count, tokens = y_ref.shape[:2]
        for mask in range(count):
            at = pl.multiple_of((where_ref[0] ^ mask) * tokens, tokens)
            order_ref[pl.ds(at, tokens), :] = y_ref[mask]
        y_high, y_low = split_float(order_ref[...].T)
        high_ref[...] = y_high
        low_ref[...] = y_low
        across = (((1,), (1,)), ((), ()))
        gram = lax.dot_general(y_high, y_high, across, preferred_element_type=F32)
        gram += lax.dot_general(y_high, y_low, across, preferred_element_type=F32)
        gram += lax.dot_general(y_low, y_high, across, preferred_element_type=F32)
        gram_ref[...] = gram * scale

    total = jnp.dot(high_ref[...], cols_ref[...], preferred_element_type=F32)
    total += jnp.dot(low_ref[...], cols_ref[...], preferred_element_type=F32)
    hr_ref[...] = (total * scale).astype(BF16)


def hr_and_gram(cols, y_blocks, where, scale):
    tokens, features = cols.shape
    rank = y_blocks.shape[2]
    tile = min(512, features)
    return pl.pallas_call(
        functools.partial(hr_kernel, scale),
        out_shape=(
            jax.ShapeDtypeStruct((rank, features), BF16),
            jax.ShapeDtypeStruct((rank, rank), F32),
        ),
        grid=(features // tile,),
        in_specs=[
            pl.BlockSpec(memory_space=pltpu.SMEM),
            pl.BlockSpec((tokens, tile), lambda j: (0, j)),
            pl.BlockSpec(y_blocks.shape, lambda j: (0, 0, 0)),
        ],
        out_specs=(
            pl.BlockSpec((rank, tile), lambda j: (0, j)),
            pl.BlockSpec((rank, rank), lambda j: (0, 0)),
        ),
        scratch_shapes=[
            pltpu.VMEM((tokens, rank), F32),
            pltpu.VMEM((rank, tokens), BF16),
            pltpu.VMEM((rank, tokens), BF16),
        ],
        compiler_params=pltpu.CompilerParams(vmem_limit_bytes=48 * MIB),
        name="hr_and_gram",
    )(where, cols, y_blocks)


def place_kernel(count, sources, where_ref, *refs):
    out_ref, sems = refs[-2:]
    me = where_ref[0]
    half = count // 2
    waits = []
    for mask in range(count):
        other = me ^ mask
        near, far = sources[mask]
        target = out_ref.at[other]

        def start(index, target=target, mask=mask):
            pltpu.make_async_copy(refs[index], target, sems.at[mask]).start()

        if far is None:
            start(near)
        elif near is None:
            start(far)
        else:
            close = jnp.abs(me - other) <= half
            pl.when(close)(functools.partial(start, near))
            pl.when(jnp.logical_not(close))(functools.partial(start, far))
        some = far if near is None else near
        waits.append(pltpu.make_async_copy(refs[some], target, sems.at[mask]))
    for wait in waits:
        wait.wait()


def place_blocks(blocks, sources, where, after):
    count = len(sources)
    return pl.pallas_call(
        functools.partial(place_kernel, count, sources),
        out_shape=jax.ShapeDtypeStruct((count,) + blocks[0].shape, BF16),
        in_specs=[pl.BlockSpec(memory_space=pltpu.SMEM)]
        + [pl.BlockSpec(memory_space=pl.ANY)] * (len(blocks) + len(after)),
        out_specs=pl.BlockSpec(memory_space=pl.ANY),
        scratch_shapes=[pltpu.SemaphoreType.DMA((count,))],
        name="place_blocks",
    )(where, *blocks, *after)


def exchange_blocks(mine):
    count = lax.axis_size("narrow")
    half = count // 2
    blocks = [mine]
    sources = [(0, None)]
    direct = {}
    order = sorted(range(1, count), key=lambda m: (m != half, m))
    for mask in order:
        pairs = [(i, i ^ mask) for i in range(count) if abs(i - (i ^ mask)) <= half]
        direct[mask] = lax.ppermute(mine, "narrow", pairs) if pairs else None
    for mask in range(1, count):
        near = far = None
        if direct[mask] is not None:
            near = len(blocks)
            blocks.append(direct[mask])
        pairs = [(i ^ half, i ^ mask) for i in range(count) if abs(i - (i ^ mask)) > half]
        if pairs:
            far = len(blocks)
            blocks.append(lax.ppermute(direct[half], "narrow", pairs))
        sources.append((near, far))
    return blocks, sources


def residual_kernel(weight_ref, codes_ref, scales_ref, *refs):
    out_ref = refs[-1]
    groups = scales_ref.shape[1]
    width = weight_ref.shape[1] // groups
    scales = scales_ref[...]
    for group in range(groups):
        at = slice(group * width, (group + 1) * width)
        quantized = codes_ref[:, at].astype(F32) * scales[:, group : group + 1]
        out_ref[:, at] = (weight_ref[:, at].astype(F32) - quantized).astype(BF16)


def residual_part(weight, codes, scales, earlier, index, count, after):
    rows, features = weight.shape
    block = min(64, rows // count)
    steps = rows // count // block
    place = lambda i: (index * steps + i, 0)
    ins = [weight, codes, scales]
    specs = [
        pl.BlockSpec((block, features), place),
        pl.BlockSpec((block, features), place),
        pl.BlockSpec((block, scales.shape[1]), place),
    ]
    aliases = {}
    if earlier is not None:
        aliases = {len(ins): 0}
        ins.append(earlier)
        specs.append(pl.BlockSpec(memory_space=pl.ANY))
    for value in after:
        ins.append(value)
        specs.append(pl.BlockSpec(memory_space=pl.ANY))
    return pl.pallas_call(
        residual_kernel,
        out_shape=jax.ShapeDtypeStruct((rows, features), BF16),
        grid=(steps,),
        in_specs=specs,
        out_specs=pl.BlockSpec((block, features), place),
        input_output_aliases=aliases,
        compiler_params=pltpu.CompilerParams(vmem_limit_bytes=48 * MIB),
        name="residual_part",
    )(*ins)


def product_kernel(residual_ref, hr_ref, out_ref):
    out_ref[...] = lax.dot_general(
        residual_ref[...], hr_ref[...], (((1,), (1,)), ((), ())), preferred_element_type=F32
    ).astype(BF16)


def partial_product(residual, hr):
    rows, features = residual.shape
    rank = hr.shape[0]
    block = min(256, rows)
    return pl.pallas_call(
        product_kernel,
        out_shape=jax.ShapeDtypeStruct((rows, rank), BF16),
        grid=(rows // block,),
        in_specs=[
            pl.BlockSpec((block, features), lambda i: (i, 0)),
            pl.BlockSpec((rank, features), lambda i: (0, 0)),
        ],
        out_specs=pl.BlockSpec((block, rank), lambda i: (i, 0)),
        compiler_params=pltpu.CompilerParams(vmem_limit_bytes=48 * MIB),
        name="partial_product",
    )(residual, hr)


def hessian_kernel(scale, rows_ref, cols_ref, *refs):
    out_ref, turned_ref = refs[-2:]

    @pl.when(pl.program_id(0) == 0)
    def _():
        turned_ref[...] = rows_ref[...].T

    total = jnp.dot(turned_ref[...], cols_ref[...], preferred_element_type=F32)
    out_ref[...] = (total * scale).astype(BF16)


def hessian_rows(rows, cols, earlier, index, shape, scale):
    tokens, height = rows.shape
    tile = min(1024, cols.shape[1])
    ins = [rows, cols]
    specs = [
        pl.BlockSpec((tokens, height), lambda j: (0, 0)),
        pl.BlockSpec((tokens, tile), lambda j: (0, j)),
    ]
    aliases = {}
    if earlier is not None:
        ins.append(earlier)
        specs.append(pl.BlockSpec(memory_space=pl.ANY))
        aliases = {2: 0}
    return pl.pallas_call(
        functools.partial(hessian_kernel, scale),
        out_shape=jax.ShapeDtypeStruct(shape, BF16),
        grid=(cols.shape[1] // tile,),
        in_specs=specs,
        out_specs=pl.BlockSpec((height, tile), lambda j: (index, j)),
        scratch_shapes=[pltpu.VMEM((height, tokens), BF16)],
        input_output_aliases=aliases,
        compiler_params=pltpu.CompilerParams(vmem_limit_bytes=48 * MIB),
        name="hessian_rows",
    )(*ins)


def body(activations, weight_tile, codes, group_scales, right_factor):
    wide_count = lax.axis_size("wide")
    narrow_count = lax.axis_size("narrow")
    narrow_index = lax.axis_index("narrow")
    tokens, features = activations.shape
    rows = weight_tile.shape[0]
    rank = right_factor.shape[1]
    split = features // rows
    scale = 1.0 / (tokens * wide_count)

    cols = lax.all_gather(activations, "wide", axis=0, tiled=True)

    height = rows // CHUNKS
    chunks = []
    for chunk in range(CHUNKS):
        mine = jnp.stack(
            [
                activations[:, s * rows + chunk * height : s * rows + (chunk + 1) * height]
                for s in range(split)
            ]
        )
        chunks.append(exchange_blocks(mine))

    right_block = lax.dynamic_slice_in_dim(right_factor, narrow_index * features, features, 0)
    product = jnp.dot(activations, right_block, preferred_element_type=F32)
    mask = 1
    while mask < narrow_count:
        product = product + flip(product, "narrow", mask)
        mask *= 2
    y_blocks = product[None]
    mask = 1
    while mask < wide_count:
        y_blocks = jnp.concatenate([y_blocks, flip(y_blocks, "wide", mask)], axis=0)
        mask *= 2

    residual = None
    for part in range(PARTS):
        residual = residual_part(
            weight_tile, codes, group_scales, residual, part, PARTS, [product] if part == 1 else []
        )

    where = narrow_index.astype(jnp.int32).reshape(1)
    row_chunks = []
    for chunk in range(CHUNKS):
        blocks, sources = chunks[chunk]
        after = [residual] if chunk == 0 else []
        every = place_blocks(blocks, sources, where, after)
        every = every.reshape(narrow_count * split, tokens, height)
        chunk_rows = lax.all_to_all(every, "wide", split_axis=0, concat_axis=0, tiled=True)
        row_chunks.append(chunk_rows.reshape(tokens * wide_count, height))

    hr, gram = hr_and_gram(cols, y_blocks, lax.axis_index("wide").astype(jnp.int32).reshape(1), scale)
    shares = partial_product(residual, hr)
    shares = shares.reshape(narrow_count, rows // narrow_count, rank)
    shares = lax.all_to_all(shares, "narrow", split_axis=0, concat_axis=0, tiled=True)
    residual_product = jnp.sum(shares.astype(F32), axis=0)

    hessian = None
    for chunk in range(CHUNKS):
        hessian = hessian_rows(row_chunks[chunk], cols, hessian, chunk, (rows, features), scale)
    return residual_product, gram, hessian


def solution(mesh):
    in_specs = (
        P("wide", "narrow"),
        P("wide", "narrow"),
        P("wide", "narrow"),
        P("wide", "narrow"),
        P(),
    )
    out_specs = (P(("wide", "narrow"), None), P(), P("wide", "narrow"))
    return jax.shard_map(body, mesh=mesh, in_specs=in_specs, out_specs=out_specs, check_vma=False)
```

time: 262 us -> 405 us (1.55)
  Pallas kernels: 65.7 us -> 227 us
  waiting for transfers between devices: 128 us -> 92.8 us
  starting transfers between devices: 31.3 us -> 54.8 us
  local copies, waits for them, and re-layouts: 11.1 us -> 4.1 us
    pallas_call x2 -> x10, Pallas kernels: 30.1 us -> 192 us  [the longest x4 132 us: place_blocks(): pl.pallas_call(functools.partial(place_kernel, count, sources), out_shape...]
    all_gather x4 -> x1, waiting for transfers between devices: 57.8 us -> 0.02 us  [body(): cols = lax.all_gather(activations, 'wide', axis=0, tiled=True)]
    ppermute x0 -> x16, waiting for transfers between devices: none -> 54.9 us  [the longest x12 31.5 us: exchange_blocks(): direct[mask] = lax.ppermute(mine, 'narrow', pairs) if pairs else None]
    ppermute x19 -> x5, waiting for transfers between devices: 70.1 us -> 37.2 us  [flip(): return lax.ppermute(value, axis, [(i, i ^ mask) for i in range(count)])]
    ppermute x0 -> x16, starting transfers between devices: none -> 27.4 us  [the longest x12 22.3 us: exchange_blocks(): direct[mask] = lax.ppermute(mine, 'narrow', pairs) if pairs else None]
    ppermute x19 -> x5, starting transfers between devices: 12.3 us -> 6.62 us  [flip(): return lax.ppermute(value, axis, [(i, i ^ mask) for i in range(count)])]
    unnamed x19 -> x37, local copies, waits for them, and re-layouts: 7.6 us -> 2.72 us
  transfers between devices with their start and end apart: 28 -> 27, of which waited for: 12 -> 9; matrix products, arithmetic and copies ran while one was open for 5% -> 2% of each run, Pallas kernels for 25% -> 56%
where the time goes in v2:
time: 405 us; the launch traced here: 403 us
  Pallas kernels  227 us (56%)
  waiting for transfers between devices  92.8 us (23%)
  starting transfers between devices  54.8 us (14%)
  between operations  14.5 us (4%)
  other arithmetic  6.75 us (2%)
  local copies, waits for them, and re-layouts  4.1 us (1%)
    pallas_call x4, Pallas kernels, place_blocks(): pl.pallas_call(functools.partial(place_kernel, count, sources), out_shape...  132 us
    pallas_call x4, Pallas kernels, residual_part(): pl.pallas_call(residual_kernel, out_shape=jax.ShapeDtypeStruct((rows, fea...  38.7 us
    ppermute x5, waiting for transfers between devices, flip(): return lax.ppermute(value, axis, [(i, i ^ mask) for i in range(count)])  37.2 us
    pallas_call x4, Pallas kernels, hessian_rows(): pl.pallas_call(functools.partial(hessian_kernel, scale), out_shape=jax.Sh...  35.4 us
    ppermute x12, waiting for transfers between devices, exchange_blocks(): direct[mask] = lax.ppermute(mine, 'narrow', pairs) if pairs else None  31.5 us
    ppermute x4, waiting for transfers between devices, exchange_blocks(): blocks.append(lax.ppermute(direct[half], 'narrow', pairs))  23.3 us
    ppermute x12, starting transfers between devices, exchange_blocks(): direct[mask] = lax.ppermute(mine, 'narrow', pairs) if pairs else None  22.3 us
    all_to_all x4, starting transfers between devices, body(): lax.all_to_all(every, 'wide', split_axis=0, concat_axis=0, tiled=True)  14.5 us
  transfers between devices with their start and end apart: 27, of which 9 were waited for; matrix products, arithmetic and copies ran while one was open for 2% of the time, Pallas kernels for 56%

profile of v2, /device:TPU:0, one launch (start us, length us, event | category | flops | bytes accessed | tf_op | source)
XLA Modules:
  0.0 402.7 jit_solution(9486651310000072069)
XLA Ops:
  7.2 0.0 all-gather.2.cloned.1.call-start
  7.2 0.7 all-gather.2.cloned.1.call-update
  7.9 1.4 slice_bitcast_fusion.1
  9.3 4.1 %collective-permute-start.6 = (bf16[2,128,512]{2,1,0:T(8,128)(2,1)S(1)}, bf16[2,128,512]{2,1,0:T(8,128)(2,1)S(1)}, u32[]{:S(2)}, u32[]{:S(2)}) collective-permute-start(bf16[2,128,512]{2,1,0:T(8,128)(2,1)S(1)} %pad_maximum_fusion.3.refs_0_), channel_id=1, source_target_pairs={{0,2},{1,3},{2,0},{3,1},{4,6},{5,7},{6,4},{7,5},{8,10},{9,11},{10,... | collective-permute-start | bytes 786440 | tf_op jit(solution)/shard_map/ppermute | solution.py:128
  13.4 1.6 collective-permute-start.5
  15.0 0.7 collective-permute-start.7
  15.7 10.5 %collective-permute-done.6.refs_2_ = bf16[2,128,512]{2,1,0:T(8,128)(2,1)S(1)} collective-permute-done((bf16[2,128,512]{2,1,0:T(8,128)(2,1)S(1)}, bf16[2,128,512]{2,1,0:T(8,128)(2,1)S(1)}, u32[]{:S(2)}, u32[]{:S(2)}) %collective-permute-start.6) | collective-permute-done | bytes 262176 | tf_op jit(solution)/shard_map/ppermute | solution.py:128
  26.2 1.3 collective-permute-start.8
  27.6 7.2 %collective-permute-done.8.refs_4_ = bf16[2,128,512]{2,1,0:T(8,128)(2,1)S(1)} collective-permute-done((bf16[2,128,512]{2,1,0:T(8,128)(2,1)S(1)}, bf16[2,128,512]{2,1,0:T(8,128)(2,1)S(1)}, u32[]{:S(2)}, u32[]{:S(2)}) %collective-permute-start.8) | collective-permute-done | bytes 262176 | tf_op jit(solution)/shard_map/ppermute | solution.py:137
  34.8 0.7 copy-done.16
  35.5 32.9 %place_blocks.4 = bf16[4,2,128,512]{3,2,1,0:T(8,128)(2,1)} custom-call(s32[1]{0:T(128)} %bitcast.4.where_ref, bf16[2,128,512]{2,1,0:T(8,128)(2,1)} %copy-done.4, bf16[2,128,512]{2,1,0:T(8,128)(2,1)} %copy-done.8, bf16[2,128,512]{2,1,0:T(8,128)(2,1)} %copy-done.7, bf16[2,128,512]{2,1,0:T(8,128)(2,1)} %copy-done.11, bf16[2,128,512]{2,1,0:T(8,128)(2,1)} %copy-done.16), custom_call_target="tpu_custom_call" | custom-call | tf_op jit(solution)/shard_map/place_blocks/pallas_call | solution.py:108
  68.4 3.8 all-to-all-start.1
  72.2 0.0 copy-start.5
  72.2 2.3 collective-permute-start.10
  74.5 2.5 collective-permute-start.9
  77.0 0.7 collective-permute-start.11
  77.7 10.2 %collective-permute-done.10.refs_2_ = bf16[2,128,512]{2,1,0:T(8,128)(2,1)S(1)} collective-permute-done((bf16[2,128,512]{2,1,0:T(8,128)(2,1)S(1)}, bf16[2,128,512]{2,1,0:T(8,128)(2,1)S(1)}, u32[]{:S(2)}, u32[]{:S(2)}) %collective-permute-start.10) | collective-permute-done | bytes 262176 | tf_op jit(solution)/shard_map/ppermute | solution.py:128
  87.9 1.3 collective-permute-start.12
  89.2 0.0 copy-start.12
  89.3 8.1 %collective-permute-done.12.refs_4_ = bf16[2,128,512]{2,1,0:T(8,128)(2,1)S(1)} collective-permute-done((bf16[2,128,512]{2,1,0:T(8,128)(2,1)S(1)}, bf16[2,128,512]{2,1,0:T(8,128)(2,1)S(1)}, u32[]{:S(2)}, u32[]{:S(2)}) %collective-permute-start.12) | collective-permute-done | bytes 262176 | tf_op jit(solution)/shard_map/ppermute | solution.py:137
  97.4 0.7 copy-done.17
  98.1 32.9 %place_blocks.5 = bf16[4,2,128,512]{3,2,1,0:T(8,128)(2,1)} custom-call(s32[1]{0:T(128)} %bitcast.4.where_ref, bf16[2,128,512]{2,1,0:T(8,128)(2,1)} %copy-done.5, bf16[2,128,512]{2,1,0:T(8,128)(2,1)} %copy-done.12, bf16[2,128,512]{2,1,0:T(8,128)(2,1)} %copy-done.9, bf16[2,128,512]{2,1,0:T(8,128)(2,1)} %copy-done.14, bf16[2,128,512]{2,1,0:T(8,128)(2,1)} %copy-done.17), custom_call_target="tpu_custom_call" | custom-call | tf_op jit(solution)/shard_map/place_blocks/pallas_call | solution.py:108
  131.0 3.6 all-to-all-start.2
  134.6 1.9 collective-permute-start.14
  136.5 2.5 collective-permute-start.13
  139.0 0.7 collective-permute-start.15
  139.7 10.7 %collective-permute-done.14.refs_2_ = bf16[2,128,512]{2,1,0:T(8,128)(2,1)S(1)} collective-permute-done((bf16[2,128,512]{2,1,0:T(8,128)(2,1)S(1)}, bf16[2,128,512]{2,1,0:T(8,128)(2,1)S(1)}, u32[]{:S(2)}, u32[]{:S(2)}) %collective-permute-start.14) | collective-permute-done | bytes 262176 | tf_op jit(solution)/shard_map/ppermute | solution.py:128
  150.4 1.3 collective-permute-start.16
  151.7 8.0 %collective-permute-done.16.refs_4_ = bf16[2,128,512]{2,1,0:T(8,128)(2,1)} collective-permute-done((bf16[2,128,512]{2,1,0:T(8,128)(2,1)S(1)}, bf16[2,128,512]{2,1,0:T(8,128)(2,1)}, u32[]{:S(2)}, u32[]{:S(2)}) %collective-permute-start.16) | collective-permute-done | bytes 262176 | tf_op jit(solution)/shard_map/ppermute | solution.py:137
  159.8 32.9 %place_blocks.6 = bf16[4,2,128,512]{3,2,1,0:T(8,128)(2,1)} custom-call(s32[1]{0:T(128)} %bitcast.4.where_ref, bf16[2,128,512]{2,1,0:T(8,128)(2,1)} %copy-done.6, bf16[2,128,512]{2,1,0:T(8,128)(2,1)} %copy-done.13, bf16[2,128,512]{2,1,0:T(8,128)(2,1)} %copy-done.10, bf16[2,128,512]{2,1,0:T(8,128)(2,1)} %copy-done.15, ...), custom_call_target="tpu_custom_call" | custom-call | tf_op jit(solution)/shard_map/place_blocks/pallas_call | solution.py:108
  192.7 3.6 all-to-all-start.3
  196.3 2.4 fusion.2
  198.7 0.1 collective-permute-start
  198.7 0.7 pad_maximum_fusion.6.refs_0_
  199.5 4.0 collective-permute-start.18
  203.5 1.1 collective-permute-done
  204.6 2.9 collective-permute-start.1
  207.5 14.1 %collective-permute-done.1 = f32[128,256]{1,0:T(8,128)S(1)} collective-permute-done((f32[128,256]{1,0:T(8,128)S(1)}, f32[128,256]{1,0:T(8,128)S(1)}, u32[]{:S(2)}, u32[]{:S(2)}) %collective-permute-start.1) | collective-permute-done | bytes 131104 | tf_op jit(solution)/shard_map/ppermute | solution.py:19
  221.6 0.1 collective-permute-start.2
  221.7 0.1 collective-permute-start.17
  221.8 1.4 collective-permute-start.19
  223.2 1.3 collective-permute-start.20
  224.5 0.7 pad_maximum_fusion.2
  225.2 1.7 collective-permute-start.3
  226.9 1.3 copy.18.scales_ref
  228.2 9.7 %residual_part.4.refs_0_ = bf16[2048,4096]{1,0:T(8,128)(2,1)} custom-call(bf16[2048,4096]{1,0:T(8,128)(2,1)} %weight_ref.7, s32[2048,4096]{1,0:T(8,128)} %codes_ref.7, f32[2048,32]{1,0:T(8,128)S(1)} %copy.18.scales_ref), custom_call_target="tpu_custom_call" | custom-call | tf_op jit(solution)/shard_map/residual_part/pallas_call | solution.py:172
  237.8 9.7 %residual_part.5.refs_0_ = bf16[2048,4096]{1,0:T(8,128)(2,1)} custom-call(bf16[2048,4096]{1,0:T(8,128)(2,1)} %weight_ref.7, s32[2048,4096]{1,0:T(8,128)} %codes_ref.7, f32[2048,32]{1,0:T(8,128)S(1)} %copy.18.scales_ref, bf16[2048,4096]{1,0:T(8,128)(2,1)} %residual_part.4.refs_0_, f32[128,256]{1,0:T(8,128)S(1)} %add.11.refs_1_), custom_call_target="tpu_custom_call", output_to_operand_aliasing={{}: (3, {})} | custom-call | tf_op jit(solution)/shard_map/residual_part/pallas_call | solution.py:172
  247.5 9.7 %residual_part.6.refs_0_ = bf16[2048,4096]{1,0:T(8,128)(2,1)} custom-call(bf16[2048,4096]{1,0:T(8,128)(2,1)} %weight_ref.7, s32[2048,4096]{1,0:T(8,128)} %codes_ref.7, f32[2048,32]{1,0:T(8,128)S(1)} %copy.18.scales_ref, bf16[2048,4096]{1,0:T(8,128)(2,1)} %residual_part.5.refs_0_), custom_call_target="tpu_custom_call", output_to_operand_aliasing={{}: (3, {})} | custom-call | tf_op jit(solution)/shard_map/residual_part/pallas_call | solution.py:172
  257.2 9.7 %residual_part.7.residual_ref.refs_5_ = bf16[2048,4096]{1,0:T(8,128)(2,1)} custom-call(bf16[2048,4096]{1,0:T(8,128)(2,1)} %weight_ref.7, s32[2048,4096]{1,0:T(8,128)} %codes_ref.7, f32[2048,32]{1,0:T(8,128)S(1)} %copy.18.scales_ref, bf16[2048,4096]{1,0:T(8,128)(2,1)} %residual_part.6.refs_0_), custom_call_target="tpu_custom_call", output_to_operand_aliasing={{}: (3, {})} | custom-call | tf_op jit(solution)/shard_map/residual_part/pallas_call | solution.py:172
  266.9 32.9 %place_blocks.7 = bf16[4,2,128,512]{3,2,1,0:T(8,128)(2,1)} custom-call(s32[1]{0:T(128)} %bitcast.4.where_ref, bf16[2,128,512]{2,1,0:T(8,128)(2,1)} %pad_maximum_fusion.6.refs_0_, bf16[2,128,512]{2,1,0:T(8,128)(2,1)} %collective-permute-done.17.refs_1_, bf16[2,128,512]{2,1,0:T(8,128)(2,1)} %collective-permute-done.18.refs_2_, ...), custom_call_target="tpu_custom_call" | custom-call | tf_op jit(solution)/shard_map/place_blocks/pallas_call | solution.py:108
  299.8 3.6 all-to-all-start.4
  303.4 1.8 pad_maximum_fusion.1
  305.2 1.9 collective-permute-start.4
  307.1 22.0 %collective-permute-done.4 = f32[4,128,256]{2,1,0:T(8,128)} collective-permute-done((f32[4,128,256]{2,1,0:T(8,128)}, f32[4,128,256]{2,1,0:T(8,128)}, u32[]{:S(2)}, u32[]{:S(2)}) %collective-permute-start.4) | collective-permute-done | bytes 524320 | tf_op jit(solution)/shard_map/ppermute | solution.py:19
  329.1 1.2 pad_maximum_fusion.y_ref
  330.3 0.0 all-gather.2.cloned.1.call-done.cols_ref
  330.3 10.4 %hr_and_gram.1 = (bf16[256,4096]{1,0:T(8,128)(2,1)S(1)}, f32[256,256]{1,0:T(8,128)}) custom-call(s32[1]{0:T(128)} %bitcast.1.where_ref, bf16[1024,4096]{1,0:T(8,128)(2,1)} %all-gather.2.cloned.1.call-done.cols_ref, f32[8,128,256]{2,1,0:T(8,128)S(1)} %pad_maximum_fusion.y_ref), custom_call_target="tpu_custom_call" | custom-call | tf_op jit(solution)/shard_map/hr_and_gram/pallas_call | solution.py:53
  340.7 11.4 %partial_product.1 = bf16[2048,256]{1,0:T(8,128)(2,1)} custom-call(bf16[2048,4096]{1,0:T(8,128)(2,1)} %residual_part.7.residual_ref.refs_5_, bf16[256,4096]{1,0:T(8,128)(2,1)S(1)} %get-tuple-element.5.hr_ref), custom_call_target="tpu_custom_call" | custom-call | tf_op jit(solution)/shard_map/partial_product/pallas_call | solution.py:194
  352.1 6.2 %all-to-all-start = ((bf16[4,512,256]{2,1,0:T(8,128)(2,1)}), bf16[4,512,256]{2,1,0:T(8,128)(2,1)}, u32[]{:S(2)}, u32[]{:S(2)}) async-start(bf16[4,512,256]{2,1,0:T(8,128)(2,1)} %bitcast.3), calls=%async_computation | async-start | bytes 2097152 | tf_op jit(solution)/shard_map/all_to_all | solution.py:299
  358.2 8.8 %hessian_rows.4.refs_0_ = bf16[2048,4096]{1,0:T(8,128)(2,1)} custom-call(bf16[1024,512]{1,0:T(8,128)(2,1)S(1)} %bitcast.31, bf16[1024,4096]{1,0:T(8,128)(2,1)} %all-gather.2.cloned.1.call-done.cols_ref), custom_call_target="tpu_custom_call" | custom-call | tf_op jit(solution)/shard_map/hessian_rows/pallas_call | solution.py:232
  367.1 8.9 %hessian_rows.5.refs_0_ = bf16[2048,4096]{1,0:T(8,128)(2,1)} custom-call(bf16[1024,512]{1,0:T(8,128)(2,1)S(1)} %bitcast.34, bf16[1024,4096]{1,0:T(8,128)(2,1)} %all-gather.2.cloned.1.call-done.cols_ref, bf16[2048,4096]{1,0:T(8,128)(2,1)} %hessian_rows.4.refs_0_), custom_call_target="tpu_custom_call", output_to_operand_aliasing={{}: (2, {})} | custom-call | tf_op jit(solution)/shard_map/hessian_rows/pallas_call | solution.py:232
  376.0 8.8 %hessian_rows.6.refs_0_ = bf16[2048,4096]{1,0:T(8,128)(2,1)} custom-call(bf16[1024,512]{1,0:T(8,128)(2,1)S(1)} %bitcast.33, bf16[1024,4096]{1,0:T(8,128)(2,1)} %all-gather.2.cloned.1.call-done.cols_ref, bf16[2048,4096]{1,0:T(8,128)(2,1)} %hessian_rows.5.refs_0_), custom_call_target="tpu_custom_call", output_to_operand_aliasing={{}: (2, {})} | custom-call | tf_op jit(solution)/shard_map/hessian_rows/pallas_call | solution.py:232
  384.8 8.8 %hessian_rows.7 = bf16[2048,4096]{1,0:T(8,128)(2,1)} custom-call(bf16[1024,512]{1,0:T(8,128)(2,1)S(1)} %bitcast.32, bf16[1024,4096]{1,0:T(8,128)(2,1)} %all-gather.2.cloned.1.call-done.cols_ref, bf16[2048,4096]{1,0:T(8,128)(2,1)} %hessian_rows.6.refs_0_), custom_call_target="tpu_custom_call", output_to_operand_aliasing={{}: (2, {})} | custom-call | tf_op jit(solution)/shard_map/hessian_rows/pallas_call | solution.py:232
  393.6 2.2 convert_reduce_fusion
  (54 shorter events, 0.2 us)
Async XLA Ops:
  7.2 323.2 %all-gather.2.cloned.1.call-start = ((), (), s32[]{:S(2)}) async-start(), calls=%async_computation.5 | async-start | bytes 9437184 | tf_op jit(solution)/shard_map/all_gather | solution.py:255
  9.3 25.5 %copy-start.4 = (bf16[2,128,512]{2,1,0:T(8,128)(2,1)}, bf16[2,128,512]{2,1,0:T(8,128)(2,1)S(1)}, u32[]{:S(2)}) copy-start(bf16[2,128,512]{2,1,0:T(8,128)(2,1)S(1)} %pad_maximum_fusion.3.refs_0_) | copy-start | bytes 786436
  9.3 16.9 %collective-permute-start.6 = (bf16[2,128,512]{2,1,0:T(8,128)(2,1)S(1)}, bf16[2,128,512]{2,1,0:T(8,128)(2,1)S(1)}, u32[]{:S(2)}, u32[]{:S(2)}) collective-permute-start(bf16[2,128,512]{2,1,0:T(8,128)(2,1)S(1)} %pad_maximum_fusion.3.refs_0_), channel_id=1, source_target_pairs={{0,2},{1,3},{2,0},{3,1},{4,6},{5,7},{6,4},{7,5},{8,10},{9,11},{10,... | collective-permute-start | bytes 786440 | tf_op jit(solution)/shard_map/ppermute | solution.py:128
  13.4 14.1 %collective-permute-start.5 = (bf16[2,128,512]{2,1,0:T(8,128)(2,1)S(1)}, bf16[2,128,512]{2,1,0:T(8,128)(2,1)S(1)}, u32[]{:S(2)}, u32[]{:S(2)}) collective-permute-start(bf16[2,128,512]{2,1,0:T(8,128)(2,1)S(1)} %pad_maximum_fusion.3.refs_0_), channel_id=1, source_target_pairs={{0,1},{1,0},{2,3},{3,2},{4,5},{5,4},{6,7},{7,6},{8,9},{9,8},{10,11... | collective-permute-start | bytes 786440 | tf_op jit(solution)/shard_map/ppermute | solution.py:128
  15.0 12.5 %collective-permute-start.7 = (bf16[2,128,512]{2,1,0:T(8,128)(2,1)S(1)}, bf16[2,128,512]{2,1,0:T(8,128)(2,1)S(1)}, u32[]{:S(2)}, u32[]{:S(2)}) collective-permute-start(bf16[2,128,512]{2,1,0:T(8,128)(2,1)S(1)} %pad_maximum_fusion.3.refs_0_), channel_id=1, source_target_pairs={{1,2},{2,1},{5,6},{6,5},{9,10},{10,9},{13,14},{14,13},{17,18},{18,... | collective-permute-start | bytes 786440 | tf_op jit(solution)/shard_map/ppermute | solution.py:128
  26.2 8.6 %copy-start.7 = (bf16[2,128,512]{2,1,0:T(8,128)(2,1)}, bf16[2,128,512]{2,1,0:T(8,128)(2,1)S(1)}, u32[]{:S(2)}) copy-start(bf16[2,128,512]{2,1,0:T(8,128)(2,1)S(1)} %collective-permute-done.6.refs_2_) | copy-start | bytes 786436
  26.2 8.5 %collective-permute-start.8 = (bf16[2,128,512]{2,1,0:T(8,128)(2,1)S(1)}, bf16[2,128,512]{2,1,0:T(8,128)(2,1)S(1)}, u32[]{:S(2)}, u32[]{:S(2)}) collective-permute-start(bf16[2,128,512]{2,1,0:T(8,128)(2,1)S(1)} %collective-permute-done.6.refs_2_), channel_id=1, source_target_pairs={{2,3},{1,0},{6,7},{5,4},{10,11},{9,8},{14,15},{13,12},{18,19},{17,... | collective-permute-start | bytes 786440 | tf_op jit(solution)/shard_map/ppermute | solution.py:137
  27.5 7.3 %copy-start.8 = (bf16[2,128,512]{2,1,0:T(8,128)(2,1)}, bf16[2,128,512]{2,1,0:T(8,128)(2,1)S(1)}, u32[]{:S(2)}) copy-start(bf16[2,128,512]{2,1,0:T(8,128)(2,1)S(1)} %collective-permute-done.5.refs_1_) | copy-start | bytes 786436
  27.6 7.2 %copy-start.11 = (bf16[2,128,512]{2,1,0:T(8,128)(2,1)}, bf16[2,128,512]{2,1,0:T(8,128)(2,1)S(1)}, u32[]{:S(2)}) copy-start(bf16[2,128,512]{2,1,0:T(8,128)(2,1)S(1)} %collective-permute-done.7.refs_3_) | copy-start | bytes 786436
  34.8 0.7 copy-start.16
  68.4 62.6 %all-to-all-start.1 = ((bf16[8,128,512]{2,1,0:T(8,128)(2,1)}), bf16[8,128,512]{2,1,0:T(8,128)(2,1)S(1)}, u32[]{:S(2)}, u32[]{:S(2)}) async-start(bf16[8,128,512]{2,1,0:T(8,128)(2,1)} %bitcast.42), calls=%async_computation.1 | async-start | bytes 2097152 | tf_op jit(solution)/shard_map/all_to_all | solution.py:293
  72.2 25.2 %copy-start.5 = (bf16[2,128,512]{2,1,0:T(8,128)(2,1)}, bf16[2,128,512]{2,1,0:T(8,128)(2,1)S(1)}, u32[]{:S(2)}) copy-start(bf16[2,128,512]{2,1,0:T(8,128)(2,1)S(1)} %pad_maximum_fusion.4.refs_0_) | copy-start | bytes 786436
  72.2 15.7 %collective-permute-start.10 = (bf16[2,128,512]{2,1,0:T(8,128)(2,1)S(1)}, bf16[2,128,512]{2,1,0:T(8,128)(2,1)S(1)}, u32[]{:S(2)}, u32[]{:S(2)}) collective-permute-start(bf16[2,128,512]{2,1,0:T(8,128)(2,1)S(1)} %pad_maximum_fusion.4.refs_0_), channel_id=1, source_target_pairs={{0,2},{1,3},{2,0},{3,1},{4,6},{5,7},{6,4},{7,5},{8,10},{9,11},{10,... | collective-permute-start | bytes 786440 | tf_op jit(solution)/shard_map/ppermute | solution.py:128
  74.5 14.7 %collective-permute-start.9 = (bf16[2,128,512]{2,1,0:T(8,128)(2,1)S(1)}, bf16[2,128,512]{2,1,0:T(8,128)(2,1)S(1)}, u32[]{:S(2)}, u32[]{:S(2)}) collective-permute-start(bf16[2,128,512]{2,1,0:T(8,128)(2,1)S(1)} %pad_maximum_fusion.4.refs_0_), channel_id=1, source_target_pairs={{0,1},{1,0},{2,3},{3,2},{4,5},{5,4},{6,7},{7,6},{8,9},{9,8},{10,11... | collective-permute-start | bytes 786440 | tf_op jit(solution)/shard_map/ppermute | solution.py:128
  77.0 12.2 %collective-permute-start.11 = (bf16[2,128,512]{2,1,0:T(8,128)(2,1)S(1)}, bf16[2,128,512]{2,1,0:T(8,128)(2,1)S(1)}, u32[]{:S(2)}, u32[]{:S(2)}) collective-permute-start(bf16[2,128,512]{2,1,0:T(8,128)(2,1)S(1)} %pad_maximum_fusion.4.refs_0_), channel_id=1, source_target_pairs={{1,2},{2,1},{5,6},{6,5},{9,10},{10,9},{13,14},{14,13},{17,18},{18,... | collective-permute-start | bytes 786440 | tf_op jit(solution)/shard_map/ppermute | solution.py:128
  87.9 9.4 %copy-start.9 = (bf16[2,128,512]{2,1,0:T(8,128)(2,1)}, bf16[2,128,512]{2,1,0:T(8,128)(2,1)S(1)}, u32[]{:S(2)}) copy-start(bf16[2,128,512]{2,1,0:T(8,128)(2,1)S(1)} %collective-permute-done.10.refs_2_) | copy-start | bytes 786436
  87.9 9.4 %collective-permute-start.12 = (bf16[2,128,512]{2,1,0:T(8,128)(2,1)S(1)}, bf16[2,128,512]{2,1,0:T(8,128)(2,1)S(1)}, u32[]{:S(2)}, u32[]{:S(2)}) collective-permute-start(bf16[2,128,512]{2,1,0:T(8,128)(2,1)S(1)} %collective-permute-done.10.refs_2_), channel_id=1, source_target_pairs={{2,3},{1,0},{6,7},{5,4},{10,11},{9,8},{14,15},{13,12},{18,19},{17,... | collective-permute-start | bytes 786440 | tf_op jit(solution)/shard_map/ppermute | solution.py:137
  89.2 8.1 %copy-start.12 = (bf16[2,128,512]{2,1,0:T(8,128)(2,1)}, bf16[2,128,512]{2,1,0:T(8,128)(2,1)S(1)}, u32[]{:S(2)}) copy-start(bf16[2,128,512]{2,1,0:T(8,128)(2,1)S(1)} %collective-permute-done.9.refs_1_) | copy-start | bytes 786436
  89.3 8.1 %copy-start.14 = (bf16[2,128,512]{2,1,0:T(8,128)(2,1)}, bf16[2,128,512]{2,1,0:T(8,128)(2,1)S(1)}, u32[]{:S(2)}) copy-start(bf16[2,128,512]{2,1,0:T(8,128)(2,1)S(1)} %collective-permute-done.11.refs_3_) | copy-start | bytes 786436
  97.4 0.7 copy-start.17
  131.0 61.7 %all-to-all-start.2 = ((bf16[8,128,512]{2,1,0:T(8,128)(2,1)}), bf16[8,128,512]{2,1,0:T(8,128)(2,1)S(1)}, u32[]{:S(2)}, u32[]{:S(2)}) async-start(bf16[8,128,512]{2,1,0:T(8,128)(2,1)} %bitcast.41), calls=%async_computation.2 | async-start | bytes 2097152 | tf_op jit(solution)/shard_map/all_to_all | solution.py:293
  134.6 25.1 %copy-start.6 = (bf16[2,128,512]{2,1,0:T(8,128)(2,1)}, bf16[2,128,512]{2,1,0:T(8,128)(2,1)S(1)}, u32[]{:S(2)}) copy-start(bf16[2,128,512]{2,1,0:T(8,128)(2,1)S(1)} %pad_maximum_fusion.5.refs_0_) | copy-start | bytes 786436
  134.6 15.7 %collective-permute-start.14 = (bf16[2,128,512]{2,1,0:T(8,128)(2,1)S(1)}, bf16[2,128,512]{2,1,0:T(8,128)(2,1)S(1)}, u32[]{:S(2)}, u32[]{:S(2)}) collective-permute-start(bf16[2,128,512]{2,1,0:T(8,128)(2,1)S(1)} %pad_maximum_fusion.5.refs_0_), channel_id=1, source_target_pairs={{0,2},{1,3},{2,0},{3,1},{4,6},{5,7},{6,4},{7,5},{8,10},{9,11},{10,... | collective-permute-start | bytes 786440 | tf_op jit(solution)/shard_map/ppermute | solution.py:128
  136.5 15.1 %collective-permute-start.13 = (bf16[2,128,512]{2,1,0:T(8,128)(2,1)S(1)}, bf16[2,128,512]{2,1,0:T(8,128)(2,1)S(1)}, u32[]{:S(2)}, u32[]{:S(2)}) collective-permute-start(bf16[2,128,512]{2,1,0:T(8,128)(2,1)S(1)} %pad_maximum_fusion.5.refs_0_), channel_id=1, source_target_pairs={{0,1},{1,0},{2,3},{3,2},{4,5},{5,4},{6,7},{7,6},{8,9},{9,8},{10,11... | collective-permute-start | bytes 786440 | tf_op jit(solution)/shard_map/ppermute | solution.py:128
  139.0 12.7 %collective-permute-start.15 = (bf16[2,128,512]{2,1,0:T(8,128)(2,1)S(1)}, bf16[2,128,512]{2,1,0:T(8,128)(2,1)S(1)}, u32[]{:S(2)}, u32[]{:S(2)}) collective-permute-start(bf16[2,128,512]{2,1,0:T(8,128)(2,1)S(1)} %pad_maximum_fusion.5.refs_0_), channel_id=1, source_target_pairs={{1,2},{2,1},{5,6},{6,5},{9,10},{10,9},{13,14},{14,13},{17,18},{18,... | collective-permute-start | bytes 786440 | tf_op jit(solution)/shard_map/ppermute | solution.py:128
  150.4 9.4 %copy-start.10 = (bf16[2,128,512]{2,1,0:T(8,128)(2,1)}, bf16[2,128,512]{2,1,0:T(8,128)(2,1)S(1)}, u32[]{:S(2)}) copy-start(bf16[2,128,512]{2,1,0:T(8,128)(2,1)S(1)} %collective-permute-done.14.refs_2_) | copy-start | bytes 786436
  150.4 9.4 %collective-permute-start.16 = (bf16[2,128,512]{2,1,0:T(8,128)(2,1)S(1)}, bf16[2,128,512]{2,1,0:T(8,128)(2,1)}, u32[]{:S(2)}, u32[]{:S(2)}) collective-permute-start(bf16[2,128,512]{2,1,0:T(8,128)(2,1)S(1)} %collective-permute-done.14.refs_2_), channel_id=1, source_target_pairs={{2,3},{1,0},{6,7},{5,4},{10,11},{9,8},{14,15},{13,12},{18,19},{17,... | collective-permute-start | bytes 786440 | tf_op jit(solution)/shard_map/ppermute | solution.py:137
  151.7 8.1 %copy-start.13 = (bf16[2,128,512]{2,1,0:T(8,128)(2,1)}, bf16[2,128,512]{2,1,0:T(8,128)(2,1)S(1)}, u32[]{:S(2)}) copy-start(bf16[2,128,512]{2,1,0:T(8,128)(2,1)S(1)} %collective-permute-done.13.refs_1_) | copy-start | bytes 786436
  151.7 8.1 %copy-start.15 = (bf16[2,128,512]{2,1,0:T(8,128)(2,1)}, bf16[2,128,512]{2,1,0:T(8,128)(2,1)S(1)}, u32[]{:S(2)}) copy-start(bf16[2,128,512]{2,1,0:T(8,128)(2,1)S(1)} %collective-permute-done.15.refs_3_) | copy-start | bytes 786436
  192.7 32.5 %copy-start = (bf16[8,128,512]{2,1,0:T(8,128)(2,1)}, bf16[8,128,512]{2,1,0:T(8,128)(2,1)S(1)}, u32[]{:S(2)}) copy-start(bf16[8,128,512]{2,1,0:T(8,128)(2,1)S(1)} %all-to-all-done.2) | copy-start | bytes 3145732
  192.7 107.1 %all-to-all-start.3 = ((bf16[8,128,512]{2,1,0:T(8,128)(2,1)}), bf16[8,128,512]{2,1,0:T(8,128)(2,1)S(1)}, u32[]{:S(2)}, u32[]{:S(2)}) async-start(bf16[8,128,512]{2,1,0:T(8,128)(2,1)} %bitcast.40), calls=%async_computation.3 | async-start | bytes 2097152 | tf_op jit(solution)/shard_map/all_to_all | solution.py:293
  198.7 5.9 %collective-permute-start = (f32[128,256]{1,0:T(8,128)S(1)}, f32[128,256]{1,0:T(8,128)S(1)}, u32[]{:S(2)}, u32[]{:S(2)}) collective-permute-start(f32[128,256]{1,0:T(8,128)S(1)} %fusion.2), channel_id=1, source_target_pairs={{0,1},{1,0},{2,3},{3,2},{4,5},{5,4},{6,7},{7,6},{8,9},{9,8},{10,11... | collective-permute-start | bytes 393224 | tf_op jit(solution)/shard_map/ppermute | solution.py:19
  199.5 23.7 %collective-permute-start.18 = (bf16[2,128,512]{2,1,0:T(8,128)(2,1)}, bf16[2,128,512]{2,1,0:T(8,128)(2,1)}, u32[]{:S(2)}, u32[]{:S(2)}) collective-permute-start(bf16[2,128,512]{2,1,0:T(8,128)(2,1)} %pad_maximum_fusion.6.refs_0_), channel_id=1, source_target_pairs={{0,2},{1,3},{2,0},{3,1},{4,6},{5,7},{6,4},{7,5},{8,10},{9,11},{10,... | collective-permute-start | bytes 786440 | tf_op jit(solution)/shard_map/ppermute | solution.py:128
  204.6 17.0 %collective-permute-start.1 = (f32[128,256]{1,0:T(8,128)S(1)}, f32[128,256]{1,0:T(8,128)S(1)}, u32[]{:S(2)}, u32[]{:S(2)}) collective-permute-start(f32[128,256]{1,0:T(8,128)S(1)} %add.10), channel_id=1, source_target_pairs={{0,2},{1,3},{2,0},{3,1},{4,6},{5,7},{6,4},{7,5},{8,10},{9,11},{10,... | collective-permute-start | bytes 393224 | tf_op jit(solution)/shard_map/ppermute | solution.py:19
  221.6 2.8 collective-permute-start.2
  221.7 45.1 %collective-permute-start.17 = (bf16[2,128,512]{2,1,0:T(8,128)(2,1)}, bf16[2,128,512]{2,1,0:T(8,128)(2,1)}, u32[]{:S(2)}, u32[]{:S(2)}) collective-permute-start(bf16[2,128,512]{2,1,0:T(8,128)(2,1)} %pad_maximum_fusion.6.refs_0_), channel_id=1, source_target_pairs={{0,1},{1,0},{2,3},{3,2},{4,5},{5,4},{6,7},{7,6},{8,9},{9,8},{10,11... | collective-permute-start | bytes 786440 | tf_op jit(solution)/shard_map/ppermute | solution.py:128
  221.8 45.1 %collective-permute-start.19 = (bf16[2,128,512]{2,1,0:T(8,128)(2,1)}, bf16[2,128,512]{2,1,0:T(8,128)(2,1)}, u32[]{:S(2)}, u32[]{:S(2)}) collective-permute-start(bf16[2,128,512]{2,1,0:T(8,128)(2,1)} %pad_maximum_fusion.6.refs_0_), channel_id=1, source_target_pairs={{1,2},{2,1},{5,6},{6,5},{9,10},{10,9},{13,14},{14,13},{17,18},{18,... | collective-permute-start | bytes 786440 | tf_op jit(solution)/shard_map/ppermute | solution.py:128
  223.2 43.7 %collective-permute-start.20 = (bf16[2,128,512]{2,1,0:T(8,128)(2,1)}, bf16[2,128,512]{2,1,0:T(8,128)(2,1)}, u32[]{:S(2)}, u32[]{:S(2)}) collective-permute-start(bf16[2,128,512]{2,1,0:T(8,128)(2,1)} %collective-permute-done.18.refs_2_), channel_id=1, source_target_pairs={{2,3},{1,0},{6,7},{5,4},{10,11},{9,8},{14,15},{13,12},{18,19},{17,... | collective-permute-start | bytes 786440 | tf_op jit(solution)/shard_map/ppermute | solution.py:137
  225.2 78.2 %collective-permute-start.3 = (f32[2,128,256]{2,1,0:T(8,128)}, f32[2,128,256]{2,1,0:T(8,128)}, u32[]{:S(2)}, u32[]{:S(2)}) collective-permute-start(f32[2,128,256]{2,1,0:T(8,128)} %pad_maximum_fusion.2), channel_id=1, source_target_pairs={{0,8},{4,12},{8,0},{12,4},{16,24},{20,28},{24,16},{28,20},{1,9},{5... | collective-permute-start | bytes 786440 | tf_op jit(solution)/shard_map/ppermute | solution.py:19
  299.8 7.3 %copy-start.2 = (bf16[8,128,512]{2,1,0:T(8,128)(2,1)}, bf16[8,128,512]{2,1,0:T(8,128)(2,1)S(1)}, u32[]{:S(2)}) copy-start(bf16[8,128,512]{2,1,0:T(8,128)(2,1)S(1)} %all-to-all-done.3) | copy-start | bytes 3145732
  299.8 52.3 %all-to-all-start.4 = ((bf16[8,128,512]{2,1,0:T(8,128)(2,1)}), bf16[8,128,512]{2,1,0:T(8,128)(2,1)S(1)}, u32[]{:S(2)}, u32[]{:S(2)}) async-start(bf16[8,128,512]{2,1,0:T(8,128)(2,1)} %bitcast.39), calls=%async_computation.4 | async-start | bytes 2097152 | tf_op jit(solution)/shard_map/all_to_all | solution.py:293
  305.2 23.9 %collective-permute-start.4 = (f32[4,128,256]{2,1,0:T(8,128)}, f32[4,128,256]{2,1,0:T(8,128)}, u32[]{:S(2)}, u32[]{:S(2)}) collective-permute-start(f32[4,128,256]{2,1,0:T(8,128)} %pad_maximum_fusion.1), channel_id=1, source_target_pairs={{0,16},{4,20},{8,24},{12,28},{16,0},{20,4},{24,8},{28,12},{1,17},{... | collective-permute-start | bytes 1572872 | tf_op jit(solution)/shard_map/ppermute | solution.py:19
  352.1 15.0 %copy-start.3 = (bf16[8,128,512]{2,1,0:T(8,128)(2,1)S(1)}, bf16[8,128,512]{2,1,0:T(8,128)(2,1)}, u32[]{:S(2)}) copy-start(bf16[8,128,512]{2,1,0:T(8,128)(2,1)} %copy-done.2) | copy-start | bytes 3145732
  352.1 41.6 %all-to-all-start = ((bf16[4,512,256]{2,1,0:T(8,128)(2,1)}), bf16[4,512,256]{2,1,0:T(8,128)(2,1)}, u32[]{:S(2)}, u32[]{:S(2)}) async-start(bf16[4,512,256]{2,1,0:T(8,128)(2,1)} %bitcast.3), calls=%async_computation | async-start | bytes 2097152 | tf_op jit(solution)/shard_map/all_to_all | solution.py:299
  367.1 8.9 %copy-start.1 = (bf16[8,128,512]{2,1,0:T(8,128)(2,1)S(1)}, bf16[8,128,512]{2,1,0:T(8,128)(2,1)}, u32[]{:S(2)}) copy-start(bf16[8,128,512]{2,1,0:T(8,128)(2,1)} %copy-done) | copy-start | bytes 3145732
Sparse Core Ops, SparseCore 0:
  9.9 57.0 all-gather.1

commit v3 on v2

v3 whole, which is shorter than its diff:
```python
import functools

import jax
import jax.numpy as jnp
from jax import lax
from jax.experimental import pallas as pl
from jax.experimental.pallas import tpu as pltpu
from jax.sharding import PartitionSpec as P

CHUNKS = 4
PARTS = 4
MIB = 1024 * 1024
BF16 = jnp.bfloat16
F32 = jnp.float32


def flip(value, axis, mask):
    count = lax.axis_size(axis)
    return lax.ppermute(value, axis, [(i, i ^ mask) for i in range(count)])


def split_float(value):
    high = value.astype(BF16)
    low = (value - high.astype(F32)).astype(BF16)
    return high, low


def hr_kernel(scale, where_ref, cols_ref, y_ref, hr_ref, gram_ref, order_ref, both_ref):
    rank = hr_ref.shape[1]

    @pl.when(pl.program_id(0) == 0)
    def _():
        count, tokens = y_ref.shape[:2]
        for mask in range(count):
            at = pl.multiple_of((where_ref[0] ^ mask) * tokens, tokens)
            order_ref[pl.ds(at, tokens), :] = y_ref[mask]
        y_high, y_low = split_float(order_ref[...].T)
        both_ref[:rank] = y_high
        both_ref[rank:] = y_low
        across = (((1,), (1,)), ((), ()))
        gram = lax.dot_general(both_ref[...], y_high, across, preferred_element_type=F32)
        cross = gram[rank:]
        gram_ref[...] = (gram[:rank] + (cross + cross.T)) * scale

    total = jnp.dot(both_ref[...], cols_ref[...], preferred_element_type=F32)
    hr_ref[...] = ((total[:rank] + total[rank:]) * scale).T.astype(BF16)


def hr_and_gram(cols, y_blocks, where, scale, after):
    tokens, features = cols.shape
    rank = y_blocks.shape[2]
    tile = min(1024, features)

    def kernel(*refs):
        hr_kernel(scale, *refs[:3], *refs[3 + len(after) :])

    return pl.pallas_call(
        kernel,
        out_shape=(
            jax.ShapeDtypeStruct((features, rank), BF16),
            jax.ShapeDtypeStruct((rank, rank), F32),
        ),
        grid=(features // tile,),
        in_specs=[
            pl.BlockSpec(memory_space=pltpu.SMEM),
            pl.BlockSpec((tokens, tile), lambda j: (0, j)),
            pl.BlockSpec(y_blocks.shape, lambda j: (0, 0, 0)),
        ]
        + [pl.BlockSpec(memory_space=pl.ANY)] * len(after),
        out_specs=(
            pl.BlockSpec((tile, rank), lambda j: (j, 0)),
            pl.BlockSpec((rank, rank), lambda j: (0, 0)),
        ),
        scratch_shapes=[
            pltpu.VMEM((tokens, rank), F32),
            pltpu.VMEM((2 * rank, tokens), BF16),
        ],
        compiler_params=pltpu.CompilerParams(vmem_limit_bytes=48 * MIB),
        name="hr_and_gram",
    )(where, cols, y_blocks, *after)


def place_kernel(sources, where_ref, *refs):
    out_ref = refs[-1]
    count = len(sources)
    me = where_ref[0]
    for mask in range(count):
        other = me ^ mask
        near, far = sources[mask]

        def put(index, other=other):
            out_ref[other] = refs[index][...]

        if far is None:
            put(near)
        elif near is None:
            put(far)
        else:
            close = jnp.abs(me - other) <= count // 2
            pl.when(close)(functools.partial(put, near))
            pl.when(jnp.logical_not(close))(functools.partial(put, far))


def place_blocks(blocks, sources, where, after):
    count = len(sources)
    return pl.pallas_call(
        functools.partial(place_kernel, sources),
        out_shape=jax.ShapeDtypeStruct((count,) + blocks[0].shape, BF16),
        in_specs=[pl.BlockSpec(memory_space=pltpu.SMEM)]
        + [pl.BlockSpec(memory_space=pltpu.VMEM)] * len(blocks)
        + [pl.BlockSpec(memory_space=pl.ANY)] * len(after),
        out_specs=pl.BlockSpec(memory_space=pltpu.VMEM),
        compiler_params=pltpu.CompilerParams(vmem_limit_bytes=48 * MIB),
        name="place_blocks",
    )(where, *blocks, *after)


def exchange_blocks(mine):
    count = lax.axis_size("narrow")
    half = count // 2
    blocks = [mine]
    sources = [(0, None)]
    direct = {}
    order = sorted(range(1, count), key=lambda m: (m != half, m))
    for mask in order:
        pairs = [(i, i ^ mask) for i in range(count) if abs(i - (i ^ mask)) <= half]
        direct[mask] = lax.ppermute(mine, "narrow", pairs) if pairs else None
    for mask in range(1, count):
        near = far = None
        if direct[mask] is not None:
            near = len(blocks)
            blocks.append(direct[mask])
        pairs = [(i ^ half, i ^ mask) for i in range(count) if abs(i - (i ^ mask)) > half]
        if pairs:
            far = len(blocks)
            blocks.append(lax.ppermute(direct[half], "narrow", pairs))
        sources.append((near, far))
    return blocks, sources


def residual_kernel(weight_ref, codes_ref, scales_ref, *refs):
    out_ref = refs[-1]
    groups = scales_ref.shape[1]
    width = weight_ref.shape[1] // groups
    scales = scales_ref[...]
    batch = min(8, groups)
    for first in range(0, groups, batch):
        parts = []
        for group in range(first, first + batch):
            at = slice(group * width, (group + 1) * width)
            quantized = codes_ref[:, at].astype(F32) * scales[:, group : group + 1]
            parts.append((weight_ref[:, at].astype(F32) - quantized).astype(BF16))
        out_ref[:, first * width : (first + batch) * width] = jnp.concatenate(parts, axis=1)


def residual_part(weight, codes, scales, earlier, index, count, after):
    rows, features = weight.shape
    block = min(128, rows // count)
    steps = rows // count // block
    place = lambda i: (index * steps + i, 0)
    ins = [weight, codes, scales]
    specs = [
        pl.BlockSpec((block, features), place),
        pl.BlockSpec((block, features), place),
        pl.BlockSpec((block, scales.shape[1]), place),
    ]
    aliases = {}
    if earlier is not None:
        aliases = {len(ins): 0}
        ins.append(earlier)
        specs.append(pl.BlockSpec(memory_space=pl.ANY))
    for value in after:
        ins.append(value)
        specs.append(pl.BlockSpec(memory_space=pl.ANY))
    return pl.pallas_call(
        residual_kernel,
        out_shape=jax.ShapeDtypeStruct((rows, features), BF16),
        grid=(steps,),
        in_specs=specs,
        out_specs=pl.BlockSpec((block, features), place),
        input_output_aliases=aliases,
        compiler_params=pltpu.CompilerParams(vmem_limit_bytes=48 * MIB),
        name="residual_part",
    )(*ins)


def product_kernel(residual_ref, hr_ref, out_ref):
    out_ref[...] = jnp.dot(residual_ref[...], hr_ref[...], preferred_element_type=F32).astype(BF16)


def partial_product(residual, hr):
    rows, features = residual.shape
    rank = hr.shape[1]
    block = min(512, rows)
    return pl.pallas_call(
        product_kernel,
        out_shape=jax.ShapeDtypeStruct((rows, rank), BF16),
        grid=(rows // block,),
        in_specs=[
            pl.BlockSpec((block, features), lambda i: (i, 0)),
            pl.BlockSpec((features, rank), lambda i: (0, 0)),
        ],
        out_specs=pl.BlockSpec((block, rank), lambda i: (i, 0)),
        compiler_params=pltpu.CompilerParams(vmem_limit_bytes=48 * MIB),
        name="partial_product",
    )(residual, hr)


def hessian_rows(row_chunks, cols, earlier, index, shape, scale, after):
    tokens, height = row_chunks[0].shape
    block = height * len(row_chunks)
    tile = min(512, cols.shape[1])
    count = len(row_chunks)
    ins = [*row_chunks, cols]
    specs = [pl.BlockSpec((tokens, height), lambda j: (0, 0))] * count
    specs.append(pl.BlockSpec((tokens, tile), lambda j: (0, j)))
    aliases = {}
    if earlier is not None:
        aliases = {len(ins): 0}
        ins.append(earlier)
        specs.append(pl.BlockSpec(memory_space=pl.ANY))
    for value in after:
        ins.append(value)
        specs.append(pl.BlockSpec(memory_space=pl.ANY))

    def kernel(*refs):
        cols_ref = refs[count]
        out_ref, turned_ref = refs[-2:]

        @pl.when(pl.program_id(0) == 0)
        def _():
            for chunk in range(count):
                turned_ref[chunk * height : (chunk + 1) * height] = refs[chunk][...].T

        total = jnp.dot(turned_ref[...], cols_ref[...], preferred_element_type=F32)
        out_ref[...] = (total * scale).astype(BF16)

    return pl.pallas_call(
        kernel,
        out_shape=jax.ShapeDtypeStruct(shape, BF16),
        grid=(cols.shape[1] // tile,),
        in_specs=specs,
        out_specs=pl.BlockSpec((block, tile), lambda j: (index, j)),
        scratch_shapes=[pltpu.VMEM((block, tokens), BF16)],
        input_output_aliases=aliases,
        compiler_params=pltpu.CompilerParams(vmem_limit_bytes=48 * MIB),
        name="hessian_rows",
    )(*ins)


def body(activations, weight_tile, codes, group_scales, right_factor):
    wide_count = lax.axis_size("wide")
    narrow_count = lax.axis_size("narrow")
    narrow_index = lax.axis_index("narrow")
    tokens, features = activations.shape
    rows = weight_tile.shape[0]
    rank = right_factor.shape[1]
    split = features // rows
    scale = 1.0 / (tokens * wide_count)

    cols = lax.all_gather(activations, "wide", axis=0, tiled=True)

    height = rows // CHUNKS
    chunks = []
    for chunk in range(CHUNKS):
        mine = jnp.stack(
            [
                activations[:, s * rows + chunk * height : s * rows + (chunk + 1) * height]
                for s in range(split)
            ]
        )
        chunks.append(exchange_blocks(mine))

    right_block = lax.dynamic_slice_in_dim(right_factor, narrow_index * features, features, 0)
    product = jnp.dot(activations, right_block, preferred_element_type=F32)
    steps = []
    mask = 1
    while mask < narrow_count:
        product = product + flip(product, "narrow", mask)
        steps.append(product)
        mask *= 2
    y_blocks = product[None]
    mask = 1
    while mask < wide_count:
        y_blocks = jnp.concatenate([y_blocks, flip(y_blocks, "wide", mask)], axis=0)
        steps.append(y_blocks)
        mask *= 2

    residual = None
    for part in range(PARTS):
        after = steps[part - 1 : part] if part else []
        residual = residual_part(
            weight_tile, codes, group_scales, residual, part, PARTS, after
        )

    where = narrow_index.astype(jnp.int32).reshape(1)
    row_chunks = []
    placed = []
    for chunk in range(CHUNKS):
        blocks, sources = chunks[chunk]
        after = placed[-1:] if chunk else [residual]
        if chunk + 1 < CHUNKS:
            after = after + [chunks[chunk + 1][0][1]]
        every = place_blocks(blocks, sources, where, after)
        placed.append(every)
        every = every.reshape(narrow_count * split, tokens, height)
        chunk_rows = lax.all_to_all(every, "wide", split_axis=0, concat_axis=0, tiled=True)
        row_chunks.append(chunk_rows.reshape(tokens * wide_count, height))

    wide_where = lax.axis_index("wide").astype(jnp.int32).reshape(1)
    hr, gram = hr_and_gram(cols, y_blocks, wide_where, scale, placed[2:3])
    partial = partial_product(residual, hr)
    shares = partial.reshape(narrow_count, rows // narrow_count, rank)
    shares = lax.all_to_all(shares, "narrow", split_axis=0, concat_axis=0, tiled=True)
    residual_product = jnp.sum(shares.astype(F32), axis=0)

    shape = (rows, features)
    hessian = hessian_rows(row_chunks[:-1], cols, None, 0, shape, scale, [placed[-1], partial])
    hessian = hessian_rows(row_chunks[-1:], cols, hessian, CHUNKS - 1, shape, scale, [])
    return residual_product, gram, hessian


def solution(mesh):
    in_specs = (
        P("wide", "narrow"),
        P("wide", "narrow"),
        P("wide", "narrow"),
        P("wide", "narrow"),
        P(),
    )
    out_specs = (P(("wide", "narrow"), None), P(), P("wide", "narrow"))
    return jax.shard_map(body, mesh=mesh, in_specs=in_specs, out_specs=out_specs, check_vma=False)
```

time: 405 us -> 281 us (0.69)
  Pallas kernels: 227 us -> 82.4 us
  blocking collectives: 0 us -> 37.5 us
  waiting for transfers between devices: 92.8 us -> 69.5 us
  local copies, waits for them, and re-layouts: 4.1 us -> 9.14 us
    pallas_call x9 -> x7, Pallas kernels: 177 us -> 41.3 us  [the longest x2 28.6 us: hessian_rows(): pl.pallas_call(kernel, out_shape=jax.ShapeDtypeStruct(shape, BF16), grid=...]
    all_to_all x0 -> x2, blocking collectives: none -> 37.5 us  [body(): lax.all_to_all(every, 'wide', split_axis=0, concat_axis=0, tiled=True)]
    ppermute x4, waiting for transfers between devices: 23.3 us -> 1.12 us  [exchange_blocks(): blocks.append(lax.ppermute(direct[half], 'narrow', pairs))]
    all_to_all x4 -> x2, waiting for transfers between devices: 0.01 us -> 13.9 us  [body(): lax.all_to_all(every, 'wide', split_axis=0, concat_axis=0, tiled=True)]
    ppermute x12, waiting for transfers between devices: 31.5 us -> 18.3 us  [exchange_blocks(): direct[mask] = lax.ppermute(mine, 'narrow', pairs) if pairs else None]
    pallas_call x4, Pallas kernels: 38.7 us -> 31.7 us  [residual_part(): pl.pallas_call(residual_kernel, out_shape=jax.ShapeDtypeStruct((rows, fea...]
    ppermute x12, starting transfers between devices: 22.3 us -> 29.1 us  [exchange_blocks(): direct[mask] = lax.ppermute(mine, 'narrow', pairs) if pairs else None]
    all_to_all x4 -> x2, starting transfers between devices: 14.5 us -> 7.81 us  [body(): lax.all_to_all(every, 'wide', split_axis=0, concat_axis=0, tiled=True)]
  transfers between devices with their start and end apart: 27 -> 25, of which waited for: 9 -> 7; matrix products, arithmetic and copies ran while one was open for 2% -> 3% of each run, Pallas kernels for 56% -> 29%
where the time goes in v3:
time: 281 us; the launch traced here: 279 us
  Pallas kernels  82.4 us (29%)
  waiting for transfers between devices  69.5 us (25%)
  starting transfers between devices  57.7 us (21%)
  blocking collectives  37.5 us (13%)
  between operations  14.3 us (5%)
  local copies, waits for them, and re-layouts  9.14 us (3%)
  other arithmetic  6.33 us (2%)
    all_to_all x2, blocking collectives, body(): lax.all_to_all(every, 'wide', split_axis=0, concat_axis=0, tiled=True)  37.5 us
    ppermute x5, waiting for transfers between devices, flip(): return lax.ppermute(value, axis, [(i, i ^ mask) for i in range(count)])  35.6 us
    pallas_call x4, Pallas kernels, residual_part(): pl.pallas_call(residual_kernel, out_shape=jax.ShapeDtypeStruct((rows, fea...  31.7 us
    ppermute x12, starting transfers between devices, exchange_blocks(): direct[mask] = lax.ppermute(mine, 'narrow', pairs) if pairs else None  29.1 us
    pallas_call x2, Pallas kernels, hessian_rows(): pl.pallas_call(kernel, out_shape=jax.ShapeDtypeStruct(shape, BF16), grid=...  28.6 us
    ppermute x12, waiting for transfers between devices, exchange_blocks(): direct[mask] = lax.ppermute(mine, 'narrow', pairs) if pairs else None  18.3 us
    all_to_all x2, waiting for transfers between devices, body(): lax.all_to_all(every, 'wide', split_axis=0, concat_axis=0, tiled=True)  13.9 us
    pallas_call x1, Pallas kernels, partial_product(): pl.pallas_call(product_kernel, out_shape=jax.ShapeDtypeStruct((rows, rank...  9.38 us
  transfers between devices with their start and end apart: 25, of which 7 were waited for; matrix products, arithmetic and copies ran while one was open for 3% of the time, Pallas kernels for 29%

profile of v3, /device:TPU:0, one launch (start us, length us, event | category | flops | bytes accessed | tf_op | source)
XLA Modules:
  0.0 279.3 jit_solution(7237611875725672060)
XLA Ops:
  7.2 0.0 all-gather.2.cloned.1.call-start
  7.2 0.7 all-gather.2.cloned.1.call-update
  7.9 2.4 fusion.2
  10.3 3.1 %collective-permute-start = (f32[128,256]{1,0:T(8,128)S(1)}, f32[128,256]{1,0:T(8,128)S(1)}, u32[]{:S(2)}, u32[]{:S(2)}) collective-permute-start(f32[128,256]{1,0:T(8,128)S(1)} %fusion.2), channel_id=1, source_target_pairs={{0,1},{1,0},{2,3},{3,2},{4,5},{5,4},{6,7},{7,6},{8,9},{9,8},{10,11... | collective-permute-start | bytes 393224 | tf_op jit(solution)/shard_map/ppermute | solution.py:19
  13.4 1.4 slice_bitcast_fusion.1
  14.8 0.1 collective-permute-start.5
  14.9 3.0 %collective-permute-start.6 = (bf16[2,128,512]{2,1,0:T(8,128)(2,1)S(1)}, bf16[2,128,512]{2,1,0:T(8,128)(2,1)}, u32[]{:S(2)}, u32[]{:S(2)}) collective-permute-start(bf16[2,128,512]{2,1,0:T(8,128)(2,1)S(1)} %pad_maximum_fusion.3.refs_0_), channel_id=1, source_target_pairs={{0,2},{1,3},{2,0},{3,1},{4,6},{5,7},{6,4},{7,5},{8,10},{9,11},{10,... | collective-permute-start | bytes 786440 | tf_op jit(solution)/shard_map/ppermute | solution.py:127
  17.9 2.1 collective-permute-start.1
  20.1 2.4 collective-permute-start.9
  22.5 0.4 collective-permute-start.10
  22.9 13.5 %collective-permute-done.1 = f32[128,256]{1,0:T(8,128)S(1)} collective-permute-done((f32[128,256]{1,0:T(8,128)S(1)}, f32[128,256]{1,0:T(8,128)S(1)}, u32[]{:S(2)}, u32[]{:S(2)}) %collective-permute-start.1) | collective-permute-done | bytes 131104 | tf_op jit(solution)/shard_map/ppermute | solution.py:19
  36.5 0.7 collective-permute-start.11
  37.1 4.7 %collective-permute-start.14 = (bf16[2,128,512]{2,1,0:T(8,128)(2,1)S(1)}, bf16[2,128,512]{2,1,0:T(8,128)(2,1)S(1)}, u32[]{:S(2)}, u32[]{:S(2)}) collective-permute-start(bf16[2,128,512]{2,1,0:T(8,128)(2,1)S(1)} %pad_maximum_fusion.5.refs_0_), channel_id=1, source_target_pairs={{0,2},{1,3},{2,0},{3,1},{4,6},{5,7},{6,4},{7,5},{8,10},{9,11},{10,... | collective-permute-start | bytes 786440 | tf_op jit(solution)/shard_map/ppermute | solution.py:127
  41.9 9.7 %collective-permute-start.13 = (bf16[2,128,512]{2,1,0:T(8,128)(2,1)S(1)}, bf16[2,128,512]{2,1,0:T(8,128)(2,1)S(1)}, u32[]{:S(2)}, u32[]{:S(2)}) collective-permute-start(bf16[2,128,512]{2,1,0:T(8,128)(2,1)S(1)} %pad_maximum_fusion.5.refs_0_), channel_id=1, source_target_pairs={{0,1},{1,0},{2,3},{3,2},{4,5},{5,4},{6,7},{7,6},{8,9},{9,8},{10,11... | collective-permute-start | bytes 786440 | tf_op jit(solution)/shard_map/ppermute | solution.py:127
  51.6 0.7 collective-permute-start.15
  52.3 2.8 collective-permute-start.18
  55.1 0.7 copy-done.13
  55.8 1.3 collective-permute-start.12
  57.1 0.7 copy-done.11
  57.8 12.4 %collective-permute-done.14.refs_2_ = bf16[2,128,512]{2,1,0:T(8,128)(2,1)S(1)} collective-permute-done((bf16[2,128,512]{2,1,0:T(8,128)(2,1)S(1)}, bf16[2,128,512]{2,1,0:T(8,128)(2,1)S(1)}, u32[]{:S(2)}, u32[]{:S(2)}) %collective-permute-start.14) | collective-permute-done | bytes 262176 | tf_op jit(solution)/shard_map/ppermute | solution.py:127
  70.1 1.3 collective-permute-start.16
  71.5 0.7 copy-done.5
  72.2 0.7 copy-done.7
  72.9 1.4 collective-permute-start.7
  74.3 5.9 %collective-permute-done.18.refs_2_ = bf16[2,128,512]{2,1,0:T(8,128)(2,1)} collective-permute-done((bf16[2,128,512]{2,1,0:T(8,128)(2,1)S(1)}, bf16[2,128,512]{2,1,0:T(8,128)(2,1)}, u32[]{:S(2)}, u32[]{:S(2)}) %collective-permute-start.18) | collective-permute-done | bytes 262176 | tf_op jit(solution)/shard_map/ppermute | solution.py:127
  80.2 1.9 collective-permute-start.17
  82.1 1.3 collective-permute-start.8
  83.4 0.7 copy-done.15
  84.1 1.4 collective-permute-start.19
  85.4 1.1 collective-permute-done.16.refs_4_
  86.6 0.7 copy-done.9
  87.3 1.3 collective-permute-start.20
  88.6 1.3 copy.16.scales_ref
  89.8 7.9 %residual_part.4.refs_0_ = bf16[2048,4096]{1,0:T(8,128)(2,1)} custom-call(bf16[2048,4096]{1,0:T(8,128)(2,1)} %weight_ref.7, s32[2048,4096]{1,0:T(8,128)} %codes_ref.7, f32[2048,32]{1,0:T(8,128)S(1)} %copy.16.scales_ref), custom_call_target="tpu_custom_call" | custom-call | tf_op jit(solution)/shard_map/residual_part/pallas_call | solution.py:175
  97.7 7.9 %residual_part.5.refs_0_ = bf16[2048,4096]{1,0:T(8,128)(2,1)} custom-call(bf16[2048,4096]{1,0:T(8,128)(2,1)} %weight_ref.7, s32[2048,4096]{1,0:T(8,128)} %codes_ref.7, f32[2048,32]{1,0:T(8,128)S(1)} %copy.16.scales_ref, bf16[2048,4096]{1,0:T(8,128)(2,1)} %residual_part.4.refs_0_, f32[128,256]{1,0:T(8,128)S(1)} %add.10.refs_1_), custom_call_target="tpu_custom_call", output_to_operand_aliasing={{}: (3, {})} | custom-call | tf_op jit(solution)/shard_map/residual_part/pallas_call | solution.py:175
  105.6 7.9 %residual_part.6.refs_0_ = bf16[2048,4096]{1,0:T(8,128)(2,1)} custom-call(bf16[2048,4096]{1,0:T(8,128)(2,1)} %weight_ref.7, s32[2048,4096]{1,0:T(8,128)} %codes_ref.7, f32[2048,32]{1,0:T(8,128)S(1)} %copy.16.scales_ref, bf16[2048,4096]{1,0:T(8,128)(2,1)} %residual_part.5.refs_0_, f32[128,256]{1,0:T(8,128)S(1)} %add.11.refs_1_), custom_call_target="tpu_custom_call", output_to_operand_aliasing={{}: (3, {})} | custom-call | tf_op jit(solution)/shard_map/residual_part/pallas_call | solution.py:175
  113.5 0.9 pad_maximum_fusion.2.refs_1_
  114.5 8.0 %residual_part.7.refs_5_.residual_ref = bf16[2048,4096]{1,0:T(8,128)(2,1)} custom-call(bf16[2048,4096]{1,0:T(8,128)(2,1)} %weight_ref.7, s32[2048,4096]{1,0:T(8,128)} %codes_ref.7, f32[2048,32]{1,0:T(8,128)S(1)} %copy.16.scales_ref, bf16[2048,4096]{1,0:T(8,128)(2,1)} %residual_part.6.refs_0_, ...), custom_call_target="tpu_custom_call", output_to_operand_aliasing={{}: (3, {})} | custom-call | tf_op jit(solution)/shard_map/residual_part/pallas_call | solution.py:175
  122.5 0.1 place_blocks.4.refs_5_
  122.6 0.8 copy-done.12
  123.4 0.1 copy-done.14
  123.5 0.1 copy-done.16
  123.6 1.0 place_blocks.5.refs_5_
  124.6 2.2 place_blocks.6.refs_3_.refs_5_
  126.8 1.2 place_blocks.7.refs_4_
  128.0 19.1 %all_to_all.25 = bf16[8,128,512]{2,1,0:T(8,128)(2,1)S(1)} all-to-all(bf16[8,128,512]{2,1,0:T(8,128)(2,1)S(1)} %bitcast.32), channel_id=1, replica_groups=mesh['wide'=8,'narrow'=4] {'wide'}, dimensions={0} | all-to-all | bytes 2097152 | tf_op jit(solution)/shard_map/all_to_all | solution.py:307
  147.0 18.5 %all_to_all.26 = bf16[8,128,512]{2,1,0:T(8,128)(2,1)} all-to-all(bf16[8,128,512]{2,1,0:T(8,128)(2,1)S(1)} %bitcast.31), channel_id=1, replica_groups=mesh['wide'=8,'narrow'=4] {'wide'}, dimensions={0} | all-to-all | bytes 2097152 | tf_op jit(solution)/shard_map/all_to_all | solution.py:307
  165.5 3.6 %all-to-all-start.3 = ((bf16[8,128,512]{2,1,0:T(8,128)(2,1)}), bf16[8,128,512]{2,1,0:T(8,128)(2,1)S(1)}, u32[]{:S(2)}, u32[]{:S(2)}) async-start(bf16[8,128,512]{2,1,0:T(8,128)(2,1)} %bitcast.17), calls=%async_computation.3 | async-start | bytes 2097152 | tf_op jit(solution)/shard_map/all_to_all | solution.py:307
  169.1 1.9 collective-permute-start.3
  171.0 13.9 %all-to-all-done.3 = bf16[8,128,512]{2,1,0:T(8,128)(2,1)S(1)} async-done(((bf16[8,128,512]{2,1,0:T(8,128)(2,1)}), bf16[8,128,512]{2,1,0:T(8,128)(2,1)S(1)}, u32[]{:S(2)}, u32[]{:S(2)}) %all-to-all-start.3) | async-done | bytes 1048608 | tf_op jit(solution)/shard_map/all_to_all | solution.py:307
  184.9 4.3 %all-to-all-start.4 = ((bf16[8,128,512]{2,1,0:T(8,128)(2,1)}), bf16[8,128,512]{2,1,0:T(8,128)(2,1)}, u32[]{:S(2)}, u32[]{:S(2)}) async-start(bf16[8,128,512]{2,1,0:T(8,128)(2,1)} %bitcast.19), calls=%async_computation.4 | async-start | bytes 2097152 | tf_op jit(solution)/shard_map/all_to_all | solution.py:307
  189.1 0.1 collective-permute-done.3
  189.2 1.8 pad_maximum_fusion.1
  191.0 1.9 collective-permute-start.4
  192.9 22.0 %collective-permute-done.4 = f32[4,128,256]{2,1,0:T(8,128)} collective-permute-done((f32[4,128,256]{2,1,0:T(8,128)}, f32[4,128,256]{2,1,0:T(8,128)}, u32[]{:S(2)}, u32[]{:S(2)}) %collective-permute-start.4) | collective-permute-done | bytes 524320 | tf_op jit(solution)/shard_map/ppermute | solution.py:19
  214.8 1.2 pad_maximum_fusion.refs_2_
  216.1 0.0 all-gather.2.cloned.1.call-done.refs_1_.refs_3_
  216.1 8.3 %hr_and_gram.1 = (bf16[4096,256]{1,0:T(8,128)(2,1)S(1)}, f32[256,256]{1,0:T(8,128)}) custom-call(s32[1]{0:T(128)} %bitcast.2.refs_0_, bf16[1024,4096]{1,0:T(8,128)(2,1)} %all-gather.2.cloned.1.call-done.refs_1_.refs_3_, f32[8,128,256]{2,1,0:T(8,128)S(1)} %pad_maximum_fusion.refs_2_, bf16[4,2,128,512]{3,2,1,0:T(8,128)(2,1)} %place_blocks.6.refs_3_.refs_5_), custom_call_target="tpu_custom_call" | custom-call | tf_op jit(solution)/shard_map/hr_and_gram/pallas_call | solution.py:57
  224.4 9.4 %partial_product.1.refs_5_ = bf16[2048,256]{1,0:T(8,128)(2,1)} custom-call(bf16[2048,4096]{1,0:T(8,128)(2,1)} %residual_part.7.refs_5_.residual_ref, bf16[4096,256]{1,0:T(8,128)(2,1)S(1)} %get-tuple-element.5.hr_ref), custom_call_target="tpu_custom_call" | custom-call | tf_op jit(solution)/shard_map/partial_product/pallas_call | solution.py:195
  233.8 6.7 %all-to-all-start = ((bf16[4,512,256]{2,1,0:T(8,128)(2,1)}), bf16[4,512,256]{2,1,0:T(8,128)(2,1)}, u32[]{:S(2)}, u32[]{:S(2)}) async-start(bf16[4,512,256]{2,1,0:T(8,128)(2,1)} %bitcast.12), calls=%async_computation | async-start | bytes 2097152 | tf_op jit(solution)/shard_map/all_to_all | solution.py:314
  240.4 1.2 copy-done.2
  241.7 18.2 %hessian_rows.2.refs_2_ = bf16[2048,4096]{1,0:T(8,128)(2,1)} custom-call(bf16[1024,512]{1,0:T(8,128)(2,1)S(1)} %bitcast.34, bf16[1024,512]{1,0:T(8,128)(2,1)S(1)} %bitcast.35, bf16[1024,512]{1,0:T(8,128)(2,1)} %bitcast.20.refs_2_, bf16[1024,4096]{1,0:T(8,128)(2,1)} %all-gather.2.cloned.1.call-done.refs_1_.refs_3_, ...), custom_call_target="tpu_custom_call" | custom-call | tf_op jit(solution)/shard_map/hessian_rows/pallas_call | solution.py:238
  259.8 10.4 %hessian_rows.3 = bf16[2048,4096]{1,0:T(8,128)(2,1)} custom-call(bf16[1024,512]{1,0:T(8,128)(2,1)S(1)} %bitcast.33, bf16[1024,4096]{1,0:T(8,128)(2,1)} %all-gather.2.cloned.1.call-done.refs_1_.refs_3_, bf16[2048,4096]{1,0:T(8,128)(2,1)} %hessian_rows.2.refs_2_), custom_call_target="tpu_custom_call", output_to_operand_aliasing={{}: (2, {})} | custom-call | tf_op jit(solution)/shard_map/hessian_rows/pallas_call | solution.py:238
  270.3 2.2 convert_reduce_fusion
  (48 shorter events, 0.2 us)
Async XLA Ops:
  7.2 209.0 %all-gather.2.cloned.1.call-start = ((), (), s32[]{:S(2)}) async-start(), calls=%async_computation.5 | async-start | bytes 9437184 | tf_op jit(solution)/shard_map/all_gather | solution.py:261
  10.3 7.6 %collective-permute-start = (f32[128,256]{1,0:T(8,128)S(1)}, f32[128,256]{1,0:T(8,128)S(1)}, u32[]{:S(2)}, u32[]{:S(2)}) collective-permute-start(f32[128,256]{1,0:T(8,128)S(1)} %fusion.2), channel_id=1, source_target_pairs={{0,1},{1,0},{2,3},{3,2},{4,5},{5,4},{6,7},{7,6},{8,9},{9,8},{10,11... | collective-permute-start | bytes 393224 | tf_op jit(solution)/shard_map/ppermute | solution.py:19
  14.8 22.3 %collective-permute-start.5 = (bf16[2,128,512]{2,1,0:T(8,128)(2,1)S(1)}, bf16[2,128,512]{2,1,0:T(8,128)(2,1)S(1)}, u32[]{:S(2)}, u32[]{:S(2)}) collective-permute-start(bf16[2,128,512]{2,1,0:T(8,128)(2,1)S(1)} %pad_maximum_fusion.3.refs_0_), channel_id=1, source_target_pairs={{0,1},{1,0},{2,3},{3,2},{4,5},{5,4},{6,7},{7,6},{8,9},{9,8},{10,11... | collective-permute-start | bytes 786440 | tf_op jit(solution)/shard_map/ppermute | solution.py:127
  14.9 27.0 %collective-permute-start.6 = (bf16[2,128,512]{2,1,0:T(8,128)(2,1)S(1)}, bf16[2,128,512]{2,1,0:T(8,128)(2,1)}, u32[]{:S(2)}, u32[]{:S(2)}) collective-permute-start(bf16[2,128,512]{2,1,0:T(8,128)(2,1)S(1)} %pad_maximum_fusion.3.refs_0_), channel_id=1, source_target_pairs={{0,2},{1,3},{2,0},{3,1},{4,6},{5,7},{6,4},{7,5},{8,10},{9,11},{10,... | collective-permute-start | bytes 786440 | tf_op jit(solution)/shard_map/ppermute | solution.py:127
  17.9 18.5 %collective-permute-start.1 = (f32[128,256]{1,0:T(8,128)S(1)}, f32[128,256]{1,0:T(8,128)S(1)}, u32[]{:S(2)}, u32[]{:S(2)}) collective-permute-start(f32[128,256]{1,0:T(8,128)S(1)} %add.10.refs_1_), channel_id=1, source_target_pairs={{0,2},{1,3},{2,0},{3,1},{4,6},{5,7},{6,4},{7,5},{8,10},{9,11},{10,... | collective-permute-start | bytes 393224 | tf_op jit(solution)/shard_map/ppermute | solution.py:19
  20.1 31.5 %collective-permute-start.9 = (bf16[2,128,512]{2,1,0:T(8,128)(2,1)S(1)}, bf16[2,128,512]{2,1,0:T(8,128)(2,1)S(1)}, u32[]{:S(2)}, u32[]{:S(2)}) collective-permute-start(bf16[2,128,512]{2,1,0:T(8,128)(2,1)S(1)} %pad_maximum_fusion.4.refs_0_), channel_id=1, source_target_pairs={{0,1},{1,0},{2,3},{3,2},{4,5},{5,4},{6,7},{7,6},{8,9},{9,8},{10,11... | collective-permute-start | bytes 786440 | tf_op jit(solution)/shard_map/ppermute | solution.py:127
  22.5 29.8 %collective-permute-start.10 = (bf16[2,128,512]{2,1,0:T(8,128)(2,1)S(1)}, bf16[2,128,512]{2,1,0:T(8,128)(2,1)S(1)}, u32[]{:S(2)}, u32[]{:S(2)}) collective-permute-start(bf16[2,128,512]{2,1,0:T(8,128)(2,1)S(1)} %pad_maximum_fusion.4.refs_0_), channel_id=1, source_target_pairs={{0,2},{1,3},{2,0},{3,1},{4,6},{5,7},{6,4},{7,5},{8,10},{9,11},{10,... | collective-permute-start | bytes 786440 | tf_op jit(solution)/shard_map/ppermute | solution.py:127
  36.5 18.6 %collective-permute-start.11 = (bf16[2,128,512]{2,1,0:T(8,128)(2,1)S(1)}, bf16[2,128,512]{2,1,0:T(8,128)(2,1)S(1)}, u32[]{:S(2)}, u32[]{:S(2)}) collective-permute-start(bf16[2,128,512]{2,1,0:T(8,128)(2,1)S(1)} %pad_maximum_fusion.4.refs_0_), channel_id=1, source_target_pairs={{1,2},{2,1},{5,6},{6,5},{9,10},{10,9},{13,14},{14,13},{17,18},{18,... | collective-permute-start | bytes 786440 | tf_op jit(solution)/shard_map/ppermute | solution.py:127
  37.1 33.0 %collective-permute-start.14 = (bf16[2,128,512]{2,1,0:T(8,128)(2,1)S(1)}, bf16[2,128,512]{2,1,0:T(8,128)(2,1)S(1)}, u32[]{:S(2)}, u32[]{:S(2)}) collective-permute-start(bf16[2,128,512]{2,1,0:T(8,128)(2,1)S(1)} %pad_maximum_fusion.5.refs_0_), channel_id=1, source_target_pairs={{0,2},{1,3},{2,0},{3,1},{4,6},{5,7},{6,4},{7,5},{8,10},{9,11},{10,... | collective-permute-start | bytes 786440 | tf_op jit(solution)/shard_map/ppermute | solution.py:127
  41.9 29.6 %collective-permute-start.13 = (bf16[2,128,512]{2,1,0:T(8,128)(2,1)S(1)}, bf16[2,128,512]{2,1,0:T(8,128)(2,1)S(1)}, u32[]{:S(2)}, u32[]{:S(2)}) collective-permute-start(bf16[2,128,512]{2,1,0:T(8,128)(2,1)S(1)} %pad_maximum_fusion.5.refs_0_), channel_id=1, source_target_pairs={{0,1},{1,0},{2,3},{3,2},{4,5},{5,4},{6,7},{7,6},{8,9},{9,8},{10,11... | collective-permute-start | bytes 786440 | tf_op jit(solution)/shard_map/ppermute | solution.py:127
  51.6 20.6 %collective-permute-start.15 = (bf16[2,128,512]{2,1,0:T(8,128)(2,1)S(1)}, bf16[2,128,512]{2,1,0:T(8,128)(2,1)S(1)}, u32[]{:S(2)}, u32[]{:S(2)}) collective-permute-start(bf16[2,128,512]{2,1,0:T(8,128)(2,1)S(1)} %pad_maximum_fusion.5.refs_0_), channel_id=1, source_target_pairs={{1,2},{2,1},{5,6},{6,5},{9,10},{10,9},{13,14},{14,13},{17,18},{18,... | collective-permute-start | bytes 786440 | tf_op jit(solution)/shard_map/ppermute | solution.py:127
  52.3 27.9 %collective-permute-start.18 = (bf16[2,128,512]{2,1,0:T(8,128)(2,1)S(1)}, bf16[2,128,512]{2,1,0:T(8,128)(2,1)}, u32[]{:S(2)}, u32[]{:S(2)}) collective-permute-start(bf16[2,128,512]{2,1,0:T(8,128)(2,1)S(1)} %pad_maximum_fusion.6.refs_0_), channel_id=1, source_target_pairs={{0,2},{1,3},{2,0},{3,1},{4,6},{5,7},{6,4},{7,5},{8,10},{9,11},{10,... | collective-permute-start | bytes 786440 | tf_op jit(solution)/shard_map/ppermute | solution.py:127
  55.1 0.7 copy-start.13
  55.8 27.6 %collective-permute-start.12 = (bf16[2,128,512]{2,1,0:T(8,128)(2,1)S(1)}, bf16[2,128,512]{2,1,0:T(8,128)(2,1)S(1)}, u32[]{:S(2)}, u32[]{:S(2)}) collective-permute-start(bf16[2,128,512]{2,1,0:T(8,128)(2,1)S(1)} %collective-permute-done.10.refs_2_), channel_id=1, source_target_pairs={{2,3},{1,0},{6,7},{5,4},{10,11},{9,8},{14,15},{13,12},{18,19},{17,... | collective-permute-start | bytes 786440 | tf_op jit(solution)/shard_map/ppermute | solution.py:136
  57.1 0.7 copy-start.11
  70.1 16.4 %copy-start.3 = (bf16[2,128,512]{2,1,0:T(8,128)(2,1)}, bf16[2,128,512]{2,1,0:T(8,128)(2,1)S(1)}, u32[]{:S(2)}) copy-start(bf16[2,128,512]{2,1,0:T(8,128)(2,1)S(1)} %collective-permute-done.14.refs_2_) | copy-start | bytes 786436
  70.1 16.4 %collective-permute-start.16 = (bf16[2,128,512]{2,1,0:T(8,128)(2,1)S(1)}, bf16[2,128,512]{2,1,0:T(8,128)(2,1)S(1)}, u32[]{:S(2)}, u32[]{:S(2)}) collective-permute-start(bf16[2,128,512]{2,1,0:T(8,128)(2,1)S(1)} %collective-permute-done.14.refs_2_), channel_id=1, source_target_pairs={{2,3},{1,0},{6,7},{5,4},{10,11},{9,8},{14,15},{13,12},{18,19},{17,... | collective-permute-start | bytes 786440 | tf_op jit(solution)/shard_map/ppermute | solution.py:136
  71.5 0.7 copy-start.5
  72.2 9.8 %collective-permute-start.2 = (f32[1,128,256]{2,1,0:T(8,128)S(1)}, f32[1,128,256]{2,1,0:T(8,128)}, u32[]{:S(2)}, u32[]{:S(2)}) collective-permute-start(f32[1,128,256]{2,1,0:T(8,128)S(1)} %bitcast.36), channel_id=1, source_target_pairs={{0,4},{4,0},{8,12},{12,8},{16,20},{20,16},{24,28},{28,24},{1,5},{5... | collective-permute-start | bytes 393224 | tf_op jit(solution)/shard_map/ppermute | solution.py:19
  72.2 0.7 copy-start.7
  72.9 51.7 %collective-permute-start.7 = (bf16[2,128,512]{2,1,0:T(8,128)(2,1)S(1)}, bf16[2,128,512]{2,1,0:T(8,128)(2,1)}, u32[]{:S(2)}, u32[]{:S(2)}) collective-permute-start(bf16[2,128,512]{2,1,0:T(8,128)(2,1)S(1)} %pad_maximum_fusion.3.refs_0_), channel_id=1, source_target_pairs={{1,2},{2,1},{5,6},{6,5},{9,10},{10,9},{13,14},{14,13},{17,18},{18,... | collective-permute-start | bytes 786440 | tf_op jit(solution)/shard_map/ppermute | solution.py:127
  80.2 44.5 %collective-permute-start.17 = (bf16[2,128,512]{2,1,0:T(8,128)(2,1)S(1)}, bf16[2,128,512]{2,1,0:T(8,128)(2,1)S(1)}, u32[]{:S(2)}, u32[]{:S(2)}) collective-permute-start(bf16[2,128,512]{2,1,0:T(8,128)(2,1)S(1)} %pad_maximum_fusion.6.refs_0_), channel_id=1, source_target_pairs={{0,1},{1,0},{2,3},{3,2},{4,5},{5,4},{6,7},{7,6},{8,9},{9,8},{10,11... | collective-permute-start | bytes 786440 | tf_op jit(solution)/shard_map/ppermute | solution.py:127
  82.1 42.6 %collective-permute-start.8 = (bf16[2,128,512]{2,1,0:T(8,128)(2,1)}, bf16[2,128,512]{2,1,0:T(8,128)(2,1)}, u32[]{:S(2)}, u32[]{:S(2)}) collective-permute-start(bf16[2,128,512]{2,1,0:T(8,128)(2,1)} %collective-permute-done.6.refs_2_), channel_id=1, source_target_pairs={{2,3},{1,0},{6,7},{5,4},{10,11},{9,8},{14,15},{13,12},{18,19},{17,... | collective-permute-start | bytes 786440 | tf_op jit(solution)/shard_map/ppermute | solution.py:136
  83.4 0.7 copy-start.15
  84.1 42.7 %collective-permute-start.19 = (bf16[2,128,512]{2,1,0:T(8,128)(2,1)S(1)}, bf16[2,128,512]{2,1,0:T(8,128)(2,1)}, u32[]{:S(2)}, u32[]{:S(2)}) collective-permute-start(bf16[2,128,512]{2,1,0:T(8,128)(2,1)S(1)} %pad_maximum_fusion.6.refs_0_), channel_id=1, source_target_pairs={{1,2},{2,1},{5,6},{6,5},{9,10},{10,9},{13,14},{14,13},{17,18},{18,... | collective-permute-start | bytes 786440 | tf_op jit(solution)/shard_map/ppermute | solution.py:127
  86.5 0.7 copy-start.9
  87.3 39.5 %collective-permute-start.20 = (bf16[2,128,512]{2,1,0:T(8,128)(2,1)}, bf16[2,128,512]{2,1,0:T(8,128)(2,1)}, u32[]{:S(2)}, u32[]{:S(2)}) collective-permute-start(bf16[2,128,512]{2,1,0:T(8,128)(2,1)} %collective-permute-done.18.refs_2_), channel_id=1, source_target_pairs={{2,3},{1,0},{6,7},{5,4},{10,11},{9,8},{14,15},{13,12},{18,19},{17,... | collective-permute-start | bytes 786440 | tf_op jit(solution)/shard_map/ppermute | solution.py:136
  114.5 8.0 %copy-start.4 = (bf16[2,128,512]{2,1,0:T(8,128)(2,1)S(1)}, bf16[2,128,512]{2,1,0:T(8,128)(2,1)}, u32[]{:S(2)}) copy-start(bf16[2,128,512]{2,1,0:T(8,128)(2,1)} %copy-done.3) | copy-start | bytes 786436
  114.5 8.0 %copy-start.6 = (bf16[2,128,512]{2,1,0:T(8,128)(2,1)S(1)}, bf16[2,128,512]{2,1,0:T(8,128)(2,1)}, u32[]{:S(2)}) copy-start(bf16[2,128,512]{2,1,0:T(8,128)(2,1)} %copy-done.5) | copy-start | bytes 786436
  114.5 8.0 %copy-start.8 = (bf16[2,128,512]{2,1,0:T(8,128)(2,1)S(1)}, bf16[2,128,512]{2,1,0:T(8,128)(2,1)}, u32[]{:S(2)}) copy-start(bf16[2,128,512]{2,1,0:T(8,128)(2,1)} %copy-done.7) | copy-start | bytes 786436
  114.5 8.0 %copy-start.10 = (bf16[2,128,512]{2,1,0:T(8,128)(2,1)S(1)}, bf16[2,128,512]{2,1,0:T(8,128)(2,1)}, u32[]{:S(2)}) copy-start(bf16[2,128,512]{2,1,0:T(8,128)(2,1)} %copy-done.9) | copy-start | bytes 786436
  122.5 0.9 copy-start.12
  122.5 1.0 copy-start.14
  122.5 1.1 copy-start.16
  165.5 19.4 %all-to-all-start.3 = ((bf16[8,128,512]{2,1,0:T(8,128)(2,1)}), bf16[8,128,512]{2,1,0:T(8,128)(2,1)S(1)}, u32[]{:S(2)}, u32[]{:S(2)}) async-start(bf16[8,128,512]{2,1,0:T(8,128)(2,1)} %bitcast.17), calls=%async_computation.3 | async-start | bytes 2097152 | tf_op jit(solution)/shard_map/all_to_all | solution.py:307
  169.1 20.1 %collective-permute-start.3 = (f32[2,128,256]{2,1,0:T(8,128)S(1)}, f32[2,128,256]{2,1,0:T(8,128)}, u32[]{:S(2)}, u32[]{:S(2)}) collective-permute-start(f32[2,128,256]{2,1,0:T(8,128)S(1)} %pad_maximum_fusion.2.refs_1_), channel_id=1, source_target_pairs={{0,8},{4,12},{8,0},{12,4},{16,24},{20,28},{24,16},{28,20},{1,9},{5... | collective-permute-start | bytes 786440 | tf_op jit(solution)/shard_map/ppermute | solution.py:19
  184.9 8.0 %copy-start.1 = (bf16[8,128,512]{2,1,0:T(8,128)(2,1)}, bf16[8,128,512]{2,1,0:T(8,128)(2,1)S(1)}, u32[]{:S(2)}) copy-start(bf16[8,128,512]{2,1,0:T(8,128)(2,1)S(1)} %all-to-all-done.3) | copy-start | bytes 3145732
  184.9 48.9 %all-to-all-start.4 = ((bf16[8,128,512]{2,1,0:T(8,128)(2,1)}), bf16[8,128,512]{2,1,0:T(8,128)(2,1)}, u32[]{:S(2)}, u32[]{:S(2)}) async-start(bf16[8,128,512]{2,1,0:T(8,128)(2,1)} %bitcast.19), calls=%async_computation.4 | async-start | bytes 2097152 | tf_op jit(solution)/shard_map/all_to_all | solution.py:307
  191.0 23.8 %collective-permute-start.4 = (f32[4,128,256]{2,1,0:T(8,128)}, f32[4,128,256]{2,1,0:T(8,128)}, u32[]{:S(2)}, u32[]{:S(2)}) collective-permute-start(f32[4,128,256]{2,1,0:T(8,128)} %pad_maximum_fusion.1), channel_id=1, source_target_pairs={{0,16},{4,20},{8,24},{12,28},{16,0},{20,4},{24,8},{28,12},{1,17},{... | collective-permute-start | bytes 1572872 | tf_op jit(solution)/shard_map/ppermute | solution.py:19
  224.4 16.0 %copy-start = (bf16[8,128,512]{2,1,0:T(8,128)(2,1)S(1)}, bf16[8,128,512]{2,1,0:T(8,128)(2,1)}, u32[]{:S(2)}) copy-start(bf16[8,128,512]{2,1,0:T(8,128)(2,1)} %all_to_all.26) | copy-start | bytes 3145732
  233.8 36.5 %all-to-all-start = ((bf16[4,512,256]{2,1,0:T(8,128)(2,1)}), bf16[4,512,256]{2,1,0:T(8,128)(2,1)}, u32[]{:S(2)}, u32[]{:S(2)}) async-start(bf16[4,512,256]{2,1,0:T(8,128)(2,1)} %bitcast.12), calls=%async_computation | async-start | bytes 2097152 | tf_op jit(solution)/shard_map/all_to_all | solution.py:314
  240.4 1.2 copy-start.2
Sparse Core Ops, SparseCore 0:
  9.9 57.0 all-gather.1

commit v4 on v0

v4 whole, which is shorter than its diff:
```python
import functools

import jax
import jax.numpy as jnp
from jax import lax
from jax.experimental import pallas as pl
from jax.experimental.pallas import tpu as pltpu
from jax.sharding import PartitionSpec as P

CHUNKS = 2
MIB = 1024 * 1024
BF16 = jnp.bfloat16
F32 = jnp.float32


def flip(value, axis, mask):
    count = lax.axis_size(axis)
    return lax.ppermute(value, axis, [(i, i ^ mask) for i in range(count)])


def split_float(value):
    high = value.astype(BF16)
    low = (value - high.astype(F32)).astype(BF16)
    return high, low


def hr_and_gram(cols, y_blocks, where, scale, after):
    count = len(y_blocks)
    tokens, rank = y_blocks[0].shape
    features = cols.shape[1]
    tile = min(1024, features)

    def kernel(where_ref, cols_ref, *refs):
        hr_ref, gram_ref, order_ref, both_ref = refs[-4:]

        @pl.when(pl.program_id(0) == 0)
        def _():
            for mask in range(count):
                at = pl.multiple_of((where_ref[0] ^ mask) * tokens, tokens)
                order_ref[pl.ds(at, tokens), :] = refs[mask][...]
            y_high, y_low = split_float(order_ref[...].T)
            both_ref[:rank] = y_high
            both_ref[rank:] = y_low
            across = (((1,), (1,)), ((), ()))
            gram = lax.dot_general(both_ref[...], y_high, across, preferred_element_type=F32)
            cross = gram[rank:]
            gram_ref[...] = (gram[:rank] + (cross + cross.T)) * scale

        total = jnp.dot(both_ref[...], cols_ref[...], preferred_element_type=F32)
        hr_ref[...] = ((total[:rank] + total[rank:]) * scale).T.astype(BF16)

    return pl.pallas_call(
        kernel,
        out_shape=(
            jax.ShapeDtypeStruct((features, rank), BF16),
            jax.ShapeDtypeStruct((rank, rank), F32),
        ),
        grid=(features // tile,),
        in_specs=[
            pl.BlockSpec(memory_space=pltpu.SMEM),
            pl.BlockSpec((count * tokens, tile), lambda j: (0, j)),
        ]
        + [pl.BlockSpec((tokens, rank), lambda j: (0, 0))] * count
        + [pl.BlockSpec(memory_space=pl.ANY)] * len(after),
        out_specs=(
            pl.BlockSpec((tile, rank), lambda j: (j, 0)),
            pl.BlockSpec((rank, rank), lambda j: (0, 0)),
        ),
        scratch_shapes=[
            pltpu.VMEM((count * tokens, rank), F32),
            pltpu.VMEM((2 * rank, count * tokens), BF16),
        ],
        compiler_params=pltpu.CompilerParams(vmem_limit_bytes=48 * MIB),
        name="hr_and_gram",
    )(where, cols, *y_blocks, *after)


def residual_kernel(weight_ref, codes_ref, scales_ref, out_ref):
    groups = scales_ref.shape[1]
    width = weight_ref.shape[1] // groups
    scales = scales_ref[...]
    parts = []
    for group in range(groups):
        at = slice(group * width, (group + 1) * width)
        quantized = codes_ref[:, at].astype(F32) * scales[:, group : group + 1]
        parts.append((weight_ref[:, at].astype(F32) - quantized).astype(BF16))
    out_ref[...] = jnp.concatenate(parts, axis=1)


def residual_tile(weight, codes, scales):
    rows, features = weight.shape
    block = min(256, rows)
    return pl.pallas_call(
        residual_kernel,
        out_shape=jax.ShapeDtypeStruct((rows, features), BF16),
        grid=(rows // block,),
        in_specs=[
            pl.BlockSpec((block, features), lambda i: (i, 0)),
            pl.BlockSpec((block, features), lambda i: (i, 0)),
            pl.BlockSpec((block, scales.shape[1]), lambda i: (i, 0)),
        ],
        out_specs=pl.BlockSpec((block, features), lambda i: (i, 0)),
        compiler_params=pltpu.CompilerParams(vmem_limit_bytes=48 * MIB),
        name="residual_tile",
    )(weight, codes, scales)


def product_kernel(residual_ref, hr_ref, out_ref):
    out_ref[...] = jnp.dot(residual_ref[...], hr_ref[...], preferred_element_type=F32).astype(BF16)


def partial_product(residual, hr):
    rows, features = residual.shape
    rank = hr.shape[1]
    block = min(512, rows)
    return pl.pallas_call(
        product_kernel,
        out_shape=jax.ShapeDtypeStruct((rows, rank), BF16),
        grid=(rows // block,),
        in_specs=[
            pl.BlockSpec((block, features), lambda i: (i, 0)),
            pl.BlockSpec((features, rank), lambda i: (0, 0)),
        ],
        out_specs=pl.BlockSpec((block, rank), lambda i: (i, 0)),
        compiler_params=pltpu.CompilerParams(vmem_limit_bytes=48 * MIB),
        name="partial_product",
    )(residual, hr)


def hessian_rows(pieces, first, cols, earlier, index, shape, scale, after):
    tokens, block = pieces[0].shape
    count = len(pieces)
    tile = min(512, cols.shape[1])
    ins = [first, *pieces, cols]
    specs = [pl.BlockSpec(memory_space=pltpu.SMEM)]
    specs += [pl.BlockSpec((tokens, block), lambda j: (0, 0))] * count
    specs.append(pl.BlockSpec((count * tokens, tile), lambda j: (0, j)))
    aliases = {}
    if earlier is not None:
        aliases = {len(ins): 0}
        ins.append(earlier)
        specs.append(pl.BlockSpec(memory_space=pl.ANY))
    for value in after:
        ins.append(value)
        specs.append(pl.BlockSpec(memory_space=pl.ANY))

    def kernel(first_ref, *refs):
        cols_ref = refs[count]
        out_ref, rows_ref, turned_ref = refs[-3:]

        @pl.when(pl.program_id(0) == 0)
        def _():
            for k in range(count):
                at = pl.multiple_of((first_ref[0] ^ k) * tokens, tokens)
                rows_ref[pl.ds(at, tokens), :] = refs[k][...]
            turned_ref[...] = rows_ref[...].T

        total = jnp.dot(turned_ref[...], cols_ref[...], preferred_element_type=F32)
        out_ref[...] = (total * scale).astype(BF16)

    return pl.pallas_call(
        kernel,
        out_shape=jax.ShapeDtypeStruct(shape, BF16),
        grid=(cols.shape[1] // tile,),
        in_specs=specs,
        out_specs=pl.BlockSpec((block, tile), lambda j: (index, j)),
        scratch_shapes=[
            pltpu.VMEM((count * tokens, block), BF16),
            pltpu.VMEM((block, count * tokens), BF16),
        ],
        input_output_aliases=aliases,
        compiler_params=pltpu.CompilerParams(vmem_limit_bytes=48 * MIB),
        name="hessian_rows",
    )(*ins)


def pair_sum(values):
    while len(values) > 1:
        values = [values[i] + values[i + 1] for i in range(0, len(values), 2)]
    return values[0]


def body(activations, weight_tile, codes, group_scales, right_factor):
    wide_count = lax.axis_size("wide")
    narrow_count = lax.axis_size("narrow")
    wide_index = lax.axis_index("wide")
    narrow_index = lax.axis_index("narrow")
    tokens, features = activations.shape
    rows = weight_tile.shape[0]
    split = features // rows
    scale = 1.0 / (tokens * wide_count)

    cols = lax.all_gather(activations, "wide", axis=0, tiled=True)

    right_block = lax.dynamic_slice_in_dim(right_factor, narrow_index * features, features, 0)
    product = jnp.dot(activations, right_block, preferred_element_type=F32)
    product = pair_sum([product] + [flip(product, "narrow", m) for m in range(1, narrow_count)])
    y_blocks = [product] + [flip(product, "wide", m) for m in range(1, wide_count)]

    height = rows // CHUNKS
    row_pieces = []
    for chunk in range(CHUNKS):
        operands = []
        for k in range(split):
            at = ((wide_index ^ k) % split) * rows + chunk * height
            operands.append(lax.dynamic_slice_in_dim(activations, at, height, 1))
        pieces = []
        for k in range(wide_count):
            pairs = []
            for w in range(wide_count):
                u = w ^ k
                for n in range(narrow_count):
                    target = (n * split + u % split) * narrow_count + u // split
                    pairs.append((w * narrow_count + n, target))
            pieces.append(lax.ppermute(operands[k % split], ("wide", "narrow"), pairs))
        row_pieces.append(pieces)
    first = (narrow_index * split + wide_index % split).astype(jnp.int32).reshape(1)

    residual = residual_tile(weight_tile, codes, group_scales)
    shape = (rows, features)
    hessian = hessian_rows(row_pieces[0], first, cols, None, 0, shape, scale, [residual])

    hr, gram = hr_and_gram(
        cols, y_blocks, wide_index.astype(jnp.int32).reshape(1), scale, [hessian]
    )
    partial = partial_product(residual, hr)
    share = rows // narrow_count
    received = []
    for m in range(narrow_count):
        piece = lax.dynamic_slice_in_dim(partial, (narrow_index ^ m) * share, share, 0)
        received.append(flip(piece, "narrow", m) if m else piece)
    residual_product = pair_sum([piece.astype(F32) for piece in received])

    for chunk in range(1, CHUNKS):
        hessian = hessian_rows(
            row_pieces[chunk], first, cols, hessian, chunk, shape, scale, [partial]
        )
    return residual_product, gram, hessian


def solution(mesh):
    in_specs = (
        P("wide", "narrow"),
        P("wide", "narrow"),
        P("wide", "narrow"),
        P("wide", "narrow"),
        P(),
    )
    out_specs = (P(("wide", "narrow"), None), P(), P("wide", "narrow"))
    return jax.shard_map(body, mesh=mesh, in_specs=in_specs, out_specs=out_specs, check_vma=False)
```

time: 510 us -> 280 us (0.55)
  the two profiles are of different devices: /device:TPU:0 before, /device:TPU:3 now
where the time goes in v4:
time: 280 us; the launch traced here: 279 us
  waiting for transfers between devices  110 us (39%)
  starting transfers between devices  70.9 us (25%)
  Pallas kernels  69.8 us (25%)
  between operations  14.3 us (5%)
  local copies, waits for them, and re-layouts  9.71 us (3%)
    ppermute x16, waiting for transfers between devices, body(): pieces.append(lax.ppermute(operands[k % split], ('wide', 'narrow'), pairs))  66.8 us
    ppermute x16, starting transfers between devices, body(): pieces.append(lax.ppermute(operands[k % split], ('wide', 'narrow'), pairs))  46.2 us
    ppermute x13, waiting for transfers between devices, flip(): return lax.ppermute(value, axis, [(i, i ^ mask) for i in range(count)])  42.4 us
    pallas_call x2, Pallas kernels, hessian_rows(): pl.pallas_call(kernel, out_shape=jax.ShapeDtypeStruct(shape, BF16), grid=...  29 us
    ppermute x13, starting transfers between devices, flip(): return lax.ppermute(value, axis, [(i, i ^ mask) for i in range(count)])  24.7 us
    pallas_call x1, Pallas kernels, residual_tile(): pl.pallas_call(residual_kernel, out_shape=jax.ShapeDtypeStruct((rows, fea...  24.1 us
    pallas_call x1, Pallas kernels, partial_product(): pl.pallas_call(product_kernel, out_shape=jax.ShapeDtypeStruct((rows, rank...  8.4 us
    pallas_call x1, Pallas kernels, hr_and_gram(): pl.pallas_call(kernel, out_shape=(jax.ShapeDtypeStruct((features, rank),...  8.29 us
  transfers between devices with their start and end apart: 30, of which 6 were waited for; matrix products, arithmetic and copies ran while one was open for 2% of the time, Pallas kernels for 25%

profile of v4, /device:TPU:3, one launch (start us, length us, event | category | flops | bytes accessed | tf_op | source)
XLA Modules:
  0.0 279.0 jit_solution(4123615293412033694)
XLA Ops:
  7.2 0.0 all-gather.2.cloned.1.call-start
  7.2 0.7 all-gather.2.cloned.1.call-update
  7.9 2.4 fusion.2
  10.3 1.4 collective-permute-start
  11.6 2.1 constant_dynamic-slice_fusion
  13.7 1.9 collective-permute-start.10
  15.7 3.5 %collective-permute-start.11 = (bf16[128,1024]{1,0:T(8,128)(2,1)S(1)}, bf16[128,1024]{1,0:T(8,128)(2,1)S(1)}, u32[]{:S(2)}, u32[]{:S(2)}) collective-permute-start(bf16[128,1024]{1,0:T(8,128)(2,1)S(1)} %get-tuple-element.8), channel_id=1, source_target_pairs={{0,4},{1,12},{2,20},{3,28},{4,0},{5,8},{6,16},{7,24},{8,5},{9,13},... | collective-permute-start | bytes 786440 | tf_op jit(solution)/shard_map/ppermute | solution.py:215
  19.2 0.0 collective-permute-start.12
  19.2 4.2 %collective-permute-start.1 = (f32[128,256]{1,0:T(8,128)S(1)}, f32[128,256]{1,0:T(8,128)S(1)}, u32[]{:S(2)}, u32[]{:S(2)}) collective-permute-start(f32[128,256]{1,0:T(8,128)S(1)} %fusion.2), channel_id=1, source_target_pairs={{0,2},{1,3},{2,0},{3,1},{4,6},{5,7},{6,4},{7,5},{8,10},{9,11},{10,... | collective-permute-start | bytes 393224 | tf_op jit(solution)/shard_map/ppermute | solution.py:18
  23.4 0.0 collective-permute-done
  23.4 2.7 collective-permute-start.2
  26.1 42.4 %collective-permute-done.1 = f32[128,256]{1,0:T(8,128)S(1)} collective-permute-done((f32[128,256]{1,0:T(8,128)S(1)}, f32[128,256]{1,0:T(8,128)S(1)}, u32[]{:S(2)}, u32[]{:S(2)}) %collective-permute-start.1) | collective-permute-done | bytes 131104 | tf_op jit(solution)/shard_map/ppermute | solution.py:18
  68.5 0.0 collective-permute-start.13
  68.5 0.0 collective-permute-done.2
  68.5 1.8 collective-permute-start.14
  70.3 9.7 %collective-permute-start.15 = (bf16[128,1024]{1,0:T(8,128)(2,1)S(1)}, bf16[128,1024]{1,0:T(8,128)(2,1)S(1)}, u32[]{:S(2)}, u32[]{:S(2)}) collective-permute-start(bf16[128,1024]{1,0:T(8,128)(2,1)S(1)} %get-tuple-element.8), channel_id=1, source_target_pairs={{0,6},{1,14},{2,22},{3,30},{4,2},{5,10},{6,18},{7,26},{8,7},{9,15}... | collective-permute-start | bytes 786440 | tf_op jit(solution)/shard_map/ppermute | solution.py:215
  80.0 0.0 collective-permute-done.11.refs_1_
  80.0 0.0 collective-permute-start.16
  80.0 0.0 collective-permute-done.12.refs_2_
  80.0 0.1 collective-permute-start.17
  80.1 5.1 %collective-permute-done.13.refs_3_ = bf16[128,1024]{1,0:T(8,128)(2,1)S(1)} collective-permute-done((bf16[128,1024]{1,0:T(8,128)(2,1)S(1)}, bf16[128,1024]{1,0:T(8,128)(2,1)S(1)}, u32[]{:S(2)}, u32[]{:S(2)}) %collective-permute-start.13) | collective-permute-done | bytes 262176 | tf_op jit(solution)/shard_map/ppermute | solution.py:215
  85.2 2.3 collective-permute-start.3
  87.5 6.7 %collective-permute-done.14.refs_4_ = bf16[128,1024]{1,0:T(8,128)(2,1)S(1)} collective-permute-done((bf16[128,1024]{1,0:T(8,128)(2,1)S(1)}, bf16[128,1024]{1,0:T(8,128)(2,1)S(1)}, u32[]{:S(2)}, u32[]{:S(2)}) %collective-permute-start.14) | collective-permute-done | bytes 262176 | tf_op jit(solution)/shard_map/ppermute | solution.py:215
  94.2 17.8 %collective-permute-done.15.refs_5_ = bf16[128,1024]{1,0:T(8,128)(2,1)S(1)} collective-permute-done((bf16[128,1024]{1,0:T(8,128)(2,1)S(1)}, bf16[128,1024]{1,0:T(8,128)(2,1)S(1)}, u32[]{:S(2)}, u32[]{:S(2)}) %collective-permute-start.15) | collective-permute-done | bytes 262176 | tf_op jit(solution)/shard_map/ppermute | solution.py:215
  112.1 1.9 collective-permute-start.21
  114.0 0.0 collective-permute-done.17.refs_7_
  114.0 0.0 copy-start
  114.0 0.7 copy-done
  114.7 0.0 collective-permute-start.6
  114.7 0.0 collective-permute-done.3.refs_1_
  114.7 0.7 copy-done.2
  115.4 4.5 %collective-permute-start.7 = (f32[128,256]{1,0:T(8,128)S(1)}, f32[128,256]{1,0:T(8,128)S(1)}, u32[]{:S(2)}, u32[]{:S(2)}) collective-permute-start(f32[128,256]{1,0:T(8,128)S(1)} %add_add_fusion.1.refs_0_), channel_id=1, source_target_pairs={{0,20},{4,16},{8,28},{12,24},{16,4},{20,0},{24,12},{28,8},{1,21},{... | collective-permute-start | bytes 393224 | tf_op jit(solution)/shard_map/ppermute | solution.py:18
  119.8 0.0 collective-permute-done.4.refs_2_
  119.8 0.7 copy-done.4
  120.5 5.6 %collective-permute-start.8 = (f32[128,256]{1,0:T(8,128)S(1)}, f32[128,256]{1,0:T(8,128)S(1)}, u32[]{:S(2)}, u32[]{:S(2)}) collective-permute-start(f32[128,256]{1,0:T(8,128)S(1)} %add_add_fusion.1.refs_0_), channel_id=1, source_target_pairs={{0,24},{4,28},{8,16},{12,20},{16,8},{20,12},{24,0},{28,4},{1,25},{... | collective-permute-start | bytes 393224 | tf_op jit(solution)/shard_map/ppermute | solution.py:18
  126.1 0.7 copy-done.6
  126.8 0.4 collective-permute-start.9
  127.2 0.7 copy-done.8
  127.9 11.2 %collective-permute-start.22 = (bf16[128,1024]{1,0:T(8,128)(2,1)}, bf16[128,1024]{1,0:T(8,128)(2,1)S(1)}, u32[]{:S(2)}, u32[]{:S(2)}) collective-permute-start(bf16[128,1024]{1,0:T(8,128)(2,1)} %get-tuple-element.7), channel_id=1, source_target_pairs={{0,4},{1,12},{2,20},{3,28},{4,0},{5,8},{6,16},{7,24},{8,5},{9,13},... | collective-permute-start | bytes 786440 | tf_op jit(solution)/shard_map/ppermute | solution.py:215
  139.1 0.0 collective-permute-done.7.refs_5_
  139.1 0.7 copy-done.10
  139.8 1.6 collective-permute-start.23
  141.3 0.6 copy-done.12
  142.0 0.7 collective-permute-start.24
  142.6 0.0 collective-permute-done.9.refs_7_
  142.6 0.7 copy-done.14
  143.3 4.3 %collective-permute-start.25 = (bf16[128,1024]{1,0:T(8,128)(2,1)}, bf16[128,1024]{1,0:T(8,128)(2,1)}, u32[]{:S(2)}, u32[]{:S(2)}) collective-permute-start(bf16[128,1024]{1,0:T(8,128)(2,1)} %get-tuple-element.10), channel_id=1, source_target_pairs={{0,2},{1,10},{2,18},{3,26},{4,6},{5,14},{6,22},{7,30},{8,3},{9,11}... | collective-permute-start | bytes 786440 | tf_op jit(solution)/shard_map/ppermute | solution.py:215
  147.6 1.0 collective-permute-start.26
  148.7 1.3 copy.9.scales_ref
  150.0 24.1 %residual_tile.1.refs_9_.residual_ref = bf16[2048,4096]{1,0:T(8,128)(2,1)} custom-call(bf16[2048,4096]{1,0:T(8,128)(2,1)} %weight_ref.1, s32[2048,4096]{1,0:T(8,128)} %codes_ref.1, f32[2048,32]{1,0:T(8,128)S(1)} %copy.9.scales_ref), custom_call_target="tpu_custom_call" | custom-call | tf_op jit(solution)/shard_map/residual_tile/pallas_call | solution.py:93
  174.1 0.9 copy-done.1
  175.1 14.4 %hessian_rows.2.refs_8_.refs_9_ = bf16[2048,4096]{1,0:T(8,128)(2,1)} custom-call(s32[1]{0:T(128)} %bitcast.2.first_ref, bf16[128,1024]{1,0:T(8,128)(2,1)S(1)} %collective-permute-done.10.refs_0_, bf16[128,1024]{1,0:T(8,128)(2,1)S(1)} %collective-permute-done.11.refs_1_, bf16[128,1024]{1,0:T(8,128)(2,1)S(1)} %collective-permute-done.12.refs_2_, ...), custom_call_target="tpu_custom_call" | custom-call | tf_op jit(solution)/shard_map/hessian_rows/pallas_call | solution.py:161
  189.5 8.3 %hr_and_gram.1 = (bf16[4096,256]{1,0:T(8,128)(2,1)S(1)}, f32[256,256]{1,0:T(8,128)}) custom-call(s32[1]{0:T(128)} %bitcast.where_ref, bf16[1024,4096]{1,0:T(8,128)(2,1)} %all-gather.2.cloned.1.call-done.refs_8_.cols_ref, f32[128,256]{1,0:T(8,128)S(1)} %add_add_fusion.1.refs_0_, f32[128,256]{1,0:T(8,128)S(1)} %copy-done.3, f32[128,256]{1,0:T(8,128)S(1)} %copy-done.5, ...), custom_call_target="tpu_custom_call" | custom-call | tf_op jit(solution)/shard_map/hr_and_gram/pallas_call | solution.py:52
  197.8 8.4 %partial_product.1.refs_10_ = bf16[2048,256]{1,0:T(8,128)(2,1)S(1)} custom-call(bf16[2048,4096]{1,0:T(8,128)(2,1)} %residual_tile.1.refs_9_.residual_ref, bf16[4096,256]{1,0:T(8,128)(2,1)S(1)} %get-tuple-element.5.hr_ref), custom_call_target="tpu_custom_call" | custom-call | tf_op jit(solution)/shard_map/partial_product/pallas_call | solution.py:116
  206.2 0.1 constant_dynamic-slice_fusion.4
  206.3 0.1 collective-permute-start.27
  206.4 8.4 %collective-permute-start.28 = (bf16[128,1024]{1,0:T(8,128)(2,1)}, bf16[128,1024]{1,0:T(8,128)(2,1)S(1)}, u32[]{:S(2)}, u32[]{:S(2)}) collective-permute-start(bf16[128,1024]{1,0:T(8,128)(2,1)} %get-tuple-element.7), channel_id=1, source_target_pairs={{0,7},{1,15},{2,23},{3,31},{4,3},{5,11},{6,19},{7,27},{8,6},{9,14}... | collective-permute-start | bytes 786440 | tf_op jit(solution)/shard_map/ppermute | solution.py:215
  214.8 0.1 collective-permute-start.18
  214.9 0.0 collective-permute-start.19
  214.9 3.5 %collective-permute-start.20 = (bf16[512,256]{1,0:T(8,128)(2,1)S(1)}, bf16[512,256]{1,0:T(8,128)(2,1)}, u32[]{:S(2)}, u32[]{:S(2)}) collective-permute-start(bf16[512,256]{1,0:T(8,128)(2,1)S(1)} %get-tuple-element.12), channel_id=1, source_target_pairs={{0,3},{1,2},{2,1},{3,0},{4,7},{5,6},{6,5},{7,4},{8,11},{9,10},{10,... | collective-permute-start | bytes 786440 | tf_op jit(solution)/shard_map/ppermute | solution.py:18
  218.4 16.0 %collective-permute-done.27.refs_6_ = bf16[128,1024]{1,0:T(8,128)(2,1)S(1)} collective-permute-done((bf16[128,1024]{1,0:T(8,128)(2,1)}, bf16[128,1024]{1,0:T(8,128)(2,1)S(1)}, u32[]{:S(2)}, u32[]{:S(2)}) %collective-permute-start.27) | collective-permute-done | bytes 262176 | tf_op jit(solution)/shard_map/ppermute | solution.py:215
  234.4 21.2 %collective-permute-done.28.refs_7_ = bf16[128,1024]{1,0:T(8,128)(2,1)S(1)} collective-permute-done((bf16[128,1024]{1,0:T(8,128)(2,1)}, bf16[128,1024]{1,0:T(8,128)(2,1)S(1)}, u32[]{:S(2)}, u32[]{:S(2)}) %collective-permute-start.28) | collective-permute-done | bytes 262176 | tf_op jit(solution)/shard_map/ppermute | solution.py:215
  255.6 14.6 %hessian_rows.3 = bf16[2048,4096]{1,0:T(8,128)(2,1)} custom-call(s32[1]{0:T(128)} %bitcast.2.first_ref, bf16[128,1024]{1,0:T(8,128)(2,1)S(1)} %collective-permute-done.21.refs_0_, bf16[128,1024]{1,0:T(8,128)(2,1)S(1)} %collective-permute-done.22.refs_1_, bf16[128,1024]{1,0:T(8,128)(2,1)} %collective-permute-done.23.refs_2_, ...), custom_call_target="tpu_custom_call", output_to_operand_aliasing={{}: (10, {})} | custom-call | tf_op jit(solution)/shard_map/hessian_rows/pallas_call | solution.py:161
  270.3 1.9 add_add_fusion
  (40 shorter events, 0.1 us)
Async XLA Ops:
  7.2 166.9 %all-gather.2.cloned.1.call-start = ((), (), s32[]{:S(2)}) async-start(), calls=%async_computation | async-start | bytes 9437184 | tf_op jit(solution)/shard_map/all_gather | solution.py:193
  10.3 13.1 %collective-permute-start = (f32[128,256]{1,0:T(8,128)S(1)}, f32[128,256]{1,0:T(8,128)S(1)}, u32[]{:S(2)}, u32[]{:S(2)}) collective-permute-start(f32[128,256]{1,0:T(8,128)S(1)} %fusion.2), channel_id=1, source_target_pairs={{0,1},{1,0},{2,3},{3,2},{4,5},{5,4},{6,7},{7,6},{8,9},{9,8},{10,11... | collective-permute-start | bytes 393224 | tf_op jit(solution)/shard_map/ppermute | solution.py:18
  13.7 56.6 %collective-permute-start.10 = (bf16[128,1024]{1,0:T(8,128)(2,1)S(1)}, bf16[128,1024]{1,0:T(8,128)(2,1)S(1)}, u32[]{:S(2)}, u32[]{:S(2)}) collective-permute-start(bf16[128,1024]{1,0:T(8,128)(2,1)S(1)} %get-tuple-element.9), channel_id=1, source_target_pairs={{0,0},{1,8},{2,16},{3,24},{4,4},{5,12},{6,20},{7,28},{8,1},{9,9},{... | collective-permute-start | bytes 786440 | tf_op jit(solution)/shard_map/ppermute | solution.py:215
  15.7 64.3 %collective-permute-start.11 = (bf16[128,1024]{1,0:T(8,128)(2,1)S(1)}, bf16[128,1024]{1,0:T(8,128)(2,1)S(1)}, u32[]{:S(2)}, u32[]{:S(2)}) collective-permute-start(bf16[128,1024]{1,0:T(8,128)(2,1)S(1)} %get-tuple-element.8), channel_id=1, source_target_pairs={{0,4},{1,12},{2,20},{3,28},{4,0},{5,8},{6,16},{7,24},{8,5},{9,13},... | collective-permute-start | bytes 786440 | tf_op jit(solution)/shard_map/ppermute | solution.py:215
  19.2 60.8 %collective-permute-start.12 = (bf16[128,1024]{1,0:T(8,128)(2,1)S(1)}, bf16[128,1024]{1,0:T(8,128)(2,1)S(1)}, u32[]{:S(2)}, u32[]{:S(2)}) collective-permute-start(bf16[128,1024]{1,0:T(8,128)(2,1)S(1)} %get-tuple-element.9), channel_id=1, source_target_pairs={{0,1},{1,9},{2,17},{3,25},{4,5},{5,13},{6,21},{7,29},{8,0},{9,8},{... | collective-permute-start | bytes 786440 | tf_op jit(solution)/shard_map/ppermute | solution.py:215
  19.2 49.3 %collective-permute-start.1 = (f32[128,256]{1,0:T(8,128)S(1)}, f32[128,256]{1,0:T(8,128)S(1)}, u32[]{:S(2)}, u32[]{:S(2)}) collective-permute-start(f32[128,256]{1,0:T(8,128)S(1)} %fusion.2), channel_id=1, source_target_pairs={{0,2},{1,3},{2,0},{3,1},{4,6},{5,7},{6,4},{7,5},{8,10},{9,11},{10,... | collective-permute-start | bytes 393224 | tf_op jit(solution)/shard_map/ppermute | solution.py:18
  23.4 45.2 %collective-permute-start.2 = (f32[128,256]{1,0:T(8,128)S(1)}, f32[128,256]{1,0:T(8,128)S(1)}, u32[]{:S(2)}, u32[]{:S(2)}) collective-permute-start(f32[128,256]{1,0:T(8,128)S(1)} %fusion.2), channel_id=1, source_target_pairs={{0,3},{1,2},{2,1},{3,0},{4,7},{5,6},{6,5},{7,4},{8,11},{9,10},{10,... | collective-permute-start | bytes 393224 | tf_op jit(solution)/shard_map/ppermute | solution.py:18
  68.5 16.7 %collective-permute-start.13 = (bf16[128,1024]{1,0:T(8,128)(2,1)S(1)}, bf16[128,1024]{1,0:T(8,128)(2,1)S(1)}, u32[]{:S(2)}, u32[]{:S(2)}) collective-permute-start(bf16[128,1024]{1,0:T(8,128)(2,1)S(1)} %get-tuple-element.8), channel_id=1, source_target_pairs={{0,5},{1,13},{2,21},{3,29},{4,1},{5,9},{6,17},{7,25},{8,4},{9,12},... | collective-permute-start | bytes 786440 | tf_op jit(solution)/shard_map/ppermute | solution.py:215
  68.5 25.7 %collective-permute-start.14 = (bf16[128,1024]{1,0:T(8,128)(2,1)S(1)}, bf16[128,1024]{1,0:T(8,128)(2,1)S(1)}, u32[]{:S(2)}, u32[]{:S(2)}) collective-permute-start(bf16[128,1024]{1,0:T(8,128)(2,1)S(1)} %get-tuple-element.9), channel_id=1, source_target_pairs={{0,2},{1,10},{2,18},{3,26},{4,6},{5,14},{6,22},{7,30},{8,3},{9,11}... | collective-permute-start | bytes 786440 | tf_op jit(solution)/shard_map/ppermute | solution.py:215
  70.3 41.7 %collective-permute-start.15 = (bf16[128,1024]{1,0:T(8,128)(2,1)S(1)}, bf16[128,1024]{1,0:T(8,128)(2,1)S(1)}, u32[]{:S(2)}, u32[]{:S(2)}) collective-permute-start(bf16[128,1024]{1,0:T(8,128)(2,1)S(1)} %get-tuple-element.8), channel_id=1, source_target_pairs={{0,6},{1,14},{2,22},{3,30},{4,2},{5,10},{6,18},{7,26},{8,7},{9,15}... | collective-permute-start | bytes 786440 | tf_op jit(solution)/shard_map/ppermute | solution.py:215
  80.0 32.1 %collective-permute-start.16 = (bf16[128,1024]{1,0:T(8,128)(2,1)S(1)}, bf16[128,1024]{1,0:T(8,128)(2,1)S(1)}, u32[]{:S(2)}, u32[]{:S(2)}) collective-permute-start(bf16[128,1024]{1,0:T(8,128)(2,1)S(1)} %get-tuple-element.9), channel_id=1, source_target_pairs={{0,3},{1,11},{2,19},{3,27},{4,7},{5,15},{6,23},{7,31},{8,2},{9,10}... | collective-permute-start | bytes 786440 | tf_op jit(solution)/shard_map/ppermute | solution.py:215
  80.0 34.0 %collective-permute-start.17 = (bf16[128,1024]{1,0:T(8,128)(2,1)S(1)}, bf16[128,1024]{1,0:T(8,128)(2,1)S(1)}, u32[]{:S(2)}, u32[]{:S(2)}) collective-permute-start(bf16[128,1024]{1,0:T(8,128)(2,1)S(1)} %get-tuple-element.8), channel_id=1, source_target_pairs={{0,7},{1,15},{2,23},{3,31},{4,3},{5,11},{6,19},{7,27},{8,6},{9,14}... | collective-permute-start | bytes 786440 | tf_op jit(solution)/shard_map/ppermute | solution.py:215
  85.2 29.5 %collective-permute-start.3 = (f32[128,256]{1,0:T(8,128)S(1)}, f32[128,256]{1,0:T(8,128)S(1)}, u32[]{:S(2)}, u32[]{:S(2)}) collective-permute-start(f32[128,256]{1,0:T(8,128)S(1)} %add_add_fusion.1.refs_0_), channel_id=1, source_target_pairs={{0,4},{4,0},{8,12},{12,8},{16,20},{20,16},{24,28},{28,24},{1,5},{5... | collective-permute-start | bytes 393224 | tf_op jit(solution)/shard_map/ppermute | solution.py:18
  94.2 25.6 %collective-permute-start.4 = (f32[128,256]{1,0:T(8,128)S(1)}, f32[128,256]{1,0:T(8,128)S(1)}, u32[]{:S(2)}, u32[]{:S(2)}) collective-permute-start(f32[128,256]{1,0:T(8,128)S(1)} %add_add_fusion.1.refs_0_), channel_id=1, source_target_pairs={{0,8},{4,12},{8,0},{12,4},{16,24},{20,28},{24,16},{28,20},{1,9},{5... | collective-permute-start | bytes 393224 | tf_op jit(solution)/shard_map/ppermute | solution.py:18
  112.0 14.1 %collective-permute-start.5 = (f32[128,256]{1,0:T(8,128)S(1)}, f32[128,256]{1,0:T(8,128)S(1)}, u32[]{:S(2)}, u32[]{:S(2)}) collective-permute-start(f32[128,256]{1,0:T(8,128)S(1)} %add_add_fusion.1.refs_0_), channel_id=1, source_target_pairs={{0,12},{4,8},{8,4},{12,0},{16,28},{20,24},{24,20},{28,16},{1,13},{... | collective-permute-start | bytes 393224 | tf_op jit(solution)/shard_map/ppermute | solution.py:18
  112.1 35.6 %collective-permute-start.21 = (bf16[128,1024]{1,0:T(8,128)(2,1)}, bf16[128,1024]{1,0:T(8,128)(2,1)S(1)}, u32[]{:S(2)}, u32[]{:S(2)}) collective-permute-start(bf16[128,1024]{1,0:T(8,128)(2,1)} %get-tuple-element.10), channel_id=1, source_target_pairs={{0,0},{1,8},{2,16},{3,24},{4,4},{5,12},{6,20},{7,28},{8,1},{9,9},{... | collective-permute-start | bytes 786440 | tf_op jit(solution)/shard_map/ppermute | solution.py:215
  114.0 0.7 copy-start
  114.7 12.5 %collective-permute-start.6 = (f32[128,256]{1,0:T(8,128)S(1)}, f32[128,256]{1,0:T(8,128)S(1)}, u32[]{:S(2)}, u32[]{:S(2)}) collective-permute-start(f32[128,256]{1,0:T(8,128)S(1)} %add_add_fusion.1.refs_0_), channel_id=1, source_target_pairs={{0,16},{4,20},{8,24},{12,28},{16,0},{20,4},{24,8},{28,12},{1,17},{... | collective-permute-start | bytes 393224 | tf_op jit(solution)/shard_map/ppermute | solution.py:18
  114.7 0.7 copy-start.2
  115.4 23.7 %collective-permute-start.7 = (f32[128,256]{1,0:T(8,128)S(1)}, f32[128,256]{1,0:T(8,128)S(1)}, u32[]{:S(2)}, u32[]{:S(2)}) collective-permute-start(f32[128,256]{1,0:T(8,128)S(1)} %add_add_fusion.1.refs_0_), channel_id=1, source_target_pairs={{0,20},{4,16},{8,28},{12,24},{16,4},{20,0},{24,12},{28,8},{1,21},{... | collective-permute-start | bytes 393224 | tf_op jit(solution)/shard_map/ppermute | solution.py:18
  119.8 0.7 copy-start.4
  120.5 20.8 %collective-permute-start.8 = (f32[128,256]{1,0:T(8,128)S(1)}, f32[128,256]{1,0:T(8,128)S(1)}, u32[]{:S(2)}, u32[]{:S(2)}) collective-permute-start(f32[128,256]{1,0:T(8,128)S(1)} %add_add_fusion.1.refs_0_), channel_id=1, source_target_pairs={{0,24},{4,28},{8,16},{12,20},{16,8},{20,12},{24,0},{28,4},{1,25},{... | collective-permute-start | bytes 393224 | tf_op jit(solution)/shard_map/ppermute | solution.py:18
  126.1 0.7 copy-start.6
  126.8 15.9 %collective-permute-start.9 = (f32[128,256]{1,0:T(8,128)S(1)}, f32[128,256]{1,0:T(8,128)S(1)}, u32[]{:S(2)}, u32[]{:S(2)}) collective-permute-start(f32[128,256]{1,0:T(8,128)S(1)} %add_add_fusion.1.refs_0_), channel_id=1, source_target_pairs={{0,28},{4,24},{8,20},{12,16},{16,12},{20,8},{24,4},{28,0},{1,29},{... | collective-permute-start | bytes 393224 | tf_op jit(solution)/shard_map/ppermute | solution.py:18
  127.2 0.7 copy-start.8
  127.9 78.4 %collective-permute-start.22 = (bf16[128,1024]{1,0:T(8,128)(2,1)}, bf16[128,1024]{1,0:T(8,128)(2,1)S(1)}, u32[]{:S(2)}, u32[]{:S(2)}) collective-permute-start(bf16[128,1024]{1,0:T(8,128)(2,1)} %get-tuple-element.7), channel_id=1, source_target_pairs={{0,4},{1,12},{2,20},{3,28},{4,0},{5,8},{6,16},{7,24},{8,5},{9,13},... | collective-permute-start | bytes 786440 | tf_op jit(solution)/shard_map/ppermute | solution.py:215
  139.1 0.7 copy-start.10
  139.8 66.6 %collective-permute-start.23 = (bf16[128,1024]{1,0:T(8,128)(2,1)}, bf16[128,1024]{1,0:T(8,128)(2,1)}, u32[]{:S(2)}, u32[]{:S(2)}) collective-permute-start(bf16[128,1024]{1,0:T(8,128)(2,1)} %get-tuple-element.10), channel_id=1, source_target_pairs={{0,1},{1,9},{2,17},{3,25},{4,5},{5,13},{6,21},{7,29},{8,0},{9,8},{... | collective-permute-start | bytes 786440 | tf_op jit(solution)/shard_map/ppermute | solution.py:215
  141.3 0.6 copy-start.12
  142.0 72.9 %collective-permute-start.24 = (bf16[128,1024]{1,0:T(8,128)(2,1)}, bf16[128,1024]{1,0:T(8,128)(2,1)}, u32[]{:S(2)}, u32[]{:S(2)}) collective-permute-start(bf16[128,1024]{1,0:T(8,128)(2,1)} %get-tuple-element.7), channel_id=1, source_target_pairs={{0,5},{1,13},{2,21},{3,29},{4,1},{5,9},{6,17},{7,25},{8,4},{9,12},... | collective-permute-start | bytes 786440 | tf_op jit(solution)/shard_map/ppermute | solution.py:215
  142.6 0.7 copy-start.14
  143.3 71.6 %collective-permute-start.25 = (bf16[128,1024]{1,0:T(8,128)(2,1)}, bf16[128,1024]{1,0:T(8,128)(2,1)}, u32[]{:S(2)}, u32[]{:S(2)}) collective-permute-start(bf16[128,1024]{1,0:T(8,128)(2,1)} %get-tuple-element.10), channel_id=1, source_target_pairs={{0,2},{1,10},{2,18},{3,26},{4,6},{5,14},{6,22},{7,30},{8,3},{9,11}... | collective-permute-start | bytes 786440 | tf_op jit(solution)/shard_map/ppermute | solution.py:215
  147.6 67.3 %collective-permute-start.26 = (bf16[128,1024]{1,0:T(8,128)(2,1)}, bf16[128,1024]{1,0:T(8,128)(2,1)}, u32[]{:S(2)}, u32[]{:S(2)}) collective-permute-start(bf16[128,1024]{1,0:T(8,128)(2,1)} %get-tuple-element.7), channel_id=1, source_target_pairs={{0,6},{1,14},{2,22},{3,30},{4,2},{5,10},{6,18},{7,26},{8,7},{9,15}... | collective-permute-start | bytes 786440 | tf_op jit(solution)/shard_map/ppermute | solution.py:215
  174.1 1.0 copy-start.1
  175.0 14.4 %copy-start.3 = (f32[128,256]{1,0:T(8,128)S(1)}, f32[128,256]{1,0:T(8,128)}, u32[]{:S(2)}) copy-start(f32[128,256]{1,0:T(8,128)} %copy-done.2) | copy-start | bytes 393220
  175.0 14.4 %copy-start.5 = (f32[128,256]{1,0:T(8,128)S(1)}, f32[128,256]{1,0:T(8,128)}, u32[]{:S(2)}) copy-start(f32[128,256]{1,0:T(8,128)} %copy-done.4) | copy-start | bytes 393220
  175.0 14.4 %copy-start.7 = (f32[128,256]{1,0:T(8,128)S(1)}, f32[128,256]{1,0:T(8,128)}, u32[]{:S(2)}) copy-start(f32[128,256]{1,0:T(8,128)} %copy-done.6) | copy-start | bytes 393220
  175.0 14.4 %copy-start.9 = (f32[128,256]{1,0:T(8,128)S(1)}, f32[128,256]{1,0:T(8,128)}, u32[]{:S(2)}) copy-start(f32[128,256]{1,0:T(8,128)} %copy-done.8) | copy-start | bytes 393220
  175.1 14.4 %copy-start.11 = (f32[128,256]{1,0:T(8,128)S(1)}, f32[128,256]{1,0:T(8,128)}, u32[]{:S(2)}) copy-start(f32[128,256]{1,0:T(8,128)} %copy-done.10) | copy-start | bytes 393220
  175.1 14.4 %copy-start.13 = (f32[128,256]{1,0:T(8,128)S(1)}, f32[128,256]{1,0:T(8,128)}, u32[]{:S(2)}) copy-start(f32[128,256]{1,0:T(8,128)} %copy-done.12) | copy-start | bytes 393220
  175.1 14.4 %copy-start.15 = (f32[128,256]{1,0:T(8,128)S(1)}, f32[128,256]{1,0:T(8,128)}, u32[]{:S(2)}) copy-start(f32[128,256]{1,0:T(8,128)} %copy-done.14) | copy-start | bytes 393220
  206.3 28.1 %collective-permute-start.27 = (bf16[128,1024]{1,0:T(8,128)(2,1)}, bf16[128,1024]{1,0:T(8,128)(2,1)S(1)}, u32[]{:S(2)}, u32[]{:S(2)}) collective-permute-start(bf16[128,1024]{1,0:T(8,128)(2,1)} %get-tuple-element.10), channel_id=1, source_target_pairs={{0,3},{1,11},{2,19},{3,27},{4,7},{5,15},{6,23},{7,31},{8,2},{9,10}... | collective-permute-start | bytes 786440 | tf_op jit(solution)/shard_map/ppermute | solution.py:215
  206.4 49.2 %collective-permute-start.28 = (bf16[128,1024]{1,0:T(8,128)(2,1)}, bf16[128,1024]{1,0:T(8,128)(2,1)S(1)}, u32[]{:S(2)}, u32[]{:S(2)}) collective-permute-start(bf16[128,1024]{1,0:T(8,128)(2,1)} %get-tuple-element.7), channel_id=1, source_target_pairs={{0,7},{1,15},{2,23},{3,31},{4,3},{5,11},{6,19},{7,27},{8,6},{9,14}... | collective-permute-start | bytes 786440 | tf_op jit(solution)/shard_map/ppermute | solution.py:215
  214.8 55.4 %collective-permute-start.18 = (bf16[512,256]{1,0:T(8,128)(2,1)S(1)}, bf16[512,256]{1,0:T(8,128)(2,1)S(1)}, u32[]{:S(2)}, u32[]{:S(2)}) collective-permute-start(bf16[512,256]{1,0:T(8,128)(2,1)S(1)} %get-tuple-element.11), channel_id=1, source_target_pairs={{0,1},{1,0},{2,3},{3,2},{4,5},{5,4},{6,7},{7,6},{8,9},{9,8},{10,11... | collective-permute-start | bytes 786440 | tf_op jit(solution)/shard_map/ppermute | solution.py:18
  214.9 55.3 %collective-permute-start.19 = (bf16[512,256]{1,0:T(8,128)(2,1)S(1)}, bf16[512,256]{1,0:T(8,128)(2,1)S(1)}, u32[]{:S(2)}, u32[]{:S(2)}) collective-permute-start(bf16[512,256]{1,0:T(8,128)(2,1)S(1)} %get-tuple-element.13), channel_id=1, source_target_pairs={{0,2},{1,3},{2,0},{3,1},{4,6},{5,7},{6,4},{7,5},{8,10},{9,11},{10,... | collective-permute-start | bytes 786440 | tf_op jit(solution)/shard_map/ppermute | solution.py:18
  214.9 55.3 %collective-permute-start.20 = (bf16[512,256]{1,0:T(8,128)(2,1)S(1)}, bf16[512,256]{1,0:T(8,128)(2,1)}, u32[]{:S(2)}, u32[]{:S(2)}) collective-permute-start(bf16[512,256]{1,0:T(8,128)(2,1)S(1)} %get-tuple-element.12), channel_id=1, source_target_pairs={{0,3},{1,2},{2,1},{3,0},{4,7},{5,6},{6,5},{7,4},{8,11},{9,10},{10,... | collective-permute-start | bytes 786440 | tf_op jit(solution)/shard_map/ppermute | solution.py:18
Sparse Core Ops, SparseCore 0:
  9.9 97.3 all-gather.1

commit v5 on v1

v5 whole, which is shorter than its diff:
```python
import functools

import jax
import jax.numpy as jnp
from jax import lax
from jax.experimental import pallas as pl
from jax.experimental.pallas import tpu as pltpu
from jax.sharding import PartitionSpec as P

PARTS = (4, 2, 2)
MIB = 1024 * 1024
BF16 = jnp.bfloat16
F32 = jnp.float32


def flip(value, axis, mask):
    count = lax.axis_size(axis)
    return lax.ppermute(value, axis, [(i, i ^ mask) for i in range(count)])


def hold(value, *after):
    return pl.pallas_call(
        lambda *refs: None,
        out_shape=jax.ShapeDtypeStruct(value.shape, value.dtype),
        in_specs=[pl.BlockSpec(memory_space=pl.ANY)] * (1 + len(after)),
        out_specs=pl.BlockSpec(memory_space=pl.ANY),
        input_output_aliases={0: 0},
        name="hold",
    )(value, *after)


def columns_hr_gram(pieces, y_blocks, where, scale):
    count, tokens, rank = y_blocks.shape
    halves = len(pieces) // count
    width = pieces[0].shape[1]
    features = halves * width
    step = min(1024, width)

    def kernel(where_ref, y_ref, *refs):
        cols_ref, hr_ref, gram_ref, order_ref, sems = refs[len(pieces) :]
        me = where_ref[0]
        copies = []
        for half in range(halves):
            for mask in range(count):
                at = pl.multiple_of((me ^ mask) * tokens, tokens)
                index = half * count + mask
                copy = pltpu.make_async_copy(
                    refs[index],
                    cols_ref.at[pl.ds(at, tokens), pl.ds(half * width, width)],
                    sems.at[index],
                )
                copy.start()
                copies.append(copy)
        for mask in range(count):
            at = pl.multiple_of((me ^ mask) * tokens, tokens)
            order_ref[pl.ds(at, tokens), :] = y_ref[mask]
        turned = order_ref[...].T
        gram = jnp.dot(turned, order_ref[...], preferred_element_type=F32)
        gram_ref[...] = gram * scale
        for half in range(halves):
            for copy in copies[half * count : (half + 1) * count]:
                copy.wait()
            for start in range(half * width, (half + 1) * width, step):
                block = cols_ref[:, start : start + step]
                total = jnp.dot(turned, block, preferred_element_type=F32) * scale
                hr_ref[start : start + step, :] = total.T.astype(BF16)

    return pl.pallas_call(
        kernel,
        out_shape=(
            jax.ShapeDtypeStruct((count * tokens, features), BF16),
            jax.ShapeDtypeStruct((features, rank), BF16),
            jax.ShapeDtypeStruct((rank, rank), F32),
        ),
        in_specs=[
            pl.BlockSpec(memory_space=pltpu.SMEM),
            pl.BlockSpec(memory_space=pltpu.VMEM),
        ]
        + [pl.BlockSpec(memory_space=pl.ANY)] * len(pieces),
        out_specs=(pl.BlockSpec(memory_space=pltpu.VMEM),) * 3,
        scratch_shapes=[
            pltpu.VMEM((count * tokens, rank), BF16),
            pltpu.SemaphoreType.DMA((len(pieces),)),
        ],
        compiler_params=pltpu.CompilerParams(vmem_limit_bytes=48 * MIB),
        name="columns_hr_gram",
    )(where, y_blocks, *pieces)


def residual_kernel(weight_ref, codes_ref, scales_ref, hr_ref, after_ref, out_ref):
    groups = scales_ref.shape[1]
    width = weight_ref.shape[1] // groups
    scales = scales_ref[...]
    parts = []
    for group in range(groups):
        at = slice(group * width, (group + 1) * width)
        quantized = codes_ref[:, at].astype(F32) * scales[:, group : group + 1]
        parts.append((weight_ref[:, at].astype(F32) - quantized).astype(BF16))
    residual = jnp.concatenate(parts, axis=1)
    out_ref[...] = jnp.dot(residual, hr_ref[...], preferred_element_type=F32).astype(BF16)


def residual_partial(weight, codes, scales, hr, after):
    rows, features = weight.shape
    rank = hr.shape[1]
    block = min(256, rows)
    return pl.pallas_call(
        residual_kernel,
        out_shape=jax.ShapeDtypeStruct((rows, rank), BF16),
        grid=(rows // block,),
        in_specs=[
            pl.BlockSpec((block, features), lambda i: (i, 0)),
            pl.BlockSpec((block, features), lambda i: (i, 0)),
            pl.BlockSpec((block, scales.shape[1]), lambda i: (i, 0)),
            pl.BlockSpec((features, rank), lambda i: (0, 0)),
            pl.BlockSpec(memory_space=pl.ANY),
        ],
        out_specs=pl.BlockSpec((block, rank), lambda i: (i, 0)),
        compiler_params=pltpu.CompilerParams(vmem_limit_bytes=48 * MIB),
        name="residual_product",
    )(weight, codes, scales, hr, after)


def hessian_rows(row_chunks, cols, earlier, index, shape, scale, after):
    tokens, height = row_chunks[0].shape
    block = height * len(row_chunks)
    tile = min(512, cols.shape[1])
    count = len(row_chunks)
    ins = [*row_chunks, cols]
    specs = [pl.BlockSpec((tokens, height), lambda j: (0, 0))] * count
    specs.append(pl.BlockSpec((tokens, tile), lambda j: (0, j)))
    aliases = {}
    if earlier is not None:
        aliases = {len(ins): 0}
        ins.append(earlier)
        specs.append(pl.BlockSpec(memory_space=pl.ANY))
    for value in after:
        ins.append(value)
        specs.append(pl.BlockSpec(memory_space=pl.ANY))

    def kernel(*refs):
        cols_ref = refs[count]
        out_ref, turned_ref = refs[-2:]

        @pl.when(pl.program_id(0) == 0)
        def _():
            for chunk in range(count):
                turned_ref[chunk * height : (chunk + 1) * height] = refs[chunk][...].T

        total = jnp.dot(turned_ref[...], cols_ref[...], preferred_element_type=F32)
        out_ref[...] = (total * scale).astype(BF16)

    return pl.pallas_call(
        kernel,
        out_shape=jax.ShapeDtypeStruct(shape, BF16),
        grid=(cols.shape[1] // tile,),
        in_specs=specs,
        out_specs=pl.BlockSpec((block, tile), lambda j: (index, j)),
        scratch_shapes=[pltpu.VMEM((block, tokens), BF16)],
        input_output_aliases=aliases,
        compiler_params=pltpu.CompilerParams(vmem_limit_bytes=48 * MIB),
        name="hessian_rows",
    )(*ins)


def pair_sum(values):
    while len(values) > 1:
        values = [values[i] + values[i + 1] for i in range(0, len(values), 2)]
    return values[0]


def body(activations, weight_tile, codes, group_scales, right_factor):
    wide_count = lax.axis_size("wide")
    narrow_count = lax.axis_size("narrow")
    wide_index = lax.axis_index("wide")
    narrow_index = lax.axis_index("narrow")
    tokens, features = activations.shape
    rows = weight_tile.shape[0]
    split = features // rows
    scale = 1.0 / (tokens * wide_count)
    bits = [1 << b for b in range(1, wide_count.bit_length() - 1)]

    right_block = lax.dynamic_slice_in_dim(right_factor, narrow_index * features, features, 0)
    product = jnp.dot(activations, right_block, preferred_element_type=F32)
    product = pair_sum([product] + [flip(product, "narrow", m) for m in range(1, narrow_count)])
    y_blocks = product.astype(BF16)[None]
    mask = 1
    while mask < wide_count:
        y_blocks = jnp.concatenate([y_blocks, flip(y_blocks, "wide", mask)], axis=0)
        mask *= 2

    middle = features // 2
    pieces = []
    for half, order in enumerate((bits[::-1], bits)):
        held = {0: activations[:, half * middle : (half + 1) * middle]}
        for bit in order + [1]:
            held.update({m | bit: flip(held[m], "wide", bit) for m in list(held)})
        pieces += [held[m] for m in range(wide_count)]

    unit = rows // sum(PARTS)
    gathered = []
    at = 0
    for part in PARTS:
        height = part * unit
        mine = jnp.stack(
            [activations[:, s * rows + at : s * rows + at + height] for s in range(split)]
        )
        gathered.append(lax.all_gather(mine, "narrow", axis=0, tiled=True))
        at += height

    cols, hr, gram = columns_hr_gram(
        pieces, y_blocks, wide_index.astype(jnp.int32).reshape(1), scale
    )
    every = [hold(gathered[0], hr)]
    partial = residual_partial(weight_tile, codes, group_scales, hr, every[0])
    every += [hold(value, partial) for value in gathered[1:]]
    share = rows // narrow_count
    received = []
    for m in range(narrow_count):
        piece = lax.dynamic_slice_in_dim(partial, (narrow_index ^ m) * share, share, 0)
        received.append(flip(piece, "narrow", m) if m else piece)
    residual_product = pair_sum([piece.astype(F32) for piece in received])

    hessian = None
    at = 0
    for index, part in enumerate(PARTS):
        height = part * unit
        chunk = lax.all_to_all(every[index], "wide", split_axis=0, concat_axis=0, tiled=True)
        chunk = chunk.reshape(tokens * wide_count, height)
        hessian = hessian_rows(
            [chunk], cols, hessian, at // height, (rows, features), scale, [] if index else [partial]
        )
        at += height
    return residual_product, gram, hessian


def solution(mesh):
    in_specs = (
        P("wide", "narrow"),
        P("wide", "narrow"),
        P("wide", "narrow"),
        P("wide", "narrow"),
        P(),
    )
    out_specs = (P(("wide", "narrow"), None), P(), P("wide", "narrow"))
    return jax.shard_map(body, mesh=mesh, in_specs=in_specs, out_specs=out_specs, check_vma=False)
```

time: 262 us -> 239 us (0.912)
  waiting for transfers between devices: 128 us -> 88.9 us
  blocking collectives: 0 us -> 19.7 us
  Pallas kernels: 65.7 us -> 61.9 us
  other arithmetic: 8.61 us -> 5.48 us
  local copies, waits for them, and re-layouts: 11.1 us -> 13.8 us
    all_gather x4 -> x3, waiting for transfers between devices: 57.8 us -> 35.1 us  [body(): gathered.append(lax.all_gather(mine, 'narrow', axis=0, tiled=True))]
    all_to_all x0 -> x1, blocking collectives: none -> 19.7 us  [body(): lax.all_to_all(every[index], 'wide', split_axis=0, concat_axis=0, tiled=T...]
    ppermute x19 -> x23, waiting for transfers between devices: 70.1 us -> 53.7 us  [flip(): return lax.ppermute(value, axis, [(i, i ^ mask) for i in range(count)])]
    all_to_all x5 -> x2, starting transfers between devices: 18.9 us -> 7.85 us  [body(): lax.all_to_all(every[index], 'wide', split_axis=0, concat_axis=0, tiled=T...]
    ppermute x19 -> x23, starting transfers between devices: 12.3 us -> 21.3 us  [flip(): return lax.ppermute(value, axis, [(i, i ^ mask) for i in range(count)])]
    pallas_call x5 -> x7, Pallas kernels: 46.5 us -> 42.5 us  [the longest x3 35.4 us: hessian_rows(): pl.pallas_call(kernel, out_shape=jax.ShapeDtypeStruct(shape, BF16), grid=...]
    concatenate x3, other arithmetic: 4.74 us -> 1.1 us  [body(): y_blocks = jnp.concatenate([y_blocks, flip(y_blocks, 'wide', mask)], axis=0)]
    unnamed x19 -> x25, local copies, waits for them, and re-layouts: 7.6 us -> 9.49 us
  transfers between devices with their start and end apart: 28 -> 28, of which waited for: 12 -> 8; matrix products, arithmetic and copies ran while one was open for 5% -> 5% of each run, Pallas kernels for 25% -> 22%
where the time goes in v5:
time: 239 us; the launch traced here: 235 us
  waiting for transfers between devices  88.9 us (37%)
  Pallas kernels  61.9 us (26%)
  starting transfers between devices  29.3 us (12%)
  blocking collectives  19.7 us (8%)
  between operations  14 us (6%)
  local copies, waits for them, and re-layouts  13.8 us (6%)
  other arithmetic  5.48 us (2%)
    ppermute x23, waiting for transfers between devices, flip(): return lax.ppermute(value, axis, [(i, i ^ mask) for i in range(count)])  53.7 us
    pallas_call x3, Pallas kernels, hessian_rows(): pl.pallas_call(kernel, out_shape=jax.ShapeDtypeStruct(shape, BF16), grid=...  35.4 us
    all_gather x3, waiting for transfers between devices, body(): gathered.append(lax.all_gather(mine, 'narrow', axis=0, tiled=True))  35.1 us
    ppermute x23, starting transfers between devices, flip(): return lax.ppermute(value, axis, [(i, i ^ mask) for i in range(count)])  21.3 us
    all_to_all x1, blocking collectives, body(): lax.all_to_all(every[index], 'wide', split_axis=0, concat_axis=0, tiled=T...  19.7 us
    pallas_call x1, Pallas kernels, residual_partial(): pl.pallas_call(residual_kernel, out_shape=jax.ShapeDtypeStruct((rows, ran...  19.4 us
    unnamed x25, local copies, waits for them, and re-layouts  9.49 us
    all_to_all x2, starting transfers between devices, body(): lax.all_to_all(every[index], 'wide', split_axis=0, concat_axis=0, tiled=T...  7.85 us
  transfers between devices with their start and end apart: 28, of which 8 were waited for; matrix products, arithmetic and copies ran while one was open for 5% of the time, Pallas kernels for 22%

profile of v5, /device:TPU:0, one launch (start us, length us, event | category | flops | bytes accessed | tf_op | source)
XLA Modules:
  0.0 235.4 jit_solution(6822312165527873527)
XLA Ops:
  7.2 0.0 all-gather.4.cloned.1.call-start
  7.2 1.1 slice_bitcast_fusion.1
  8.3 0.9 pad_maximum_fusion.1
  9.1 0.0 all-gather.4.cloned.1.call-update
  9.2 0.0 all-gather.8.cloned.1.call-start
  9.2 2.4 %fusion.2 = f32[128,256]{1,0:T(8,128)S(1)} fusion(bf16[128,4096]{1,0:T(8,128)(2,1)} %param.5, bf16[16384,256]{1,0:T(8,128)(2,1)} %param.9, s32[]{:T(128)S(6)} %select_n.15), kind=kOutput, calls=%fused_computation.2 | convolution fusion | flops 268435456 | bytes 3276804 | tf_op jit(solution)/shard_map/dot_general | solution.py:184
  11.6 3.1 %collective-permute-start = (f32[128,256]{1,0:T(8,128)S(1)}, f32[128,256]{1,0:T(8,128)S(1)}, u32[]{:S(2)}, u32[]{:S(2)}) collective-permute-start(f32[128,256]{1,0:T(8,128)S(1)} %fusion.2), channel_id=1, source_target_pairs={{0,1},{1,0},{2,3},{3,2},{4,5},{5,4},{6,7},{7,6},{8,9},{9,8},{10,11... | collective-permute-start | bytes 393224 | tf_op jit(solution)/shard_map/ppermute | solution.py:18
  14.7 2.6 %collective-permute-start.1 = (f32[128,256]{1,0:T(8,128)S(1)}, f32[128,256]{1,0:T(8,128)S(1)}, u32[]{:S(2)}, u32[]{:S(2)}) collective-permute-start(f32[128,256]{1,0:T(8,128)S(1)} %fusion.2), channel_id=1, source_target_pairs={{0,2},{1,3},{2,0},{3,1},{4,6},{5,7},{6,4},{7,5},{8,10},{9,11},{10,... | collective-permute-start | bytes 393224 | tf_op jit(solution)/shard_map/ppermute | solution.py:18
  17.3 1.3 fusion.7
  18.6 1.8 collective-permute-start.14
  20.3 1.5 collective-permute-start.16
  21.9 1.1 slice_bitcast_fusion.3
  23.0 0.6 collective-permute-start.9
  23.6 9.7 %collective-permute-done.1 = f32[128,256]{1,0:T(8,128)S(1)} collective-permute-done((f32[128,256]{1,0:T(8,128)S(1)}, f32[128,256]{1,0:T(8,128)S(1)}, u32[]{:S(2)}, u32[]{:S(2)}) %collective-permute-start.1) | collective-permute-done | bytes 131104 | tf_op jit(solution)/shard_map/ppermute | solution.py:18
  33.3 1.5 collective-permute-start.7
  34.9 0.1 collective-permute-start.3
  35.0 0.7 pad_maximum_fusion.4
  35.7 0.0 all-gather.8.cloned.1.call-update
  35.7 0.5 collective-permute-done.3
  36.2 0.6 collective-permute-start.4
  36.8 9.0 %collective-permute-done.4 = bf16[2,128,256]{2,1,0:T(8,128)(2,1)S(1)} collective-permute-done((bf16[2,128,256]{2,1,0:T(8,128)(2,1)S(1)}, bf16[2,128,256]{2,1,0:T(8,128)(2,1)S(1)}, u32[]{:S(2)}, u32[]{:S(2)}) %collective-permute-start.4) | collective-permute-done | bytes 131104 | tf_op jit(solution)/shard_map/ppermute | solution.py:18
  45.8 0.5 collective-permute-start.6
  46.3 1.5 collective-permute-start.11
  47.8 1.5 collective-permute-start.18
  49.4 0.8 copy-done.4
  50.1 0.5 collective-permute-start.5
  50.7 0.8 copy-done.6
  51.4 0.2 collective-permute-start.15
  51.7 15.6 %collective-permute-done.5 = bf16[4,128,256]{2,1,0:T(8,128)(2,1)S(1)} collective-permute-done((bf16[4,128,256]{2,1,0:T(8,128)(2,1)S(1)}, bf16[4,128,256]{2,1,0:T(8,128)(2,1)S(1)}, u32[]{:S(2)}, u32[]{:S(2)}) %collective-permute-start.5) | collective-permute-done | bytes 262176 | tf_op jit(solution)/shard_map/ppermute | solution.py:18
  67.2 0.5 collective-permute-start.8
  67.7 0.1 collective-permute-start.12
  67.8 0.1 copy-done.11
  67.9 0.8 copy-done.8
  68.7 0.3 collective-permute-start.19
  69.1 1.3 copy.16.scales_ref
  70.3 1.1 pad_maximum_fusion.y_ref
  71.5 0.3 collective-permute-done.19.refs_15_
  71.7 1.1 copy-done.5
  72.8 1.0 copy-done.7
  73.8 1.0 copy-done.9
  74.9 7.1 %columns_hr_gram.1 = (bf16[1024,4096]{1,0:T(8,128)(2,1)}, bf16[4096,256]{1,0:T(8,128)(2,1)}, f32[256,256]{1,0:T(8,128)}) custom-call(s32[1]{0:T(128)} %bitcast.where_ref, bf16[8,128,256]{2,1,0:T(8,128)(2,1)S(1)} %pad_maximum_fusion.y_ref, bf16[128,2048]{1,0:T(8,128)(2,1)S(1)} %get-tuple-element.19.refs_0_, bf16[128,2048]{1,0:T(8,128)(2,1)S(1)} %copy-done.7, ...), custom_call_target="tpu_custom_call" | custom-call | tf_op jit(solution)/shard_map/columns_hr_gram/pallas_call | solution.py:68
  82.0 0.0 all-gather.4.cloned.1.call-done.refs_0_
  82.0 0.0 copy-start.2
  82.0 1.6 copy-done.2
  83.6 19.4 %residual_product.1.refs_1_.refs_2_ = bf16[2048,256]{1,0:T(8,128)(2,1)S(1)} custom-call(bf16[2048,4096]{1,0:T(8,128)(2,1)} %weight_ref.1, s32[2048,4096]{1,0:T(8,128)} %codes_ref.1, f32[2048,32]{1,0:T(8,128)S(1)} %copy.16.scales_ref, bf16[4096,256]{1,0:T(8,128)(2,1)S(1)} %copy-done.2, bf16[8,128,1024]{2,1,0:T(8,128)(2,1)} %hold.3.after_ref), custom_call_target="tpu_custom_call" | custom-call | tf_op jit(solution)/shard_map/residual_product/pallas_call | solution.py:107
  103.0 0.0 copy-start
  103.0 1.0 copy-done
  103.9 19.7 %all_to_all.15 = bf16[8,128,512]{2,1,0:T(8,128)(2,1)} all-to-all(bf16[8,128,512]{2,1,0:T(8,128)(2,1)} %hold.5), channel_id=1, replica_groups=mesh['wide'=8,'narrow'=4] {'wide'}, dimensions={0} | all-to-all | bytes 2097152 | tf_op jit(solution)/shard_map/all_to_all | solution.py:228
  123.7 3.6 %all-to-all-start.2 = ((bf16[8,128,1024]{2,1,0:T(8,128)(2,1)}), bf16[8,128,1024]{2,1,0:T(8,128)(2,1)S(1)}, u32[]{:S(2)}, u32[]{:S(2)}) async-start(bf16[8,128,1024]{2,1,0:T(8,128)(2,1)} %hold.3.after_ref), calls=%async_computation.2 | async-start | bytes 4194304 | tf_op jit(solution)/shard_map/all_to_all | solution.py:228
  127.3 0.0 all-gather.6.cloned.1.call-start
  127.3 0.7 pad_maximum_fusion.3
  128.1 0.0 all-gather.6.cloned.1.call-update
  128.1 35.0 %all-gather.6.cloned.1.call-done.refs_0_ = bf16[8,128,512]{2,1,0:T(8,128)(2,1)} async-done(((bf16[2,128,512]{2,1,0:T(8,128)(2,1)}), bf16[8,128,512]{2,1,0:T(8,128)(2,1)}) %all-gather.6.cloned.1.call-update) | async-done | bytes 1048592 | tf_op jit(solution)/shard_map/all_gather | solution.py:208
  163.1 4.2 %all-to-all-start = ((bf16[8,128,512]{2,1,0:T(8,128)(2,1)}), bf16[8,128,512]{2,1,0:T(8,128)(2,1)}, u32[]{:S(2)}, u32[]{:S(2)}) async-start(bf16[8,128,512]{2,1,0:T(8,128)(2,1)} %hold.4), calls=%async_computation | async-start | bytes 2097152 | tf_op jit(solution)/shard_map/all_to_all | solution.py:228
  167.4 0.8 constant_dynamic-slice_fusion.2
  168.3 1.4 collective-permute-start.20
  169.7 1.0 collective-permute-start.21
  170.8 1.9 collective-permute-start.22
  172.7 9.3 %collective-permute-done.20 = bf16[512,256]{1,0:T(8,128)(2,1)} collective-permute-done((bf16[512,256]{1,0:T(8,128)(2,1)}, bf16[512,256]{1,0:T(8,128)(2,1)}, u32[]{:S(2)}, u32[]{:S(2)}) %collective-permute-start.20) | collective-permute-done | bytes 262176 | tf_op jit(solution)/shard_map/ppermute | solution.py:18
  182.0 9.4 %collective-permute-done.21 = bf16[512,256]{1,0:T(8,128)(2,1)} collective-permute-done((bf16[512,256]{1,0:T(8,128)(2,1)}, bf16[512,256]{1,0:T(8,128)(2,1)}, u32[]{:S(2)}, u32[]{:S(2)}) %collective-permute-start.21) | collective-permute-done | bytes 262176 | tf_op jit(solution)/shard_map/ppermute | solution.py:18
  191.4 2.0 add_add_fusion
  193.4 14.2 %hessian_rows.3.refs_2_ = bf16[2048,4096]{1,0:T(8,128)(2,1)} custom-call(bf16[1024,1024]{1,0:T(8,128)(2,1)S(1)} %bitcast.21, bf16[1024,4096]{1,0:T(8,128)(2,1)} %get-tuple-element.8.refs_1_, bf16[2048,256]{1,0:T(8,128)(2,1)S(1)} %copy-done.1), custom_call_target="tpu_custom_call" | custom-call | tf_op jit(solution)/shard_map/hessian_rows/pallas_call | solution.py:153
  207.6 10.4 %hessian_rows.4.refs_2_ = bf16[2048,4096]{1,0:T(8,128)(2,1)} custom-call(bf16[1024,512]{1,0:T(8,128)(2,1)S(1)} %bitcast.22, bf16[1024,4096]{1,0:T(8,128)(2,1)} %get-tuple-element.8.refs_1_, bf16[2048,4096]{1,0:T(8,128)(2,1)} %hessian_rows.3.refs_2_), custom_call_target="tpu_custom_call", output_to_operand_aliasing={{}: (2, {})} | custom-call | tf_op jit(solution)/shard_map/hessian_rows/pallas_call | solution.py:153
  218.1 10.8 %hessian_rows.5 = bf16[2048,4096]{1,0:T(8,128)(2,1)} custom-call(bf16[1024,512]{1,0:T(8,128)(2,1)} %bitcast.7.refs_0_, bf16[1024,4096]{1,0:T(8,128)(2,1)} %get-tuple-element.8.refs_1_, bf16[2048,4096]{1,0:T(8,128)(2,1)} %hessian_rows.4.refs_2_), custom_call_target="tpu_custom_call", output_to_operand_aliasing={{}: (2, {})} | custom-call | tf_op jit(solution)/shard_map/hessian_rows/pallas_call | solution.py:153
  (42 shorter events, 0.2 us)
Async XLA Ops:
  7.2 74.8 %all-gather.4.cloned.1.call-start = ((), (), s32[]{:S(2)}) async-start(), calls=%async_computation.3 | async-start | bytes 2621440 | tf_op jit(solution)/shard_map/all_gather | solution.py:208
  9.2 94.8 %all-gather.8.cloned.1.call-start = ((), (), s32[]{:S(2)}) async-start(), calls=%async_computation.5 | async-start | bytes 1310720 | tf_op jit(solution)/shard_map/all_gather | solution.py:208
  11.6 11.4 %collective-permute-start = (f32[128,256]{1,0:T(8,128)S(1)}, f32[128,256]{1,0:T(8,128)S(1)}, u32[]{:S(2)}, u32[]{:S(2)}) collective-permute-start(f32[128,256]{1,0:T(8,128)S(1)} %fusion.2), channel_id=1, source_target_pairs={{0,1},{1,0},{2,3},{3,2},{4,5},{5,4},{6,7},{7,6},{8,9},{9,8},{10,11... | collective-permute-start | bytes 393224 | tf_op jit(solution)/shard_map/ppermute | solution.py:18
  14.7 18.6 %collective-permute-start.1 = (f32[128,256]{1,0:T(8,128)S(1)}, f32[128,256]{1,0:T(8,128)S(1)}, u32[]{:S(2)}, u32[]{:S(2)}) collective-permute-start(f32[128,256]{1,0:T(8,128)S(1)} %fusion.2), channel_id=1, source_target_pairs={{0,2},{1,3},{2,0},{3,1},{4,6},{5,7},{6,4},{7,5},{8,10},{9,11},{10,... | collective-permute-start | bytes 393224 | tf_op jit(solution)/shard_map/ppermute | solution.py:18
  17.3 17.6 %collective-permute-start.2 = (f32[128,256]{1,0:T(8,128)S(1)}, f32[128,256]{1,0:T(8,128)S(1)}, u32[]{:S(2)}, u32[]{:S(2)}) collective-permute-start(f32[128,256]{1,0:T(8,128)S(1)} %fusion.2), channel_id=1, source_target_pairs={{0,3},{1,2},{2,1},{3,0},{4,7},{5,6},{6,5},{7,4},{8,11},{9,10},{10,... | collective-permute-start | bytes 393224 | tf_op jit(solution)/shard_map/ppermute | solution.py:18
  18.6 27.7 %collective-permute-start.14 = (bf16[128,2048]{1,0:T(8,128)(2,1)S(1)}, bf16[128,2048]{1,0:T(8,128)(2,1)}, u32[]{:S(2)}, u32[]{:S(2)}) collective-permute-start(bf16[128,2048]{1,0:T(8,128)(2,1)S(1)} %get-tuple-element.18.refs_8_), channel_id=1, source_target_pairs={{0,8},{4,12},{8,0},{12,4},{16,24},{20,28},{24,16},{28,20},{1,9},{5... | collective-permute-start | bytes 1572872 | tf_op jit(solution)/shard_map/ppermute | solution.py:18
  20.3 27.4 %collective-permute-start.16 = (bf16[128,2048]{1,0:T(8,128)(2,1)S(1)}, bf16[128,2048]{1,0:T(8,128)(2,1)}, u32[]{:S(2)}, u32[]{:S(2)}) collective-permute-start(bf16[128,2048]{1,0:T(8,128)(2,1)S(1)} %get-tuple-element.18.refs_8_), channel_id=1, source_target_pairs={{0,16},{4,20},{8,24},{12,28},{16,0},{20,4},{24,8},{28,12},{1,17},{... | collective-permute-start | bytes 1572872 | tf_op jit(solution)/shard_map/ppermute | solution.py:18
  23.0 22.8 %collective-permute-start.9 = (bf16[128,2048]{1,0:T(8,128)(2,1)S(1)}, bf16[128,2048]{1,0:T(8,128)(2,1)S(1)}, u32[]{:S(2)}, u32[]{:S(2)}) collective-permute-start(bf16[128,2048]{1,0:T(8,128)(2,1)S(1)} %get-tuple-element.19.refs_0_), channel_id=1, source_target_pairs={{0,16},{4,20},{8,24},{12,28},{16,0},{20,4},{24,8},{28,12},{1,17},{... | collective-permute-start | bytes 1572872 | tf_op jit(solution)/shard_map/ppermute | solution.py:18
  33.3 16.0 %collective-permute-start.7 = (bf16[128,2048]{1,0:T(8,128)(2,1)S(1)}, bf16[128,2048]{1,0:T(8,128)(2,1)S(1)}, u32[]{:S(2)}, u32[]{:S(2)}) collective-permute-start(bf16[128,2048]{1,0:T(8,128)(2,1)S(1)} %get-tuple-element.19.refs_0_), channel_id=1, source_target_pairs={{0,8},{4,12},{8,0},{12,4},{16,24},{20,28},{24,16},{28,20},{1,9},{5... | collective-permute-start | bytes 1572872 | tf_op jit(solution)/shard_map/ppermute | solution.py:18
  34.9 1.3 collective-permute-start.3
  36.2 9.6 %collective-permute-start.4 = (bf16[2,128,256]{2,1,0:T(8,128)(2,1)S(1)}, bf16[2,128,256]{2,1,0:T(8,128)(2,1)S(1)}, u32[]{:S(2)}, u32[]{:S(2)}) collective-permute-start(bf16[2,128,256]{2,1,0:T(8,128)(2,1)S(1)} %pad_maximum_fusion.5), channel_id=1, source_target_pairs={{0,8},{4,12},{8,0},{12,4},{16,24},{20,28},{24,16},{28,20},{1,9},{5... | collective-permute-start | bytes 393224 | tf_op jit(solution)/shard_map/ppermute | solution.py:18
  45.8 23.3 %copy-start.10 = (bf16[2,128,256]{2,1,0:T(8,128)(2,1)}, bf16[2,128,256]{2,1,0:T(8,128)(2,1)S(1)}, u32[]{:S(2)}) copy-start(bf16[2,128,256]{2,1,0:T(8,128)(2,1)S(1)} %collective-permute-done.4) | copy-start | bytes 393220
  45.8 3.6 %collective-permute-start.13 = (bf16[128,2048]{1,0:T(8,128)(2,1)S(1)}, bf16[128,2048]{1,0:T(8,128)(2,1)S(1)}, u32[]{:S(2)}, u32[]{:S(2)}) collective-permute-start(bf16[128,2048]{1,0:T(8,128)(2,1)S(1)} %get-tuple-element.18.refs_8_), channel_id=1, source_target_pairs={{0,4},{4,0},{8,12},{12,8},{16,20},{20,16},{24,28},{28,24},{1,5},{5... | collective-permute-start | bytes 1572872 | tf_op jit(solution)/shard_map/ppermute | solution.py:18
  45.8 4.9 %collective-permute-start.6 = (bf16[128,2048]{1,0:T(8,128)(2,1)S(1)}, bf16[128,2048]{1,0:T(8,128)(2,1)S(1)}, u32[]{:S(2)}, u32[]{:S(2)}) collective-permute-start(bf16[128,2048]{1,0:T(8,128)(2,1)S(1)} %get-tuple-element.19.refs_0_), channel_id=1, source_target_pairs={{0,4},{4,0},{8,12},{12,8},{16,20},{20,16},{24,28},{28,24},{1,5},{5... | collective-permute-start | bytes 1572872 | tf_op jit(solution)/shard_map/ppermute | solution.py:18
  46.3 20.9 %collective-permute-start.11 = (bf16[128,2048]{1,0:T(8,128)(2,1)S(1)}, bf16[128,2048]{1,0:T(8,128)(2,1)}, u32[]{:S(2)}, u32[]{:S(2)}) collective-permute-start(bf16[128,2048]{1,0:T(8,128)(2,1)S(1)} %collective-permute-done.9.refs_4_), channel_id=1, source_target_pairs={{0,8},{4,12},{8,0},{12,4},{16,24},{20,28},{24,16},{28,20},{1,9},{5... | collective-permute-start | bytes 1572872 | tf_op jit(solution)/shard_map/ppermute | solution.py:18
  47.8 20.0 %collective-permute-start.18 = (bf16[128,2048]{1,0:T(8,128)(2,1)}, bf16[128,2048]{1,0:T(8,128)(2,1)}, u32[]{:S(2)}, u32[]{:S(2)}) collective-permute-start(bf16[128,2048]{1,0:T(8,128)(2,1)} %collective-permute-done.14.refs_10_), channel_id=1, source_target_pairs={{0,16},{4,20},{8,24},{12,28},{16,0},{20,4},{24,8},{28,12},{1,17},{... | collective-permute-start | bytes 1572872 | tf_op jit(solution)/shard_map/ppermute | solution.py:18
  49.3 18.5 %collective-permute-start.10 = (bf16[128,2048]{1,0:T(8,128)(2,1)S(1)}, bf16[128,2048]{1,0:T(8,128)(2,1)S(1)}, u32[]{:S(2)}, u32[]{:S(2)}) collective-permute-start(bf16[128,2048]{1,0:T(8,128)(2,1)S(1)} %collective-permute-done.9.refs_4_), channel_id=1, source_target_pairs={{0,4},{4,0},{8,12},{12,8},{16,20},{20,16},{24,28},{28,24},{1,5},{5... | collective-permute-start | bytes 1572872 | tf_op jit(solution)/shard_map/ppermute | solution.py:18
  49.3 0.8 copy-start.4
  50.1 17.1 %collective-permute-start.5 = (bf16[4,128,256]{2,1,0:T(8,128)(2,1)S(1)}, bf16[4,128,256]{2,1,0:T(8,128)(2,1)S(1)}, u32[]{:S(2)}, u32[]{:S(2)}) collective-permute-start(bf16[4,128,256]{2,1,0:T(8,128)(2,1)S(1)} %pad_maximum_fusion.2), channel_id=1, source_target_pairs={{0,16},{4,20},{8,24},{12,28},{16,0},{20,4},{24,8},{28,12},{1,17},{... | collective-permute-start | bytes 786440 | tf_op jit(solution)/shard_map/ppermute | solution.py:18
  50.7 0.8 copy-start.6
  51.4 20.0 %collective-permute-start.15 = (bf16[128,2048]{1,0:T(8,128)(2,1)}, bf16[128,2048]{1,0:T(8,128)(2,1)}, u32[]{:S(2)}, u32[]{:S(2)}) collective-permute-start(bf16[128,2048]{1,0:T(8,128)(2,1)} %collective-permute-done.14.refs_10_), channel_id=1, source_target_pairs={{0,4},{4,0},{8,12},{12,8},{16,20},{20,16},{24,28},{28,24},{1,5},{5... | collective-permute-start | bytes 1572872 | tf_op jit(solution)/shard_map/ppermute | solution.py:18
  67.2 0.7 copy-start.11
  67.2 4.2 %collective-permute-start.17 = (bf16[128,2048]{1,0:T(8,128)(2,1)}, bf16[128,2048]{1,0:T(8,128)(2,1)}, u32[]{:S(2)}, u32[]{:S(2)}) collective-permute-start(bf16[128,2048]{1,0:T(8,128)(2,1)} %collective-permute-done.16.refs_12_), channel_id=1, source_target_pairs={{0,4},{4,0},{8,12},{12,8},{16,20},{20,16},{24,28},{28,24},{1,5},{5... | collective-permute-start | bytes 1572872 | tf_op jit(solution)/shard_map/ppermute | solution.py:18
  67.2 4.2 %collective-permute-start.8 = (bf16[128,2048]{1,0:T(8,128)(2,1)S(1)}, bf16[128,2048]{1,0:T(8,128)(2,1)}, u32[]{:S(2)}, u32[]{:S(2)}) collective-permute-start(bf16[128,2048]{1,0:T(8,128)(2,1)S(1)} %collective-permute-done.7.refs_2_), channel_id=1, source_target_pairs={{0,4},{4,0},{8,12},{12,8},{16,20},{20,16},{24,28},{28,24},{1,5},{5... | collective-permute-start | bytes 1572872 | tf_op jit(solution)/shard_map/ppermute | solution.py:18
  67.7 3.7 %collective-permute-start.12 = (bf16[128,2048]{1,0:T(8,128)(2,1)}, bf16[128,2048]{1,0:T(8,128)(2,1)}, u32[]{:S(2)}, u32[]{:S(2)}) collective-permute-start(bf16[128,2048]{1,0:T(8,128)(2,1)} %collective-permute-done.11.refs_6_), channel_id=1, source_target_pairs={{0,4},{4,0},{8,12},{12,8},{16,20},{20,16},{24,28},{28,24},{1,5},{5... | collective-permute-start | bytes 1572872 | tf_op jit(solution)/shard_map/ppermute | solution.py:18
  67.9 0.8 copy-start.8
  68.7 3.0 %collective-permute-start.19 = (bf16[128,2048]{1,0:T(8,128)(2,1)}, bf16[128,2048]{1,0:T(8,128)(2,1)}, u32[]{:S(2)}, u32[]{:S(2)}) collective-permute-start(bf16[128,2048]{1,0:T(8,128)(2,1)} %collective-permute-done.18.refs_14_), channel_id=1, source_target_pairs={{0,4},{4,0},{8,12},{12,8},{16,20},{20,16},{24,28},{28,24},{1,5},{5... | collective-permute-start | bytes 1572872 | tf_op jit(solution)/shard_map/ppermute | solution.py:18
  71.7 1.1 copy-start.5
  72.8 1.0 copy-start.7
  73.8 1.0 copy-start.9
  82.0 1.6 copy-start.2
  103.0 1.0 copy-start
  103.9 63.5 %copy-start.1 = (bf16[2048,256]{1,0:T(8,128)(2,1)S(1)}, bf16[2048,256]{1,0:T(8,128)(2,1)}, u32[]{:S(2)}) copy-start(bf16[2048,256]{1,0:T(8,128)(2,1)} %copy-done) | copy-start | bytes 3145732
  123.7 39.5 %all-to-all-start.2 = ((bf16[8,128,1024]{2,1,0:T(8,128)(2,1)}), bf16[8,128,1024]{2,1,0:T(8,128)(2,1)S(1)}, u32[]{:S(2)}, u32[]{:S(2)}) async-start(bf16[8,128,1024]{2,1,0:T(8,128)(2,1)} %hold.3.after_ref), calls=%async_computation.2 | async-start | bytes 4194304 | tf_op jit(solution)/shard_map/all_to_all | solution.py:228
  127.3 35.8 %all-gather.6.cloned.1.call-start = ((), (), s32[]{:S(2)}) async-start(), calls=%async_computation.4 | async-start | bytes 1310720 | tf_op jit(solution)/shard_map/all_gather | solution.py:208
  163.1 54.9 %all-to-all-start = ((bf16[8,128,512]{2,1,0:T(8,128)(2,1)}), bf16[8,128,512]{2,1,0:T(8,128)(2,1)}, u32[]{:S(2)}, u32[]{:S(2)}) async-start(bf16[8,128,512]{2,1,0:T(8,128)(2,1)} %hold.4), calls=%async_computation | async-start | bytes 2097152 | tf_op jit(solution)/shard_map/all_to_all | solution.py:228
  168.3 13.7 %collective-permute-start.20 = (bf16[512,256]{1,0:T(8,128)(2,1)}, bf16[512,256]{1,0:T(8,128)(2,1)}, u32[]{:S(2)}, u32[]{:S(2)}) collective-permute-start(bf16[512,256]{1,0:T(8,128)(2,1)} %get-tuple-element.13), channel_id=1, source_target_pairs={{0,1},{1,0},{2,3},{3,2},{4,5},{5,4},{6,7},{7,6},{8,9},{9,8},{10,11... | collective-permute-start | bytes 786440 | tf_op jit(solution)/shard_map/ppermute | solution.py:18
  169.7 21.7 %collective-permute-start.21 = (bf16[512,256]{1,0:T(8,128)(2,1)}, bf16[512,256]{1,0:T(8,128)(2,1)}, u32[]{:S(2)}, u32[]{:S(2)}) collective-permute-start(bf16[512,256]{1,0:T(8,128)(2,1)} %get-tuple-element.15), channel_id=1, source_target_pairs={{0,2},{1,3},{2,0},{3,1},{4,6},{5,7},{6,4},{7,5},{8,10},{9,11},{10,... | collective-permute-start | bytes 786440 | tf_op jit(solution)/shard_map/ppermute | solution.py:18
  170.8 20.6 %collective-permute-start.22 = (bf16[512,256]{1,0:T(8,128)(2,1)S(1)}, bf16[512,256]{1,0:T(8,128)(2,1)}, u32[]{:S(2)}, u32[]{:S(2)}) collective-permute-start(bf16[512,256]{1,0:T(8,128)(2,1)S(1)} %get-tuple-element.14), channel_id=1, source_target_pairs={{0,3},{1,2},{2,1},{3,0},{4,7},{5,6},{6,5},{7,4},{8,11},{9,10},{10,... | collective-permute-start | bytes 786440 | tf_op jit(solution)/shard_map/ppermute | solution.py:18
  193.4 14.2 %copy-start.3 = (bf16[8,128,512]{2,1,0:T(8,128)(2,1)S(1)}, bf16[8,128,512]{2,1,0:T(8,128)(2,1)}, u32[]{:S(2)}) copy-start(bf16[8,128,512]{2,1,0:T(8,128)(2,1)} %all_to_all.15) | copy-start | bytes 3145732
Sparse Core Ops, SparseCore 0:
  9.6 53.6 all-gather.3
  64.8 28.0 all-gather.7
  130.3 32.8 all-gather.5

commit v6 on v3

v6 whole, which is shorter than its diff:
```python
import functools

import jax
import jax.numpy as jnp
from jax import lax
from jax.experimental import pallas as pl
from jax.experimental.pallas import tpu as pltpu
from jax.sharding import PartitionSpec as P

CHUNKS = 2
MIB = 1024 * 1024
BF16 = jnp.bfloat16
F32 = jnp.float32


def flip(value, axis, mask):
    count = lax.axis_size(axis)
    return lax.ppermute(value, axis, [(i, i ^ mask) for i in range(count)])


def cost(flops, moved):
    return pl.CostEstimate(flops=int(flops), bytes_accessed=int(moved), transcendentals=0)


def hr_and_gram(cols, y_blocks, where, scale):
    count, tokens, rank = y_blocks.shape
    features = cols.shape[1]
    tile = min(1024, features)

    def kernel(where_ref, cols_ref, y_ref, hr_ref, gram_ref, order_ref, turned_ref):
        @pl.when(pl.program_id(0) == 0)
        def _():
            for mask in range(count):
                at = pl.multiple_of((where_ref[0] ^ mask) * tokens, tokens)
                order_ref[pl.ds(at, tokens), :] = y_ref[mask]
            turned_ref[...] = order_ref[...].T
            gram = jnp.dot(turned_ref[...], order_ref[...], preferred_element_type=F32)
            gram_ref[...] = gram * scale

        total = jnp.dot(turned_ref[...], cols_ref[...], preferred_element_type=F32) * scale
        hr_ref[...] = total.T.astype(BF16)

    return pl.pallas_call(
        kernel,
        out_shape=(
            jax.ShapeDtypeStruct((features, rank), BF16),
            jax.ShapeDtypeStruct((rank, rank), F32),
        ),
        grid=(features // tile,),
        in_specs=[
            pl.BlockSpec(memory_space=pltpu.SMEM),
            pl.BlockSpec((count * tokens, tile), lambda j: (0, j)),
            pl.BlockSpec(y_blocks.shape, lambda j: (0, 0, 0)),
        ],
        out_specs=(
            pl.BlockSpec((tile, rank), lambda j: (j, 0)),
            pl.BlockSpec((rank, rank), lambda j: (0, 0)),
        ),
        scratch_shapes=[
            pltpu.VMEM((count * tokens, rank), BF16),
            pltpu.VMEM((rank, count * tokens), BF16),
        ],
        cost_estimate=cost(4 * count * tokens * features * rank, 4 * cols.size),
        compiler_params=pltpu.CompilerParams(vmem_limit_bytes=48 * MIB),
        name="hr_and_gram",
    )(where, cols, y_blocks)


def place_kernel(sources, where_ref, *refs):
    out_ref = refs[-1]
    count = len(sources)
    me = where_ref[0]
    for mask in range(count):
        other = me ^ mask
        near, far = sources[mask]

        def put(index, other=other):
            out_ref[other] = refs[index][...]

        if far is None:
            put(near)
        elif near is None:
            put(far)
        else:
            close = jnp.abs(me - other) <= count // 2
            pl.when(close)(functools.partial(put, near))
            pl.when(jnp.logical_not(close))(functools.partial(put, far))


def place_blocks(blocks, sources, where, after):
    count = len(sources)
    return pl.pallas_call(
        functools.partial(place_kernel, sources),
        out_shape=jax.ShapeDtypeStruct((count,) + blocks[0].shape, BF16),
        in_specs=[pl.BlockSpec(memory_space=pltpu.SMEM)]
        + [pl.BlockSpec(memory_space=pltpu.VMEM)] * len(blocks)
        + [pl.BlockSpec(memory_space=pl.ANY)] * len(after),
        out_specs=pl.BlockSpec(memory_space=pltpu.VMEM),
        cost_estimate=cost(0, 4 * count * blocks[0].size),
        compiler_params=pltpu.CompilerParams(vmem_limit_bytes=48 * MIB),
        name="place_blocks",
    )(where, *blocks, *after)


def exchange_blocks(mine):
    count = lax.axis_size("narrow")
    half = count // 2
    blocks = [mine]
    sources = [(0, None)]
    direct = {}
    order = sorted(range(1, count), key=lambda m: (m != half, m))
    for mask in order:
        pairs = [(i, i ^ mask) for i in range(count) if abs(i - (i ^ mask)) <= half]
        direct[mask] = lax.ppermute(mine, "narrow", pairs) if pairs else None
    for mask in range(1, count):
        near = far = None
        if direct[mask] is not None:
            near = len(blocks)
            blocks.append(direct[mask])
        pairs = [(i ^ half, i ^ mask) for i in range(count) if abs(i - (i ^ mask)) > half]
        if pairs:
            far = len(blocks)
            blocks.append(lax.ppermute(direct[half], "narrow", pairs))
        sources.append((near, far))
    return blocks, sources


def residual_kernel(weight_ref, codes_ref, scales_ref, hr_ref, after_ref, out_ref):
    groups = scales_ref.shape[1]
    width = weight_ref.shape[1] // groups
    scales = scales_ref[...]
    parts = []
    for group in range(groups):
        at = slice(group * width, (group + 1) * width)
        quantized = codes_ref[:, at].astype(F32) * scales[:, group : group + 1]
        parts.append((weight_ref[:, at].astype(F32) - quantized).astype(BF16))
    residual = jnp.concatenate(parts, axis=1)
    out_ref[...] = jnp.dot(residual, hr_ref[...], preferred_element_type=F32).astype(BF16)


def residual_partial(weight, codes, scales, hr, after):
    rows, features = weight.shape
    rank = hr.shape[1]
    block = min(256, rows)
    return pl.pallas_call(
        residual_kernel,
        out_shape=jax.ShapeDtypeStruct((rows, rank), BF16),
        grid=(rows // block,),
        in_specs=[
            pl.BlockSpec((block, features), lambda i: (i, 0)),
            pl.BlockSpec((block, features), lambda i: (i, 0)),
            pl.BlockSpec((block, scales.shape[1]), lambda i: (i, 0)),
            pl.BlockSpec((features, rank), lambda i: (0, 0)),
            pl.BlockSpec(memory_space=pl.ANY),
        ],
        out_specs=pl.BlockSpec((block, rank), lambda i: (i, 0)),
        cost_estimate=cost(4 * rows * features * rank, 8 * rows * features),
        compiler_params=pltpu.CompilerParams(vmem_limit_bytes=48 * MIB),
        name="residual_product",
    )(weight, codes, scales, hr, after)


def hessian_rows(row_chunks, cols, earlier, index, shape, scale, after):
    tokens, height = row_chunks[0].shape
    block = height * len(row_chunks)
    tile = min(512, cols.shape[1])
    count = len(row_chunks)
    ins = [*row_chunks, cols]
    specs = [pl.BlockSpec((tokens, height), lambda j: (0, 0))] * count
    specs.append(pl.BlockSpec((tokens, tile), lambda j: (0, j)))
    aliases = {}
    if earlier is not None:
        aliases = {len(ins): 0}
        ins.append(earlier)
        specs.append(pl.BlockSpec(memory_space=pl.ANY))
    for value in after:
        ins.append(value)
        specs.append(pl.BlockSpec(memory_space=pl.ANY))

    def kernel(*refs):
        cols_ref = refs[count]
        out_ref, turned_ref = refs[-2:]

        @pl.when(pl.program_id(0) == 0)
        def _():
            for chunk in range(count):
                turned_ref[chunk * height : (chunk + 1) * height] = refs[chunk][...].T

        total = jnp.dot(turned_ref[...], cols_ref[...], preferred_element_type=F32)
        out_ref[...] = (total * scale).astype(BF16)

    return pl.pallas_call(
        kernel,
        out_shape=jax.ShapeDtypeStruct(shape, BF16),
        grid=(cols.shape[1] // tile,),
        in_specs=specs,
        out_specs=pl.BlockSpec((block, tile), lambda j: (index, j)),
        scratch_shapes=[pltpu.VMEM((block, tokens), BF16)],
        input_output_aliases=aliases,
        cost_estimate=cost(
            4 * block * cols.size, 2 * cols.size + 2 * block * (tokens + cols.shape[1])
        ),
        compiler_params=pltpu.CompilerParams(vmem_limit_bytes=48 * MIB),
        name="hessian_rows",
    )(*ins)


def add_pieces(pieces, after):
    rows, rank = pieces[0].shape

    def kernel(*refs):
        total = refs[0][...].astype(F32)
        for ref in refs[1 : len(pieces)]:
            total += ref[...].astype(F32)
        refs[-1][...] = total

    return pl.pallas_call(
        kernel,
        out_shape=jax.ShapeDtypeStruct((rows, rank), F32),
        in_specs=[pl.BlockSpec(memory_space=pltpu.VMEM)] * len(pieces)
        + [pl.BlockSpec(memory_space=pl.ANY)],
        out_specs=pl.BlockSpec(memory_space=pltpu.VMEM),
        cost_estimate=cost(0, 12 * rows * rank),
        name="add_pieces",
    )(*pieces, after)


def pair_sum(values):
    while len(values) > 1:
        values = [values[i] + values[i + 1] for i in range(0, len(values), 2)]
    return values[0]


def body(activations, weight_tile, codes, group_scales, right_factor):
    wide_count = lax.axis_size("wide")
    narrow_count = lax.axis_size("narrow")
    wide_index = lax.axis_index("wide").astype(jnp.int32)
    narrow_index = lax.axis_index("narrow").astype(jnp.int32)
    tokens, features = activations.shape
    rows = weight_tile.shape[0]
    split = features // rows
    scale = 1.0 / (tokens * wide_count)

    cols = lax.all_gather(activations, "wide", axis=0, tiled=True)

    height = rows // CHUNKS
    chunks = []
    for chunk in range(CHUNKS):
        mine = jnp.stack(
            [
                activations[:, s * rows + chunk * height : s * rows + (chunk + 1) * height]
                for s in range(split)
            ]
        )
        chunks.append(exchange_blocks(mine))

    right_block = lax.dynamic_slice_in_dim(right_factor, narrow_index * features, features, 0)
    product = jnp.dot(activations, right_block, preferred_element_type=F32)
    product = pair_sum([product] + [flip(product, "narrow", m) for m in range(1, narrow_count)])
    y_blocks = product.astype(BF16)[None]
    mask = 1
    while mask < wide_count:
        y_blocks = jnp.concatenate([y_blocks, flip(y_blocks, "wide", mask)], axis=0)
        mask *= 2

    where = narrow_index.reshape(1)
    row_chunks = []
    placed = []
    for chunk in range(CHUNKS):
        blocks, sources = chunks[chunk]
        after = placed[-1:]
        every = place_blocks(blocks, sources, where, after)
        placed.append(every)
        every = every.reshape(narrow_count * split, tokens, height)
        chunk_rows = lax.all_to_all(every, "wide", split_axis=0, concat_axis=0, tiled=True)
        row_chunks.append(chunk_rows.reshape(tokens * wide_count, height))

    hr, gram = hr_and_gram(cols, y_blocks, wide_index.reshape(1), scale)
    partial = residual_partial(weight_tile, codes, group_scales, hr, placed[-1])
    share = rows // narrow_count
    received = []
    for m in range(narrow_count):
        piece = lax.dynamic_slice_in_dim(partial, (narrow_index ^ m) * share, share, 0)
        received.append(flip(piece, "narrow", m) if m else piece)

    hessian = None
    for chunk in range(CHUNKS):
        hessian = hessian_rows(
            [row_chunks[chunk]], cols, hessian, chunk, (rows, features), scale, [partial]
        )
    return add_pieces(received, hessian), gram, hessian


def solution(mesh):
    in_specs = (
        P("wide", "narrow"),
        P("wide", "narrow"),
        P("wide", "narrow"),
        P("wide", "narrow"),
        P(),
    )
    out_specs = (P(("wide", "narrow"), None), P(), P("wide", "narrow"))
    return jax.shard_map(body, mesh=mesh, in_specs=in_specs, out_specs=out_specs, check_vma=False)
```

time: 281 us -> 204 us (0.73)
  blocking collectives: 37.5 us -> 0 us
  starting transfers between devices: 57.7 us -> 36.9 us
  Pallas kernels: 82.4 us -> 61.7 us
  waiting for transfers between devices: 69.5 us -> 76 us
  other arithmetic: 6.33 us -> 3.47 us
    all_to_all x2 -> x0, blocking collectives: 37.5 us -> none  [body(): lax.all_to_all(every, 'wide', split_axis=0, concat_axis=0, tiled=True)]
    ppermute x4 -> x2, waiting for transfers between devices: 1.12 us -> 23.2 us  [exchange_blocks(): blocks.append(lax.ppermute(direct[half], 'narrow', pairs))]
    pallas_call x5 -> x2, Pallas kernels: 41.1 us -> 21.5 us  [the longest x1 19.4 us: residual_partial(): pl.pallas_call(residual_kernel, out_shape=jax.ShapeDtypeStruct((rows, ran...]
    ppermute x12 -> x6, starting transfers between devices: 29.1 us -> 12.7 us  [exchange_blocks(): direct[mask] = lax.ppermute(mine, 'narrow', pairs) if pairs else None]
    all_to_all x2, waiting for transfers between devices: 13.9 us -> 0.01 us  [body(): lax.all_to_all(every, 'wide', split_axis=0, concat_axis=0, tiled=True)]
    ppermute x5 -> x9, waiting for transfers between devices: 35.6 us -> 24.4 us  [flip(): return lax.ppermute(value, axis, [(i, i ^ mask) for i in range(count)])]
    ppermute x12 -> x6, waiting for transfers between devices: 18.3 us -> 27.6 us  [exchange_blocks(): direct[mask] = lax.ppermute(mine, 'narrow', pairs) if pairs else None]
    all_to_all x1 -> x0, starting transfers between devices: 6.66 us -> none  [body(): lax.all_to_all(shares, 'narrow', split_axis=0, concat_axis=0, tiled=True)]
  transfers between devices with their start and end apart: 25 -> 20, of which waited for: 7 -> 7; matrix products, arithmetic and copies ran while one was open for 3% -> 5% of each run, Pallas kernels for 29% -> 29%
where the time goes in v6:
time: 204 us; the launch traced here: 203 us
  waiting for transfers between devices  76 us (37%)
  Pallas kernels  61.7 us (30%)
  starting transfers between devices  36.9 us (18%)
  between operations  14.2 us (7%)
  local copies, waits for them, and re-layouts  8.16 us (4%)
  other arithmetic  3.47 us (2%)
  matrix products  2.41 us (1%)
    pallas_call x2, Pallas kernels, hessian_rows(): pl.pallas_call(kernel, out_shape=jax.ShapeDtypeStruct(shape, BF16), grid=...  29 us
    ppermute x6, waiting for transfers between devices, exchange_blocks(): direct[mask] = lax.ppermute(mine, 'narrow', pairs) if pairs else None  27.6 us
    ppermute x9, waiting for transfers between devices, flip(): return lax.ppermute(value, axis, [(i, i ^ mask) for i in range(count)])  24.4 us
    ppermute x2, waiting for transfers between devices, exchange_blocks(): blocks.append(lax.ppermute(direct[half], 'narrow', pairs))  23.2 us
    pallas_call x1, Pallas kernels, residual_partial(): pl.pallas_call(residual_kernel, out_shape=jax.ShapeDtypeStruct((rows, ran...  19.4 us
    ppermute x9, starting transfers between devices, flip(): return lax.ppermute(value, axis, [(i, i ^ mask) for i in range(count)])  13.6 us
    ppermute x6, starting transfers between devices, exchange_blocks(): direct[mask] = lax.ppermute(mine, 'narrow', pairs) if pairs else None  12.7 us
    all_to_all x2, starting transfers between devices, body(): lax.all_to_all(every, 'wide', split_axis=0, concat_axis=0, tiled=True)  7.97 us
  transfers between devices with their start and end apart: 20, of which 7 were waited for; matrix products, arithmetic and copies ran while one was open for 5% of the time, Pallas kernels for 29%

profile of v6, /device:TPU:0, one launch (start us, length us, event | category | flops | bytes accessed | tf_op | source)
XLA Modules:
  0.0 202.8 jit_solution(5397375060749235700)
XLA Ops:
  7.2 0.0 all-gather.2.cloned.1.call-start
  7.2 0.7 all-gather.2.cloned.1.call-update
  7.9 1.3 slice_bitcast_fusion.1
  9.2 0.1 pad_maximum_fusion.2.refs_0_
  9.2 4.1 %collective-permute-start.11 = (bf16[2,128,1024]{2,1,0:T(8,128)(2,1)S(1)}, bf16[2,128,1024]{2,1,0:T(8,128)(2,1)S(1)}, u32[]{:S(2)}, u32[]{:S(2)}) collective-permute-start(bf16[2,128,1024]{2,1,0:T(8,128)(2,1)S(1)} %pad_maximum_fusion.2.refs_0_), channel_id=1, source_target_pairs={{0,2},{1,3},{2,0},{3,1},{4,6},{5,7},{6,4},{7,5},{8,10},{9,11},{10,... | collective-permute-start | bytes 1572872 | tf_op jit(solution)/shard_map/ppermute | solution.py:114
  13.3 1.6 collective-permute-start.10
  14.9 0.7 collective-permute-start.12
  15.6 21.8 %collective-permute-done.11.refs_2_ = bf16[2,128,1024]{2,1,0:T(8,128)(2,1)S(1)} collective-permute-done((bf16[2,128,1024]{2,1,0:T(8,128)(2,1)S(1)}, bf16[2,128,1024]{2,1,0:T(8,128)(2,1)S(1)}, u32[]{:S(2)}, u32[]{:S(2)}) %collective-permute-start.11) | collective-permute-done | bytes 524320 | tf_op jit(solution)/shard_map/ppermute | solution.py:114
  37.4 1.3 collective-permute-start.13
  38.7 0.0 collective-permute-done.10.refs_1_
  38.7 0.0 collective-permute-done.12.refs_3_
  38.7 12.8 %collective-permute-done.13.refs_4_ = bf16[2,128,1024]{2,1,0:T(8,128)(2,1)S(1)} collective-permute-done((bf16[2,128,1024]{2,1,0:T(8,128)(2,1)S(1)}, bf16[2,128,1024]{2,1,0:T(8,128)(2,1)S(1)}, u32[]{:S(2)}, u32[]{:S(2)}) %collective-permute-start.13) | collective-permute-done | bytes 524320 | tf_op jit(solution)/shard_map/ppermute | solution.py:123
  51.5 1.5 place_blocks.2.refs_5_
  53.0 3.6 %all-to-all-start.1 = ((bf16[8,128,1024]{2,1,0:T(8,128)(2,1)}), bf16[8,128,1024]{2,1,0:T(8,128)(2,1)S(1)}, u32[]{:S(2)}, u32[]{:S(2)}) async-start(bf16[8,128,1024]{2,1,0:T(8,128)(2,1)} %bitcast.10), calls=%async_computation.1 | async-start | bytes 4194304 | tf_op jit(solution)/shard_map/all_to_all | solution.py:275
  56.6 2.4 %fusion.2 = f32[128,256]{1,0:T(8,128)S(1)} fusion(bf16[128,4096]{1,0:T(8,128)(2,1)} %param.5, bf16[16384,256]{1,0:T(8,128)(2,1)} %param.9, s32[]{:T(128)S(6)} %select_n.15), kind=kOutput, calls=%fused_computation.2 | convolution fusion | flops 268435456 | bytes 3276804 | tf_op jit(solution)/shard_map/dot_general | solution.py:258
  59.1 0.1 collective-permute-start
  59.1 4.8 %collective-permute-start.1 = (f32[128,256]{1,0:T(8,128)S(1)}, f32[128,256]{1,0:T(8,128)S(1)}, u32[]{:S(2)}, u32[]{:S(2)}) collective-permute-start(f32[128,256]{1,0:T(8,128)S(1)} %fusion.2), channel_id=1, source_target_pairs={{0,2},{1,3},{2,0},{3,1},{4,6},{5,7},{6,4},{7,5},{8,10},{9,11},{10,... | collective-permute-start | bytes 393224 | tf_op jit(solution)/shard_map/ppermute | solution.py:18
  64.0 0.0 collective-permute-start.2
  64.0 0.8 pad_maximum_fusion.1.refs_0_
  64.8 1.5 collective-permute-start.7
  66.4 0.0 collective-permute-done
  66.4 18.7 %collective-permute-done.1 = f32[128,256]{1,0:T(8,128)S(1)} collective-permute-done((f32[128,256]{1,0:T(8,128)S(1)}, f32[128,256]{1,0:T(8,128)S(1)}, u32[]{:S(2)}, u32[]{:S(2)}) %collective-permute-start.1) | collective-permute-done | bytes 131104 | tf_op jit(solution)/shard_map/ppermute | solution.py:18
  85.1 0.0 collective-permute-done.2
  85.2 0.1 collective-permute-start.3
  85.2 1.2 collective-permute-done.3
  86.5 2.1 %collective-permute-start.4 = (bf16[2,128,256]{2,1,0:T(8,128)(2,1)S(1)}, bf16[2,128,256]{2,1,0:T(8,128)(2,1)S(1)}, u32[]{:S(2)}, u32[]{:S(2)}) collective-permute-start(bf16[2,128,256]{2,1,0:T(8,128)(2,1)S(1)} %pad_maximum_fusion.4), channel_id=1, source_target_pairs={{0,8},{4,12},{8,0},{12,4},{16,24},{20,28},{24,16},{28,20},{1,9},{5... | collective-permute-start | bytes 393224 | tf_op jit(solution)/shard_map/ppermute | solution.py:18
  88.6 3.4 %collective-permute-start.6 = (bf16[2,128,1024]{2,1,0:T(8,128)(2,1)}, bf16[2,128,1024]{2,1,0:T(8,128)(2,1)}, u32[]{:S(2)}, u32[]{:S(2)}) collective-permute-start(bf16[2,128,1024]{2,1,0:T(8,128)(2,1)} %pad_maximum_fusion.1.refs_0_), channel_id=1, source_target_pairs={{0,1},{1,0},{2,3},{3,2},{4,5},{5,4},{6,7},{7,6},{8,9},{9,8},{10,11... | collective-permute-start | bytes 1572872 | tf_op jit(solution)/shard_map/ppermute | solution.py:114
  92.0 1.4 collective-permute-start.8
  93.4 5.9 %collective-permute-done.7.refs_2_ = bf16[2,128,1024]{2,1,0:T(8,128)(2,1)} collective-permute-done((bf16[2,128,1024]{2,1,0:T(8,128)(2,1)}, bf16[2,128,1024]{2,1,0:T(8,128)(2,1)}, u32[]{:S(2)}, u32[]{:S(2)}) %collective-permute-start.7) | collective-permute-done | bytes 524320 | tf_op jit(solution)/shard_map/ppermute | solution.py:114
  99.3 1.3 collective-permute-start.9
  100.6 0.0 collective-permute-done.4
  100.6 0.7 pad_maximum_fusion.3
  101.3 2.1 %collective-permute-start.5 = (bf16[4,128,256]{2,1,0:T(8,128)(2,1)}, bf16[4,128,256]{2,1,0:T(8,128)(2,1)}, u32[]{:S(2)}, u32[]{:S(2)}) collective-permute-start(bf16[4,128,256]{2,1,0:T(8,128)(2,1)} %pad_maximum_fusion.3), channel_id=1, source_target_pairs={{0,16},{4,20},{8,24},{12,28},{16,0},{20,4},{24,8},{28,12},{1,17},{... | collective-permute-start | bytes 786440 | tf_op jit(solution)/shard_map/ppermute | solution.py:18
  103.4 1.3 copy.10.scales_ref
  104.7 4.4 %collective-permute-done.5 = bf16[4,128,256]{2,1,0:T(8,128)(2,1)} collective-permute-done((bf16[4,128,256]{2,1,0:T(8,128)(2,1)}, bf16[4,128,256]{2,1,0:T(8,128)(2,1)}, u32[]{:S(2)}, u32[]{:S(2)}) %collective-permute-start.5) | collective-permute-done | bytes 262176 | tf_op jit(solution)/shard_map/ppermute | solution.py:18
  109.2 1.8 pad_maximum_fusion.y_ref
  111.0 0.0 collective-permute-done.6.refs_1_
  111.0 0.0 collective-permute-done.8.refs_3_
  111.0 10.3 %collective-permute-done.9.refs_4_ = bf16[2,128,1024]{2,1,0:T(8,128)(2,1)} collective-permute-done((bf16[2,128,1024]{2,1,0:T(8,128)(2,1)}, bf16[2,128,1024]{2,1,0:T(8,128)(2,1)}, u32[]{:S(2)}, u32[]{:S(2)}) %collective-permute-start.9) | collective-permute-done | bytes 524320 | tf_op jit(solution)/shard_map/ppermute | solution.py:123
  121.3 3.2 %place_blocks.3.after_ref = bf16[4,2,128,1024]{3,2,1,0:T(8,128)(2,1)} custom-call(s32[1]{0:T(128)} %bitcast.3.where_ref, bf16[2,128,1024]{2,1,0:T(8,128)(2,1)} %pad_maximum_fusion.1.refs_0_, bf16[2,128,1024]{2,1,0:T(8,128)(2,1)} %collective-permute-done.6.refs_1_, bf16[2,128,1024]{2,1,0:T(8,128)(2,1)} %collective-permute-done.7.refs_2_, ...), custom_call_target="tpu_custom_call" | custom-call | bytes 4194304 | tf_op jit(solution)/shard_map/place_blocks/pallas_call | solution.py:92
  124.5 1.0 copy-done.4
  125.5 6.5 %hr_and_gram.1 = (bf16[4096,256]{1,0:T(8,128)(2,1)S(1)}, f32[256,256]{1,0:T(8,128)}) custom-call(s32[1]{0:T(128)} %bitcast.where_ref, bf16[1024,4096]{1,0:T(8,128)(2,1)} %all-gather.2.cloned.1.call-done.cols_ref.refs_1_, bf16[8,128,256]{2,1,0:T(8,128)(2,1)S(1)} %copy-done.4), custom_call_target="tpu_custom_call" | custom-call | flops 4294967296 | bytes 16777216 | tf_op jit(solution)/shard_map/hr_and_gram/pallas_call | solution.py:43
  132.0 1.3 copy-done
  133.3 0.0 all-to-all-done.1
  133.4 4.4 %all-to-all-start = ((bf16[8,128,1024]{2,1,0:T(8,128)(2,1)}), bf16[8,128,1024]{2,1,0:T(8,128)(2,1)}, u32[]{:S(2)}, u32[]{:S(2)}) async-start(bf16[8,128,1024]{2,1,0:T(8,128)(2,1)} %bitcast.8), calls=%async_computation | async-start | bytes 4194304 | tf_op jit(solution)/shard_map/all_to_all | solution.py:275
  137.7 0.0 copy-done.2
  137.7 0.0 copy-start.1
  137.7 1.6 copy-done.1
  139.3 19.4 %residual_product.1.refs_2_.refs_3_ = bf16[2048,256]{1,0:T(8,128)(2,1)S(1)} custom-call(bf16[2048,4096]{1,0:T(8,128)(2,1)} %weight_ref.1, s32[2048,4096]{1,0:T(8,128)} %codes_ref.1, f32[2048,32]{1,0:T(8,128)S(1)} %copy.10.scales_ref, bf16[4096,256]{1,0:T(8,128)(2,1)S(1)} %copy-done.1, bf16[4,2,128,1024]{3,2,1,0:T(8,128)(2,1)} %place_blocks.3.after_ref), custom_call_target="tpu_custom_call" | custom-call | flops 8589934592 | bytes 67108864 | tf_op jit(solution)/shard_map/residual_product/pallas_call | solution.py:145
  158.8 0.8 constant_dynamic-slice_fusion
  159.6 0.0 collective-permute-start.14
  159.6 3.1 %collective-permute-start.15 = (bf16[512,256]{1,0:T(8,128)(2,1)S(1)}, bf16[512,256]{1,0:T(8,128)(2,1)S(1)}, u32[]{:S(2)}, u32[]{:S(2)}) collective-permute-start(bf16[512,256]{1,0:T(8,128)(2,1)S(1)} %get-tuple-element.8), channel_id=1, source_target_pairs={{0,2},{1,3},{2,0},{3,1},{4,6},{5,7},{6,4},{7,5},{8,10},{9,11},{10,... | collective-permute-start | bytes 786440 | tf_op jit(solution)/shard_map/ppermute | solution.py:18
  162.6 1.3 collective-permute-start.16
  164.0 0.0 copy-done.3
  164.0 14.1 %hessian_rows.2.refs_2_ = bf16[2048,4096]{1,0:T(8,128)(2,1)} custom-call(bf16[1024,1024]{1,0:T(8,128)(2,1)S(1)} %bitcast.19, bf16[1024,4096]{1,0:T(8,128)(2,1)} %all-gather.2.cloned.1.call-done.cols_ref.refs_1_, bf16[2048,256]{1,0:T(8,128)(2,1)S(1)} %residual_product.1.refs_2_.refs_3_), custom_call_target="tpu_custom_call" | custom-call | flops 17179869184 | bytes 18874368 | tf_op jit(solution)/shard_map/hessian_rows/pallas_call | solution.py:192
  178.1 0.0 all-to-all-done
  178.1 14.9 %hessian_rows.3.refs_4_ = bf16[2048,4096]{1,0:T(8,128)(2,1)} custom-call(bf16[1024,1024]{1,0:T(8,128)(2,1)} %bitcast.9.refs_0_, bf16[1024,4096]{1,0:T(8,128)(2,1)} %all-gather.2.cloned.1.call-done.cols_ref.refs_1_, bf16[2048,4096]{1,0:T(8,128)(2,1)} %hessian_rows.2.refs_2_, ...), custom_call_target="tpu_custom_call", output_to_operand_aliasing={{}: (2, {})} | custom-call | flops 17179869184 | bytes 18874368 | tf_op jit(solution)/shard_map/hessian_rows/pallas_call | solution.py:192
  193.0 0.0 collective-permute-done.14.refs_1_
  193.0 0.0 collective-permute-done.15.refs_2_
  193.0 0.0 collective-permute-done.16.refs_3_
  193.0 0.7 copy-done.5
  193.7 0.1 copy-done.6
  193.8 0.1 copy-done.7
  193.9 2.1 %add_pieces.1 = f32[512,256]{1,0:T(8,128)} custom-call(bf16[512,256]{1,0:T(8,128)(2,1)} %get-tuple-element.10.refs_0_, bf16[512,256]{1,0:T(8,128)(2,1)} %copy-done.5, bf16[512,256]{1,0:T(8,128)(2,1)} %copy-done.6, bf16[512,256]{1,0:T(8,128)(2,1)} %copy-done.7, bf16[2048,4096]{1,0:T(8,128)(2,1)} %hessian_rows.3.refs_4_), custom_call_target="tpu_custom_call" | custom-call | bytes 1572864 | tf_op jit(solution)/shard_map/add_pieces/pallas_call | solution.py:217
  (10 shorter events, 0.1 us)
Async XLA Ops:
  7.2 117.3 %all-gather.2.cloned.1.call-start = ((), (), s32[]{:S(2)}) async-start(), calls=%async_computation.2 | async-start | bytes 9437184 | tf_op jit(solution)/shard_map/all_gather | solution.py:244
  9.2 28.1 %collective-permute-start.11 = (bf16[2,128,1024]{2,1,0:T(8,128)(2,1)S(1)}, bf16[2,128,1024]{2,1,0:T(8,128)(2,1)S(1)}, u32[]{:S(2)}, u32[]{:S(2)}) collective-permute-start(bf16[2,128,1024]{2,1,0:T(8,128)(2,1)S(1)} %pad_maximum_fusion.2.refs_0_), channel_id=1, source_target_pairs={{0,2},{1,3},{2,0},{3,1},{4,6},{5,7},{6,4},{7,5},{8,10},{9,11},{10,... | collective-permute-start | bytes 1572872 | tf_op jit(solution)/shard_map/ppermute | solution.py:114
  13.3 25.3 %collective-permute-start.10 = (bf16[2,128,1024]{2,1,0:T(8,128)(2,1)S(1)}, bf16[2,128,1024]{2,1,0:T(8,128)(2,1)S(1)}, u32[]{:S(2)}, u32[]{:S(2)}) collective-permute-start(bf16[2,128,1024]{2,1,0:T(8,128)(2,1)S(1)} %pad_maximum_fusion.2.refs_0_), channel_id=1, source_target_pairs={{0,1},{1,0},{2,3},{3,2},{4,5},{5,4},{6,7},{7,6},{8,9},{9,8},{10,11... | collective-permute-start | bytes 1572872 | tf_op jit(solution)/shard_map/ppermute | solution.py:114
  14.9 23.8 %collective-permute-start.12 = (bf16[2,128,1024]{2,1,0:T(8,128)(2,1)S(1)}, bf16[2,128,1024]{2,1,0:T(8,128)(2,1)S(1)}, u32[]{:S(2)}, u32[]{:S(2)}) collective-permute-start(bf16[2,128,1024]{2,1,0:T(8,128)(2,1)S(1)} %pad_maximum_fusion.2.refs_0_), channel_id=1, source_target_pairs={{1,2},{2,1},{5,6},{6,5},{9,10},{10,9},{13,14},{14,13},{17,18},{18,... | collective-permute-start | bytes 1572872 | tf_op jit(solution)/shard_map/ppermute | solution.py:114
  37.4 14.2 %collective-permute-start.13 = (bf16[2,128,1024]{2,1,0:T(8,128)(2,1)S(1)}, bf16[2,128,1024]{2,1,0:T(8,128)(2,1)S(1)}, u32[]{:S(2)}, u32[]{:S(2)}) collective-permute-start(bf16[2,128,1024]{2,1,0:T(8,128)(2,1)S(1)} %collective-permute-done.11.refs_2_), channel_id=1, source_target_pairs={{2,3},{1,0},{6,7},{5,4},{10,11},{9,8},{14,15},{13,12},{18,19},{17,... | collective-permute-start | bytes 1572872 | tf_op jit(solution)/shard_map/ppermute | solution.py:123
  53.0 80.3 %all-to-all-start.1 = ((bf16[8,128,1024]{2,1,0:T(8,128)(2,1)}), bf16[8,128,1024]{2,1,0:T(8,128)(2,1)S(1)}, u32[]{:S(2)}, u32[]{:S(2)}) async-start(bf16[8,128,1024]{2,1,0:T(8,128)(2,1)} %bitcast.10), calls=%async_computation.1 | async-start | bytes 4194304 | tf_op jit(solution)/shard_map/all_to_all | solution.py:275
  59.1 7.3 %collective-permute-start = (f32[128,256]{1,0:T(8,128)S(1)}, f32[128,256]{1,0:T(8,128)S(1)}, u32[]{:S(2)}, u32[]{:S(2)}) collective-permute-start(f32[128,256]{1,0:T(8,128)S(1)} %fusion.2), channel_id=1, source_target_pairs={{0,1},{1,0},{2,3},{3,2},{4,5},{5,4},{6,7},{7,6},{8,9},{9,8},{10,11... | collective-permute-start | bytes 393224 | tf_op jit(solution)/shard_map/ppermute | solution.py:18
  59.1 26.0 %collective-permute-start.1 = (f32[128,256]{1,0:T(8,128)S(1)}, f32[128,256]{1,0:T(8,128)S(1)}, u32[]{:S(2)}, u32[]{:S(2)}) collective-permute-start(f32[128,256]{1,0:T(8,128)S(1)} %fusion.2), channel_id=1, source_target_pairs={{0,2},{1,3},{2,0},{3,1},{4,6},{5,7},{6,4},{7,5},{8,10},{9,11},{10,... | collective-permute-start | bytes 393224 | tf_op jit(solution)/shard_map/ppermute | solution.py:18
  64.0 21.1 %collective-permute-start.2 = (f32[128,256]{1,0:T(8,128)S(1)}, f32[128,256]{1,0:T(8,128)S(1)}, u32[]{:S(2)}, u32[]{:S(2)}) collective-permute-start(f32[128,256]{1,0:T(8,128)S(1)} %fusion.2), channel_id=1, source_target_pairs={{0,3},{1,2},{2,1},{3,0},{4,7},{5,6},{6,5},{7,4},{8,11},{9,10},{10,... | collective-permute-start | bytes 393224 | tf_op jit(solution)/shard_map/ppermute | solution.py:18
  64.8 34.5 %collective-permute-start.7 = (bf16[2,128,1024]{2,1,0:T(8,128)(2,1)}, bf16[2,128,1024]{2,1,0:T(8,128)(2,1)}, u32[]{:S(2)}, u32[]{:S(2)}) collective-permute-start(bf16[2,128,1024]{2,1,0:T(8,128)(2,1)} %pad_maximum_fusion.1.refs_0_), channel_id=1, source_target_pairs={{0,2},{1,3},{2,0},{3,1},{4,6},{5,7},{6,4},{7,5},{8,10},{9,11},{10,... | collective-permute-start | bytes 1572872 | tf_op jit(solution)/shard_map/ppermute | solution.py:114
  85.2 1.3 collective-permute-start.3
  86.5 14.1 %collective-permute-start.4 = (bf16[2,128,256]{2,1,0:T(8,128)(2,1)S(1)}, bf16[2,128,256]{2,1,0:T(8,128)(2,1)S(1)}, u32[]{:S(2)}, u32[]{:S(2)}) collective-permute-start(bf16[2,128,256]{2,1,0:T(8,128)(2,1)S(1)} %pad_maximum_fusion.4), channel_id=1, source_target_pairs={{0,8},{4,12},{8,0},{12,4},{16,24},{20,28},{24,16},{28,20},{1,9},{5... | collective-permute-start | bytes 393224 | tf_op jit(solution)/shard_map/ppermute | solution.py:18
  88.6 22.4 %collective-permute-start.6 = (bf16[2,128,1024]{2,1,0:T(8,128)(2,1)}, bf16[2,128,1024]{2,1,0:T(8,128)(2,1)}, u32[]{:S(2)}, u32[]{:S(2)}) collective-permute-start(bf16[2,128,1024]{2,1,0:T(8,128)(2,1)} %pad_maximum_fusion.1.refs_0_), channel_id=1, source_target_pairs={{0,1},{1,0},{2,3},{3,2},{4,5},{5,4},{6,7},{7,6},{8,9},{9,8},{10,11... | collective-permute-start | bytes 1572872 | tf_op jit(solution)/shard_map/ppermute | solution.py:114
  92.0 19.0 %collective-permute-start.8 = (bf16[2,128,1024]{2,1,0:T(8,128)(2,1)}, bf16[2,128,1024]{2,1,0:T(8,128)(2,1)}, u32[]{:S(2)}, u32[]{:S(2)}) collective-permute-start(bf16[2,128,1024]{2,1,0:T(8,128)(2,1)} %pad_maximum_fusion.1.refs_0_), channel_id=1, source_target_pairs={{1,2},{2,1},{5,6},{6,5},{9,10},{10,9},{13,14},{14,13},{17,18},{18,... | collective-permute-start | bytes 1572872 | tf_op jit(solution)/shard_map/ppermute | solution.py:114
  99.3 22.0 %collective-permute-start.9 = (bf16[2,128,1024]{2,1,0:T(8,128)(2,1)}, bf16[2,128,1024]{2,1,0:T(8,128)(2,1)}, u32[]{:S(2)}, u32[]{:S(2)}) collective-permute-start(bf16[2,128,1024]{2,1,0:T(8,128)(2,1)} %collective-permute-done.7.refs_2_), channel_id=1, source_target_pairs={{2,3},{1,0},{6,7},{5,4},{10,11},{9,8},{14,15},{13,12},{18,19},{17,... | collective-permute-start | bytes 1572872 | tf_op jit(solution)/shard_map/ppermute | solution.py:123
  101.3 7.9 %collective-permute-start.5 = (bf16[4,128,256]{2,1,0:T(8,128)(2,1)}, bf16[4,128,256]{2,1,0:T(8,128)(2,1)}, u32[]{:S(2)}, u32[]{:S(2)}) collective-permute-start(bf16[4,128,256]{2,1,0:T(8,128)(2,1)} %pad_maximum_fusion.3), channel_id=1, source_target_pairs={{0,16},{4,20},{8,24},{12,28},{16,0},{20,4},{24,8},{28,12},{1,17},{... | collective-permute-start | bytes 786440 | tf_op jit(solution)/shard_map/ppermute | solution.py:18
  124.5 1.0 copy-start.4
  132.0 1.3 copy-start
  133.4 4.4 %copy-start.2 = (bf16[8,128,1024]{2,1,0:T(8,128)(2,1)}, bf16[8,128,1024]{2,1,0:T(8,128)(2,1)S(1)}, u32[]{:S(2)}) copy-start(bf16[8,128,1024]{2,1,0:T(8,128)(2,1)S(1)} %all-to-all-done.1) | copy-start | bytes 6291460
  133.4 44.8 %all-to-all-start = ((bf16[8,128,1024]{2,1,0:T(8,128)(2,1)}), bf16[8,128,1024]{2,1,0:T(8,128)(2,1)}, u32[]{:S(2)}, u32[]{:S(2)}) async-start(bf16[8,128,1024]{2,1,0:T(8,128)(2,1)} %bitcast.8), calls=%async_computation | async-start | bytes 4194304 | tf_op jit(solution)/shard_map/all_to_all | solution.py:275
  137.7 1.6 copy-start.1
  139.3 24.6 %copy-start.3 = (bf16[8,128,1024]{2,1,0:T(8,128)(2,1)S(1)}, bf16[8,128,1024]{2,1,0:T(8,128)(2,1)}, u32[]{:S(2)}) copy-start(bf16[8,128,1024]{2,1,0:T(8,128)(2,1)} %copy-done.2) | copy-start | bytes 6291460
  159.6 33.4 %collective-permute-start.14 = (bf16[512,256]{1,0:T(8,128)(2,1)S(1)}, bf16[512,256]{1,0:T(8,128)(2,1)S(1)}, u32[]{:S(2)}, u32[]{:S(2)}) collective-permute-start(bf16[512,256]{1,0:T(8,128)(2,1)S(1)} %get-tuple-element.9), channel_id=1, source_target_pairs={{0,1},{1,0},{2,3},{3,2},{4,5},{5,4},{6,7},{7,6},{8,9},{9,8},{10,11... | collective-permute-start | bytes 786440 | tf_op jit(solution)/shard_map/ppermute | solution.py:18
  159.6 33.4 %collective-permute-start.15 = (bf16[512,256]{1,0:T(8,128)(2,1)S(1)}, bf16[512,256]{1,0:T(8,128)(2,1)S(1)}, u32[]{:S(2)}, u32[]{:S(2)}) collective-permute-start(bf16[512,256]{1,0:T(8,128)(2,1)S(1)} %get-tuple-element.8), channel_id=1, source_target_pairs={{0,2},{1,3},{2,0},{3,1},{4,6},{5,7},{6,4},{7,5},{8,10},{9,11},{10,... | collective-permute-start | bytes 786440 | tf_op jit(solution)/shard_map/ppermute | solution.py:18
  162.6 30.4 %collective-permute-start.16 = (bf16[512,256]{1,0:T(8,128)(2,1)S(1)}, bf16[512,256]{1,0:T(8,128)(2,1)S(1)}, u32[]{:S(2)}, u32[]{:S(2)}) collective-permute-start(bf16[512,256]{1,0:T(8,128)(2,1)S(1)} %get-tuple-element.7), channel_id=1, source_target_pairs={{0,3},{1,2},{2,1},{3,0},{4,7},{5,6},{6,5},{7,4},{8,11},{9,10},{10,... | collective-permute-start | bytes 786440 | tf_op jit(solution)/shard_map/ppermute | solution.py:18
  193.0 0.7 copy-start.5
  193.0 0.8 copy-start.6
  193.0 0.9 copy-start.7
Sparse Core Ops, SparseCore 0:
  9.9 62.3 all-gather.1

commit v7 on v6

--- a/solution.py
+++ b/solution.py
@@ -16,6 +16,11 @@
 def flip(value, axis, mask):
     count = lax.axis_size(axis)
     return lax.ppermute(value, axis, [(i, i ^ mask) for i in range(count)])
+
+
+def first_tile(value):
+    shape = (1,) * (value.ndim - 2) + (16, 128)
+    return pl.BlockSpec(shape, lambda *at: (0,) * value.ndim)
 
 
 def cost(flops, moved):
@@ -92,14 +97,36 @@
     return pl.pallas_call(
         functools.partial(place_kernel, sources),
         out_shape=jax.ShapeDtypeStruct((count,) + blocks[0].shape, BF16),
+        grid=(1,),
         in_specs=[pl.BlockSpec(memory_space=pltpu.SMEM)]
         + [pl.BlockSpec(memory_space=pltpu.VMEM)] * len(blocks)
-        + [pl.BlockSpec(memory_space=pl.ANY)] * len(after),
+        + [first_tile(value) for value in after],
         out_specs=pl.BlockSpec(memory_space=pltpu.VMEM),
         cost_estimate=cost(0, 4 * count * blocks[0].size),
         compiler_params=pltpu.CompilerParams(vmem_limit_bytes=48 * MIB),
         name="place_blocks",
     )(where, *blocks, *after)
+
+
+def take_chunk(activations, chunk, height, split, after):
+    tokens, features = activations.shape
+    rows = features // split
+
+    def kernel(activations_ref, *refs):
+        for s in range(split):
+            at = s * rows + chunk * height
+            refs[-1][s] = activations_ref[:, at : at + height]
+
+    return pl.pallas_call(
+        kernel,
+        out_shape=jax.ShapeDtypeStruct((split, tokens, height), BF16),
+        grid=(1,),
+        in_specs=[pl.BlockSpec((tokens, features), lambda i: (0, 0))]
+        + [first_tile(value) for value in after],
+        out_specs=pl.BlockSpec((split, tokens, height), lambda i: (0, 0, 0)),
+        cost_estimate=cost(0, 4 * split * tokens * height),
+        name="take_chunk",
+    )(activations, *after)
 
 
 def exchange_blocks(mine):
@@ -125,7 +152,8 @@
     return blocks, sources
 
 
-def residual_kernel(weight_ref, codes_ref, scales_ref, hr_ref, after_ref, out_ref):
+def residual_kernel(weight_ref, codes_ref, scales_ref, hr_ref, *refs):
+    out_ref = refs[-1]
     groups = scales_ref.shape[1]
     width = weight_ref.shape[1] // groups
     scales = scales_ref[...]
@@ -138,26 +166,28 @@
     out_ref[...] = jnp.dot(residual, hr_ref[...], preferred_element_type=F32).astype(BF16)
 
 
-def residual_partial(weight, codes, scales, hr, after):
+def residual_partial(weight, codes, scales, hr, part, count, after):
     rows, features = weight.shape
     rank = hr.shape[1]
+    rows //= count
     block = min(256, rows)
+    first = part * (rows // block)
     return pl.pallas_call(
         residual_kernel,
         out_shape=jax.ShapeDtypeStruct((rows, rank), BF16),
         grid=(rows // block,),
         in_specs=[
-            pl.BlockSpec((block, features), lambda i: (i, 0)),
-            pl.BlockSpec((block, features), lambda i: (i, 0)),
-            pl.BlockSpec((block, scales.shape[1]), lambda i: (i, 0)),
+            pl.BlockSpec((block, features), lambda i: (first + i, 0)),
+            pl.BlockSpec((block, features), lambda i: (first + i, 0)),
+            pl.BlockSpec((block, scales.shape[1]), lambda i: (first + i, 0)),
             pl.BlockSpec((features, rank), lambda i: (0, 0)),
-            pl.BlockSpec(memory_space=pl.ANY),
-        ],
+        ]
+        + [first_tile(value) for value in after],
         out_specs=pl.BlockSpec((block, rank), lambda i: (i, 0)),
         cost_estimate=cost(4 * rows * features * rank, 8 * rows * features),
         compiler_params=pltpu.CompilerParams(vmem_limit_bytes=48 * MIB),
         name="residual_product",
-    )(weight, codes, scales, hr, after)
+    )(weight, codes, scales, hr, *after)
 
 
 def hessian_rows(row_chunks, cols, earlier, index, shape, scale, after):
@@ -175,7 +205,7 @@
         specs.append(pl.BlockSpec(memory_space=pl.ANY))
     for value in after:
         ins.append(value)
-        specs.append(pl.BlockSpec(memory_space=pl.ANY))
+        specs.append(first_tile(value))
 
     def kernel(*refs):
         cols_ref = refs[count]
@@ -217,8 +247,9 @@
     return pl.pallas_call(
         kernel,
         out_shape=jax.ShapeDtypeStruct((rows, rank), F32),
+        grid=(1,),
         in_specs=[pl.BlockSpec(memory_space=pltpu.VMEM)] * len(pieces)
-        + [pl.BlockSpec(memory_space=pl.ANY)],
+        + [first_tile(after)],
         out_specs=pl.BlockSpec(memory_space=pltpu.VMEM),
         cost_estimate=cost(0, 12 * rows * rank),
         name="add_pieces",
@@ -243,32 +274,30 @@
 
     cols = lax.all_gather(activations, "wide", axis=0, tiled=True)
 
-    height = rows // CHUNKS
-    chunks = []
-    for chunk in range(CHUNKS):
-        mine = jnp.stack(
-            [
-                activations[:, s * rows + chunk * height : s * rows + (chunk + 1) * height]
-                for s in range(split)
-            ]
-        )
-        chunks.append(exchange_blocks(mine))
-
     right_block = lax.dynamic_slice_in_dim(right_factor, narrow_index * features, features, 0)
     product = jnp.dot(activations, right_block, preferred_element_type=F32)
     product = pair_sum([product] + [flip(product, "narrow", m) for m in range(1, narrow_count)])
+    steps = [product]
     y_blocks = product.astype(BF16)[None]
     mask = 1
     while mask < wide_count:
         y_blocks = jnp.concatenate([y_blocks, flip(y_blocks, "wide", mask)], axis=0)
+        steps.append(y_blocks)
         mask *= 2
+
+    height = rows // CHUNKS
+    chunks = []
+    after = []
+    for chunk in range(CHUNKS):
+        chunks.append(exchange_blocks(take_chunk(activations, chunk, height, split, after)))
+        after = [steps[0], chunks[-1][0][-1 if narrow_count < 4 else narrow_count // 2]]
 
     where = narrow_index.reshape(1)
     row_chunks = []
     placed = []
     for chunk in range(CHUNKS):
         blocks, sources = chunks[chunk]
-        after = placed[-1:]
+        after = placed[-1:] if chunk else steps[-2:-1]
         every = place_blocks(blocks, sources, where, after)
         placed.append(every)
         every = every.reshape(narrow_count * split, tokens, height)
@@ -276,7 +305,13 @@
         row_chunks.append(chunk_rows.reshape(tokens * wide_count, height))
 
     hr, gram = hr_and_gram(cols, y_blocks, wide_index.reshape(1), scale)
-    partial = residual_partial(weight_tile, codes, group_scales, hr, placed[-1])
+    partial = []
+    for part in range(2):
+        after = [placed[-1], partial[0]] if part else []
+        partial.append(
+            residual_partial(weight_tile, codes, group_scales, hr, part, 2, after)
+        )
+    partial = jnp.concatenate(partial, axis=0)
     share = rows // narrow_count
     received = []
     for m in range(narrow_count):

time: 204 us -> 226 us (1.11)
  waiting for transfers between devices: 76 us -> 95.6 us
  Pallas kernels: 61.7 us -> 67.6 us
  local copies, waits for them, and re-layouts: 8.16 us -> 3.05 us
    ppermute x9, waiting for transfers between devices: 24.4 us -> 65.8 us  [flip(): return lax.ppermute(value, axis, [(i, i ^ mask) for i in range(count)])]
    ppermute x6, waiting for transfers between devices: 27.6 us -> 10.6 us  [exchange_blocks(): direct[mask] = lax.ppermute(mine, 'narrow', pairs) if pairs else None]
    ppermute x2, waiting for transfers between devices: 23.2 us -> 7.03 us  [exchange_blocks(): blocks.append(lax.ppermute(direct[half], 'narrow', pairs))]
    all_to_all x2, waiting for transfers between devices: 0.01 us -> 11.5 us  [body(): lax.all_to_all(every, 'wide', split_axis=0, concat_axis=0, tiled=True)]
    pallas_call x0 -> x2, Pallas kernels: none -> 4.13 us  [take_chunk(): pl.pallas_call(kernel, out_shape=jax.ShapeDtypeStruct((split, tokens, hei...]
    concatenate x0 -> x2, other arithmetic: none -> 3.74 us  [body(): partial = jnp.concatenate(partial, axis=0)]
    unnamed x17 -> x21, local copies, waits for them, and re-layouts: 6.1 us -> 3.05 us
    pallas_call x1 -> x2, Pallas kernels: 19.4 us -> 21 us  [residual_partial(): pl.pallas_call(residual_kernel, out_shape=jax.ShapeDtypeStruct((rows, ran...]
  transfers between devices with their start and end apart: 20 -> 20, of which waited for: 7 -> 8; matrix products, arithmetic and copies ran while one was open for 5% -> 4% of each run, Pallas kernels for 29% -> 29%
where the time goes in v7:
time: 226 us; the launch traced here: 225 us
  waiting for transfers between devices  95.6 us (42%)
  Pallas kernels  67.6 us (30%)
  starting transfers between devices  36.9 us (16%)
  between operations  14.3 us (6%)
  other arithmetic  5.51 us (2%)
  local copies, waits for them, and re-layouts  3.05 us (1%)
    ppermute x9, waiting for transfers between devices, flip(): return lax.ppermute(value, axis, [(i, i ^ mask) for i in range(count)])  65.8 us
    pallas_call x2, Pallas kernels, hessian_rows(): pl.pallas_call(kernel, out_shape=jax.ShapeDtypeStruct(shape, BF16), grid=...  29.7 us
    pallas_call x2, Pallas kernels, residual_partial(): pl.pallas_call(residual_kernel, out_shape=jax.ShapeDtypeStruct((rows, ran...  21 us
    ppermute x6, starting transfers between devices, exchange_blocks(): direct[mask] = lax.ppermute(mine, 'narrow', pairs) if pairs else None  12.9 us
    ppermute x9, starting transfers between devices, flip(): return lax.ppermute(value, axis, [(i, i ^ mask) for i in range(count)])  12.4 us
    all_to_all x2, waiting for transfers between devices, body(): lax.all_to_all(every, 'wide', split_axis=0, concat_axis=0, tiled=True)  11.5 us
    ppermute x6, waiting for transfers between devices, exchange_blocks(): direct[mask] = lax.ppermute(mine, 'narrow', pairs) if pairs else None  10.6 us
    all_to_all x2, starting transfers between devices, body(): lax.all_to_all(every, 'wide', split_axis=0, concat_axis=0, tiled=True)  9.06 us
  transfers between devices with their start and end apart: 20, of which 8 were waited for; matrix products, arithmetic and copies ran while one was open for 4% of the time, Pallas kernels for 29%

profile of v7, /device:TPU:0, one launch (start us, length us, event | category | flops | bytes accessed | tf_op | source)
XLA Modules:
  0.0 225.0 jit_solution(4623061459489433459)
XLA Ops:
  7.2 0.0 copy-start.4
  7.2 0.0 all-gather.2.cloned.1.call-start
  7.2 0.7 all-gather.2.cloned.1.call-update
  7.9 2.1 take_chunk.2.refs_0_
  10.0 4.0 %collective-permute-start.6 = (bf16[2,128,1024]{2,1,0:T(8,128)(2,1)}, bf16[2,128,1024]{2,1,0:T(8,128)(2,1)S(1)}, u32[]{:S(2)}, u32[]{:S(2)}) collective-permute-start(bf16[2,128,1024]{2,1,0:T(8,128)(2,1)} %take_chunk.2.refs_0_), channel_id=1, source_target_pairs={{0,2},{1,3},{2,0},{3,1},{4,6},{5,7},{6,4},{7,5},{8,10},{9,11},{10,... | collective-permute-start | bytes 1572872 | tf_op jit(solution)/shard_map/ppermute | solution.py:141
  14.0 0.0 copy-done.4
  14.0 2.0 fusion.2
  16.0 1.4 collective-permute-start.2
  17.5 1.7 collective-permute-start.1
  19.1 1.4 collective-permute-start
  20.5 0.0 copy-done
  20.5 0.7 collective-permute-start.12
  21.2 10.0 %collective-permute-done.2 = f32[128,256]{1,0:T(8,128)S(1)} collective-permute-done((f32[128,256]{1,0:T(8,128)S(1)}, f32[128,256]{1,0:T(8,128)S(1)}, u32[]{:S(2)}, u32[]{:S(2)}) %collective-permute-start.2) | collective-permute-done | bytes 131104 | tf_op jit(solution)/shard_map/ppermute | solution.py:18
  31.2 18.3 %collective-permute-done.1 = f32[128,256]{1,0:T(8,128)S(1)} collective-permute-done((f32[128,256]{1,0:T(8,128)S(1)}, f32[128,256]{1,0:T(8,128)S(1)}, u32[]{:S(2)}, u32[]{:S(2)}) %collective-permute-start.1) | collective-permute-done | bytes 131104 | tf_op jit(solution)/shard_map/ppermute | solution.py:18
  49.5 0.0 collective-permute-done
  49.5 0.7 convert_bitcast_fusion
  50.2 0.0 collective-permute-done.6.refs_1_.refs_2_
  50.2 0.8 copy-done.1
  51.0 2.1 take_chunk.3.refs_0_
  53.1 0.0 collective-permute-start.8
  53.1 3.3 %collective-permute-start.11 = (bf16[2,128,1024]{2,1,0:T(8,128)(2,1)S(1)}, bf16[2,128,1024]{2,1,0:T(8,128)(2,1)S(1)}, u32[]{:S(2)}, u32[]{:S(2)}) collective-permute-start(bf16[2,128,1024]{2,1,0:T(8,128)(2,1)S(1)} %copy-done), channel_id=1, source_target_pairs={{0,1},{1,0},{2,3},{3,2},{4,5},{5,4},{6,7},{7,6},{8,9},{9,8},{10,11... | collective-permute-start | bytes 1572872 | tf_op jit(solution)/shard_map/ppermute | solution.py:141
  56.4 1.3 collective-permute-start.13
  57.7 0.1 collective-permute-start.3
  57.7 1.2 collective-permute-done.3
  59.0 1.6 collective-permute-start.4
  60.6 7.2 %collective-permute-done.4 = bf16[2,128,256]{2,1,0:T(8,128)(2,1)S(1)} collective-permute-done((bf16[2,128,256]{2,1,0:T(8,128)(2,1)S(1)}, bf16[2,128,256]{2,1,0:T(8,128)(2,1)S(1)}, u32[]{:S(2)}, u32[]{:S(2)}) %collective-permute-start.4) | collective-permute-done | bytes 131104 | tf_op jit(solution)/shard_map/ppermute | solution.py:18
  67.8 0.7 collective-permute-start.9
  68.5 0.0 collective-permute-done.12.refs_3_
  68.5 4.2 %collective-permute-start.7 = (bf16[2,128,1024]{2,1,0:T(8,128)(2,1)}, bf16[2,128,1024]{2,1,0:T(8,128)(2,1)}, u32[]{:S(2)}, u32[]{:S(2)}) collective-permute-start(bf16[2,128,1024]{2,1,0:T(8,128)(2,1)} %take_chunk.3.refs_0_), channel_id=1, source_target_pairs={{0,1},{1,0},{2,3},{3,2},{4,5},{5,4},{6,7},{7,6},{8,9},{9,8},{10,11... | collective-permute-start | bytes 1572872 | tf_op jit(solution)/shard_map/ppermute | solution.py:141
  72.7 10.6 %collective-permute-done.8.refs_2_ = bf16[2,128,1024]{2,1,0:T(8,128)(2,1)S(1)} collective-permute-done((bf16[2,128,1024]{2,1,0:T(8,128)(2,1)}, bf16[2,128,1024]{2,1,0:T(8,128)(2,1)S(1)}, u32[]{:S(2)}, u32[]{:S(2)}) %collective-permute-start.8) | collective-permute-done | bytes 524320 | tf_op jit(solution)/shard_map/ppermute | solution.py:141
  83.3 1.3 collective-permute-start.10
  84.6 0.0 collective-permute-done.11.refs_1_
  84.6 7.0 %collective-permute-done.13.refs_4_ = bf16[2,128,1024]{2,1,0:T(8,128)(2,1)S(1)} collective-permute-done((bf16[2,128,1024]{2,1,0:T(8,128)(2,1)}, bf16[2,128,1024]{2,1,0:T(8,128)(2,1)S(1)}, u32[]{:S(2)}, u32[]{:S(2)}) %collective-permute-start.13) | collective-permute-done | bytes 524320 | tf_op jit(solution)/shard_map/ppermute | solution.py:150
  91.6 1.0 copy-done.2
  92.7 1.5 place_blocks.2.refs_5_
  94.1 4.5 %all-to-all-start.1 = ((bf16[8,128,1024]{2,1,0:T(8,128)(2,1)}), bf16[8,128,1024]{2,1,0:T(8,128)(2,1)}, u32[]{:S(2)}, u32[]{:S(2)}) async-start(bf16[8,128,1024]{2,1,0:T(8,128)(2,1)} %bitcast.6), calls=%async_computation.1 | async-start | bytes 4194304 | tf_op jit(solution)/shard_map/all_to_all | solution.py:304
  98.7 1.9 collective-permute-start.5
  100.6 0.3 copy.10.scales_ref
  100.9 29.0 %collective-permute-done.5 = bf16[4,128,256]{2,1,0:T(8,128)(2,1)} collective-permute-done((bf16[4,128,256]{2,1,0:T(8,128)(2,1)S(1)}, bf16[4,128,256]{2,1,0:T(8,128)(2,1)}, u32[]{:S(2)}, u32[]{:S(2)}) %collective-permute-start.5) | collective-permute-done | bytes 262176 | tf_op jit(solution)/shard_map/ppermute | solution.py:18
  130.0 1.0 pad_maximum_fusion.1.y_ref
  131.0 0.0 collective-permute-done.9.refs_3_
  131.0 0.0 collective-permute-done.7.refs_1_
  131.0 0.0 collective-permute-done.10.refs_4_
  131.0 2.7 %place_blocks.3.refs_0_ = bf16[4,2,128,1024]{3,2,1,0:T(8,128)(2,1)} custom-call(s32[1]{0:T(128)} %bitcast.3.where_ref, bf16[2,128,1024]{2,1,0:T(8,128)(2,1)S(1)} %copy-done.3, bf16[2,128,1024]{2,1,0:T(8,128)(2,1)} %collective-permute-done.7.refs_1_, bf16[2,128,1024]{2,1,0:T(8,128)(2,1)S(1)} %collective-permute-done.8.refs_2_, ...), custom_call_target="tpu_custom_call" | custom-call | bytes 4194304 | tf_op jit(solution)/shard_map/place_blocks/pallas_call | solution.py:97
  133.7 6.5 %hr_and_gram.1 = (bf16[4096,256]{1,0:T(8,128)(2,1)S(1)}, f32[256,256]{1,0:T(8,128)}) custom-call(s32[1]{0:T(128)} %bitcast.where_ref, bf16[1024,4096]{1,0:T(8,128)(2,1)} %all-gather.2.cloned.1.call-done.cols_ref.refs_1_, bf16[8,128,256]{2,1,0:T(8,128)(2,1)S(1)} %pad_maximum_fusion.1.y_ref), custom_call_target="tpu_custom_call" | custom-call | flops 4294967296 | bytes 16777216 | tf_op jit(solution)/shard_map/hr_and_gram/pallas_call | solution.py:48
  140.2 10.5 %residual_product.2.refs_1_ = bf16[1024,256]{1,0:T(8,128)(2,1)S(1)} custom-call(bf16[2048,4096]{1,0:T(8,128)(2,1)} %weight_ref.3, s32[2048,4096]{1,0:T(8,128)} %codes_ref.3, f32[2048,32]{1,0:T(8,128)S(1)} %copy.10.scales_ref, bf16[4096,256]{1,0:T(8,128)(2,1)S(1)} %get-tuple-element.5.hr_ref), custom_call_target="tpu_custom_call" | custom-call | flops 4294967296 | bytes 33554432 | tf_op jit(solution)/shard_map/residual_product/pallas_call | solution.py:175
  150.7 10.5 %residual_product.3 = bf16[1024,256]{1,0:T(8,128)(2,1)S(1)} custom-call(bf16[2048,4096]{1,0:T(8,128)(2,1)} %weight_ref.3, s32[2048,4096]{1,0:T(8,128)} %codes_ref.3, f32[2048,32]{1,0:T(8,128)S(1)} %copy.10.scales_ref, bf16[4096,256]{1,0:T(8,128)(2,1)S(1)} %get-tuple-element.5.hr_ref, bf16[4,2,128,1024]{3,2,1,0:T(8,128)(2,1)} %place_blocks.3.refs_0_, ...), custom_call_target="tpu_custom_call" | custom-call | flops 4294967296 | bytes 33554432 | tf_op jit(solution)/shard_map/residual_product/pallas_call | solution.py:175
  161.2 3.7 %fusion.8 = (bf16[512,256]{1,0:T(8,128)(2,1)}, bf16[512,256]{1,0:T(8,128)(2,1)}, bf16[512,256]{1,0:T(8,128)(2,1)S(1)}, bf16[512,256]{1,0:T(8,128)(2,1)S(1)}) fusion(s32[]{:T(128)S(6)} %select_n.19, bf16[1024,256]{1,0:T(8,128)(2,1)S(1)} %residual_product.2.refs_1_, bf16[1024,256]{1,0:T(8,128)(2,1)S(1)} %residual_product.3, s32[]{:T(128)S(6)} %select_n.16, ...), kind=kLoop, calls=%fused_computation.16 | loop fusion | flops 2097152 | bytes 2097168 | tf_op jit(solution)/shard_map/concatenate | solution.py:314
  164.9 1.5 collective-permute-start.16
  166.4 0.0 collective-permute-start.14
  166.4 2.9 %collective-permute-start.15 = (bf16[512,256]{1,0:T(8,128)(2,1)S(1)}, bf16[512,256]{1,0:T(8,128)(2,1)S(1)}, u32[]{:S(2)}, u32[]{:S(2)}) collective-permute-start(bf16[512,256]{1,0:T(8,128)(2,1)S(1)} %get-tuple-element.12), channel_id=1, source_target_pairs={{0,2},{1,3},{2,0},{3,1},{4,6},{5,7},{6,4},{7,5},{8,10},{9,11},{10,... | collective-permute-start | bytes 786440 | tf_op jit(solution)/shard_map/ppermute | solution.py:18
  169.3 0.0 all-to-all-done.1
  169.3 4.6 %all-to-all-start = ((bf16[8,128,1024]{2,1,0:T(8,128)(2,1)}), bf16[8,128,1024]{2,1,0:T(8,128)(2,1)}, u32[]{:S(2)}, u32[]{:S(2)}) async-start(bf16[8,128,1024]{2,1,0:T(8,128)(2,1)} %bitcast.4), calls=%async_computation | async-start | bytes 4194304 | tf_op jit(solution)/shard_map/all_to_all | solution.py:304
  173.8 0.1 pad_maximum_fusion.refs_2_.refs_3_
  173.9 14.9 %hessian_rows.2.refs_2_ = bf16[2048,4096]{1,0:T(8,128)(2,1)} custom-call(bf16[1024,1024]{1,0:T(8,128)(2,1)} %bitcast.7.refs_0_, bf16[1024,4096]{1,0:T(8,128)(2,1)} %all-gather.2.cloned.1.call-done.cols_ref.refs_1_, bf16[2048,256]{1,0:T(8,128)(2,1)S(1)} %pad_maximum_fusion.refs_2_.refs_3_), custom_call_target="tpu_custom_call" | custom-call | flops 17179869184 | bytes 18874368 | tf_op jit(solution)/shard_map/hessian_rows/pallas_call | solution.py:222
  188.8 11.5 %all-to-all-done = bf16[8,128,1024]{2,1,0:T(8,128)(2,1)} async-done(((bf16[8,128,1024]{2,1,0:T(8,128)(2,1)}), bf16[8,128,1024]{2,1,0:T(8,128)(2,1)}, u32[]{:S(2)}, u32[]{:S(2)}) %all-to-all-start) | async-done | bytes 2097184 | tf_op jit(solution)/shard_map/all_to_all | solution.py:304
  200.3 14.8 %hessian_rows.3.refs_4_ = bf16[2048,4096]{1,0:T(8,128)(2,1)} custom-call(bf16[1024,1024]{1,0:T(8,128)(2,1)} %bitcast.5.refs_0_, bf16[1024,4096]{1,0:T(8,128)(2,1)} %all-gather.2.cloned.1.call-done.cols_ref.refs_1_, bf16[2048,4096]{1,0:T(8,128)(2,1)} %hessian_rows.2.refs_2_, ...), custom_call_target="tpu_custom_call", output_to_operand_aliasing={{}: (2, {})} | custom-call | flops 17179869184 | bytes 18874368 | tf_op jit(solution)/shard_map/hessian_rows/pallas_call | solution.py:222
  215.2 0.0 collective-permute-done.16.refs_3_
  215.2 0.0 collective-permute-done.14.refs_1_
  215.2 0.0 collective-permute-done.15.refs_2_
  215.2 0.7 copy-done.6
  215.9 0.1 copy-done.7
  216.0 0.1 copy-done.8
  216.1 2.1 add_pieces.1
  (15 shorter events, 0.1 us)
Async XLA Ops:
  7.2 6.8 %copy-start.4 = (bf16[128,4096]{1,0:T(8,128)(2,1)S(1)}, bf16[128,4096]{1,0:T(8,128)(2,1)}, u32[]{:S(2)}) copy-start(bf16[128,4096]{1,0:T(8,128)(2,1)} %activations_ref.3) | copy-start | bytes 3145732
  7.2 126.6 %all-gather.2.cloned.1.call-start = ((), (), s32[]{:S(2)}) async-start(), calls=%async_computation.2 | async-start | bytes 9437184 | tf_op jit(solution)/shard_map/all_gather | solution.py:275
  10.0 10.5 %copy-start = (bf16[2,128,1024]{2,1,0:T(8,128)(2,1)S(1)}, bf16[2,128,1024]{2,1,0:T(8,128)(2,1)}, u32[]{:S(2)}) copy-start(bf16[2,128,1024]{2,1,0:T(8,128)(2,1)} %take_chunk.2.refs_0_) | copy-start | bytes 1572868
  10.0 40.2 %collective-permute-start.6 = (bf16[2,128,1024]{2,1,0:T(8,128)(2,1)}, bf16[2,128,1024]{2,1,0:T(8,128)(2,1)S(1)}, u32[]{:S(2)}, u32[]{:S(2)}) collective-permute-start(bf16[2,128,1024]{2,1,0:T(8,128)(2,1)} %take_chunk.2.refs_0_), channel_id=1, source_target_pairs={{0,2},{1,3},{2,0},{3,1},{4,6},{5,7},{6,4},{7,5},{8,10},{9,11},{10,... | collective-permute-start | bytes 1572872 | tf_op jit(solution)/shard_map/ppermute | solution.py:141
  16.0 15.2 %collective-permute-start.2 = (f32[128,256]{1,0:T(8,128)S(1)}, f32[128,256]{1,0:T(8,128)S(1)}, u32[]{:S(2)}, u32[]{:S(2)}) collective-permute-start(f32[128,256]{1,0:T(8,128)S(1)} %fusion.2), channel_id=1, source_target_pairs={{0,3},{1,2},{2,1},{3,0},{4,7},{5,6},{6,5},{7,4},{8,11},{9,10},{10,... | collective-permute-start | bytes 393224 | tf_op jit(solution)/shard_map/ppermute | solution.py:18
  17.5 32.0 %collective-permute-start.1 = (f32[128,256]{1,0:T(8,128)S(1)}, f32[128,256]{1,0:T(8,128)S(1)}, u32[]{:S(2)}, u32[]{:S(2)}) collective-permute-start(f32[128,256]{1,0:T(8,128)S(1)} %fusion.2), channel_id=1, source_target_pairs={{0,2},{1,3},{2,0},{3,1},{4,6},{5,7},{6,4},{7,5},{8,10},{9,11},{10,... | collective-permute-start | bytes 393224 | tf_op jit(solution)/shard_map/ppermute | solution.py:18
  19.1 30.4 %collective-permute-start = (f32[128,256]{1,0:T(8,128)S(1)}, f32[128,256]{1,0:T(8,128)S(1)}, u32[]{:S(2)}, u32[]{:S(2)}) collective-permute-start(f32[128,256]{1,0:T(8,128)S(1)} %fusion.2), channel_id=1, source_target_pairs={{0,1},{1,0},{2,3},{3,2},{4,5},{5,4},{6,7},{7,6},{8,9},{9,8},{10,11... | collective-permute-start | bytes 393224 | tf_op jit(solution)/shard_map/ppermute | solution.py:18
  20.5 48.0 %collective-permute-start.12 = (bf16[2,128,1024]{2,1,0:T(8,128)(2,1)S(1)}, bf16[2,128,1024]{2,1,0:T(8,128)(2,1)S(1)}, u32[]{:S(2)}, u32[]{:S(2)}) collective-permute-start(bf16[2,128,1024]{2,1,0:T(8,128)(2,1)S(1)} %copy-done), channel_id=1, source_target_pairs={{1,2},{2,1},{5,6},{6,5},{9,10},{10,9},{13,14},{14,13},{17,18},{18,... | collective-permute-start | bytes 1572872 | tf_op jit(solution)/shard_map/ppermute | solution.py:141
  50.2 0.8 copy-start.1
  53.1 30.2 %collective-permute-start.8 = (bf16[2,128,1024]{2,1,0:T(8,128)(2,1)}, bf16[2,128,1024]{2,1,0:T(8,128)(2,1)S(1)}, u32[]{:S(2)}, u32[]{:S(2)}) collective-permute-start(bf16[2,128,1024]{2,1,0:T(8,128)(2,1)} %take_chunk.3.refs_0_), channel_id=1, source_target_pairs={{0,2},{1,3},{2,0},{3,1},{4,6},{5,7},{6,4},{7,5},{8,10},{9,11},{10,... | collective-permute-start | bytes 1572872 | tf_op jit(solution)/shard_map/ppermute | solution.py:141
  53.1 31.5 %collective-permute-start.11 = (bf16[2,128,1024]{2,1,0:T(8,128)(2,1)S(1)}, bf16[2,128,1024]{2,1,0:T(8,128)(2,1)S(1)}, u32[]{:S(2)}, u32[]{:S(2)}) collective-permute-start(bf16[2,128,1024]{2,1,0:T(8,128)(2,1)S(1)} %copy-done), channel_id=1, source_target_pairs={{0,1},{1,0},{2,3},{3,2},{4,5},{5,4},{6,7},{7,6},{8,9},{9,8},{10,11... | collective-permute-start | bytes 1572872 | tf_op jit(solution)/shard_map/ppermute | solution.py:141
  56.4 35.2 %collective-permute-start.13 = (bf16[2,128,1024]{2,1,0:T(8,128)(2,1)}, bf16[2,128,1024]{2,1,0:T(8,128)(2,1)S(1)}, u32[]{:S(2)}, u32[]{:S(2)}) collective-permute-start(bf16[2,128,1024]{2,1,0:T(8,128)(2,1)} %copy-done.1), channel_id=1, source_target_pairs={{2,3},{1,0},{6,7},{5,4},{10,11},{9,8},{14,15},{13,12},{18,19},{17,... | collective-permute-start | bytes 1572872 | tf_op jit(solution)/shard_map/ppermute | solution.py:150
  57.7 1.3 collective-permute-start.3
  59.0 8.8 %collective-permute-start.4 = (bf16[2,128,256]{2,1,0:T(8,128)(2,1)S(1)}, bf16[2,128,256]{2,1,0:T(8,128)(2,1)S(1)}, u32[]{:S(2)}, u32[]{:S(2)}) collective-permute-start(bf16[2,128,256]{2,1,0:T(8,128)(2,1)S(1)} %pad_maximum_fusion.3), channel_id=1, source_target_pairs={{0,8},{4,12},{8,0},{12,4},{16,24},{20,28},{24,16},{28,20},{1,9},{5... | collective-permute-start | bytes 393224 | tf_op jit(solution)/shard_map/ppermute | solution.py:18
  67.8 23.9 %copy-start.5 = (bf16[2,128,256]{2,1,0:T(8,128)(2,1)}, bf16[2,128,256]{2,1,0:T(8,128)(2,1)S(1)}, u32[]{:S(2)}) copy-start(bf16[2,128,256]{2,1,0:T(8,128)(2,1)S(1)} %collective-permute-done.4) | copy-start | bytes 393220
  67.8 63.2 %collective-permute-start.9 = (bf16[2,128,1024]{2,1,0:T(8,128)(2,1)}, bf16[2,128,1024]{2,1,0:T(8,128)(2,1)S(1)}, u32[]{:S(2)}, u32[]{:S(2)}) collective-permute-start(bf16[2,128,1024]{2,1,0:T(8,128)(2,1)} %take_chunk.3.refs_0_), channel_id=1, source_target_pairs={{1,2},{2,1},{5,6},{6,5},{9,10},{10,9},{13,14},{14,13},{17,18},{18,... | collective-permute-start | bytes 1572872 | tf_op jit(solution)/shard_map/ppermute | solution.py:141
  68.5 62.5 %collective-permute-start.7 = (bf16[2,128,1024]{2,1,0:T(8,128)(2,1)}, bf16[2,128,1024]{2,1,0:T(8,128)(2,1)}, u32[]{:S(2)}, u32[]{:S(2)}) collective-permute-start(bf16[2,128,1024]{2,1,0:T(8,128)(2,1)} %take_chunk.3.refs_0_), channel_id=1, source_target_pairs={{0,1},{1,0},{2,3},{3,2},{4,5},{5,4},{6,7},{7,6},{8,9},{9,8},{10,11... | collective-permute-start | bytes 1572872 | tf_op jit(solution)/shard_map/ppermute | solution.py:141
  83.3 47.8 %collective-permute-start.10 = (bf16[2,128,1024]{2,1,0:T(8,128)(2,1)S(1)}, bf16[2,128,1024]{2,1,0:T(8,128)(2,1)}, u32[]{:S(2)}, u32[]{:S(2)}) collective-permute-start(bf16[2,128,1024]{2,1,0:T(8,128)(2,1)S(1)} %collective-permute-done.8.refs_2_), channel_id=1, source_target_pairs={{2,3},{1,0},{6,7},{5,4},{10,11},{9,8},{14,15},{13,12},{18,19},{17,... | collective-permute-start | bytes 1572872 | tf_op jit(solution)/shard_map/ppermute | solution.py:150
  91.6 1.0 copy-start.2
  94.1 6.4 %copy-start.9 = (f32[2048,32]{0,1:T(8,128)S(1)}, f32[2048,32]{0,1:T(8,128)}, u32[]{:S(2)}) copy-start(f32[2048,32]{0,1:T(8,128)} %param.8) | copy-start | bytes 786436
  94.1 75.2 %all-to-all-start.1 = ((bf16[8,128,1024]{2,1,0:T(8,128)(2,1)}), bf16[8,128,1024]{2,1,0:T(8,128)(2,1)}, u32[]{:S(2)}, u32[]{:S(2)}) async-start(bf16[8,128,1024]{2,1,0:T(8,128)(2,1)} %bitcast.6), calls=%async_computation.1 | async-start | bytes 4194304 | tf_op jit(solution)/shard_map/all_to_all | solution.py:304
  98.6 32.4 %copy-start.3 = (bf16[2,128,1024]{2,1,0:T(8,128)(2,1)S(1)}, bf16[2,128,1024]{2,1,0:T(8,128)(2,1)}, u32[]{:S(2)}) copy-start(bf16[2,128,1024]{2,1,0:T(8,128)(2,1)} %take_chunk.3.refs_0_) | copy-start | bytes 1572868
  98.7 31.3 %collective-permute-start.5 = (bf16[4,128,256]{2,1,0:T(8,128)(2,1)S(1)}, bf16[4,128,256]{2,1,0:T(8,128)(2,1)}, u32[]{:S(2)}, u32[]{:S(2)}) collective-permute-start(bf16[4,128,256]{2,1,0:T(8,128)(2,1)S(1)} %pad_maximum_fusion.2.refs_5_), channel_id=1, source_target_pairs={{0,16},{4,20},{8,24},{12,28},{16,0},{20,4},{24,8},{28,12},{1,17},{... | collective-permute-start | bytes 786440 | tf_op jit(solution)/shard_map/ppermute | solution.py:18
  164.9 50.3 %collective-permute-start.16 = (bf16[512,256]{1,0:T(8,128)(2,1)}, bf16[512,256]{1,0:T(8,128)(2,1)S(1)}, u32[]{:S(2)}, u32[]{:S(2)}) collective-permute-start(bf16[512,256]{1,0:T(8,128)(2,1)} %get-tuple-element.9), channel_id=1, source_target_pairs={{0,3},{1,2},{2,1},{3,0},{4,7},{5,6},{6,5},{7,4},{8,11},{9,10},{10,... | collective-permute-start | bytes 786440 | tf_op jit(solution)/shard_map/ppermute | solution.py:18
  166.4 48.8 %collective-permute-start.14 = (bf16[512,256]{1,0:T(8,128)(2,1)S(1)}, bf16[512,256]{1,0:T(8,128)(2,1)S(1)}, u32[]{:S(2)}, u32[]{:S(2)}) collective-permute-start(bf16[512,256]{1,0:T(8,128)(2,1)S(1)} %get-tuple-element.11), channel_id=1, source_target_pairs={{0,1},{1,0},{2,3},{3,2},{4,5},{5,4},{6,7},{7,6},{8,9},{9,8},{10,11... | collective-permute-start | bytes 786440 | tf_op jit(solution)/shard_map/ppermute | solution.py:18
  166.4 48.8 %collective-permute-start.15 = (bf16[512,256]{1,0:T(8,128)(2,1)S(1)}, bf16[512,256]{1,0:T(8,128)(2,1)S(1)}, u32[]{:S(2)}, u32[]{:S(2)}) collective-permute-start(bf16[512,256]{1,0:T(8,128)(2,1)S(1)} %get-tuple-element.12), channel_id=1, source_target_pairs={{0,2},{1,3},{2,0},{3,1},{4,6},{5,7},{6,4},{7,5},{8,10},{9,11},{10,... | collective-permute-start | bytes 786440 | tf_op jit(solution)/shard_map/ppermute | solution.py:18
  169.3 31.0 %all-to-all-start = ((bf16[8,128,1024]{2,1,0:T(8,128)(2,1)}), bf16[8,128,1024]{2,1,0:T(8,128)(2,1)}, u32[]{:S(2)}, u32[]{:S(2)}) async-start(bf16[8,128,1024]{2,1,0:T(8,128)(2,1)} %bitcast.4), calls=%async_computation | async-start | bytes 4194304 | tf_op jit(solution)/shard_map/all_to_all | solution.py:304
  215.2 0.7 copy-start.6
  215.2 0.8 copy-start.7
  215.2 0.9 copy-start.8
Sparse Core Ops, SparseCore 0:
  9.9 59.5 all-gather.1

commit v8 on v7

--- a/solution.py
+++ b/solution.py
@@ -166,15 +166,20 @@
     out_ref[...] = jnp.dot(residual, hr_ref[...], preferred_element_type=F32).astype(BF16)
 
 
-def residual_partial(weight, codes, scales, hr, part, count, after):
-    rows, features = weight.shape
+def residual_partial(weight, codes, scales, hr, earlier, part, count, after):
+    features = weight.shape[1]
     rank = hr.shape[1]
-    rows //= count
+    rows = weight.shape[0] // count
     block = min(256, rows)
     first = part * (rows // block)
+    ins = [weight, codes, scales, hr]
+    aliases = {}
+    if earlier is not None:
+        aliases = {len(ins): 0}
+        ins.append(earlier)
     return pl.pallas_call(
         residual_kernel,
-        out_shape=jax.ShapeDtypeStruct((rows, rank), BF16),
+        out_shape=jax.ShapeDtypeStruct((weight.shape[0], rank), BF16),
         grid=(rows // block,),
         in_specs=[
             pl.BlockSpec((block, features), lambda i: (first + i, 0)),
@@ -182,18 +187,20 @@
             pl.BlockSpec((block, scales.shape[1]), lambda i: (first + i, 0)),
             pl.BlockSpec((features, rank), lambda i: (0, 0)),
         ]
+        + [pl.BlockSpec(memory_space=pl.ANY)] * len(aliases)
         + [first_tile(value) for value in after],
-        out_specs=pl.BlockSpec((block, rank), lambda i: (i, 0)),
+        out_specs=pl.BlockSpec((block, rank), lambda i: (first + i, 0)),
+        input_output_aliases=aliases,
         cost_estimate=cost(4 * rows * features * rank, 8 * rows * features),
         compiler_params=pltpu.CompilerParams(vmem_limit_bytes=48 * MIB),
         name="residual_product",
-    )(weight, codes, scales, hr, *after)
+    )(*ins, *after)
 
 
 def hessian_rows(row_chunks, cols, earlier, index, shape, scale, after):
     tokens, height = row_chunks[0].shape
     block = height * len(row_chunks)
-    tile = min(512, cols.shape[1])
+    tile = min(1024, cols.shape[1])
     count = len(row_chunks)
     ins = [*row_chunks, cols]
     specs = [pl.BlockSpec((tokens, height), lambda j: (0, 0))] * count
@@ -275,29 +282,27 @@
     cols = lax.all_gather(activations, "wide", axis=0, tiled=True)
 
     right_block = lax.dynamic_slice_in_dim(right_factor, narrow_index * features, features, 0)
-    product = jnp.dot(activations, right_block, preferred_element_type=F32)
-    product = pair_sum([product] + [flip(product, "narrow", m) for m in range(1, narrow_count)])
-    steps = [product]
+    own = jnp.dot(activations, right_block, preferred_element_type=F32)
+    product = pair_sum([own] + [flip(own, "narrow", m) for m in range(1, narrow_count)])
     y_blocks = product.astype(BF16)[None]
     mask = 1
     while mask < wide_count:
         y_blocks = jnp.concatenate([y_blocks, flip(y_blocks, "wide", mask)], axis=0)
-        steps.append(y_blocks)
         mask *= 2
 
     height = rows // CHUNKS
     chunks = []
-    after = []
+    after = [own]
     for chunk in range(CHUNKS):
         chunks.append(exchange_blocks(take_chunk(activations, chunk, height, split, after)))
-        after = [steps[0], chunks[-1][0][-1 if narrow_count < 4 else narrow_count // 2]]
+        after = [chunks[-1][0][near] for near, _ in chunks[-1][1] if near]
 
     where = narrow_index.reshape(1)
     row_chunks = []
     placed = []
     for chunk in range(CHUNKS):
         blocks, sources = chunks[chunk]
-        after = placed[-1:] if chunk else steps[-2:-1]
+        after = placed[-1:] if chunk else [y_blocks]
         every = place_blocks(blocks, sources, where, after)
         placed.append(every)
         every = every.reshape(narrow_count * split, tokens, height)
@@ -305,13 +310,12 @@
         row_chunks.append(chunk_rows.reshape(tokens * wide_count, height))
 
     hr, gram = hr_and_gram(cols, y_blocks, wide_index.reshape(1), scale)
-    partial = []
+    partial = None
     for part in range(2):
-        after = [placed[-1], partial[0]] if part else []
-        partial.append(
-            residual_partial(weight_tile, codes, group_scales, hr, part, 2, after)
+        after = placed[-1:] if part else []
+        partial = residual_partial(
+            weight_tile, codes, group_scales, hr, partial, part, 2, after
         )
-    partial = jnp.concatenate(partial, axis=0)
     share = rows // narrow_count
     received = []
     for m in range(narrow_count):

time: 226 us -> 194 us (0.86)
  waiting for transfers between devices: 95.6 us -> 64.6 us
  local copies, waits for them, and re-layouts: 3.05 us -> 10.6 us
  other arithmetic: 5.51 us -> 1.98 us
  Pallas kernels: 67.6 us -> 65 us
  starting transfers between devices: 36.9 us -> 34.6 us
    ppermute x9, waiting for transfers between devices: 65.8 us -> 18.7 us  [flip(): return lax.ppermute(value, axis, [(i, i ^ mask) for i in range(count)])]
    ppermute x6, waiting for transfers between devices: 10.6 us -> 29.3 us  [exchange_blocks(): direct[mask] = lax.ppermute(mine, 'narrow', pairs) if pairs else None]
    all_to_all x2, waiting for transfers between devices: 11.5 us -> 0.01 us  [body(): lax.all_to_all(every, 'wide', split_axis=0, concat_axis=0, tiled=True)]
    ppermute x2, waiting for transfers between devices: 7.03 us -> 15.9 us  [exchange_blocks(): blocks.append(lax.ppermute(direct[half], 'narrow', pairs))]
    unnamed x21 -> x31, local copies, waits for them, and re-layouts: 3.05 us -> 9.85 us
    concatenate x2 -> x0, other arithmetic: 3.74 us -> none  [body(): partial = jnp.concatenate(partial, axis=0)]
    ppermute x6, starting transfers between devices: 12.9 us -> 10 us  [exchange_blocks(): direct[mask] = lax.ppermute(mine, 'narrow', pairs) if pairs else None]
    pallas_call x2, Pallas kernels: 29.7 us -> 27.2 us  [hessian_rows(): pl.pallas_call(kernel, out_shape=jax.ShapeDtypeStruct(shape, BF16), grid=...]
  transfers between devices with their start and end apart: 20 -> 20, of which waited for: 8 -> 8; matrix products, arithmetic and copies ran while one was open for 4% -> 3% of each run, Pallas kernels for 29% -> 32%
where the time goes in v8:
time: 194 us
  Pallas kernels  65 us (34%)
  waiting for transfers between devices  64.6 us (33%)
  starting transfers between devices  34.6 us (18%)
  between operations  14.3 us (7%)
  local copies, waits for them, and re-layouts  10.6 us (5%)
  matrix products  2.37 us (1%)
  other arithmetic  1.98 us (1%)
    ppermute x6, waiting for transfers between devices, exchange_blocks(): direct[mask] = lax.ppermute(mine, 'narrow', pairs) if pairs else None  29.3 us
    pallas_call x2, Pallas kernels, hessian_rows(): pl.pallas_call(kernel, out_shape=jax.ShapeDtypeStruct(shape, BF16), grid=...  27.2 us
    pallas_call x2, Pallas kernels, residual_partial(): pl.pallas_call(residual_kernel, out_shape=jax.ShapeDtypeStruct((weight.sh...  20.9 us
    ppermute x9, waiting for transfers between devices, flip(): return lax.ppermute(value, axis, [(i, i ^ mask) for i in range(count)])  18.7 us
    ppermute x2, waiting for transfers between devices, exchange_blocks(): blocks.append(lax.ppermute(direct[half], 'narrow', pairs))  15.9 us
    ppermute x9, starting transfers between devices, flip(): return lax.ppermute(value, axis, [(i, i ^ mask) for i in range(count)])  13.3 us
    ppermute x6, starting transfers between devices, exchange_blocks(): direct[mask] = lax.ppermute(mine, 'narrow', pairs) if pairs else None  10 us
    unnamed x31, local copies, waits for them, and re-layouts  9.85 us
  transfers between devices with their start and end apart: 20, of which 8 were waited for; matrix products, arithmetic and copies ran while one was open for 3% of the time, Pallas kernels for 32%

profile of v8, /device:TPU:0, one launch (start us, length us, event | category | flops | bytes accessed | tf_op | source)
XLA Modules:
  0.0 193.6 jit_solution(14331018073605266805)
XLA Ops:
  7.2 0.0 all-gather.2.cloned.1.call-start
  7.2 0.7 all-gather.2.cloned.1.call-update
  7.9 2.4 %fusion.2.refs_0_ = f32[128,256]{1,0:T(8,128)S(1)} fusion(bf16[128,4096]{1,0:T(8,128)(2,1)} %activations_ref.3, bf16[16384,256]{1,0:T(8,128)(2,1)} %param.9, s32[]{:T(128)S(6)} %select_n.15), kind=kOutput, calls=%fused_computation.2 | convolution fusion | flops 268435456 | bytes 3276804 | tf_op jit(solution)/shard_map/dot_general | solution.py:285
  10.3 0.0 copy-start.10
  10.3 0.0 copy-start.14
  10.3 3.1 %collective-permute-start = (f32[128,256]{1,0:T(8,128)S(1)}, f32[128,256]{1,0:T(8,128)S(1)}, u32[]{:S(2)}, u32[]{:S(2)}) collective-permute-start(f32[128,256]{1,0:T(8,128)S(1)} %fusion.2.refs_0_), channel_id=1, source_target_pairs={{0,1},{1,0},{2,3},{3,2},{4,5},{5,4},{6,7},{7,6},{8,9},{9,8},{10,11... | collective-permute-start | bytes 393224 | tf_op jit(solution)/shard_map/ppermute | solution.py:18
  13.4 2.6 %collective-permute-start.1 = (f32[128,256]{1,0:T(8,128)S(1)}, f32[128,256]{1,0:T(8,128)S(1)}, u32[]{:S(2)}, u32[]{:S(2)}) collective-permute-start(f32[128,256]{1,0:T(8,128)S(1)} %fusion.2.refs_0_), channel_id=1, source_target_pairs={{0,2},{1,3},{2,0},{3,1},{4,6},{5,7},{6,4},{7,5},{8,10},{9,11},{10,... | collective-permute-start | bytes 393224 | tf_op jit(solution)/shard_map/ppermute | solution.py:18
  16.0 0.0 collective-permute-start.2
  16.0 2.1 %take_chunk.2.refs_0_ = bf16[2,128,1024]{2,1,0:T(8,128)(2,1)} custom-call(bf16[128,4096]{1,0:T(8,128)(2,1)} %activations_ref.3, f32[128,256]{1,0:T(8,128)} %copy-done.10), custom_call_target="tpu_custom_call" | custom-call | bytes 1048576 | tf_op jit(solution)/shard_map/take_chunk/pallas_call | solution.py:120
  18.0 1.9 collective-permute-start.7
  19.9 0.0 collective-permute-done
  20.0 17.6 %collective-permute-done.1 = f32[128,256]{1,0:T(8,128)S(1)} collective-permute-done((f32[128,256]{1,0:T(8,128)S(1)}, f32[128,256]{1,0:T(8,128)S(1)}, u32[]{:S(2)}, u32[]{:S(2)}) %collective-permute-start.1) | collective-permute-done | bytes 131104 | tf_op jit(solution)/shard_map/ppermute | solution.py:18
  37.6 0.0 collective-permute-done.2
  37.6 0.9 fusion.5
  38.5 0.1 collective-permute-start.3
  38.6 3.4 %collective-permute-start.6 = (bf16[2,128,1024]{2,1,0:T(8,128)(2,1)}, bf16[2,128,1024]{2,1,0:T(8,128)(2,1)S(1)}, u32[]{:S(2)}, u32[]{:S(2)}) collective-permute-start(bf16[2,128,1024]{2,1,0:T(8,128)(2,1)} %take_chunk.2.refs_0_), channel_id=1, source_target_pairs={{0,1},{1,0},{2,3},{3,2},{4,5},{5,4},{6,7},{7,6},{8,9},{9,8},{10,11... | collective-permute-start | bytes 1572872 | tf_op jit(solution)/shard_map/ppermute | solution.py:141
  42.0 0.7 collective-permute-start.8
  42.7 0.0 collective-permute-done.3
  42.7 1.6 collective-permute-start.4
  44.3 7.4 %collective-permute-done.7.refs_1_.refs_2_ = bf16[2,128,1024]{2,1,0:T(8,128)(2,1)S(1)} collective-permute-done((bf16[2,128,1024]{2,1,0:T(8,128)(2,1)}, bf16[2,128,1024]{2,1,0:T(8,128)(2,1)S(1)}, u32[]{:S(2)}, u32[]{:S(2)}) %collective-permute-start.7) | collective-permute-done | bytes 524320 | tf_op jit(solution)/shard_map/ppermute | solution.py:141
  51.7 1.3 collective-permute-start.13
  53.0 1.6 collective-permute-start.5
  54.6 6.9 %collective-permute-done.6.refs_0_.refs_1_ = bf16[2,128,1024]{2,1,0:T(8,128)(2,1)S(1)} collective-permute-done((bf16[2,128,1024]{2,1,0:T(8,128)(2,1)}, bf16[2,128,1024]{2,1,0:T(8,128)(2,1)S(1)}, u32[]{:S(2)}, u32[]{:S(2)}) %collective-permute-start.6) | collective-permute-done | bytes 524320 | tf_op jit(solution)/shard_map/ppermute | solution.py:141
  61.5 0.8 copy-done.6
  62.2 0.8 copy-done.8
  63.0 2.1 %take_chunk.3.refs_0_ = bf16[2,128,1024]{2,1,0:T(8,128)(2,1)} custom-call(bf16[128,4096]{1,0:T(8,128)(2,1)} %activations_ref.3, bf16[2,128,1024]{2,1,0:T(8,128)(2,1)} %copy-done.6, bf16[2,128,1024]{2,1,0:T(8,128)(2,1)} %copy-done.4, bf16[2,128,1024]{2,1,0:T(8,128)(2,1)} %copy-done.8), custom_call_target="tpu_custom_call" | custom-call | bytes 1048576 | tf_op jit(solution)/shard_map/take_chunk/pallas_call | solution.py:120
  65.1 0.8 collective-permute-start.10
  65.9 1.0 collective-permute-done.5
  67.0 1.0 pad_maximum_fusion.y_ref.refs_5_
  68.0 4.8 %collective-permute-done.13.refs_4_ = bf16[2,128,1024]{2,1,0:T(8,128)(2,1)S(1)} collective-permute-done((bf16[2,128,1024]{2,1,0:T(8,128)(2,1)S(1)}, bf16[2,128,1024]{2,1,0:T(8,128)(2,1)S(1)}, u32[]{:S(2)}, u32[]{:S(2)}) %collective-permute-start.13) | collective-permute-done | bytes 524320 | tf_op jit(solution)/shard_map/ppermute | solution.py:150
  72.8 1.0 copy-done.2
  73.8 1.0 copy-done.5
  74.8 1.0 copy-done.7
  75.9 1.0 copy-done.9
  76.9 1.5 place_blocks.2.refs_5_
  78.4 4.4 %all-to-all-start.1 = ((bf16[8,128,1024]{2,1,0:T(8,128)(2,1)}), bf16[8,128,1024]{2,1,0:T(8,128)(2,1)}, u32[]{:S(2)}, u32[]{:S(2)}) async-start(bf16[8,128,1024]{2,1,0:T(8,128)(2,1)} %bitcast.6), calls=%async_computation.1 | async-start | bytes 4194304 | tf_op jit(solution)/shard_map/all_to_all | solution.py:309
  82.8 0.7 collective-permute-start.11
  83.6 2.5 %collective-permute-start.9 = (bf16[2,128,1024]{2,1,0:T(8,128)(2,1)S(1)}, bf16[2,128,1024]{2,1,0:T(8,128)(2,1)}, u32[]{:S(2)}, u32[]{:S(2)}) collective-permute-start(bf16[2,128,1024]{2,1,0:T(8,128)(2,1)S(1)} %copy-done.3), channel_id=1, source_target_pairs={{0,1},{1,0},{2,3},{3,2},{4,5},{5,4},{6,7},{7,6},{8,9},{9,8},{10,11... | collective-permute-start | bytes 1572872 | tf_op jit(solution)/shard_map/ppermute | solution.py:141
  86.0 5.5 %collective-permute-done.10.refs_2_ = bf16[2,128,1024]{2,1,0:T(8,128)(2,1)S(1)} collective-permute-done((bf16[2,128,1024]{2,1,0:T(8,128)(2,1)}, bf16[2,128,1024]{2,1,0:T(8,128)(2,1)S(1)}, u32[]{:S(2)}, u32[]{:S(2)}) %collective-permute-start.10) | collective-permute-done | bytes 524320 | tf_op jit(solution)/shard_map/ppermute | solution.py:141
  91.5 1.3 collective-permute-start.12
  92.8 0.3 copy.12.scales_ref
  93.2 9.6 %collective-permute-done.9.refs_1_ = bf16[2,128,1024]{2,1,0:T(8,128)(2,1)} collective-permute-done((bf16[2,128,1024]{2,1,0:T(8,128)(2,1)S(1)}, bf16[2,128,1024]{2,1,0:T(8,128)(2,1)}, u32[]{:S(2)}, u32[]{:S(2)}) %collective-permute-start.9) | collective-permute-done | bytes 524320 | tf_op jit(solution)/shard_map/ppermute | solution.py:141
  102.8 11.2 %collective-permute-done.12.refs_4_ = bf16[2,128,1024]{2,1,0:T(8,128)(2,1)} collective-permute-done((bf16[2,128,1024]{2,1,0:T(8,128)(2,1)S(1)}, bf16[2,128,1024]{2,1,0:T(8,128)(2,1)}, u32[]{:S(2)}, u32[]{:S(2)}) %collective-permute-start.12) | collective-permute-done | bytes 524320 | tf_op jit(solution)/shard_map/ppermute | solution.py:150
  114.0 2.7 %place_blocks.3.refs_1_ = bf16[4,2,128,1024]{3,2,1,0:T(8,128)(2,1)} custom-call(s32[1]{0:T(128)} %bitcast.3.where_ref, bf16[2,128,1024]{2,1,0:T(8,128)(2,1)S(1)} %copy-done.3, bf16[2,128,1024]{2,1,0:T(8,128)(2,1)} %collective-permute-done.9.refs_1_, bf16[2,128,1024]{2,1,0:T(8,128)(2,1)S(1)} %collective-permute-done.10.refs_2_, ...), custom_call_target="tpu_custom_call" | custom-call | bytes 4194304 | tf_op jit(solution)/shard_map/place_blocks/pallas_call | solution.py:97
  116.6 6.5 %hr_and_gram.1 = (bf16[4096,256]{1,0:T(8,128)(2,1)S(1)}, f32[256,256]{1,0:T(8,128)}) custom-call(s32[1]{0:T(128)} %bitcast.where_ref, bf16[1024,4096]{1,0:T(8,128)(2,1)} %all-gather.2.cloned.1.call-done.cols_ref.refs_1_, bf16[8,128,256]{2,1,0:T(8,128)(2,1)S(1)} %pad_maximum_fusion.y_ref.refs_5_), custom_call_target="tpu_custom_call" | custom-call | flops 4294967296 | bytes 16777216 | tf_op jit(solution)/shard_map/hr_and_gram/pallas_call | solution.py:48
  123.1 10.5 %residual_product.2.refs_0_ = bf16[2048,256]{1,0:T(8,128)(2,1)S(1)} custom-call(bf16[2048,4096]{1,0:T(8,128)(2,1)} %weight_ref.3, s32[2048,4096]{1,0:T(8,128)} %codes_ref.3, f32[2048,32]{1,0:T(8,128)S(1)} %copy.12.scales_ref, bf16[4096,256]{1,0:T(8,128)(2,1)S(1)} %get-tuple-element.5.hr_ref), custom_call_target="tpu_custom_call" | custom-call | flops 4294967296 | bytes 33554432 | tf_op jit(solution)/shard_map/residual_product/pallas_call | solution.py:180
  133.6 0.0 copy-start
  133.6 1.3 copy-done
  134.9 4.4 %all-to-all-start = ((bf16[8,128,1024]{2,1,0:T(8,128)(2,1)}), bf16[8,128,1024]{2,1,0:T(8,128)(2,1)}, u32[]{:S(2)}, u32[]{:S(2)}) async-start(bf16[8,128,1024]{2,1,0:T(8,128)(2,1)} %bitcast.4), calls=%async_computation | async-start | bytes 4194304 | tf_op jit(solution)/shard_map/all_to_all | solution.py:309
  139.3 0.0 copy-start.1
  139.3 1.6 copy-done.1
  140.9 10.5 %residual_product.3.refs_2_.refs_3_ = bf16[2048,256]{1,0:T(8,128)(2,1)S(1)} custom-call(bf16[2048,4096]{1,0:T(8,128)(2,1)} %weight_ref.3, s32[2048,4096]{1,0:T(8,128)} %codes_ref.3, f32[2048,32]{1,0:T(8,128)S(1)} %copy.12.scales_ref, bf16[4096,256]{1,0:T(8,128)(2,1)S(1)} %copy-done.1, ...), custom_call_target="tpu_custom_call", output_to_operand_aliasing={{}: (4, {})} | custom-call | flops 4294967296 | bytes 33554432 | tf_op jit(solution)/shard_map/residual_product/pallas_call | solution.py:180
  151.3 0.8 constant_dynamic-slice_fusion
  152.1 0.0 collective-permute-start.14
  152.1 2.1 %collective-permute-start.15 = (bf16[512,256]{1,0:T(8,128)(2,1)S(1)}, bf16[512,256]{1,0:T(8,128)(2,1)S(1)}, u32[]{:S(2)}, u32[]{:S(2)}) collective-permute-start(bf16[512,256]{1,0:T(8,128)(2,1)S(1)} %get-tuple-element.8), channel_id=1, source_target_pairs={{0,2},{1,3},{2,0},{3,1},{4,6},{5,7},{6,4},{7,5},{8,10},{9,11},{10,... | collective-permute-start | bytes 786440 | tf_op jit(solution)/shard_map/ppermute | solution.py:18
  154.3 2.3 %collective-permute-start.16 = (bf16[512,256]{1,0:T(8,128)(2,1)S(1)}, bf16[512,256]{1,0:T(8,128)(2,1)S(1)}, u32[]{:S(2)}, u32[]{:S(2)}) collective-permute-start(bf16[512,256]{1,0:T(8,128)(2,1)S(1)} %get-tuple-element.7), channel_id=1, source_target_pairs={{0,3},{1,2},{2,1},{3,0},{4,7},{5,6},{6,5},{7,4},{8,11},{9,10},{10,... | collective-permute-start | bytes 786440 | tf_op jit(solution)/shard_map/ppermute | solution.py:18
  156.5 13.6 %hessian_rows.2.refs_2_ = bf16[2048,4096]{1,0:T(8,128)(2,1)} custom-call(bf16[1024,1024]{1,0:T(8,128)(2,1)} %bitcast.7.refs_0_, bf16[1024,4096]{1,0:T(8,128)(2,1)} %all-gather.2.cloned.1.call-done.cols_ref.refs_1_, bf16[2048,256]{1,0:T(8,128)(2,1)S(1)} %residual_product.3.refs_2_.refs_3_), custom_call_target="tpu_custom_call" | custom-call | flops 17179869184 | bytes 18874368 | tf_op jit(solution)/shard_map/hessian_rows/pallas_call | solution.py:229
  170.1 13.6 %hessian_rows.3.refs_4_ = bf16[2048,4096]{1,0:T(8,128)(2,1)} custom-call(bf16[1024,1024]{1,0:T(8,128)(2,1)} %bitcast.5.refs_0_, bf16[1024,4096]{1,0:T(8,128)(2,1)} %all-gather.2.cloned.1.call-done.cols_ref.refs_1_, bf16[2048,4096]{1,0:T(8,128)(2,1)} %hessian_rows.2.refs_2_, ...), custom_call_target="tpu_custom_call", output_to_operand_aliasing={{}: (2, {})} | custom-call | flops 17179869184 | bytes 18874368 | tf_op jit(solution)/shard_map/hessian_rows/pallas_call | solution.py:229
  183.7 0.0 collective-permute-done.14.refs_1_
  183.7 0.0 collective-permute-done.16.refs_3_
  183.8 0.7 copy-done.11
  184.4 0.1 copy-done.12
  184.5 0.1 copy-done.13
  184.6 2.1 %add_pieces.1 = f32[512,256]{1,0:T(8,128)} custom-call(bf16[512,256]{1,0:T(8,128)(2,1)} %get-tuple-element.10.refs_0_, bf16[512,256]{1,0:T(8,128)(2,1)} %copy-done.11, bf16[512,256]{1,0:T(8,128)(2,1)} %copy-done.12, bf16[512,256]{1,0:T(8,128)(2,1)} %copy-done.13, bf16[2048,4096]{1,0:T(8,128)(2,1)} %hessian_rows.3.refs_4_), custom_call_target="tpu_custom_call" | custom-call | bytes 1572864 | tf_op jit(solution)/shard_map/add_pieces/pallas_call | solution.py:254
  (24 shorter events, 0.1 us)
Async XLA Ops:
  7.2 109.5 %all-gather.2.cloned.1.call-start = ((), (), s32[]{:S(2)}) async-start(), calls=%async_computation.2 | async-start | bytes 9437184 | tf_op jit(solution)/shard_map/all_gather | solution.py:282
  10.3 5.7 %copy-start.10 = (f32[128,256]{1,0:T(8,128)}, f32[128,256]{1,0:T(8,128)S(1)}, u32[]{:S(2)}) copy-start(f32[128,256]{1,0:T(8,128)S(1)} %fusion.2.refs_0_) | copy-start | bytes 393220
  10.3 82.5 %copy-start.14 = (f32[2048,32]{0,1:T(8,128)S(1)}, f32[2048,32]{0,1:T(8,128)}, u32[]{:S(2)}) copy-start(f32[2048,32]{0,1:T(8,128)} %param.8) | copy-start | bytes 786436
  10.3 9.6 %collective-permute-start = (f32[128,256]{1,0:T(8,128)S(1)}, f32[128,256]{1,0:T(8,128)S(1)}, u32[]{:S(2)}, u32[]{:S(2)}) collective-permute-start(f32[128,256]{1,0:T(8,128)S(1)} %fusion.2.refs_0_), channel_id=1, source_target_pairs={{0,1},{1,0},{2,3},{3,2},{4,5},{5,4},{6,7},{7,6},{8,9},{9,8},{10,11... | collective-permute-start | bytes 393224 | tf_op jit(solution)/shard_map/ppermute | solution.py:18
  13.4 24.2 %collective-permute-start.1 = (f32[128,256]{1,0:T(8,128)S(1)}, f32[128,256]{1,0:T(8,128)S(1)}, u32[]{:S(2)}, u32[]{:S(2)}) collective-permute-start(f32[128,256]{1,0:T(8,128)S(1)} %fusion.2.refs_0_), channel_id=1, source_target_pairs={{0,2},{1,3},{2,0},{3,1},{4,6},{5,7},{6,4},{7,5},{8,10},{9,11},{10,... | collective-permute-start | bytes 393224 | tf_op jit(solution)/shard_map/ppermute | solution.py:18
  16.0 21.6 %collective-permute-start.2 = (f32[128,256]{1,0:T(8,128)S(1)}, f32[128,256]{1,0:T(8,128)S(1)}, u32[]{:S(2)}, u32[]{:S(2)}) collective-permute-start(f32[128,256]{1,0:T(8,128)S(1)} %fusion.2.refs_0_), channel_id=1, source_target_pairs={{0,3},{1,2},{2,1},{3,0},{4,7},{5,6},{6,5},{7,4},{8,11},{9,10},{10,... | collective-permute-start | bytes 393224 | tf_op jit(solution)/shard_map/ppermute | solution.py:18
  18.0 33.6 %collective-permute-start.7 = (bf16[2,128,1024]{2,1,0:T(8,128)(2,1)}, bf16[2,128,1024]{2,1,0:T(8,128)(2,1)S(1)}, u32[]{:S(2)}, u32[]{:S(2)}) collective-permute-start(bf16[2,128,1024]{2,1,0:T(8,128)(2,1)} %take_chunk.2.refs_0_), channel_id=1, source_target_pairs={{0,2},{1,3},{2,0},{3,1},{4,6},{5,7},{6,4},{7,5},{8,10},{9,11},{10,... | collective-permute-start | bytes 1572872 | tf_op jit(solution)/shard_map/ppermute | solution.py:141
  38.5 4.2 %collective-permute-start.3 = (bf16[1,128,256]{2,1,0:T(8,128)(2,1)S(1)}, bf16[1,128,256]{2,1,0:T(8,128)(2,1)S(1)}, u32[]{:S(2)}, u32[]{:S(2)}) collective-permute-start(bf16[1,128,256]{2,1,0:T(8,128)(2,1)S(1)} %fusion.5), channel_id=1, source_target_pairs={{0,4},{4,0},{8,12},{12,8},{16,20},{20,16},{24,28},{28,24},{1,5},{5... | collective-permute-start | bytes 196616 | tf_op jit(solution)/shard_map/ppermute | solution.py:18
  38.6 22.9 %collective-permute-start.6 = (bf16[2,128,1024]{2,1,0:T(8,128)(2,1)}, bf16[2,128,1024]{2,1,0:T(8,128)(2,1)S(1)}, u32[]{:S(2)}, u32[]{:S(2)}) collective-permute-start(bf16[2,128,1024]{2,1,0:T(8,128)(2,1)} %take_chunk.2.refs_0_), channel_id=1, source_target_pairs={{0,1},{1,0},{2,3},{3,2},{4,5},{5,4},{6,7},{7,6},{8,9},{9,8},{10,11... | collective-permute-start | bytes 1572872 | tf_op jit(solution)/shard_map/ppermute | solution.py:141
  42.0 19.4 %collective-permute-start.8 = (bf16[2,128,1024]{2,1,0:T(8,128)(2,1)}, bf16[2,128,1024]{2,1,0:T(8,128)(2,1)S(1)}, u32[]{:S(2)}, u32[]{:S(2)}) collective-permute-start(bf16[2,128,1024]{2,1,0:T(8,128)(2,1)} %take_chunk.2.refs_0_), channel_id=1, source_target_pairs={{1,2},{2,1},{5,6},{6,5},{9,10},{10,9},{13,14},{14,13},{17,18},{18,... | collective-permute-start | bytes 1572872 | tf_op jit(solution)/shard_map/ppermute | solution.py:141
  42.7 10.2 %collective-permute-start.4 = (bf16[2,128,256]{2,1,0:T(8,128)(2,1)S(1)}, bf16[2,128,256]{2,1,0:T(8,128)(2,1)S(1)}, u32[]{:S(2)}, u32[]{:S(2)}) collective-permute-start(bf16[2,128,256]{2,1,0:T(8,128)(2,1)S(1)} %pad_maximum_fusion.2), channel_id=1, source_target_pairs={{0,8},{4,12},{8,0},{12,4},{16,24},{20,28},{24,16},{28,20},{1,9},{5... | collective-permute-start | bytes 393224 | tf_op jit(solution)/shard_map/ppermute | solution.py:18
  51.7 9.8 %copy-start.4 = (bf16[2,128,1024]{2,1,0:T(8,128)(2,1)}, bf16[2,128,1024]{2,1,0:T(8,128)(2,1)S(1)}, u32[]{:S(2)}) copy-start(bf16[2,128,1024]{2,1,0:T(8,128)(2,1)S(1)} %collective-permute-done.7.refs_1_.refs_2_) | copy-start | bytes 1572868
  51.7 21.1 %collective-permute-start.13 = (bf16[2,128,1024]{2,1,0:T(8,128)(2,1)S(1)}, bf16[2,128,1024]{2,1,0:T(8,128)(2,1)S(1)}, u32[]{:S(2)}, u32[]{:S(2)}) collective-permute-start(bf16[2,128,1024]{2,1,0:T(8,128)(2,1)S(1)} %collective-permute-done.7.refs_1_.refs_2_), channel_id=1, source_target_pairs={{2,3},{1,0},{6,7},{5,4},{10,11},{9,8},{14,15},{13,12},{18,19},{17,... | collective-permute-start | bytes 1572872 | tf_op jit(solution)/shard_map/ppermute | solution.py:150
  53.0 14.0 %collective-permute-start.5 = (bf16[4,128,256]{2,1,0:T(8,128)(2,1)S(1)}, bf16[4,128,256]{2,1,0:T(8,128)(2,1)}, u32[]{:S(2)}, u32[]{:S(2)}) collective-permute-start(bf16[4,128,256]{2,1,0:T(8,128)(2,1)S(1)} %pad_maximum_fusion.1), channel_id=1, source_target_pairs={{0,16},{4,20},{8,24},{12,28},{16,0},{20,4},{24,8},{28,12},{1,17},{... | collective-permute-start | bytes 786440 | tf_op jit(solution)/shard_map/ppermute | solution.py:18
  61.4 0.8 copy-start.6
  62.2 0.8 copy-start.8
  65.1 17.7 %copy-start.3 = (bf16[2,128,1024]{2,1,0:T(8,128)(2,1)S(1)}, bf16[2,128,1024]{2,1,0:T(8,128)(2,1)}, u32[]{:S(2)}) copy-start(bf16[2,128,1024]{2,1,0:T(8,128)(2,1)} %take_chunk.3.refs_0_) | copy-start | bytes 1572868
  65.1 26.4 %collective-permute-start.10 = (bf16[2,128,1024]{2,1,0:T(8,128)(2,1)}, bf16[2,128,1024]{2,1,0:T(8,128)(2,1)S(1)}, u32[]{:S(2)}, u32[]{:S(2)}) collective-permute-start(bf16[2,128,1024]{2,1,0:T(8,128)(2,1)} %take_chunk.3.refs_0_), channel_id=1, source_target_pairs={{0,2},{1,3},{2,0},{3,1},{4,6},{5,7},{6,4},{7,5},{8,10},{9,11},{10,... | collective-permute-start | bytes 1572872 | tf_op jit(solution)/shard_map/ppermute | solution.py:141
  72.8 1.0 copy-start.2
  73.8 1.0 copy-start.5
  74.8 1.0 copy-start.7
  75.9 1.0 copy-start.9
  78.4 56.5 %all-to-all-start.1 = ((bf16[8,128,1024]{2,1,0:T(8,128)(2,1)}), bf16[8,128,1024]{2,1,0:T(8,128)(2,1)}, u32[]{:S(2)}, u32[]{:S(2)}) async-start(bf16[8,128,1024]{2,1,0:T(8,128)(2,1)} %bitcast.6), calls=%async_computation.1 | async-start | bytes 4194304 | tf_op jit(solution)/shard_map/all_to_all | solution.py:309
  82.8 10.3 %collective-permute-start.11 = (bf16[2,128,1024]{2,1,0:T(8,128)(2,1)S(1)}, bf16[2,128,1024]{2,1,0:T(8,128)(2,1)S(1)}, u32[]{:S(2)}, u32[]{:S(2)}) collective-permute-start(bf16[2,128,1024]{2,1,0:T(8,128)(2,1)S(1)} %copy-done.3), channel_id=1, source_target_pairs={{1,2},{2,1},{5,6},{6,5},{9,10},{10,9},{13,14},{14,13},{17,18},{18,... | collective-permute-start | bytes 1572872 | tf_op jit(solution)/shard_map/ppermute | solution.py:141
  83.6 19.2 %collective-permute-start.9 = (bf16[2,128,1024]{2,1,0:T(8,128)(2,1)S(1)}, bf16[2,128,1024]{2,1,0:T(8,128)(2,1)}, u32[]{:S(2)}, u32[]{:S(2)}) collective-permute-start(bf16[2,128,1024]{2,1,0:T(8,128)(2,1)S(1)} %copy-done.3), channel_id=1, source_target_pairs={{0,1},{1,0},{2,3},{3,2},{4,5},{5,4},{6,7},{7,6},{8,9},{9,8},{10,11... | collective-permute-start | bytes 1572872 | tf_op jit(solution)/shard_map/ppermute | solution.py:141
  91.5 22.5 %collective-permute-start.12 = (bf16[2,128,1024]{2,1,0:T(8,128)(2,1)S(1)}, bf16[2,128,1024]{2,1,0:T(8,128)(2,1)}, u32[]{:S(2)}, u32[]{:S(2)}) collective-permute-start(bf16[2,128,1024]{2,1,0:T(8,128)(2,1)S(1)} %collective-permute-done.10.refs_2_), channel_id=1, source_target_pairs={{2,3},{1,0},{6,7},{5,4},{10,11},{9,8},{14,15},{13,12},{18,19},{17,... | collective-permute-start | bytes 1572872 | tf_op jit(solution)/shard_map/ppermute | solution.py:150
  133.6 1.3 copy-start
  134.9 35.2 %all-to-all-start = ((bf16[8,128,1024]{2,1,0:T(8,128)(2,1)}), bf16[8,128,1024]{2,1,0:T(8,128)(2,1)}, u32[]{:S(2)}, u32[]{:S(2)}) async-start(bf16[8,128,1024]{2,1,0:T(8,128)(2,1)} %bitcast.4), calls=%async_computation | async-start | bytes 4194304 | tf_op jit(solution)/shard_map/all_to_all | solution.py:309
  139.3 1.6 copy-start.1
  152.1 31.6 %collective-permute-start.14 = (bf16[512,256]{1,0:T(8,128)(2,1)S(1)}, bf16[512,256]{1,0:T(8,128)(2,1)S(1)}, u32[]{:S(2)}, u32[]{:S(2)}) collective-permute-start(bf16[512,256]{1,0:T(8,128)(2,1)S(1)} %get-tuple-element.9), channel_id=1, source_target_pairs={{0,1},{1,0},{2,3},{3,2},{4,5},{5,4},{6,7},{7,6},{8,9},{9,8},{10,11... | collective-permute-start | bytes 786440 | tf_op jit(solution)/shard_map/ppermute | solution.py:18
  152.1 31.6 %collective-permute-start.15 = (bf16[512,256]{1,0:T(8,128)(2,1)S(1)}, bf16[512,256]{1,0:T(8,128)(2,1)S(1)}, u32[]{:S(2)}, u32[]{:S(2)}) collective-permute-start(bf16[512,256]{1,0:T(8,128)(2,1)S(1)} %get-tuple-element.8), channel_id=1, source_target_pairs={{0,2},{1,3},{2,0},{3,1},{4,6},{5,7},{6,4},{7,5},{8,10},{9,11},{10,... | collective-permute-start | bytes 786440 | tf_op jit(solution)/shard_map/ppermute | solution.py:18
  154.3 29.5 %collective-permute-start.16 = (bf16[512,256]{1,0:T(8,128)(2,1)S(1)}, bf16[512,256]{1,0:T(8,128)(2,1)S(1)}, u32[]{:S(2)}, u32[]{:S(2)}) collective-permute-start(bf16[512,256]{1,0:T(8,128)(2,1)S(1)} %get-tuple-element.7), channel_id=1, source_target_pairs={{0,3},{1,2},{2,1},{3,0},{4,7},{5,6},{6,5},{7,4},{8,11},{9,10},{10,... | collective-permute-start | bytes 786440 | tf_op jit(solution)/shard_map/ppermute | solution.py:18
  183.7 0.7 copy-start.11
  183.7 0.8 copy-start.12
  183.7 0.9 copy-start.13
Sparse Core Ops, SparseCore 0:
  9.9 62.6 all-gather.1

commit v9 on v6

--- a/solution.py
+++ b/solution.py
@@ -16,6 +16,11 @@
 def flip(value, axis, mask):
     count = lax.axis_size(axis)
     return lax.ppermute(value, axis, [(i, i ^ mask) for i in range(count)])
+
+
+def first_tile(value):
+    shape = (1,) * (value.ndim - 2) + (16, 128)
+    return pl.BlockSpec(shape, lambda *at: (0,) * value.ndim)
 
 
 def cost(flops, moved):
@@ -75,7 +80,7 @@
         near, far = sources[mask]
 
         def put(index, other=other):
-            out_ref[other] = refs[index][...]
+            out_ref[other] = refs[index][:, :, : out_ref.shape[3]]
 
         if far is None:
             put(near)
@@ -87,14 +92,15 @@
             pl.when(jnp.logical_not(close))(functools.partial(put, far))
 
 
-def place_blocks(blocks, sources, where, after):
+def place_blocks(blocks, sources, where, height, after):
     count = len(sources)
     return pl.pallas_call(
         functools.partial(place_kernel, sources),
-        out_shape=jax.ShapeDtypeStruct((count,) + blocks[0].shape, BF16),
+        out_shape=jax.ShapeDtypeStruct((count,) + blocks[0].shape[:2] + (height,), BF16),
+        grid=(1,),
         in_specs=[pl.BlockSpec(memory_space=pltpu.SMEM)]
         + [pl.BlockSpec(memory_space=pltpu.VMEM)] * len(blocks)
-        + [pl.BlockSpec(memory_space=pl.ANY)] * len(after),
+        + [first_tile(value) for value in after],
         out_specs=pl.BlockSpec(memory_space=pltpu.VMEM),
         cost_estimate=cost(0, 4 * count * blocks[0].size),
         compiler_params=pltpu.CompilerParams(vmem_limit_bytes=48 * MIB),
@@ -102,7 +108,88 @@
     )(where, *blocks, *after)
 
 
-def exchange_blocks(mine):
+def take_chunk(activations, chunk, height, split, tail, after):
+    tokens, features = activations.shape
+    rows = features // split
+    share = tail[0].shape[1] // split if tail else 0
+
+    def kernel(activations_ref, *refs):
+        for s in range(split):
+            at = s * rows + chunk * height
+            refs[-1][s, :, :height] = activations_ref[:, at : at + height]
+            if tail:
+                refs[-1][s, :, height:] = refs[0][:, s * share : (s + 1) * share].astype(BF16)
+
+    shape = (split, tokens, height + share)
+    return pl.pallas_call(
+        kernel,
+        out_shape=jax.ShapeDtypeStruct(shape, BF16),
+        grid=(1,),
+        in_specs=[pl.BlockSpec((tokens, features), lambda i: (0, 0))]
+        + [pl.BlockSpec(value.shape, lambda i: (0, 0)) for value in tail]
+        + [first_tile(value) for value in after],
+        out_specs=pl.BlockSpec(shape, lambda i: (0, 0, 0)),
+        cost_estimate=cost(0, 4 * split * tokens * height),
+        name="take_chunk",
+    )(activations, *tail, *after)
+
+
+def sum_tails(blocks, sources, where, height):
+    split, tokens, width = blocks[0].shape
+    share = width - height
+    count = len(sources)
+    spec = pl.BlockSpec((split, tokens, share), lambda i: (0, 0, height // share))
+
+    def kernel(where_ref, *refs):
+        out_ref, held_ref = refs[-2:]
+        me = where_ref[0]
+        for mask in range(count):
+            near, far = sources[mask]
+
+            def put(index, mask=mask):
+                held_ref[mask] = refs[index][...].astype(F32)
+
+            if far is None:
+                put(near)
+            elif near is None:
+                put(far)
+            else:
+                close = jnp.abs(me - (me ^ mask)) <= count // 2
+                pl.when(close)(functools.partial(put, near))
+                pl.when(jnp.logical_not(close))(functools.partial(put, far))
+        total = pair_sum([held_ref[mask] for mask in range(count)])
+        for s in range(split):
+            out_ref[0, :, s * share : (s + 1) * share] = total[s].astype(BF16)
+
+    return pl.pallas_call(
+        kernel,
+        out_shape=jax.ShapeDtypeStruct((1, tokens, split * share), BF16),
+        grid=(1,),
+        in_specs=[pl.BlockSpec(memory_space=pltpu.SMEM)] + [spec] * len(blocks),
+        out_specs=pl.BlockSpec((1, tokens, split * share), lambda i: (0, 0, 0)),
+        scratch_shapes=[pltpu.VMEM((count, split, tokens, share), F32)],
+        cost_estimate=cost(0, 4 * count * split * tokens * share),
+        name="sum_tails",
+    )(where, *blocks)
+
+
+def relay(value, after):
+    def kernel(value_ref, *refs):
+        refs[-1][...] = value_ref[...]
+
+    spec = pl.BlockSpec(value.shape, lambda i: (0, 0, 0))
+    return pl.pallas_call(
+        kernel,
+        out_shape=jax.ShapeDtypeStruct(value.shape, value.dtype),
+        grid=(1,),
+        in_specs=[spec] + [first_tile(other) for other in after],
+        out_specs=spec,
+        cost_estimate=cost(0, 4 * value.size),
+        name="relay",
+    )(value, *after)
+
+
+def exchange_blocks(mine, after):
     count = lax.axis_size("narrow")
     half = count // 2
     blocks = [mine]
@@ -112,6 +199,9 @@
     for mask in order:
         pairs = [(i, i ^ mask) for i in range(count) if abs(i - (i ^ mask)) <= half]
         direct[mask] = lax.ppermute(mine, "narrow", pairs) if pairs else None
+    onward = direct.get(half)
+    if after and count > 2:
+        onward = relay(onward, after)
     for mask in range(1, count):
         near = far = None
         if direct[mask] is not None:
@@ -120,12 +210,12 @@
         pairs = [(i ^ half, i ^ mask) for i in range(count) if abs(i - (i ^ mask)) > half]
         if pairs:
             far = len(blocks)
-            blocks.append(lax.ppermute(direct[half], "narrow", pairs))
+            blocks.append(lax.ppermute(onward, "narrow", pairs))
         sources.append((near, far))
     return blocks, sources
 
 
-def residual_kernel(weight_ref, codes_ref, scales_ref, hr_ref, after_ref, out_ref):
+def residual_kernel(weight_ref, codes_ref, scales_ref, out_ref):
     groups = scales_ref.shape[1]
     width = weight_ref.shape[1] // groups
     scales = scales_ref[...]
@@ -134,36 +224,55 @@
         at = slice(group * width, (group + 1) * width)
         quantized = codes_ref[:, at].astype(F32) * scales[:, group : group + 1]
         parts.append((weight_ref[:, at].astype(F32) - quantized).astype(BF16))
-    residual = jnp.concatenate(parts, axis=1)
-    out_ref[...] = jnp.dot(residual, hr_ref[...], preferred_element_type=F32).astype(BF16)
-
-
-def residual_partial(weight, codes, scales, hr, after):
+    out_ref[...] = jnp.concatenate(parts, axis=1)
+
+
+def residual_tile(weight, codes, scales):
     rows, features = weight.shape
-    rank = hr.shape[1]
     block = min(256, rows)
     return pl.pallas_call(
         residual_kernel,
-        out_shape=jax.ShapeDtypeStruct((rows, rank), BF16),
+        out_shape=jax.ShapeDtypeStruct((rows, features), BF16),
         grid=(rows // block,),
         in_specs=[
             pl.BlockSpec((block, features), lambda i: (i, 0)),
             pl.BlockSpec((block, features), lambda i: (i, 0)),
             pl.BlockSpec((block, scales.shape[1]), lambda i: (i, 0)),
+        ],
+        out_specs=pl.BlockSpec((block, features), lambda i: (i, 0)),
+        compiler_params=pltpu.CompilerParams(vmem_limit_bytes=48 * MIB),
+        cost_estimate=cost(0, 11 * rows * features),
+        name="residual_tile",
+    )(weight, codes, scales)
+
+
+def product_kernel(residual_ref, hr_ref, out_ref):
+    out_ref[...] = jnp.dot(residual_ref[...], hr_ref[...], preferred_element_type=F32).astype(BF16)
+
+
+def partial_product(residual, hr):
+    rows, features = residual.shape
+    rank = hr.shape[1]
+    block = min(512, rows)
+    return pl.pallas_call(
+        product_kernel,
+        out_shape=jax.ShapeDtypeStruct((rows, rank), BF16),
+        grid=(rows // block,),
+        in_specs=[
+            pl.BlockSpec((block, features), lambda i: (i, 0)),
             pl.BlockSpec((features, rank), lambda i: (0, 0)),
-            pl.BlockSpec(memory_space=pl.ANY),
         ],
         out_specs=pl.BlockSpec((block, rank), lambda i: (i, 0)),
-        cost_estimate=cost(4 * rows * features * rank, 8 * rows * features),
         compiler_params=pltpu.CompilerParams(vmem_limit_bytes=48 * MIB),
-        name="residual_product",
-    )(weight, codes, scales, hr, after)
+        cost_estimate=cost(4 * rows * features * rank, 3 * rows * features),
+        name="partial_product",
+    )(residual, hr)
 
 
 def hessian_rows(row_chunks, cols, earlier, index, shape, scale, after):
     tokens, height = row_chunks[0].shape
     block = height * len(row_chunks)
-    tile = min(512, cols.shape[1])
+    tile = min(1024, cols.shape[1])
     count = len(row_chunks)
     ins = [*row_chunks, cols]
     specs = [pl.BlockSpec((tokens, height), lambda j: (0, 0))] * count
@@ -175,7 +284,7 @@
         specs.append(pl.BlockSpec(memory_space=pl.ANY))
     for value in after:
         ins.append(value)
-        specs.append(pl.BlockSpec(memory_space=pl.ANY))
+        specs.append(first_tile(value))
 
     def kernel(*refs):
         cols_ref = refs[count]
@@ -217,8 +326,9 @@
     return pl.pallas_call(
         kernel,
         out_shape=jax.ShapeDtypeStruct((rows, rank), F32),
+        grid=(1,),
         in_specs=[pl.BlockSpec(memory_space=pltpu.VMEM)] * len(pieces)
-        + [pl.BlockSpec(memory_space=pl.ANY)],
+        + [first_tile(after)],
         out_specs=pl.BlockSpec(memory_space=pltpu.VMEM),
         cost_estimate=cost(0, 12 * rows * rank),
         name="add_pieces",
@@ -243,40 +353,40 @@
 
     cols = lax.all_gather(activations, "wide", axis=0, tiled=True)
 
+    right_block = lax.dynamic_slice_in_dim(right_factor, narrow_index * features, features, 0)
+    own = jnp.dot(activations, right_block, preferred_element_type=F32)
+    residual = residual_tile(weight_tile, codes, group_scales)
+
     height = rows // CHUNKS
     chunks = []
+    tail = [own]
+    after = []
     for chunk in range(CHUNKS):
-        mine = jnp.stack(
-            [
-                activations[:, s * rows + chunk * height : s * rows + (chunk + 1) * height]
-                for s in range(split)
-            ]
-        )
-        chunks.append(exchange_blocks(mine))
-
-    right_block = lax.dynamic_slice_in_dim(right_factor, narrow_index * features, features, 0)
-    product = jnp.dot(activations, right_block, preferred_element_type=F32)
-    product = pair_sum([product] + [flip(product, "narrow", m) for m in range(1, narrow_count)])
-    y_blocks = product.astype(BF16)[None]
+        mine = take_chunk(activations, chunk, height, split, tail, after)
+        blocks, sources = exchange_blocks(mine, [] if chunk else [residual])
+        chunks.append((blocks, sources))
+        tail = []
+        after = [blocks[near] for near, _ in sources if near] + [residual]
+
+    where = narrow_index.reshape(1)
+    y_blocks = sum_tails(*chunks[0], where, height)
     mask = 1
     while mask < wide_count:
         y_blocks = jnp.concatenate([y_blocks, flip(y_blocks, "wide", mask)], axis=0)
         mask *= 2
 
-    where = narrow_index.reshape(1)
     row_chunks = []
     placed = []
     for chunk in range(CHUNKS):
-        blocks, sources = chunks[chunk]
-        after = placed[-1:]
-        every = place_blocks(blocks, sources, where, after)
+        after = placed[-1:] if chunk else [y_blocks]
+        every = place_blocks(*chunks[chunk], where, height, after)
         placed.append(every)
         every = every.reshape(narrow_count * split, tokens, height)
         chunk_rows = lax.all_to_all(every, "wide", split_axis=0, concat_axis=0, tiled=True)
         row_chunks.append(chunk_rows.reshape(tokens * wide_count, height))
 
     hr, gram = hr_and_gram(cols, y_blocks, wide_index.reshape(1), scale)
-    partial = residual_partial(weight_tile, codes, group_scales, hr, placed[-1])
+    partial = partial_product(residual, hr)
     share = rows // narrow_count
     received = []
     for m in range(narrow_count):

time: 204 us -> 211 us (1.034)
  Pallas kernels: 61.7 us -> 81 us
  waiting for transfers between devices: 76 us -> 64.6 us
  starting transfers between devices: 36.9 us -> 31.1 us
  local copies, waits for them, and re-layouts: 8.16 us -> 12.8 us
    pallas_call x1 -> x6, Pallas kernels: 19.4 us -> 41.6 us  [the longest x1 25.4 us: residual_tile(): pl.pallas_call(residual_kernel, out_shape=jax.ShapeDtypeStruct((rows, fea...]
    ppermute x9 -> x6, waiting for transfers between devices: 24.4 us -> 11.7 us  [flip(): return lax.ppermute(value, axis, [(i, i ^ mask) for i in range(count)])]
    ppermute x2, waiting for transfers between devices: 23.2 us -> 30 us  [exchange_blocks(): blocks.append(lax.ppermute(onward, 'narrow', pairs))]
    ppermute x9 -> x6, starting transfers between devices: 13.6 us -> 7.39 us  [flip(): return lax.ppermute(value, axis, [(i, i ^ mask) for i in range(count)])]
    unnamed x17 -> x27, local copies, waits for them, and re-layouts: 6.1 us -> 11.8 us
    ppermute x6, waiting for transfers between devices: 27.6 us -> 22.2 us  [exchange_blocks(): direct[mask] = lax.ppermute(mine, 'narrow', pairs) if pairs else None]
    pallas_call x2, Pallas kernels: 29 us -> 26.5 us  [hessian_rows(): pl.pallas_call(kernel, out_shape=jax.ShapeDtypeStruct(shape, BF16), grid=...]
  transfers between devices with their start and end apart: 20 -> 17, of which waited for: 7 -> 7; matrix products, arithmetic and copies ran while one was open for 5% -> 4% of each run, Pallas kernels for 29% -> 38%
where the time goes in v9:
time: 211 us; the launch traced here: 209 us
  Pallas kernels  81 us (38%)
  waiting for transfers between devices  64.6 us (31%)
  starting transfers between devices  31.1 us (15%)
  between operations  14.2 us (7%)
  local copies, waits for them, and re-layouts  12.8 us (6%)
  matrix products  3.03 us (1%)
  other arithmetic  2.61 us (1%)
    ppermute x2, waiting for transfers between devices, exchange_blocks(): blocks.append(lax.ppermute(onward, 'narrow', pairs))  30 us
    pallas_call x2, Pallas kernels, hessian_rows(): pl.pallas_call(kernel, out_shape=jax.ShapeDtypeStruct(shape, BF16), grid=...  26.5 us
    pallas_call x1, Pallas kernels, residual_tile(): pl.pallas_call(residual_kernel, out_shape=jax.ShapeDtypeStruct((rows, fea...  25.4 us
    ppermute x6, waiting for transfers between devices, exchange_blocks(): direct[mask] = lax.ppermute(mine, 'narrow', pairs) if pairs else None  22.2 us
    ppermute x6, starting transfers between devices, exchange_blocks(): direct[mask] = lax.ppermute(mine, 'narrow', pairs) if pairs else None  13 us
    unnamed x27, local copies, waits for them, and re-layouts  11.8 us
    ppermute x6, waiting for transfers between devices, flip(): return lax.ppermute(value, axis, [(i, i ^ mask) for i in range(count)])  11.7 us
    pallas_call x1, Pallas kernels, partial_product(): pl.pallas_call(product_kernel, out_shape=jax.ShapeDtypeStruct((rows, rank...  8.41 us
  transfers between devices with their start and end apart: 17, of which 7 were waited for; matrix products, arithmetic and copies ran while one was open for 4% of the time, Pallas kernels for 38%

profile of v9, /device:TPU:0, one launch (start us, length us, event | category | flops | bytes accessed | tf_op | source)
XLA Modules:
  0.0 209.4 jit_solution(5458198600518472149)
XLA Ops:
  7.2 0.0 all-gather.2.cloned.1.call-start
  7.2 0.7 all-gather.2.cloned.1.call-update
  7.9 3.0 %fusion.2.refs_0_ = f32[128,256]{1,0:T(8,128)} fusion(bf16[128,4096]{1,0:T(8,128)(2,1)} %activations_ref.3, bf16[16384,256]{1,0:T(8,128)(2,1)} %param.9, s32[]{:T(128)S(6)} %select_n.15), kind=kOutput, calls=%fused_computation.2 | convolution fusion | flops 268435456 | bytes 3276804 | tf_op jit(solution)/shard_map/dot_general | solution.py:357
  10.9 2.1 %take_chunk.2.refs_0_ = bf16[2,128,1152]{2,1,0:T(8,128)(2,1)} custom-call(bf16[128,4096]{1,0:T(8,128)(2,1)} %activations_ref.3, f32[128,256]{1,0:T(8,128)} %fusion.2.refs_0_), custom_call_target="tpu_custom_call" | custom-call | bytes 1048576 | tf_op jit(solution)/shard_map/take_chunk/pallas_call | solution.py:124
  13.1 4.0 %collective-permute-start.1 = (bf16[2,128,1152]{2,1,0:T(8,128)(2,1)}, bf16[2,128,1152]{2,1,0:T(8,128)(2,1)S(1)}, u32[]{:S(2)}, u32[]{:S(2)}) collective-permute-start(bf16[2,128,1152]{2,1,0:T(8,128)(2,1)} %take_chunk.2.refs_0_), channel_id=1, source_target_pairs={{0,2},{1,3},{2,0},{3,1},{4,6},{5,7},{6,4},{7,5},{8,10},{9,11},{10,... | collective-permute-start | bytes 1769480 | tf_op jit(solution)/shard_map/ppermute | solution.py:201
  17.1 0.7 collective-permute-start.2
  17.8 2.9 %collective-permute-start = (bf16[2,128,1152]{2,1,0:T(8,128)(2,1)}, bf16[2,128,1152]{2,1,0:T(8,128)(2,1)S(1)}, u32[]{:S(2)}, u32[]{:S(2)}) collective-permute-start(bf16[2,128,1152]{2,1,0:T(8,128)(2,1)} %take_chunk.2.refs_0_), channel_id=1, source_target_pairs={{0,1},{1,0},{2,3},{3,2},{4,5},{5,4},{6,7},{7,6},{8,9},{9,8},{10,11... | collective-permute-start | bytes 1769480 | tf_op jit(solution)/shard_map/ppermute | solution.py:201
  20.7 1.3 copy.9.scales_ref
  22.0 25.4 %residual_tile.1.refs_0_.residual_ref.refs_3_ = bf16[2048,4096]{1,0:T(8,128)(2,1)} custom-call(bf16[2048,4096]{1,0:T(8,128)(2,1)} %weight_ref.1, s32[2048,4096]{1,0:T(8,128)} %codes_ref.1, f32[2048,32]{1,0:T(8,128)S(1)} %copy.9.scales_ref), custom_call_target="tpu_custom_call" | custom-call | bytes 92274688 | tf_op jit(solution)/shard_map/residual_tile/pallas_call | solution.py:233
  47.3 0.0 collective-permute-done.1.value_ref.refs_2_.refs_1_
  47.4 0.8 copy-done
  48.2 1.9 relay.1
  50.1 1.3 collective-permute-start.3
  51.4 0.0 collective-permute-done.2.refs_3_.refs_2_
  51.4 0.0 copy-start.2
  51.4 0.0 collective-permute-done.refs_1_.refs_0_
  51.4 0.0 copy-start.4
  51.4 16.5 %collective-permute-done.3.refs_4_ = bf16[2,128,1152]{2,1,0:T(8,128)(2,1)S(1)} collective-permute-done((bf16[2,128,1152]{2,1,0:T(8,128)(2,1)}, bf16[2,128,1152]{2,1,0:T(8,128)(2,1)S(1)}, u32[]{:S(2)}, u32[]{:S(2)}) %collective-permute-start.3) | collective-permute-done | bytes 589856 | tf_op jit(solution)/shard_map/ppermute | solution.py:213
  68.0 0.8 copy-done.7
  68.8 1.7 sum_tails.1
  70.5 0.0 collective-permute-start.4
  70.5 1.5 collective-permute-done.4
  71.9 0.9 pad_maximum_fusion.2
  72.8 1.5 collective-permute-start.5
  74.2 4.1 %collective-permute-done.5 = bf16[2,128,256]{2,1,0:T(8,128)(2,1)S(1)} collective-permute-done((bf16[2,128,256]{2,1,0:T(8,128)(2,1)S(1)}, bf16[2,128,256]{2,1,0:T(8,128)(2,1)S(1)}, u32[]{:S(2)}, u32[]{:S(2)}) %collective-permute-start.5) | collective-permute-done | bytes 131104 | tf_op jit(solution)/shard_map/ppermute | solution.py:18
  78.4 0.9 pad_maximum_fusion.1
  79.3 1.5 collective-permute-start.6
  80.8 6.1 %collective-permute-done.6 = bf16[4,128,256]{2,1,0:T(8,128)(2,1)S(1)} collective-permute-done((bf16[4,128,256]{2,1,0:T(8,128)(2,1)S(1)}, bf16[4,128,256]{2,1,0:T(8,128)(2,1)S(1)}, u32[]{:S(2)}, u32[]{:S(2)}) %collective-permute-start.6) | collective-permute-done | bytes 262176 | tf_op jit(solution)/shard_map/ppermute | solution.py:18
  86.9 0.9 pad_maximum_fusion.y_ref.refs_5_
  87.8 1.1 copy-done.1
  88.8 1.1 copy-done.3
  89.9 1.1 copy-done.5
  91.0 1.1 copy-done.8
  92.0 1.5 place_blocks.2.refs_5_
  93.5 3.7 %all-to-all-start.1 = ((bf16[8,128,1024]{2,1,0:T(8,128)(2,1)}), bf16[8,128,1024]{2,1,0:T(8,128)(2,1)S(1)}, u32[]{:S(2)}, u32[]{:S(2)}) async-start(bf16[8,128,1024]{2,1,0:T(8,128)(2,1)} %bitcast.5), calls=%async_computation.1 | async-start | bytes 4194304 | tf_op jit(solution)/shard_map/all_to_all | solution.py:385
  97.2 2.1 take_chunk.3.refs_0_
  99.3 0.7 collective-permute-start.11
  99.9 1.4 collective-permute-start.12
  101.4 3.3 %collective-permute-start.10 = (bf16[2,128,1024]{2,1,0:T(8,128)(2,1)}, bf16[2,128,1024]{2,1,0:T(8,128)(2,1)}, u32[]{:S(2)}, u32[]{:S(2)}) collective-permute-start(bf16[2,128,1024]{2,1,0:T(8,128)(2,1)} %take_chunk.3.refs_0_), channel_id=1, source_target_pairs={{0,1},{1,0},{2,3},{3,2},{4,5},{5,4},{6,7},{7,6},{8,9},{9,8},{10,11... | collective-permute-start | bytes 1572872 | tf_op jit(solution)/shard_map/ppermute | solution.py:201
  104.7 21.2 %collective-permute-done.11.refs_2_ = bf16[2,128,1024]{2,1,0:T(8,128)(2,1)S(1)} collective-permute-done((bf16[2,128,1024]{2,1,0:T(8,128)(2,1)}, bf16[2,128,1024]{2,1,0:T(8,128)(2,1)S(1)}, u32[]{:S(2)}, u32[]{:S(2)}) %collective-permute-start.11) | collective-permute-done | bytes 524320 | tf_op jit(solution)/shard_map/ppermute | solution.py:201
  125.9 1.3 collective-permute-start.13
  127.2 0.0 collective-permute-done.12.refs_3_
  127.2 1.0 collective-permute-done.10.refs_1_
  128.2 13.5 %collective-permute-done.13.refs_4_ = bf16[2,128,1024]{2,1,0:T(8,128)(2,1)} collective-permute-done((bf16[2,128,1024]{2,1,0:T(8,128)(2,1)S(1)}, bf16[2,128,1024]{2,1,0:T(8,128)(2,1)}, u32[]{:S(2)}, u32[]{:S(2)}) %collective-permute-start.13) | collective-permute-done | bytes 524320 | tf_op jit(solution)/shard_map/ppermute | solution.py:213
  141.7 1.0 copy-done.9
  142.8 2.9 %place_blocks.3 = bf16[4,2,128,1024]{3,2,1,0:T(8,128)(2,1)} custom-call(s32[1]{0:T(128)} %bitcast.1.where_ref, bf16[2,128,1024]{2,1,0:T(8,128)(2,1)S(1)} %copy-done.9, bf16[2,128,1024]{2,1,0:T(8,128)(2,1)} %collective-permute-done.10.refs_1_, bf16[2,128,1024]{2,1,0:T(8,128)(2,1)S(1)} %collective-permute-done.11.refs_2_, ...), custom_call_target="tpu_custom_call" | custom-call | bytes 4194304 | tf_op jit(solution)/shard_map/place_blocks/pallas_call | solution.py:97
  145.6 6.5 %hr_and_gram.1 = (bf16[4096,256]{1,0:T(8,128)(2,1)S(1)}, f32[256,256]{1,0:T(8,128)}) custom-call(s32[1]{0:T(128)} %bitcast.where_ref, bf16[1024,4096]{1,0:T(8,128)(2,1)} %all-gather.2.cloned.1.call-done.cols_ref.refs_1_, bf16[8,128,256]{2,1,0:T(8,128)(2,1)S(1)} %pad_maximum_fusion.y_ref.refs_5_), custom_call_target="tpu_custom_call" | custom-call | flops 4294967296 | bytes 16777216 | tf_op jit(solution)/shard_map/hr_and_gram/pallas_call | solution.py:48
  152.1 1.3 copy-done.10
  153.4 0.0 all-to-all-done.1
  153.4 4.4 %all-to-all-start = ((bf16[8,128,1024]{2,1,0:T(8,128)(2,1)}), bf16[8,128,1024]{2,1,0:T(8,128)(2,1)}, u32[]{:S(2)}, u32[]{:S(2)}) async-start(bf16[8,128,1024]{2,1,0:T(8,128)(2,1)} %bitcast.3), calls=%async_computation | async-start | bytes 4194304 | tf_op jit(solution)/shard_map/all_to_all | solution.py:385
  157.8 1.6 copy-done.11
  159.4 8.4 %partial_product.1.refs_2_.refs_3_ = bf16[2048,256]{1,0:T(8,128)(2,1)S(1)} custom-call(bf16[2048,4096]{1,0:T(8,128)(2,1)} %residual_tile.1.refs_0_.residual_ref.refs_3_, bf16[4096,256]{1,0:T(8,128)(2,1)S(1)} %copy-done.11), custom_call_target="tpu_custom_call" | custom-call | flops 8589934592 | bytes 25165824 | tf_op jit(solution)/shard_map/partial_product/pallas_call | solution.py:257
  167.8 1.0 constant_dynamic-slice_fusion
  168.8 1.7 collective-permute-start.9
  170.5 0.0 collective-permute-start.8
  170.5 2.7 %collective-permute-start.7 = (bf16[512,256]{1,0:T(8,128)(2,1)}, bf16[512,256]{1,0:T(8,128)(2,1)}, u32[]{:S(2)}, u32[]{:S(2)}) collective-permute-start(bf16[512,256]{1,0:T(8,128)(2,1)} %get-tuple-element.9), channel_id=1, source_target_pairs={{0,1},{1,0},{2,3},{3,2},{4,5},{5,4},{6,7},{7,6},{8,9},{9,8},{10,11... | collective-permute-start | bytes 786440 | tf_op jit(solution)/shard_map/ppermute | solution.py:18
  173.2 12.9 %hessian_rows.2.refs_2_ = bf16[2048,4096]{1,0:T(8,128)(2,1)} custom-call(bf16[1024,1024]{1,0:T(8,128)(2,1)S(1)} %bitcast.9, bf16[1024,4096]{1,0:T(8,128)(2,1)} %all-gather.2.cloned.1.call-done.cols_ref.refs_1_, bf16[2048,256]{1,0:T(8,128)(2,1)S(1)} %partial_product.1.refs_2_.refs_3_), custom_call_target="tpu_custom_call" | custom-call | flops 17179869184 | bytes 18874368 | tf_op jit(solution)/shard_map/hessian_rows/pallas_call | solution.py:301
  186.1 0.0 all-to-all-done
  186.1 13.6 %hessian_rows.3.refs_4_ = bf16[2048,4096]{1,0:T(8,128)(2,1)} custom-call(bf16[1024,1024]{1,0:T(8,128)(2,1)} %bitcast.4.refs_0_, bf16[1024,4096]{1,0:T(8,128)(2,1)} %all-gather.2.cloned.1.call-done.cols_ref.refs_1_, bf16[2048,4096]{1,0:T(8,128)(2,1)} %hessian_rows.2.refs_2_, ...), custom_call_target="tpu_custom_call", output_to_operand_aliasing={{}: (2, {})} | custom-call | flops 17179869184 | bytes 18874368 | tf_op jit(solution)/shard_map/hessian_rows/pallas_call | solution.py:301
  199.7 0.0 collective-permute-done.9.refs_3_
  199.7 0.0 collective-permute-done.8.refs_2_
  199.7 0.0 collective-permute-done.7.refs_1_
  199.7 0.7 copy-done.12
  200.4 2.1 %add_pieces.1 = f32[512,256]{1,0:T(8,128)} custom-call(bf16[512,256]{1,0:T(8,128)(2,1)} %get-tuple-element.10.refs_0_, bf16[512,256]{1,0:T(8,128)(2,1)} %collective-permute-done.7.refs_1_, bf16[512,256]{1,0:T(8,128)(2,1)} %collective-permute-done.8.refs_2_, bf16[512,256]{1,0:T(8,128)(2,1)} %copy-done.12, bf16[2048,4096]{1,0:T(8,128)(2,1)} %hessian_rows.3.refs_4_), custom_call_target="tpu_custom_call" | custom-call | bytes 1572864 | tf_op jit(solution)/shard_map/add_pieces/pallas_call | solution.py:326
  (15 shorter events, 0.0 us)
Async XLA Ops:
  7.2 138.5 %all-gather.2.cloned.1.call-start = ((), (), s32[]{:S(2)}) async-start(), calls=%async_computation.2 | async-start | bytes 9437184 | tf_op jit(solution)/shard_map/all_gather | solution.py:354
  13.1 34.3 %collective-permute-start.1 = (bf16[2,128,1152]{2,1,0:T(8,128)(2,1)}, bf16[2,128,1152]{2,1,0:T(8,128)(2,1)S(1)}, u32[]{:S(2)}, u32[]{:S(2)}) collective-permute-start(bf16[2,128,1152]{2,1,0:T(8,128)(2,1)} %take_chunk.2.refs_0_), channel_id=1, source_target_pairs={{0,2},{1,3},{2,0},{3,1},{4,6},{5,7},{6,4},{7,5},{8,10},{9,11},{10,... | collective-permute-start | bytes 1769480 | tf_op jit(solution)/shard_map/ppermute | solution.py:201
  17.1 34.3 %collective-permute-start.2 = (bf16[2,128,1152]{2,1,0:T(8,128)(2,1)}, bf16[2,128,1152]{2,1,0:T(8,128)(2,1)S(1)}, u32[]{:S(2)}, u32[]{:S(2)}) collective-permute-start(bf16[2,128,1152]{2,1,0:T(8,128)(2,1)} %take_chunk.2.refs_0_), channel_id=1, source_target_pairs={{1,2},{2,1},{5,6},{6,5},{9,10},{10,9},{13,14},{14,13},{17,18},{18,... | collective-permute-start | bytes 1769480 | tf_op jit(solution)/shard_map/ppermute | solution.py:201
  17.8 33.6 %collective-permute-start = (bf16[2,128,1152]{2,1,0:T(8,128)(2,1)}, bf16[2,128,1152]{2,1,0:T(8,128)(2,1)S(1)}, u32[]{:S(2)}, u32[]{:S(2)}) collective-permute-start(bf16[2,128,1152]{2,1,0:T(8,128)(2,1)} %take_chunk.2.refs_0_), channel_id=1, source_target_pairs={{0,1},{1,0},{2,3},{3,2},{4,5},{5,4},{6,7},{7,6},{8,9},{9,8},{10,11... | collective-permute-start | bytes 1769480 | tf_op jit(solution)/shard_map/ppermute | solution.py:201
  47.3 40.4 %copy-start.6 = (bf16[2,128,1152]{2,1,0:T(8,128)(2,1)S(1)}, bf16[2,128,1152]{2,1,0:T(8,128)(2,1)}, u32[]{:S(2)}) copy-start(bf16[2,128,1152]{2,1,0:T(8,128)(2,1)} %take_chunk.2.refs_0_) | copy-start | bytes 1769476
  47.3 0.8 copy-start
  50.1 17.8 %collective-permute-start.3 = (bf16[2,128,1152]{2,1,0:T(8,128)(2,1)}, bf16[2,128,1152]{2,1,0:T(8,128)(2,1)S(1)}, u32[]{:S(2)}, u32[]{:S(2)}) collective-permute-start(bf16[2,128,1152]{2,1,0:T(8,128)(2,1)} %relay.1), channel_id=1, source_target_pairs={{2,3},{1,0},{6,7},{5,4},{10,11},{9,8},{14,15},{13,12},{18,19},{17,... | collective-permute-start | bytes 1769480 | tf_op jit(solution)/shard_map/ppermute | solution.py:213
  51.4 16.5 %copy-start.2 = (bf16[2,128,1152]{2,1,0:T(8,128)(2,1)}, bf16[2,128,1152]{2,1,0:T(8,128)(2,1)S(1)}, u32[]{:S(2)}) copy-start(bf16[2,128,1152]{2,1,0:T(8,128)(2,1)S(1)} %collective-permute-done.2.refs_3_.refs_2_) | copy-start | bytes 1769476
  51.4 16.5 %copy-start.4 = (bf16[2,128,1152]{2,1,0:T(8,128)(2,1)}, bf16[2,128,1152]{2,1,0:T(8,128)(2,1)S(1)}, u32[]{:S(2)}) copy-start(bf16[2,128,1152]{2,1,0:T(8,128)(2,1)S(1)} %collective-permute-done.refs_1_.refs_0_) | copy-start | bytes 1769476
  68.0 0.8 copy-start.7
  70.5 1.5 collective-permute-start.4
  72.8 5.6 %collective-permute-start.5 = (bf16[2,128,256]{2,1,0:T(8,128)(2,1)S(1)}, bf16[2,128,256]{2,1,0:T(8,128)(2,1)S(1)}, u32[]{:S(2)}, u32[]{:S(2)}) collective-permute-start(bf16[2,128,256]{2,1,0:T(8,128)(2,1)S(1)} %pad_maximum_fusion.2), channel_id=1, source_target_pairs={{0,8},{4,12},{8,0},{12,4},{16,24},{20,28},{24,16},{28,20},{1,9},{5... | collective-permute-start | bytes 393224 | tf_op jit(solution)/shard_map/ppermute | solution.py:18
  79.3 7.6 %collective-permute-start.6 = (bf16[4,128,256]{2,1,0:T(8,128)(2,1)S(1)}, bf16[4,128,256]{2,1,0:T(8,128)(2,1)S(1)}, u32[]{:S(2)}, u32[]{:S(2)}) collective-permute-start(bf16[4,128,256]{2,1,0:T(8,128)(2,1)S(1)} %pad_maximum_fusion.1), channel_id=1, source_target_pairs={{0,16},{4,20},{8,24},{12,28},{16,0},{20,4},{24,8},{28,12},{1,17},{... | collective-permute-start | bytes 786440 | tf_op jit(solution)/shard_map/ppermute | solution.py:18
  87.8 1.1 copy-start.1
  88.8 1.1 copy-start.3
  89.9 1.1 copy-start.5
  91.0 1.1 copy-start.8
  93.5 59.9 %all-to-all-start.1 = ((bf16[8,128,1024]{2,1,0:T(8,128)(2,1)}), bf16[8,128,1024]{2,1,0:T(8,128)(2,1)S(1)}, u32[]{:S(2)}, u32[]{:S(2)}) async-start(bf16[8,128,1024]{2,1,0:T(8,128)(2,1)} %bitcast.5), calls=%async_computation.1 | async-start | bytes 4194304 | tf_op jit(solution)/shard_map/all_to_all | solution.py:385
  99.3 26.6 %collective-permute-start.11 = (bf16[2,128,1024]{2,1,0:T(8,128)(2,1)}, bf16[2,128,1024]{2,1,0:T(8,128)(2,1)S(1)}, u32[]{:S(2)}, u32[]{:S(2)}) collective-permute-start(bf16[2,128,1024]{2,1,0:T(8,128)(2,1)} %take_chunk.3.refs_0_), channel_id=1, source_target_pairs={{0,2},{1,3},{2,0},{3,1},{4,6},{5,7},{6,4},{7,5},{8,10},{9,11},{10,... | collective-permute-start | bytes 1572872 | tf_op jit(solution)/shard_map/ppermute | solution.py:201
  99.9 27.3 %collective-permute-start.12 = (bf16[2,128,1024]{2,1,0:T(8,128)(2,1)}, bf16[2,128,1024]{2,1,0:T(8,128)(2,1)}, u32[]{:S(2)}, u32[]{:S(2)}) collective-permute-start(bf16[2,128,1024]{2,1,0:T(8,128)(2,1)} %take_chunk.3.refs_0_), channel_id=1, source_target_pairs={{1,2},{2,1},{5,6},{6,5},{9,10},{10,9},{13,14},{14,13},{17,18},{18,... | collective-permute-start | bytes 1572872 | tf_op jit(solution)/shard_map/ppermute | solution.py:201
  101.4 26.8 %collective-permute-start.10 = (bf16[2,128,1024]{2,1,0:T(8,128)(2,1)}, bf16[2,128,1024]{2,1,0:T(8,128)(2,1)}, u32[]{:S(2)}, u32[]{:S(2)}) collective-permute-start(bf16[2,128,1024]{2,1,0:T(8,128)(2,1)} %take_chunk.3.refs_0_), channel_id=1, source_target_pairs={{0,1},{1,0},{2,3},{3,2},{4,5},{5,4},{6,7},{7,6},{8,9},{9,8},{10,11... | collective-permute-start | bytes 1572872 | tf_op jit(solution)/shard_map/ppermute | solution.py:201
  125.9 15.8 %collective-permute-start.13 = (bf16[2,128,1024]{2,1,0:T(8,128)(2,1)S(1)}, bf16[2,128,1024]{2,1,0:T(8,128)(2,1)}, u32[]{:S(2)}, u32[]{:S(2)}) collective-permute-start(bf16[2,128,1024]{2,1,0:T(8,128)(2,1)S(1)} %collective-permute-done.11.refs_2_), channel_id=1, source_target_pairs={{2,3},{1,0},{6,7},{5,4},{10,11},{9,8},{14,15},{13,12},{18,19},{17,... | collective-permute-start | bytes 1572872 | tf_op jit(solution)/shard_map/ppermute | solution.py:213
  141.7 1.0 copy-start.9
  152.1 1.3 copy-start.10
  153.4 32.7 %all-to-all-start = ((bf16[8,128,1024]{2,1,0:T(8,128)(2,1)}), bf16[8,128,1024]{2,1,0:T(8,128)(2,1)}, u32[]{:S(2)}, u32[]{:S(2)}) async-start(bf16[8,128,1024]{2,1,0:T(8,128)(2,1)} %bitcast.3), calls=%async_computation | async-start | bytes 4194304 | tf_op jit(solution)/shard_map/all_to_all | solution.py:385
  157.8 1.6 copy-start.11
  168.8 30.9 %collective-permute-start.9 = (bf16[512,256]{1,0:T(8,128)(2,1)}, bf16[512,256]{1,0:T(8,128)(2,1)S(1)}, u32[]{:S(2)}, u32[]{:S(2)}) collective-permute-start(bf16[512,256]{1,0:T(8,128)(2,1)} %get-tuple-element.7), channel_id=1, source_target_pairs={{0,3},{1,2},{2,1},{3,0},{4,7},{5,6},{6,5},{7,4},{8,11},{9,10},{10,... | collective-permute-start | bytes 786440 | tf_op jit(solution)/shard_map/ppermute | solution.py:18
  170.5 29.2 %collective-permute-start.8 = (bf16[512,256]{1,0:T(8,128)(2,1)}, bf16[512,256]{1,0:T(8,128)(2,1)}, u32[]{:S(2)}, u32[]{:S(2)}) collective-permute-start(bf16[512,256]{1,0:T(8,128)(2,1)} %get-tuple-element.8), channel_id=1, source_target_pairs={{0,2},{1,3},{2,0},{3,1},{4,6},{5,7},{6,4},{7,5},{8,10},{9,11},{10,... | collective-permute-start | bytes 786440 | tf_op jit(solution)/shard_map/ppermute | solution.py:18
  170.5 29.2 %collective-permute-start.7 = (bf16[512,256]{1,0:T(8,128)(2,1)}, bf16[512,256]{1,0:T(8,128)(2,1)}, u32[]{:S(2)}, u32[]{:S(2)}) collective-permute-start(bf16[512,256]{1,0:T(8,128)(2,1)} %get-tuple-element.9), channel_id=1, source_target_pairs={{0,1},{1,0},{2,3},{3,2},{4,5},{5,4},{6,7},{7,6},{8,9},{9,8},{10,11... | collective-permute-start | bytes 786440 | tf_op jit(solution)/shard_map/ppermute | solution.py:18
  199.7 0.7 copy-start.12
Sparse Core Ops, SparseCore 0:
  9.9 57.0 all-gather.1

commit v10 on v9

--- a/solution.py
+++ b/solution.py
@@ -134,7 +134,7 @@
     )(activations, *tail, *after)
 
 
-def sum_tails(blocks, sources, where, height):
+def sum_tails(blocks, sources, where, height, after):
     split, tokens, width = blocks[0].shape
     share = width - height
     count = len(sources)
@@ -165,12 +165,14 @@
         kernel,
         out_shape=jax.ShapeDtypeStruct((1, tokens, split * share), BF16),
         grid=(1,),
-        in_specs=[pl.BlockSpec(memory_space=pltpu.SMEM)] + [spec] * len(blocks),
+        in_specs=[pl.BlockSpec(memory_space=pltpu.SMEM)]
+        + [spec] * len(blocks)
+        + [first_tile(value) for value in after],
         out_specs=pl.BlockSpec((1, tokens, split * share), lambda i: (0, 0, 0)),
         scratch_shapes=[pltpu.VMEM((count, split, tokens, share), F32)],
         cost_estimate=cost(0, 4 * count * split * tokens * share),
         name="sum_tails",
-    )(where, *blocks)
+    )(where, *blocks, *after)
 
 
 def relay(value, after):
@@ -369,23 +371,24 @@
         after = [blocks[near] for near, _ in sources if near] + [residual]
 
     where = narrow_index.reshape(1)
-    y_blocks = sum_tails(*chunks[0], where, height)
+    y_blocks = sum_tails(*chunks[0], where, height, [blocks[0] for blocks, _ in chunks[1:]])
     mask = 1
     while mask < wide_count:
         y_blocks = jnp.concatenate([y_blocks, flip(y_blocks, "wide", mask)], axis=0)
         mask *= 2
 
+    hr, gram = hr_and_gram(cols, y_blocks, wide_index.reshape(1), scale)
+
     row_chunks = []
     placed = []
     for chunk in range(CHUNKS):
-        after = placed[-1:] if chunk else [y_blocks]
+        after = placed[-1:] + [hr] if chunk else [y_blocks]
         every = place_blocks(*chunks[chunk], where, height, after)
         placed.append(every)
         every = every.reshape(narrow_count * split, tokens, height)
         chunk_rows = lax.all_to_all(every, "wide", split_axis=0, concat_axis=0, tiled=True)
         row_chunks.append(chunk_rows.reshape(tokens * wide_count, height))
 
-    hr, gram = hr_and_gram(cols, y_blocks, wide_index.reshape(1), scale)
     partial = partial_product(residual, hr)
     share = rows // narrow_count
     received = []

time: 211 us -> 197 us (0.934)
  waiting for transfers between devices: 64.6 us -> 51.8 us
    ppermute x2, waiting for transfers between devices: 30 us -> 17.4 us  [exchange_blocks(): blocks.append(lax.ppermute(onward, 'narrow', pairs))]
    ppermute x6, starting transfers between devices: 13 us -> 10.4 us  [exchange_blocks(): direct[mask] = lax.ppermute(mine, 'narrow', pairs) if pairs else None]
    unnamed x27 -> x35, local copies, waits for them, and re-layouts: 11.8 us -> 11.8 us
  transfers between devices with their start and end apart: 17 -> 17, of which waited for: 7 -> 6; matrix products, arithmetic and copies ran while one was open for 4% -> 4% of each run, Pallas kernels for 38% -> 41%
where the time goes in v10:
time: 197 us; the launch traced here: 196 us
  Pallas kernels  82.6 us (42%)
  waiting for transfers between devices  51.8 us (26%)
  starting transfers between devices  29 us (15%)
  between operations  14.3 us (7%)
  local copies, waits for them, and re-layouts  12.5 us (6%)
  matrix products  3.03 us (2%)
  other arithmetic  2.61 us (1%)
    pallas_call x2, Pallas kernels, hessian_rows(): pl.pallas_call(kernel, out_shape=jax.ShapeDtypeStruct(shape, BF16), grid=...  27.2 us
    pallas_call x1, Pallas kernels, residual_tile(): pl.pallas_call(residual_kernel, out_shape=jax.ShapeDtypeStruct((rows, fea...  26.5 us
    ppermute x6, waiting for transfers between devices, exchange_blocks(): direct[mask] = lax.ppermute(mine, 'narrow', pairs) if pairs else None  21.7 us
    ppermute x2, waiting for transfers between devices, exchange_blocks(): blocks.append(lax.ppermute(onward, 'narrow', pairs))  17.4 us
    ppermute x6, waiting for transfers between devices, flip(): return lax.ppermute(value, axis, [(i, i ^ mask) for i in range(count)])  12 us
    unnamed x35, local copies, waits for them, and re-layouts  11.8 us
    ppermute x6, starting transfers between devices, exchange_blocks(): direct[mask] = lax.ppermute(mine, 'narrow', pairs) if pairs else None  10.4 us
    all_to_all x2, starting transfers between devices, body(): lax.all_to_all(every, 'wide', split_axis=0, concat_axis=0, tiled=True)  8.72 us
  transfers between devices with their start and end apart: 17, of which 6 were waited for; matrix products, arithmetic and copies ran while one was open for 4% of the time, Pallas kernels for 41%

profile of v10, /device:TPU:0, one launch (start us, length us, event | category | flops | bytes accessed | tf_op | source)
XLA Modules:
  0.0 195.8 jit_solution(7628232471734176035)
XLA Ops:
  7.2 0.0 all-gather.2.cloned.1.call-start
  7.2 0.7 all-gather.2.cloned.1.call-update
  7.9 3.0 %fusion.2.refs_0_ = f32[128,256]{1,0:T(8,128)} fusion(bf16[128,4096]{1,0:T(8,128)(2,1)} %activations_ref.3, bf16[16384,256]{1,0:T(8,128)(2,1)} %param.9, s32[]{:T(128)S(6)} %select_n.15), kind=kOutput, calls=%fused_computation.2 | convolution fusion | flops 268435456 | bytes 3276804 | tf_op jit(solution)/shard_map/dot_general | solution.py:359
  10.9 2.1 %take_chunk.2.refs_0_ = bf16[2,128,1152]{2,1,0:T(8,128)(2,1)} custom-call(bf16[128,4096]{1,0:T(8,128)(2,1)} %activations_ref.3, f32[128,256]{1,0:T(8,128)} %fusion.2.refs_0_), custom_call_target="tpu_custom_call" | custom-call | bytes 1048576 | tf_op jit(solution)/shard_map/take_chunk/pallas_call | solution.py:124
  13.1 4.0 %collective-permute-start.1 = (bf16[2,128,1152]{2,1,0:T(8,128)(2,1)}, bf16[2,128,1152]{2,1,0:T(8,128)(2,1)S(1)}, u32[]{:S(2)}, u32[]{:S(2)}) collective-permute-start(bf16[2,128,1152]{2,1,0:T(8,128)(2,1)} %take_chunk.2.refs_0_), channel_id=1, source_target_pairs={{0,2},{1,3},{2,0},{3,1},{4,6},{5,7},{6,4},{7,5},{8,10},{9,11},{10,... | collective-permute-start | bytes 1769480 | tf_op jit(solution)/shard_map/ppermute | solution.py:203
  17.1 1.6 collective-permute-start
  18.7 0.7 collective-permute-start.2
  19.4 1.3 copy.9.scales_ref
  20.7 26.5 %residual_tile.1.refs_0_.refs_3_.residual_ref = bf16[2048,4096]{1,0:T(8,128)(2,1)} custom-call(bf16[2048,4096]{1,0:T(8,128)(2,1)} %weight_ref.1, s32[2048,4096]{1,0:T(8,128)} %codes_ref.1, f32[2048,32]{1,0:T(8,128)S(1)} %copy.9.scales_ref), custom_call_target="tpu_custom_call" | custom-call | bytes 92274688 | tf_op jit(solution)/shard_map/residual_tile/pallas_call | solution.py:235
  47.2 0.0 collective-permute-done.1.value_ref.refs_1_.refs_2_
  47.2 0.8 copy-done
  48.0 1.9 relay.1
  50.0 1.4 collective-permute-start.3
  51.4 0.0 collective-permute-done.refs_0_.refs_1_
  51.4 0.0 collective-permute-done.2.refs_2_.refs_3_
  51.4 0.8 copy-done.2
  52.2 0.8 copy-done.4
  53.0 2.1 %take_chunk.3.refs_5_.refs_0_ = bf16[2,128,1024]{2,1,0:T(8,128)(2,1)} custom-call(bf16[128,4096]{1,0:T(8,128)(2,1)} %activations_ref.3, bf16[2,128,1152]{2,1,0:T(8,128)(2,1)} %copy-done.2, bf16[2,128,1152]{2,1,0:T(8,128)(2,1)} %copy-done, bf16[2,128,1152]{2,1,0:T(8,128)(2,1)} %copy-done.4, bf16[2048,4096]{1,0:T(8,128)(2,1)} %residual_tile.1.refs_0_.refs_3_.residual_ref), custom_call_target="tpu_custom_call" | custom-call | bytes 1048576 | tf_op jit(solution)/shard_map/take_chunk/pallas_call | solution.py:124
  55.1 11.4 %collective-permute-done.3.refs_4_ = bf16[2,128,1152]{2,1,0:T(8,128)(2,1)S(1)} collective-permute-done((bf16[2,128,1152]{2,1,0:T(8,128)(2,1)}, bf16[2,128,1152]{2,1,0:T(8,128)(2,1)S(1)}, u32[]{:S(2)}, u32[]{:S(2)}) %collective-permute-start.3) | collective-permute-done | bytes 589856 | tf_op jit(solution)/shard_map/ppermute | solution.py:215
  66.5 0.8 copy-done.8
  67.3 1.7 sum_tails.1
  69.0 0.0 collective-permute-start.4
  69.0 1.5 collective-permute-done.4
  70.5 0.9 pad_maximum_fusion.2
  71.3 1.3 collective-permute-start.5
  72.7 4.3 %collective-permute-done.5 = bf16[2,128,256]{2,1,0:T(8,128)(2,1)S(1)} collective-permute-done((bf16[2,128,256]{2,1,0:T(8,128)(2,1)S(1)}, bf16[2,128,256]{2,1,0:T(8,128)(2,1)S(1)}, u32[]{:S(2)}, u32[]{:S(2)}) %collective-permute-start.5) | collective-permute-done | bytes 131104 | tf_op jit(solution)/shard_map/ppermute | solution.py:18
  76.9 0.9 pad_maximum_fusion.1
  77.8 1.4 collective-permute-start.6
  79.2 6.2 %collective-permute-done.6 = bf16[4,128,256]{2,1,0:T(8,128)(2,1)S(1)} collective-permute-done((bf16[4,128,256]{2,1,0:T(8,128)(2,1)S(1)}, bf16[4,128,256]{2,1,0:T(8,128)(2,1)S(1)}, u32[]{:S(2)}, u32[]{:S(2)}) %collective-permute-start.6) | collective-permute-done | bytes 262176 | tf_op jit(solution)/shard_map/ppermute | solution.py:18
  85.4 0.9 pad_maximum_fusion.y_ref.refs_5_
  86.3 1.1 copy-done.3
  87.4 1.1 copy-done.5
  88.5 1.1 copy-done.9
  89.5 1.5 place_blocks.2.refs_5_
  91.0 4.4 %all-to-all-start.1 = ((bf16[8,128,1024]{2,1,0:T(8,128)(2,1)}), bf16[8,128,1024]{2,1,0:T(8,128)(2,1)}, u32[]{:S(2)}, u32[]{:S(2)}) async-start(bf16[8,128,1024]{2,1,0:T(8,128)(2,1)} %bitcast.5), calls=%async_computation.1 | async-start | bytes 4194304 | tf_op jit(solution)/shard_map/all_to_all | solution.py:389
  95.4 0.3 collective-permute-start.11
  95.7 2.4 %collective-permute-start.10 = (bf16[2,128,1024]{2,1,0:T(8,128)(2,1)S(1)}, bf16[2,128,1024]{2,1,0:T(8,128)(2,1)S(1)}, u32[]{:S(2)}, u32[]{:S(2)}) collective-permute-start(bf16[2,128,1024]{2,1,0:T(8,128)(2,1)S(1)} %copy-done.7), channel_id=1, source_target_pairs={{0,1},{1,0},{2,3},{3,2},{4,5},{5,4},{6,7},{7,6},{8,9},{9,8},{10,11... | collective-permute-start | bytes 1572872 | tf_op jit(solution)/shard_map/ppermute | solution.py:203
  98.1 1.4 collective-permute-start.12
  99.5 21.7 %collective-permute-done.11.refs_2_ = bf16[2,128,1024]{2,1,0:T(8,128)(2,1)S(1)} collective-permute-done((bf16[2,128,1024]{2,1,0:T(8,128)(2,1)S(1)}, bf16[2,128,1024]{2,1,0:T(8,128)(2,1)S(1)}, u32[]{:S(2)}, u32[]{:S(2)}) %collective-permute-start.11) | collective-permute-done | bytes 524320 | tf_op jit(solution)/shard_map/ppermute | solution.py:203
  121.2 1.3 collective-permute-start.13
  122.6 0.0 all-gather.2.cloned.1.call-done.cols_ref.refs_1_
  122.6 6.5 %hr_and_gram.1 = (bf16[4096,256]{1,0:T(8,128)(2,1)S(1)}, f32[256,256]{1,0:T(8,128)}) custom-call(s32[1]{0:T(128)} %bitcast.where_ref, bf16[1024,4096]{1,0:T(8,128)(2,1)} %all-gather.2.cloned.1.call-done.cols_ref.refs_1_, bf16[8,128,256]{2,1,0:T(8,128)(2,1)S(1)} %pad_maximum_fusion.y_ref.refs_5_), custom_call_target="tpu_custom_call" | custom-call | flops 4294967296 | bytes 16777216 | tf_op jit(solution)/shard_map/hr_and_gram/pallas_call | solution.py:48
  129.1 1.3 copy-done.10
  130.4 0.0 collective-permute-done.10.refs_1_
  130.4 0.8 copy-done.12
  131.2 0.0 collective-permute-done.12.refs_3_
  131.2 6.0 %collective-permute-done.13.refs_4_ = bf16[2,128,1024]{2,1,0:T(8,128)(2,1)} collective-permute-done((bf16[2,128,1024]{2,1,0:T(8,128)(2,1)S(1)}, bf16[2,128,1024]{2,1,0:T(8,128)(2,1)}, u32[]{:S(2)}, u32[]{:S(2)}) %collective-permute-start.13) | collective-permute-done | bytes 524320 | tf_op jit(solution)/shard_map/ppermute | solution.py:215
  137.2 1.0 copy-done.13
  138.2 2.6 %place_blocks.3 = bf16[4,2,128,1024]{3,2,1,0:T(8,128)(2,1)} custom-call(s32[1]{0:T(128)} %bitcast.1.where_ref, bf16[2,128,1024]{2,1,0:T(8,128)(2,1)S(1)} %copy-done.7, bf16[2,128,1024]{2,1,0:T(8,128)(2,1)S(1)} %copy-done.13, bf16[2,128,1024]{2,1,0:T(8,128)(2,1)S(1)} %collective-permute-done.11.refs_2_, ...), custom_call_target="tpu_custom_call" | custom-call | bytes 4194304 | tf_op jit(solution)/shard_map/place_blocks/pallas_call | solution.py:97
  140.8 0.0 all-to-all-done.1
  140.8 4.4 %all-to-all-start = ((bf16[8,128,1024]{2,1,0:T(8,128)(2,1)}), bf16[8,128,1024]{2,1,0:T(8,128)(2,1)}, u32[]{:S(2)}, u32[]{:S(2)}) async-start(bf16[8,128,1024]{2,1,0:T(8,128)(2,1)} %bitcast.3), calls=%async_computation | async-start | bytes 4194304 | tf_op jit(solution)/shard_map/all_to_all | solution.py:389
  145.2 8.4 %partial_product.1.refs_2_.refs_3_ = bf16[2048,256]{1,0:T(8,128)(2,1)S(1)} custom-call(bf16[2048,4096]{1,0:T(8,128)(2,1)} %residual_tile.1.refs_0_.refs_3_.residual_ref, bf16[4096,256]{1,0:T(8,128)(2,1)S(1)} %copy-done.11), custom_call_target="tpu_custom_call" | custom-call | flops 8589934592 | bytes 25165824 | tf_op jit(solution)/shard_map/partial_product/pallas_call | solution.py:259
  153.6 0.8 constant_dynamic-slice_fusion
  154.4 0.0 collective-permute-start.7
  154.4 2.4 %collective-permute-start.8 = (bf16[512,256]{1,0:T(8,128)(2,1)S(1)}, bf16[512,256]{1,0:T(8,128)(2,1)S(1)}, u32[]{:S(2)}, u32[]{:S(2)}) collective-permute-start(bf16[512,256]{1,0:T(8,128)(2,1)S(1)} %get-tuple-element.8), channel_id=1, source_target_pairs={{0,2},{1,3},{2,0},{3,1},{4,6},{5,7},{6,4},{7,5},{8,10},{9,11},{10,... | collective-permute-start | bytes 786440 | tf_op jit(solution)/shard_map/ppermute | solution.py:18
  156.8 2.0 %collective-permute-start.9 = (bf16[512,256]{1,0:T(8,128)(2,1)S(1)}, bf16[512,256]{1,0:T(8,128)(2,1)S(1)}, u32[]{:S(2)}, u32[]{:S(2)}) collective-permute-start(bf16[512,256]{1,0:T(8,128)(2,1)S(1)} %get-tuple-element.7), channel_id=1, source_target_pairs={{0,3},{1,2},{2,1},{3,0},{4,7},{5,6},{6,5},{7,4},{8,11},{9,10},{10,... | collective-permute-start | bytes 786440 | tf_op jit(solution)/shard_map/ppermute | solution.py:18
  158.8 13.6 %hessian_rows.2.refs_2_ = bf16[2048,4096]{1,0:T(8,128)(2,1)} custom-call(bf16[1024,1024]{1,0:T(8,128)(2,1)} %bitcast.6.refs_0_, bf16[1024,4096]{1,0:T(8,128)(2,1)} %all-gather.2.cloned.1.call-done.cols_ref.refs_1_, bf16[2048,256]{1,0:T(8,128)(2,1)S(1)} %partial_product.1.refs_2_.refs_3_), custom_call_target="tpu_custom_call" | custom-call | flops 17179869184 | bytes 18874368 | tf_op jit(solution)/shard_map/hessian_rows/pallas_call | solution.py:303
  172.4 0.0 all-to-all-done
  172.4 13.6 %hessian_rows.3.refs_4_ = bf16[2048,4096]{1,0:T(8,128)(2,1)} custom-call(bf16[1024,1024]{1,0:T(8,128)(2,1)} %bitcast.4.refs_0_, bf16[1024,4096]{1,0:T(8,128)(2,1)} %all-gather.2.cloned.1.call-done.cols_ref.refs_1_, bf16[2048,4096]{1,0:T(8,128)(2,1)} %hessian_rows.2.refs_2_, ...), custom_call_target="tpu_custom_call", output_to_operand_aliasing={{}: (2, {})} | custom-call | flops 17179869184 | bytes 18874368 | tf_op jit(solution)/shard_map/hessian_rows/pallas_call | solution.py:303
  186.0 0.0 collective-permute-done.9.refs_3_
  186.0 0.7 copy-done.14
  186.7 0.1 copy-done.15
  186.8 0.1 copy-done.16
  186.9 2.1 %add_pieces.1 = f32[512,256]{1,0:T(8,128)} custom-call(bf16[512,256]{1,0:T(8,128)(2,1)} %get-tuple-element.10.refs_0_, bf16[512,256]{1,0:T(8,128)(2,1)} %copy-done.14, bf16[512,256]{1,0:T(8,128)(2,1)} %copy-done.15, bf16[512,256]{1,0:T(8,128)(2,1)} %copy-done.16, bf16[2048,4096]{1,0:T(8,128)(2,1)} %hessian_rows.3.refs_4_), custom_call_target="tpu_custom_call" | custom-call | bytes 1572864 | tf_op jit(solution)/shard_map/add_pieces/pallas_call | solution.py:328
  (23 shorter events, 0.0 us)
Async XLA Ops:
  7.2 115.4 %all-gather.2.cloned.1.call-start = ((), (), s32[]{:S(2)}) async-start(), calls=%async_computation.2 | async-start | bytes 9437184 | tf_op jit(solution)/shard_map/all_gather | solution.py:356
  13.1 34.1 %collective-permute-start.1 = (bf16[2,128,1152]{2,1,0:T(8,128)(2,1)}, bf16[2,128,1152]{2,1,0:T(8,128)(2,1)S(1)}, u32[]{:S(2)}, u32[]{:S(2)}) collective-permute-start(bf16[2,128,1152]{2,1,0:T(8,128)(2,1)} %take_chunk.2.refs_0_), channel_id=1, source_target_pairs={{0,2},{1,3},{2,0},{3,1},{4,6},{5,7},{6,4},{7,5},{8,10},{9,11},{10,... | collective-permute-start | bytes 1769480 | tf_op jit(solution)/shard_map/ppermute | solution.py:203
  17.1 34.3 %collective-permute-start = (bf16[2,128,1152]{2,1,0:T(8,128)(2,1)}, bf16[2,128,1152]{2,1,0:T(8,128)(2,1)S(1)}, u32[]{:S(2)}, u32[]{:S(2)}) collective-permute-start(bf16[2,128,1152]{2,1,0:T(8,128)(2,1)} %take_chunk.2.refs_0_), channel_id=1, source_target_pairs={{0,1},{1,0},{2,3},{3,2},{4,5},{5,4},{6,7},{7,6},{8,9},{9,8},{10,11... | collective-permute-start | bytes 1769480 | tf_op jit(solution)/shard_map/ppermute | solution.py:203
  18.7 32.7 %collective-permute-start.2 = (bf16[2,128,1152]{2,1,0:T(8,128)(2,1)}, bf16[2,128,1152]{2,1,0:T(8,128)(2,1)S(1)}, u32[]{:S(2)}, u32[]{:S(2)}) collective-permute-start(bf16[2,128,1152]{2,1,0:T(8,128)(2,1)} %take_chunk.2.refs_0_), channel_id=1, source_target_pairs={{1,2},{2,1},{5,6},{6,5},{9,10},{10,9},{13,14},{14,13},{17,18},{18,... | collective-permute-start | bytes 1769480 | tf_op jit(solution)/shard_map/ppermute | solution.py:203
  47.2 0.8 copy-start
  50.0 36.3 %copy-start.1 = (bf16[2,128,1152]{2,1,0:T(8,128)(2,1)S(1)}, bf16[2,128,1152]{2,1,0:T(8,128)(2,1)}, u32[]{:S(2)}) copy-start(bf16[2,128,1152]{2,1,0:T(8,128)(2,1)} %copy-done) | copy-start | bytes 1769476
  50.0 36.4 %copy-start.6 = (bf16[2,128,1152]{2,1,0:T(8,128)(2,1)S(1)}, bf16[2,128,1152]{2,1,0:T(8,128)(2,1)}, u32[]{:S(2)}) copy-start(bf16[2,128,1152]{2,1,0:T(8,128)(2,1)} %take_chunk.2.refs_0_) | copy-start | bytes 1769476
  50.0 16.5 %collective-permute-start.3 = (bf16[2,128,1152]{2,1,0:T(8,128)(2,1)}, bf16[2,128,1152]{2,1,0:T(8,128)(2,1)S(1)}, u32[]{:S(2)}, u32[]{:S(2)}) collective-permute-start(bf16[2,128,1152]{2,1,0:T(8,128)(2,1)} %relay.1), channel_id=1, source_target_pairs={{2,3},{1,0},{6,7},{5,4},{10,11},{9,8},{14,15},{13,12},{18,19},{17,... | collective-permute-start | bytes 1769480 | tf_op jit(solution)/shard_map/ppermute | solution.py:215
  51.4 0.8 copy-start.2
  52.2 0.8 copy-start.4
  55.1 40.3 %copy-start.7 = (bf16[2,128,1024]{2,1,0:T(8,128)(2,1)S(1)}, bf16[2,128,1024]{2,1,0:T(8,128)(2,1)}, u32[]{:S(2)}) copy-start(bf16[2,128,1024]{2,1,0:T(8,128)(2,1)} %take_chunk.3.refs_5_.refs_0_) | copy-start | bytes 1572868
  66.5 0.8 copy-start.8
  69.0 1.5 collective-permute-start.4
  71.3 5.6 %collective-permute-start.5 = (bf16[2,128,256]{2,1,0:T(8,128)(2,1)S(1)}, bf16[2,128,256]{2,1,0:T(8,128)(2,1)S(1)}, u32[]{:S(2)}, u32[]{:S(2)}) collective-permute-start(bf16[2,128,256]{2,1,0:T(8,128)(2,1)S(1)} %pad_maximum_fusion.2), channel_id=1, source_target_pairs={{0,8},{4,12},{8,0},{12,4},{16,24},{20,28},{24,16},{28,20},{1,9},{5... | collective-permute-start | bytes 393224 | tf_op jit(solution)/shard_map/ppermute | solution.py:18
  77.8 7.6 %collective-permute-start.6 = (bf16[4,128,256]{2,1,0:T(8,128)(2,1)S(1)}, bf16[4,128,256]{2,1,0:T(8,128)(2,1)S(1)}, u32[]{:S(2)}, u32[]{:S(2)}) collective-permute-start(bf16[4,128,256]{2,1,0:T(8,128)(2,1)S(1)} %pad_maximum_fusion.1), channel_id=1, source_target_pairs={{0,16},{4,20},{8,24},{12,28},{16,0},{20,4},{24,8},{28,12},{1,17},{... | collective-permute-start | bytes 786440 | tf_op jit(solution)/shard_map/ppermute | solution.py:18
  86.3 1.1 copy-start.3
  87.4 1.1 copy-start.5
  88.5 1.1 copy-start.9
  91.0 49.8 %all-to-all-start.1 = ((bf16[8,128,1024]{2,1,0:T(8,128)(2,1)}), bf16[8,128,1024]{2,1,0:T(8,128)(2,1)}, u32[]{:S(2)}, u32[]{:S(2)}) async-start(bf16[8,128,1024]{2,1,0:T(8,128)(2,1)} %bitcast.5), calls=%async_computation.1 | async-start | bytes 4194304 | tf_op jit(solution)/shard_map/all_to_all | solution.py:389
  95.4 25.8 %collective-permute-start.11 = (bf16[2,128,1024]{2,1,0:T(8,128)(2,1)S(1)}, bf16[2,128,1024]{2,1,0:T(8,128)(2,1)S(1)}, u32[]{:S(2)}, u32[]{:S(2)}) collective-permute-start(bf16[2,128,1024]{2,1,0:T(8,128)(2,1)S(1)} %copy-done.7), channel_id=1, source_target_pairs={{0,2},{1,3},{2,0},{3,1},{4,6},{5,7},{6,4},{7,5},{8,10},{9,11},{10,... | collective-permute-start | bytes 1572872 | tf_op jit(solution)/shard_map/ppermute | solution.py:203
  95.7 34.7 %collective-permute-start.10 = (bf16[2,128,1024]{2,1,0:T(8,128)(2,1)S(1)}, bf16[2,128,1024]{2,1,0:T(8,128)(2,1)S(1)}, u32[]{:S(2)}, u32[]{:S(2)}) collective-permute-start(bf16[2,128,1024]{2,1,0:T(8,128)(2,1)S(1)} %copy-done.7), channel_id=1, source_target_pairs={{0,1},{1,0},{2,3},{3,2},{4,5},{5,4},{6,7},{7,6},{8,9},{9,8},{10,11... | collective-permute-start | bytes 1572872 | tf_op jit(solution)/shard_map/ppermute | solution.py:203
  98.1 33.1 %collective-permute-start.12 = (bf16[2,128,1024]{2,1,0:T(8,128)(2,1)S(1)}, bf16[2,128,1024]{2,1,0:T(8,128)(2,1)}, u32[]{:S(2)}, u32[]{:S(2)}) collective-permute-start(bf16[2,128,1024]{2,1,0:T(8,128)(2,1)S(1)} %copy-done.7), channel_id=1, source_target_pairs={{1,2},{2,1},{5,6},{6,5},{9,10},{10,9},{13,14},{14,13},{17,18},{18,... | collective-permute-start | bytes 1572872 | tf_op jit(solution)/shard_map/ppermute | solution.py:203
  121.2 15.9 %collective-permute-start.13 = (bf16[2,128,1024]{2,1,0:T(8,128)(2,1)S(1)}, bf16[2,128,1024]{2,1,0:T(8,128)(2,1)}, u32[]{:S(2)}, u32[]{:S(2)}) collective-permute-start(bf16[2,128,1024]{2,1,0:T(8,128)(2,1)S(1)} %collective-permute-done.11.refs_2_), channel_id=1, source_target_pairs={{2,3},{1,0},{6,7},{5,4},{10,11},{9,8},{14,15},{13,12},{18,19},{17,... | collective-permute-start | bytes 1572872 | tf_op jit(solution)/shard_map/ppermute | solution.py:215
  129.1 1.3 copy-start.10
  130.4 0.8 copy-start.12
  131.2 14.0 %copy-start.11 = (bf16[4096,256]{1,0:T(8,128)(2,1)S(1)}, bf16[4096,256]{1,0:T(8,128)(2,1)}, u32[]{:S(2)}) copy-start(bf16[4096,256]{1,0:T(8,128)(2,1)} %copy-done.10) | copy-start | bytes 6291460
  137.2 1.0 copy-start.13
  140.8 31.6 %all-to-all-start = ((bf16[8,128,1024]{2,1,0:T(8,128)(2,1)}), bf16[8,128,1024]{2,1,0:T(8,128)(2,1)}, u32[]{:S(2)}, u32[]{:S(2)}) async-start(bf16[8,128,1024]{2,1,0:T(8,128)(2,1)} %bitcast.3), calls=%async_computation | async-start | bytes 4194304 | tf_op jit(solution)/shard_map/all_to_all | solution.py:389
  154.4 31.6 %collective-permute-start.7 = (bf16[512,256]{1,0:T(8,128)(2,1)S(1)}, bf16[512,256]{1,0:T(8,128)(2,1)S(1)}, u32[]{:S(2)}, u32[]{:S(2)}) collective-permute-start(bf16[512,256]{1,0:T(8,128)(2,1)S(1)} %get-tuple-element.9), channel_id=1, source_target_pairs={{0,1},{1,0},{2,3},{3,2},{4,5},{5,4},{6,7},{7,6},{8,9},{9,8},{10,11... | collective-permute-start | bytes 786440 | tf_op jit(solution)/shard_map/ppermute | solution.py:18
  154.4 31.6 %collective-permute-start.8 = (bf16[512,256]{1,0:T(8,128)(2,1)S(1)}, bf16[512,256]{1,0:T(8,128)(2,1)S(1)}, u32[]{:S(2)}, u32[]{:S(2)}) collective-permute-start(bf16[512,256]{1,0:T(8,128)(2,1)S(1)} %get-tuple-element.8), channel_id=1, source_target_pairs={{0,2},{1,3},{2,0},{3,1},{4,6},{5,7},{6,4},{7,5},{8,10},{9,11},{10,... | collective-permute-start | bytes 786440 | tf_op jit(solution)/shard_map/ppermute | solution.py:18
  156.8 29.2 %collective-permute-start.9 = (bf16[512,256]{1,0:T(8,128)(2,1)S(1)}, bf16[512,256]{1,0:T(8,128)(2,1)S(1)}, u32[]{:S(2)}, u32[]{:S(2)}) collective-permute-start(bf16[512,256]{1,0:T(8,128)(2,1)S(1)} %get-tuple-element.7), channel_id=1, source_target_pairs={{0,3},{1,2},{2,1},{3,0},{4,7},{5,6},{6,5},{7,4},{8,11},{9,10},{10,... | collective-permute-start | bytes 786440 | tf_op jit(solution)/shard_map/ppermute | solution.py:18
  186.0 0.7 copy-start.14
  186.0 0.8 copy-start.15
  186.0 0.9 copy-start.16
Sparse Core Ops, SparseCore 0:
  9.9 57.0 all-gather.1

commit v11 on v10

--- a/solution.py
+++ b/solution.py
@@ -371,10 +371,15 @@
         after = [blocks[near] for near, _ in sources if near] + [residual]
 
     where = narrow_index.reshape(1)
-    y_blocks = sum_tails(*chunks[0], where, height, [blocks[0] for blocks, _ in chunks[1:]])
+    later, later_at = chunks[1]
+    direct = [later[near] for near, _ in later_at if near]
+    y_blocks = sum_tails(*chunks[0], where, height, [later[0]] + direct[-1:])
     mask = 1
     while mask < wide_count:
-        y_blocks = jnp.concatenate([y_blocks, flip(y_blocks, "wide", mask)], axis=0)
+        sent = y_blocks
+        if 2 * mask == wide_count:
+            sent = relay(y_blocks, [later[later_at[narrow_count // 2][0]]])
+        y_blocks = jnp.concatenate([sent, flip(sent, "wide", mask)], axis=0)
         mask *= 2
 
     hr, gram = hr_and_gram(cols, y_blocks, wide_index.reshape(1), scale)
@@ -382,7 +387,7 @@
     row_chunks = []
     placed = []
     for chunk in range(CHUNKS):
-        after = placed[-1:] + [hr] if chunk else [y_blocks]
+        after = placed[-1:] + [hr] if chunk else [y_blocks] + direct
         every = place_blocks(*chunks[chunk], where, height, after)
         placed.append(every)
         every = every.reshape(narrow_count * split, tokens, height)

time: 197 us -> 204 us (1.036)
  starting transfers between devices: 29 us -> 54.5 us
  waiting for transfers between devices: 51.8 us -> 28.9 us
  local copies, waits for them, and re-layouts: 12.5 us -> 15.3 us
    ppermute x6, starting transfers between devices: 10.4 us -> 36.6 us  [exchange_blocks(): direct[mask] = lax.ppermute(mine, 'narrow', pairs) if pairs else None]
    ppermute x6, waiting for transfers between devices: 21.7 us -> 2.12 us  [exchange_blocks(): direct[mask] = lax.ppermute(mine, 'narrow', pairs) if pairs else None]
    all_to_all x2, waiting for transfers between devices: 0.01 us -> 8.21 us  [body(): lax.all_to_all(every, 'wide', split_axis=0, concat_axis=0, tiled=True)]
    ppermute x2, waiting for transfers between devices: 17.4 us -> 9.97 us  [exchange_blocks(): blocks.append(lax.ppermute(onward, 'narrow', pairs))]
    ppermute x6, waiting for transfers between devices: 12 us -> 7.89 us  [flip(): return lax.ppermute(value, axis, [(i, i ^ mask) for i in range(count)])]
    unnamed x35 -> x39, local copies, waits for them, and re-layouts: 11.8 us -> 14.3 us
  transfers between devices with their start and end apart: 17 -> 17, of which waited for: 6 -> 6; matrix products, arithmetic and copies ran while one was open for 4% -> 4% of each run, Pallas kernels for 41% -> 40%
where the time goes in v11:
time: 204 us; the launch traced here: 202 us
  Pallas kernels  83.1 us (41%)
  starting transfers between devices  54.5 us (27%)
  waiting for transfers between devices  28.9 us (14%)
  local copies, waits for them, and re-layouts  15.3 us (8%)
  between operations  14.3 us (7%)
  other arithmetic  3.42 us (2%)
  matrix products  3.03 us (1%)
    ppermute x6, starting transfers between devices, exchange_blocks(): direct[mask] = lax.ppermute(mine, 'narrow', pairs) if pairs else None  36.6 us
    pallas_call x1, Pallas kernels, residual_tile(): pl.pallas_call(residual_kernel, out_shape=jax.ShapeDtypeStruct((rows, fea...  26.5 us
    pallas_call x2, Pallas kernels, hessian_rows(): pl.pallas_call(kernel, out_shape=jax.ShapeDtypeStruct(shape, BF16), grid=...  26.5 us
    unnamed x39, local copies, waits for them, and re-layouts  14.3 us
    ppermute x2, waiting for transfers between devices, exchange_blocks(): blocks.append(lax.ppermute(onward, 'narrow', pairs))  9.97 us
    pallas_call x1, Pallas kernels, partial_product(): pl.pallas_call(product_kernel, out_shape=jax.ShapeDtypeStruct((rows, rank...  8.4 us
    all_to_all x2, waiting for transfers between devices, body(): lax.all_to_all(every, 'wide', split_axis=0, concat_axis=0, tiled=True)  8.21 us
    all_to_all x2, starting transfers between devices, body(): lax.all_to_all(every, 'wide', split_axis=0, concat_axis=0, tiled=True)  7.97 us
  transfers between devices with their start and end apart: 17, of which 6 were waited for; matrix products, arithmetic and copies ran while one was open for 4% of the time, Pallas kernels for 40%

profile of v11, /device:TPU:0, one launch (start us, length us, event | category | flops | bytes accessed | tf_op | source)
XLA Modules:
  0.0 202.5 jit_solution(4542982686579826520)
XLA Ops:
  7.2 0.0 all-gather.2.cloned.1.call-start
  7.2 0.7 all-gather.2.cloned.1.call-update
  7.9 3.0 %fusion.2.refs_0_ = f32[128,256]{1,0:T(8,128)} fusion(bf16[128,4096]{1,0:T(8,128)(2,1)} %activations_ref.3, bf16[16384,256]{1,0:T(8,128)(2,1)} %param.9, s32[]{:T(128)S(6)} %select_n.15), kind=kOutput, calls=%fused_computation.2 | convolution fusion | flops 268435456 | bytes 3276804 | tf_op jit(solution)/shard_map/dot_general | solution.py:359
  10.9 2.1 %take_chunk.2.refs_0_ = bf16[2,128,1152]{2,1,0:T(8,128)(2,1)} custom-call(bf16[128,4096]{1,0:T(8,128)(2,1)} %activations_ref.3, f32[128,256]{1,0:T(8,128)} %fusion.2.refs_0_), custom_call_target="tpu_custom_call" | custom-call | bytes 1048576 | tf_op jit(solution)/shard_map/take_chunk/pallas_call | solution.py:124
  13.1 4.0 %collective-permute-start.1 = (bf16[2,128,1152]{2,1,0:T(8,128)(2,1)}, bf16[2,128,1152]{2,1,0:T(8,128)(2,1)S(1)}, u32[]{:S(2)}, u32[]{:S(2)}) collective-permute-start(bf16[2,128,1152]{2,1,0:T(8,128)(2,1)} %take_chunk.2.refs_0_), channel_id=1, source_target_pairs={{0,2},{1,3},{2,0},{3,1},{4,6},{5,7},{6,4},{7,5},{8,10},{9,11},{10,... | collective-permute-start | bytes 1769480 | tf_op jit(solution)/shard_map/ppermute | solution.py:203
  17.1 1.6 collective-permute-start
  18.7 0.7 collective-permute-start.2
  19.4 1.3 copy.9.scales_ref
  20.7 26.5 %residual_tile.1.refs_0_.refs_3_.residual_ref = bf16[2048,4096]{1,0:T(8,128)(2,1)} custom-call(bf16[2048,4096]{1,0:T(8,128)(2,1)} %weight_ref.1, s32[2048,4096]{1,0:T(8,128)} %codes_ref.1, f32[2048,32]{1,0:T(8,128)S(1)} %copy.9.scales_ref), custom_call_target="tpu_custom_call" | custom-call | bytes 92274688 | tf_op jit(solution)/shard_map/residual_tile/pallas_call | solution.py:235
  47.2 0.0 collective-permute-done.1.value_ref.refs_1_.refs_2_
  47.2 0.8 copy-done
  48.1 1.9 relay.2
  50.0 1.4 collective-permute-start.3
  51.4 0.0 collective-permute-done.refs_0_.refs_1_
  51.4 0.0 collective-permute-done.2.refs_2_.refs_3_
  51.4 0.8 copy-done.2
  52.2 0.8 copy-done.4
  53.1 2.1 %take_chunk.3.refs_5_.refs_0_ = bf16[2,128,1024]{2,1,0:T(8,128)(2,1)} custom-call(bf16[128,4096]{1,0:T(8,128)(2,1)} %activations_ref.3, bf16[2,128,1152]{2,1,0:T(8,128)(2,1)} %copy-done.2, bf16[2,128,1152]{2,1,0:T(8,128)(2,1)} %copy-done, bf16[2,128,1152]{2,1,0:T(8,128)(2,1)} %copy-done.4, bf16[2048,4096]{1,0:T(8,128)(2,1)} %residual_tile.1.refs_0_.refs_3_.residual_ref), custom_call_target="tpu_custom_call" | custom-call | bytes 1048576 | tf_op jit(solution)/shard_map/take_chunk/pallas_call | solution.py:124
  55.1 0.7 collective-permute-start.4
  55.8 7.7 %collective-permute-start.7 = (bf16[2,128,1024]{2,1,0:T(8,128)(2,1)}, bf16[2,128,1024]{2,1,0:T(8,128)(2,1)S(1)}, u32[]{:S(2)}, u32[]{:S(2)}) collective-permute-start(bf16[2,128,1024]{2,1,0:T(8,128)(2,1)} %take_chunk.3.refs_5_.refs_0_), channel_id=1, source_target_pairs={{0,2},{1,3},{2,0},{3,1},{4,6},{5,7},{6,4},{7,5},{8,10},{9,11},{10,... | collective-permute-start | bytes 1572872 | tf_op jit(solution)/shard_map/ppermute | solution.py:203
  63.5 0.0 collective-permute-done.4.refs_6_.refs_8_.refs_3_
  63.5 3.0 %collective-permute-done.3.refs_4_ = bf16[2,128,1152]{2,1,0:T(8,128)(2,1)S(1)} collective-permute-done((bf16[2,128,1152]{2,1,0:T(8,128)(2,1)}, bf16[2,128,1152]{2,1,0:T(8,128)(2,1)S(1)}, u32[]{:S(2)}, u32[]{:S(2)}) %collective-permute-start.3) | collective-permute-done | bytes 589856 | tf_op jit(solution)/shard_map/ppermute | solution.py:215
  66.5 0.8 copy-done.14
  67.3 1.7 sum_tails.1
  69.0 0.0 collective-permute-start.5
  69.0 1.5 collective-permute-done.5
  70.5 0.9 pad_maximum_fusion.2
  71.3 1.3 collective-permute-start.6
  72.7 22.0 %collective-permute-start.12 = (bf16[2,128,1024]{2,1,0:T(8,128)(2,1)}, bf16[2,128,1024]{2,1,0:T(8,128)(2,1)S(1)}, u32[]{:S(2)}, u32[]{:S(2)}) collective-permute-start(bf16[2,128,1024]{2,1,0:T(8,128)(2,1)} %take_chunk.3.refs_5_.refs_0_), channel_id=1, source_target_pairs={{0,1},{1,0},{2,3},{3,2},{4,5},{5,4},{6,7},{7,6},{8,9},{9,8},{10,11... | collective-permute-start | bytes 1572872 | tf_op jit(solution)/shard_map/ppermute | solution.py:203
  94.7 1.6 pad_maximum_fusion.1.value_ref
  96.2 2.1 %collective-permute-done.7.refs_0_.refs_7_.refs_2_ = bf16[2,128,1024]{2,1,0:T(8,128)(2,1)S(1)} collective-permute-done((bf16[2,128,1024]{2,1,0:T(8,128)(2,1)}, bf16[2,128,1024]{2,1,0:T(8,128)(2,1)S(1)}, u32[]{:S(2)}, u32[]{:S(2)}) %collective-permute-start.7) | collective-permute-done | bytes 524320 | tf_op jit(solution)/shard_map/ppermute | solution.py:203
  98.3 0.8 copy-done.10
  99.2 1.7 relay.3
  100.9 1.5 collective-permute-start.8
  102.4 6.4 %collective-permute-done.8 = bf16[4,128,256]{2,1,0:T(8,128)(2,1)S(1)} collective-permute-done((bf16[4,128,256]{2,1,0:T(8,128)(2,1)}, bf16[4,128,256]{2,1,0:T(8,128)(2,1)S(1)}, u32[]{:S(2)}, u32[]{:S(2)}) %collective-permute-start.8) | collective-permute-done | bytes 262176 | tf_op jit(solution)/shard_map/ppermute | solution.py:18
  108.8 1.0 pad_maximum_fusion.y_ref.refs_5_
  109.8 1.1 copy-done.3
  110.9 1.1 copy-done.5
  112.0 1.0 copy-done.8
  113.0 1.0 copy-done.11
  114.0 1.1 copy-done.15
  115.1 1.4 place_blocks.2.refs_5_
  116.6 4.4 %all-to-all-start.1 = ((bf16[8,128,1024]{2,1,0:T(8,128)(2,1)}), bf16[8,128,1024]{2,1,0:T(8,128)(2,1)}, u32[]{:S(2)}, u32[]{:S(2)}) async-start(bf16[8,128,1024]{2,1,0:T(8,128)(2,1)} %bitcast.10), calls=%async_computation.1 | async-start | bytes 4194304 | tf_op jit(solution)/shard_map/all_to_all | solution.py:394
  121.0 0.0 copy-start.13
  121.0 1.4 collective-permute-start.13
  122.4 0.0 all-gather.2.cloned.1.call-done.cols_ref.refs_1_
  122.4 6.5 %hr_and_gram.1 = (bf16[4096,256]{1,0:T(8,128)(2,1)S(1)}, f32[256,256]{1,0:T(8,128)}) custom-call(s32[1]{0:T(128)} %bitcast.where_ref, bf16[1024,4096]{1,0:T(8,128)(2,1)} %all-gather.2.cloned.1.call-done.cols_ref.refs_1_, bf16[8,128,256]{2,1,0:T(8,128)(2,1)S(1)} %pad_maximum_fusion.y_ref.refs_5_), custom_call_target="tpu_custom_call" | custom-call | flops 4294967296 | bytes 16777216 | tf_op jit(solution)/shard_map/hr_and_gram/pallas_call | solution.py:48
  128.9 1.3 copy-done.16
  130.2 6.9 %collective-permute-done.13.refs_4_ = bf16[2,128,1024]{2,1,0:T(8,128)(2,1)S(1)} collective-permute-done((bf16[2,128,1024]{2,1,0:T(8,128)(2,1)S(1)}, bf16[2,128,1024]{2,1,0:T(8,128)(2,1)S(1)}, u32[]{:S(2)}, u32[]{:S(2)}) %collective-permute-start.13) | collective-permute-done | bytes 524320 | tf_op jit(solution)/shard_map/ppermute | solution.py:215
  137.2 2.2 %place_blocks.3 = bf16[4,2,128,1024]{3,2,1,0:T(8,128)(2,1)} custom-call(s32[1]{0:T(128)} %bitcast.1.where_ref, bf16[2,128,1024]{2,1,0:T(8,128)(2,1)S(1)} %copy-done.13, bf16[2,128,1024]{2,1,0:T(8,128)(2,1)S(1)} %collective-permute-done.12.refs_6_.refs_1_, bf16[2,128,1024]{2,1,0:T(8,128)(2,1)S(1)} %copy-done.12, bf16[2,128,1024]{2,1,0:T(8,128)(2,1)S(1)} %copy-done.9, ...), custom_call_target="tpu_custom_call" | custom-call | bytes 4194304 | tf_op jit(solution)/shard_map/place_blocks/pallas_call | solution.py:97
  139.4 8.2 %all-to-all-done.1 = bf16[8,128,1024]{2,1,0:T(8,128)(2,1)} async-done(((bf16[8,128,1024]{2,1,0:T(8,128)(2,1)}), bf16[8,128,1024]{2,1,0:T(8,128)(2,1)}, u32[]{:S(2)}, u32[]{:S(2)}) %all-to-all-start.1) | async-done | bytes 2097184 | tf_op jit(solution)/shard_map/all_to_all | solution.py:394
  147.6 3.6 %all-to-all-start = ((bf16[8,128,1024]{2,1,0:T(8,128)(2,1)}), bf16[8,128,1024]{2,1,0:T(8,128)(2,1)S(1)}, u32[]{:S(2)}, u32[]{:S(2)}) async-start(bf16[8,128,1024]{2,1,0:T(8,128)(2,1)} %bitcast.3), calls=%async_computation | async-start | bytes 4194304 | tf_op jit(solution)/shard_map/all_to_all | solution.py:394
  151.2 1.6 copy-done.17
  152.8 8.4 %partial_product.1.refs_2_.refs_3_ = bf16[2048,256]{1,0:T(8,128)(2,1)S(1)} custom-call(bf16[2048,4096]{1,0:T(8,128)(2,1)} %residual_tile.1.refs_0_.refs_3_.residual_ref, bf16[4096,256]{1,0:T(8,128)(2,1)S(1)} %copy-done.17), custom_call_target="tpu_custom_call" | custom-call | flops 8589934592 | bytes 25165824 | tf_op jit(solution)/shard_map/partial_product/pallas_call | solution.py:259
  161.2 1.0 constant_dynamic-slice_fusion
  162.2 3.3 %collective-permute-start.10 = (bf16[512,256]{1,0:T(8,128)(2,1)}, bf16[512,256]{1,0:T(8,128)(2,1)S(1)}, u32[]{:S(2)}, u32[]{:S(2)}) collective-permute-start(bf16[512,256]{1,0:T(8,128)(2,1)} %get-tuple-element.8), channel_id=1, source_target_pairs={{0,2},{1,3},{2,0},{3,1},{4,6},{5,7},{6,4},{7,5},{8,10},{9,11},{10,... | collective-permute-start | bytes 786440 | tf_op jit(solution)/shard_map/ppermute | solution.py:18
  165.5 0.9 collective-permute-start.11
  166.3 0.0 collective-permute-start.9
  166.3 13.6 %hessian_rows.2.refs_2_ = bf16[2048,4096]{1,0:T(8,128)(2,1)} custom-call(bf16[1024,1024]{1,0:T(8,128)(2,1)} %bitcast.6.refs_0_, bf16[1024,4096]{1,0:T(8,128)(2,1)} %all-gather.2.cloned.1.call-done.cols_ref.refs_1_, bf16[2048,256]{1,0:T(8,128)(2,1)S(1)} %partial_product.1.refs_2_.refs_3_), custom_call_target="tpu_custom_call" | custom-call | flops 17179869184 | bytes 18874368 | tf_op jit(solution)/shard_map/hessian_rows/pallas_call | solution.py:303
  179.9 12.9 %hessian_rows.3.refs_4_ = bf16[2048,4096]{1,0:T(8,128)(2,1)} custom-call(bf16[1024,1024]{1,0:T(8,128)(2,1)S(1)} %bitcast.9, bf16[1024,4096]{1,0:T(8,128)(2,1)} %all-gather.2.cloned.1.call-done.cols_ref.refs_1_, bf16[2048,4096]{1,0:T(8,128)(2,1)} %hessian_rows.2.refs_2_, ...), custom_call_target="tpu_custom_call", output_to_operand_aliasing={{}: (2, {})} | custom-call | flops 17179869184 | bytes 18874368 | tf_op jit(solution)/shard_map/hessian_rows/pallas_call | solution.py:303
  192.8 0.0 collective-permute-done.10.refs_2_
  192.8 0.0 collective-permute-done.9.refs_1_
  192.9 0.7 copy-done.18
  193.5 2.1 %add_pieces.1 = f32[512,256]{1,0:T(8,128)} custom-call(bf16[512,256]{1,0:T(8,128)(2,1)} %get-tuple-element.10.refs_0_, bf16[512,256]{1,0:T(8,128)(2,1)} %collective-permute-done.9.refs_1_, bf16[512,256]{1,0:T(8,128)(2,1)} %copy-done.18, bf16[512,256]{1,0:T(8,128)(2,1)} %collective-permute-done.11.refs_3_, bf16[2048,4096]{1,0:T(8,128)(2,1)} %hessian_rows.3.refs_4_), custom_call_target="tpu_custom_call" | custom-call | bytes 1572864 | tf_op jit(solution)/shard_map/add_pieces/pallas_call | solution.py:328
  (28 shorter events, 0.1 us)
Async XLA Ops:
  7.2 115.3 %all-gather.2.cloned.1.call-start = ((), (), s32[]{:S(2)}) async-start(), calls=%async_computation.2 | async-start | bytes 9437184 | tf_op jit(solution)/shard_map/all_gather | solution.py:356
  13.1 34.1 %collective-permute-start.1 = (bf16[2,128,1152]{2,1,0:T(8,128)(2,1)}, bf16[2,128,1152]{2,1,0:T(8,128)(2,1)S(1)}, u32[]{:S(2)}, u32[]{:S(2)}) collective-permute-start(bf16[2,128,1152]{2,1,0:T(8,128)(2,1)} %take_chunk.2.refs_0_), channel_id=1, source_target_pairs={{0,2},{1,3},{2,0},{3,1},{4,6},{5,7},{6,4},{7,5},{8,10},{9,11},{10,... | collective-permute-start | bytes 1769480 | tf_op jit(solution)/shard_map/ppermute | solution.py:203
  17.1 34.3 %collective-permute-start = (bf16[2,128,1152]{2,1,0:T(8,128)(2,1)}, bf16[2,128,1152]{2,1,0:T(8,128)(2,1)S(1)}, u32[]{:S(2)}, u32[]{:S(2)}) collective-permute-start(bf16[2,128,1152]{2,1,0:T(8,128)(2,1)} %take_chunk.2.refs_0_), channel_id=1, source_target_pairs={{0,1},{1,0},{2,3},{3,2},{4,5},{5,4},{6,7},{7,6},{8,9},{9,8},{10,11... | collective-permute-start | bytes 1769480 | tf_op jit(solution)/shard_map/ppermute | solution.py:203
  18.7 32.7 %collective-permute-start.2 = (bf16[2,128,1152]{2,1,0:T(8,128)(2,1)}, bf16[2,128,1152]{2,1,0:T(8,128)(2,1)S(1)}, u32[]{:S(2)}, u32[]{:S(2)}) collective-permute-start(bf16[2,128,1152]{2,1,0:T(8,128)(2,1)} %take_chunk.2.refs_0_), channel_id=1, source_target_pairs={{1,2},{2,1},{5,6},{6,5},{9,10},{10,9},{13,14},{14,13},{17,18},{18,... | collective-permute-start | bytes 1769480 | tf_op jit(solution)/shard_map/ppermute | solution.py:203
  47.2 0.8 copy-start
  50.0 59.8 %copy-start.1 = (bf16[2,128,1152]{2,1,0:T(8,128)(2,1)S(1)}, bf16[2,128,1152]{2,1,0:T(8,128)(2,1)}, u32[]{:S(2)}) copy-start(bf16[2,128,1152]{2,1,0:T(8,128)(2,1)} %copy-done) | copy-start | bytes 1769476
  50.0 59.9 %copy-start.6 = (bf16[2,128,1152]{2,1,0:T(8,128)(2,1)S(1)}, bf16[2,128,1152]{2,1,0:T(8,128)(2,1)}, u32[]{:S(2)}) copy-start(bf16[2,128,1152]{2,1,0:T(8,128)(2,1)} %take_chunk.2.refs_0_) | copy-start | bytes 1769476
  50.0 16.5 %collective-permute-start.3 = (bf16[2,128,1152]{2,1,0:T(8,128)(2,1)}, bf16[2,128,1152]{2,1,0:T(8,128)(2,1)S(1)}, u32[]{:S(2)}, u32[]{:S(2)}) collective-permute-start(bf16[2,128,1152]{2,1,0:T(8,128)(2,1)} %relay.2), channel_id=1, source_target_pairs={{2,3},{1,0},{6,7},{5,4},{10,11},{9,8},{14,15},{13,12},{18,19},{17,... | collective-permute-start | bytes 1769480 | tf_op jit(solution)/shard_map/ppermute | solution.py:215
  51.4 0.8 copy-start.2
  52.2 0.8 copy-start.4
  55.1 8.4 %collective-permute-start.4 = (bf16[2,128,1024]{2,1,0:T(8,128)(2,1)}, bf16[2,128,1024]{2,1,0:T(8,128)(2,1)S(1)}, u32[]{:S(2)}, u32[]{:S(2)}) collective-permute-start(bf16[2,128,1024]{2,1,0:T(8,128)(2,1)} %take_chunk.3.refs_5_.refs_0_), channel_id=1, source_target_pairs={{1,2},{2,1},{5,6},{6,5},{9,10},{10,9},{13,14},{14,13},{17,18},{18,... | collective-permute-start | bytes 1572872 | tf_op jit(solution)/shard_map/ppermute | solution.py:203
  55.8 42.5 %collective-permute-start.7 = (bf16[2,128,1024]{2,1,0:T(8,128)(2,1)}, bf16[2,128,1024]{2,1,0:T(8,128)(2,1)S(1)}, u32[]{:S(2)}, u32[]{:S(2)}) collective-permute-start(bf16[2,128,1024]{2,1,0:T(8,128)(2,1)} %take_chunk.3.refs_5_.refs_0_), channel_id=1, source_target_pairs={{0,2},{1,3},{2,0},{3,1},{4,6},{5,7},{6,4},{7,5},{8,10},{9,11},{10,... | collective-permute-start | bytes 1572872 | tf_op jit(solution)/shard_map/ppermute | solution.py:203
  63.5 3.0 %copy-start.7 = (bf16[2,128,1024]{2,1,0:T(8,128)(2,1)}, bf16[2,128,1024]{2,1,0:T(8,128)(2,1)S(1)}, u32[]{:S(2)}) copy-start(bf16[2,128,1024]{2,1,0:T(8,128)(2,1)S(1)} %collective-permute-done.4.refs_6_.refs_8_.refs_3_) | copy-start | bytes 1572868
  66.5 0.8 copy-start.14
  69.0 1.5 collective-permute-start.5
  71.3 23.3 %collective-permute-start.6 = (bf16[2,128,256]{2,1,0:T(8,128)(2,1)S(1)}, bf16[2,128,256]{2,1,0:T(8,128)(2,1)S(1)}, u32[]{:S(2)}, u32[]{:S(2)}) collective-permute-start(bf16[2,128,256]{2,1,0:T(8,128)(2,1)S(1)} %pad_maximum_fusion.2), channel_id=1, source_target_pairs={{0,8},{4,12},{8,0},{12,4},{16,24},{20,28},{24,16},{28,20},{1,9},{5... | collective-permute-start | bytes 393224 | tf_op jit(solution)/shard_map/ppermute | solution.py:18
  72.7 37.1 %collective-permute-start.12 = (bf16[2,128,1024]{2,1,0:T(8,128)(2,1)}, bf16[2,128,1024]{2,1,0:T(8,128)(2,1)S(1)}, u32[]{:S(2)}, u32[]{:S(2)}) collective-permute-start(bf16[2,128,1024]{2,1,0:T(8,128)(2,1)} %take_chunk.3.refs_5_.refs_0_), channel_id=1, source_target_pairs={{0,1},{1,0},{2,3},{3,2},{4,5},{5,4},{6,7},{7,6},{8,9},{9,8},{10,11... | collective-permute-start | bytes 1572872 | tf_op jit(solution)/shard_map/ppermute | solution.py:203
  98.3 0.8 copy-start.10
  100.9 20.1 %copy-start.12 = (bf16[2,128,1024]{2,1,0:T(8,128)(2,1)S(1)}, bf16[2,128,1024]{2,1,0:T(8,128)(2,1)}, u32[]{:S(2)}) copy-start(bf16[2,128,1024]{2,1,0:T(8,128)(2,1)} %copy-done.10) | copy-start | bytes 1572868
  100.9 7.9 %collective-permute-start.8 = (bf16[4,128,256]{2,1,0:T(8,128)(2,1)}, bf16[4,128,256]{2,1,0:T(8,128)(2,1)S(1)}, u32[]{:S(2)}, u32[]{:S(2)}) collective-permute-start(bf16[4,128,256]{2,1,0:T(8,128)(2,1)} %relay.3), channel_id=1, source_target_pairs={{0,16},{4,20},{8,24},{12,28},{16,0},{20,4},{24,8},{28,12},{1,17},{... | collective-permute-start | bytes 786440 | tf_op jit(solution)/shard_map/ppermute | solution.py:18
  109.8 1.1 copy-start.3
  110.9 1.1 copy-start.5
  112.0 1.0 copy-start.8
  113.0 1.0 copy-start.11
  114.0 1.1 copy-start.15
  116.6 31.0 %all-to-all-start.1 = ((bf16[8,128,1024]{2,1,0:T(8,128)(2,1)}), bf16[8,128,1024]{2,1,0:T(8,128)(2,1)}, u32[]{:S(2)}, u32[]{:S(2)}) async-start(bf16[8,128,1024]{2,1,0:T(8,128)(2,1)} %bitcast.10), calls=%async_computation.1 | async-start | bytes 4194304 | tf_op jit(solution)/shard_map/all_to_all | solution.py:394
  120.9 16.2 %copy-start.9 = (bf16[2,128,1024]{2,1,0:T(8,128)(2,1)S(1)}, bf16[2,128,1024]{2,1,0:T(8,128)(2,1)}, u32[]{:S(2)}) copy-start(bf16[2,128,1024]{2,1,0:T(8,128)(2,1)} %copy-done.7) | copy-start | bytes 1572868
  121.0 16.2 %copy-start.13 = (bf16[2,128,1024]{2,1,0:T(8,128)(2,1)S(1)}, bf16[2,128,1024]{2,1,0:T(8,128)(2,1)}, u32[]{:S(2)}) copy-start(bf16[2,128,1024]{2,1,0:T(8,128)(2,1)} %take_chunk.3.refs_5_.refs_0_) | copy-start | bytes 1572868
  121.0 16.2 %collective-permute-start.13 = (bf16[2,128,1024]{2,1,0:T(8,128)(2,1)S(1)}, bf16[2,128,1024]{2,1,0:T(8,128)(2,1)S(1)}, u32[]{:S(2)}, u32[]{:S(2)}) collective-permute-start(bf16[2,128,1024]{2,1,0:T(8,128)(2,1)S(1)} %copy-done.12), channel_id=1, source_target_pairs={{2,3},{1,0},{6,7},{5,4},{10,11},{9,8},{14,15},{13,12},{18,19},{17,... | collective-permute-start | bytes 1572872 | tf_op jit(solution)/shard_map/ppermute | solution.py:215
  128.9 1.3 copy-start.16
  147.6 32.3 %all-to-all-start = ((bf16[8,128,1024]{2,1,0:T(8,128)(2,1)}), bf16[8,128,1024]{2,1,0:T(8,128)(2,1)S(1)}, u32[]{:S(2)}, u32[]{:S(2)}) async-start(bf16[8,128,1024]{2,1,0:T(8,128)(2,1)} %bitcast.3), calls=%async_computation | async-start | bytes 4194304 | tf_op jit(solution)/shard_map/all_to_all | solution.py:394
  151.2 1.6 copy-start.17
  162.2 30.6 %collective-permute-start.10 = (bf16[512,256]{1,0:T(8,128)(2,1)}, bf16[512,256]{1,0:T(8,128)(2,1)S(1)}, u32[]{:S(2)}, u32[]{:S(2)}) collective-permute-start(bf16[512,256]{1,0:T(8,128)(2,1)} %get-tuple-element.8), channel_id=1, source_target_pairs={{0,2},{1,3},{2,0},{3,1},{4,6},{5,7},{6,4},{7,5},{8,10},{9,11},{10,... | collective-permute-start | bytes 786440 | tf_op jit(solution)/shard_map/ppermute | solution.py:18
  165.5 27.4 %collective-permute-start.11 = (bf16[512,256]{1,0:T(8,128)(2,1)}, bf16[512,256]{1,0:T(8,128)(2,1)}, u32[]{:S(2)}, u32[]{:S(2)}) collective-permute-start(bf16[512,256]{1,0:T(8,128)(2,1)} %get-tuple-element.7), channel_id=1, source_target_pairs={{0,3},{1,2},{2,1},{3,0},{4,7},{5,6},{6,5},{7,4},{8,11},{9,10},{10,... | collective-permute-start | bytes 786440 | tf_op jit(solution)/shard_map/ppermute | solution.py:18
  166.3 26.5 %collective-permute-start.9 = (bf16[512,256]{1,0:T(8,128)(2,1)}, bf16[512,256]{1,0:T(8,128)(2,1)}, u32[]{:S(2)}, u32[]{:S(2)}) collective-permute-start(bf16[512,256]{1,0:T(8,128)(2,1)} %get-tuple-element.9), channel_id=1, source_target_pairs={{0,1},{1,0},{2,3},{3,2},{4,5},{5,4},{6,7},{7,6},{8,9},{9,8},{10,11... | collective-permute-start | bytes 786440 | tf_op jit(solution)/shard_map/ppermute | solution.py:18
  192.8 0.7 copy-start.18
Sparse Core Ops, SparseCore 0:
  9.9 57.0 all-gather.1

commit v12 on v10

--- a/solution.py
+++ b/solution.py
@@ -27,19 +27,16 @@
     return pl.CostEstimate(flops=int(flops), bytes_accessed=int(moved), transcendentals=0)
 
 
-def hr_and_gram(cols, y_blocks, where, scale):
-    count, tokens, rank = y_blocks.shape
+def hr_and_gram(cols, y, scale):
+    tokens, rank = y.shape
     features = cols.shape[1]
     tile = min(1024, features)
 
-    def kernel(where_ref, cols_ref, y_ref, hr_ref, gram_ref, order_ref, turned_ref):
+    def kernel(cols_ref, y_ref, hr_ref, gram_ref, turned_ref):
         @pl.when(pl.program_id(0) == 0)
         def _():
-            for mask in range(count):
-                at = pl.multiple_of((where_ref[0] ^ mask) * tokens, tokens)
-                order_ref[pl.ds(at, tokens), :] = y_ref[mask]
-            turned_ref[...] = order_ref[...].T
-            gram = jnp.dot(turned_ref[...], order_ref[...], preferred_element_type=F32)
+            turned_ref[...] = y_ref[...].T
+            gram = jnp.dot(turned_ref[...], y_ref[...], preferred_element_type=F32)
             gram_ref[...] = gram * scale
 
         total = jnp.dot(turned_ref[...], cols_ref[...], preferred_element_type=F32) * scale
@@ -53,22 +50,18 @@
         ),
         grid=(features // tile,),
         in_specs=[
-            pl.BlockSpec(memory_space=pltpu.SMEM),
-            pl.BlockSpec((count * tokens, tile), lambda j: (0, j)),
-            pl.BlockSpec(y_blocks.shape, lambda j: (0, 0, 0)),
+            pl.BlockSpec((tokens, tile), lambda j: (0, j)),
+            pl.BlockSpec((tokens, rank), lambda j: (0, 0)),
         ],
         out_specs=(
             pl.BlockSpec((tile, rank), lambda j: (j, 0)),
             pl.BlockSpec((rank, rank), lambda j: (0, 0)),
         ),
-        scratch_shapes=[
-            pltpu.VMEM((count * tokens, rank), BF16),
-            pltpu.VMEM((rank, count * tokens), BF16),
-        ],
-        cost_estimate=cost(4 * count * tokens * features * rank, 4 * cols.size),
+        scratch_shapes=[pltpu.VMEM((rank, tokens), BF16)],
+        cost_estimate=cost(4 * tokens * features * rank, 4 * cols.size),
         compiler_params=pltpu.CompilerParams(vmem_limit_bytes=48 * MIB),
         name="hr_and_gram",
-    )(where, cols, y_blocks)
+    )(cols, y)
 
 
 def place_kernel(sources, where_ref, *refs):
@@ -371,18 +364,15 @@
         after = [blocks[near] for near, _ in sources if near] + [residual]
 
     where = narrow_index.reshape(1)
-    y_blocks = sum_tails(*chunks[0], where, height, [blocks[0] for blocks, _ in chunks[1:]])
-    mask = 1
-    while mask < wide_count:
-        y_blocks = jnp.concatenate([y_blocks, flip(y_blocks, "wide", mask)], axis=0)
-        mask *= 2
-
-    hr, gram = hr_and_gram(cols, y_blocks, wide_index.reshape(1), scale)
+    product = sum_tails(*chunks[0], where, height, [blocks[0] for blocks, _ in chunks[1:]])
+    y = lax.all_gather(product, "wide", axis=0, tiled=True)
+    y = y.reshape(tokens * wide_count, y.shape[2])
+    hr, gram = hr_and_gram(cols, y, scale)
 
     row_chunks = []
     placed = []
     for chunk in range(CHUNKS):
-        after = placed[-1:] + [hr] if chunk else [y_blocks]
+        after = placed[-1:] + [hr] if chunk else []
         every = place_blocks(*chunks[chunk], where, height, after)
         placed.append(every)
         every = every.reshape(narrow_count * split, tokens, height)

time: 197 us -> 186 us (0.944)
  waiting for transfers between devices: 51.8 us -> 37.8 us
  blocking collectives: 0 us -> 10.4 us
  local copies, waits for them, and re-layouts: 12.5 us -> 9.71 us
  other arithmetic: 2.61 us -> 0 us
    ppermute x6 -> x3, waiting for transfers between devices: 12 us -> 0.01 us  [flip(): return lax.ppermute(value, axis, [(i, i ^ mask) for i in range(count)])]
    all_gather x0 -> x1, blocking collectives: none -> 10.4 us  [body(): y = lax.all_gather(product, 'wide', axis=0, tiled=True)]
    unnamed x35 -> x33, local copies, waits for them, and re-layouts: 11.8 us -> 8.84 us
    concatenate x3 -> x0, other arithmetic: 2.61 us -> none  [body(): y_blocks = jnp.concatenate([y_blocks, flip(y_blocks, 'wide', mask)], axis=0)]
    ppermute x2, waiting for transfers between devices: 17.4 us -> 15.1 us  [exchange_blocks(): blocks.append(lax.ppermute(onward, 'narrow', pairs))]
    ppermute x6 -> x3, starting transfers between devices: 7.15 us -> 5.8 us  [flip(): return lax.ppermute(value, axis, [(i, i ^ mask) for i in range(count)])]
  transfers between devices with their start and end apart: 17 -> 14, of which waited for: 6 -> 2; matrix products, arithmetic and copies ran while one was open for 4% -> 3% of each run, Pallas kernels for 41% -> 43%
where the time goes in v12:
time: 186 us; the launch traced here: 185 us
  Pallas kernels  82.6 us (44%)
  waiting for transfers between devices  37.8 us (20%)
  starting transfers between devices  27.5 us (15%)
  between operations  14.2 us (8%)
  blocking collectives  10.4 us (6%)
  local copies, waits for them, and re-layouts  9.71 us (5%)
  matrix products  3.03 us (2%)
    pallas_call x2, Pallas kernels, hessian_rows(): pl.pallas_call(kernel, out_shape=jax.ShapeDtypeStruct(shape, BF16), grid=...  27.2 us
    pallas_call x1, Pallas kernels, residual_tile(): pl.pallas_call(residual_kernel, out_shape=jax.ShapeDtypeStruct((rows, fea...  26.5 us
    ppermute x6, waiting for transfers between devices, exchange_blocks(): direct[mask] = lax.ppermute(mine, 'narrow', pairs) if pairs else None  22 us
    ppermute x2, waiting for transfers between devices, exchange_blocks(): blocks.append(lax.ppermute(onward, 'narrow', pairs))  15.1 us
    ppermute x6, starting transfers between devices, exchange_blocks(): direct[mask] = lax.ppermute(mine, 'narrow', pairs) if pairs else None  10.4 us
    all_gather x1, blocking collectives, body(): y = lax.all_gather(product, 'wide', axis=0, tiled=True)  10.4 us
    unnamed x33, local copies, waits for them, and re-layouts  8.84 us
    all_to_all x2, starting transfers between devices, body(): lax.all_to_all(every, 'wide', split_axis=0, concat_axis=0, tiled=True)  8.72 us
  transfers between devices with their start and end apart: 14, of which 2 were waited for; matrix products, arithmetic and copies ran while one was open for 3% of the time, Pallas kernels for 43%

profile of v12, /device:TPU:0, one launch (start us, length us, event | category | flops | bytes accessed | tf_op | source)
XLA Modules:
  0.0 185.3 jit_solution(16989836685310536018)
XLA Ops:
  7.2 0.0 all-gather.2.cloned.1.call-start
  7.2 0.7 all-gather.2.cloned.1.call-update
  7.9 3.0 %fusion.2.refs_0_ = f32[128,256]{1,0:T(8,128)} fusion(bf16[128,4096]{1,0:T(8,128)(2,1)} %activations_ref.3, bf16[16384,256]{1,0:T(8,128)(2,1)} %param.9, s32[]{:T(128)S(6)} %select_n.15), kind=kOutput, calls=%fused_computation.2 | convolution fusion | flops 268435456 | bytes 3276804 | tf_op jit(solution)/shard_map/dot_general | solution.py:352
  10.9 2.1 %take_chunk.2.refs_0_ = bf16[2,128,1152]{2,1,0:T(8,128)(2,1)} custom-call(bf16[128,4096]{1,0:T(8,128)(2,1)} %activations_ref.3, f32[128,256]{1,0:T(8,128)} %fusion.2.refs_0_), custom_call_target="tpu_custom_call" | custom-call | bytes 1048576 | tf_op jit(solution)/shard_map/take_chunk/pallas_call | solution.py:117
  13.1 4.0 %collective-permute-start.1 = (bf16[2,128,1152]{2,1,0:T(8,128)(2,1)}, bf16[2,128,1152]{2,1,0:T(8,128)(2,1)S(1)}, u32[]{:S(2)}, u32[]{:S(2)}) collective-permute-start(bf16[2,128,1152]{2,1,0:T(8,128)(2,1)} %take_chunk.2.refs_0_), channel_id=1, source_target_pairs={{0,2},{1,3},{2,0},{3,1},{4,6},{5,7},{6,4},{7,5},{8,10},{9,11},{10,... | collective-permute-start | bytes 1769480 | tf_op jit(solution)/shard_map/ppermute | solution.py:196
  17.1 1.6 collective-permute-start
  18.7 0.7 collective-permute-start.2
  19.4 1.3 copy.11.scales_ref
  20.7 26.5 %residual_tile.1.refs_0_.refs_3_.residual_ref = bf16[2048,4096]{1,0:T(8,128)(2,1)} custom-call(bf16[2048,4096]{1,0:T(8,128)(2,1)} %weight_ref.1, s32[2048,4096]{1,0:T(8,128)} %codes_ref.1, f32[2048,32]{1,0:T(8,128)S(1)} %copy.11.scales_ref), custom_call_target="tpu_custom_call" | custom-call | bytes 92274688 | tf_op jit(solution)/shard_map/residual_tile/pallas_call | solution.py:228
  47.2 0.0 collective-permute-done.1.value_ref.refs_1_.refs_2_
  47.2 0.8 copy-done
  48.0 2.0 %relay.1 = bf16[2,128,1152]{2,1,0:T(8,128)(2,1)} custom-call(bf16[2,128,1152]{2,1,0:T(8,128)(2,1)} %copy-done, bf16[2048,4096]{1,0:T(8,128)(2,1)} %residual_tile.1.refs_0_.refs_3_.residual_ref), custom_call_target="tpu_custom_call" | custom-call | bytes 1179648 | tf_op jit(solution)/shard_map/relay/pallas_call | solution.py:176
  50.0 1.3 collective-permute-start.3
  51.3 0.0 collective-permute-done.refs_0_.refs_1_
  51.3 0.0 copy-start.2
  51.3 0.0 collective-permute-done.2.refs_2_.refs_3_
  51.3 0.0 copy-start.3
  51.3 15.1 %collective-permute-done.3.refs_4_ = bf16[2,128,1152]{2,1,0:T(8,128)(2,1)S(1)} collective-permute-done((bf16[2,128,1152]{2,1,0:T(8,128)(2,1)}, bf16[2,128,1152]{2,1,0:T(8,128)(2,1)S(1)}, u32[]{:S(2)}, u32[]{:S(2)}) %collective-permute-start.3) | collective-permute-done | bytes 589856 | tf_op jit(solution)/shard_map/ppermute | solution.py:208
  66.4 0.0 copy-done.4
  66.4 1.3 copy-done.1
  67.7 1.5 place_blocks.2.refs_5_
  69.2 4.4 %all-to-all-start.1 = ((bf16[8,128,1024]{2,1,0:T(8,128)(2,1)}), bf16[8,128,1024]{2,1,0:T(8,128)(2,1)}, u32[]{:S(2)}, u32[]{:S(2)}) async-start(bf16[8,128,1024]{2,1,0:T(8,128)(2,1)} %bitcast.5), calls=%async_computation.1 | async-start | bytes 4194304 | tf_op jit(solution)/shard_map/all_to_all | solution.py:379
  73.5 0.0 copy-done.2
  73.5 0.0 copy-done.3
  73.6 2.1 %take_chunk.3.refs_5_.refs_0_ = bf16[2,128,1024]{2,1,0:T(8,128)(2,1)} custom-call(bf16[128,4096]{1,0:T(8,128)(2,1)} %activations_ref.3, bf16[2,128,1152]{2,1,0:T(8,128)(2,1)} %copy-done.2, bf16[2,128,1152]{2,1,0:T(8,128)(2,1)} %copy-done, bf16[2,128,1152]{2,1,0:T(8,128)(2,1)} %copy-done.3, bf16[2048,4096]{1,0:T(8,128)(2,1)} %residual_tile.1.refs_0_.refs_3_.residual_ref), custom_call_target="tpu_custom_call" | custom-call | bytes 1048576 | tf_op jit(solution)/shard_map/take_chunk/pallas_call | solution.py:117
  75.6 0.0 copy-done.6
  75.6 0.3 collective-permute-start.8
  75.9 2.4 %collective-permute-start.7 = (bf16[2,128,1024]{2,1,0:T(8,128)(2,1)}, bf16[2,128,1024]{2,1,0:T(8,128)(2,1)S(1)}, u32[]{:S(2)}, u32[]{:S(2)}) collective-permute-start(bf16[2,128,1024]{2,1,0:T(8,128)(2,1)} %take_chunk.3.refs_5_.refs_0_), channel_id=1, source_target_pairs={{0,1},{1,0},{2,3},{3,2},{4,5},{5,4},{6,7},{7,6},{8,9},{9,8},{10,11... | collective-permute-start | bytes 1572872 | tf_op jit(solution)/shard_map/ppermute | solution.py:196
  78.3 1.4 collective-permute-start.9
  79.8 22.0 %collective-permute-done.8.refs_2_ = bf16[2,128,1024]{2,1,0:T(8,128)(2,1)S(1)} collective-permute-done((bf16[2,128,1024]{2,1,0:T(8,128)(2,1)}, bf16[2,128,1024]{2,1,0:T(8,128)(2,1)S(1)}, u32[]{:S(2)}, u32[]{:S(2)}) %collective-permute-start.8) | collective-permute-done | bytes 524320 | tf_op jit(solution)/shard_map/ppermute | solution.py:196
  101.8 1.3 collective-permute-start.10
  103.1 1.7 sum_tails.1
  104.7 10.4 %all_gather.7 = bf16[8,128,256]{2,1,0:T(8,128)(2,1)S(1)} all-gather(bf16[1,128,256]{2,1,0:T(8,128)(2,1)} %sum_tails.1), channel_id=1, replica_groups=mesh['wide'=8,'narrow'=4] {'wide'}, dimensions={0}, use_global_device_ids=true | all-gather | bytes 589824 | tf_op jit(solution)/shard_map/all_gather | solution.py:368
  115.2 6.4 %hr_and_gram.1 = (bf16[4096,256]{1,0:T(8,128)(2,1)S(1)}, f32[256,256]{1,0:T(8,128)}) custom-call(bf16[1024,4096]{1,0:T(8,128)(2,1)} %all-gather.2.cloned.1.call-done.cols_ref.refs_1_, bf16[1024,256]{1,0:T(8,128)(2,1)S(1)} %bitcast.9), custom_call_target="tpu_custom_call" | custom-call | flops 4294967296 | bytes 16777216 | tf_op jit(solution)/shard_map/hr_and_gram/pallas_call | solution.py:45
  121.6 1.3 copy-done.7
  122.9 0.0 collective-permute-done.7.refs_1_
  122.9 0.8 copy-done.11
  123.8 0.0 collective-permute-done.9.refs_3_
  123.8 0.0 collective-permute-done.10.refs_4_
  123.8 0.0 copy-done.5
  123.8 0.0 copy-start.12
  123.8 1.2 copy-done.12
  125.0 2.6 %place_blocks.3 = bf16[4,2,128,1024]{3,2,1,0:T(8,128)(2,1)} custom-call(s32[1]{0:T(128)} %bitcast.where_ref, bf16[2,128,1024]{2,1,0:T(8,128)(2,1)S(1)} %copy-done.5, bf16[2,128,1024]{2,1,0:T(8,128)(2,1)S(1)} %copy-done.12, bf16[2,128,1024]{2,1,0:T(8,128)(2,1)S(1)} %collective-permute-done.8.refs_2_, bf16[2,128,1024]{2,1,0:T(8,128)(2,1)} %collective-permute-done.9.refs_3_, ...), custom_call_target="tpu_custom_call" | custom-call | bytes 4194304 | tf_op jit(solution)/shard_map/place_blocks/pallas_call | solution.py:90
  127.6 0.0 all-to-all-done.1
  127.6 4.3 %all-to-all-start = ((bf16[8,128,1024]{2,1,0:T(8,128)(2,1)}), bf16[8,128,1024]{2,1,0:T(8,128)(2,1)}, u32[]{:S(2)}, u32[]{:S(2)}) async-start(bf16[8,128,1024]{2,1,0:T(8,128)(2,1)} %bitcast.3), calls=%async_computation | async-start | bytes 4194304 | tf_op jit(solution)/shard_map/all_to_all | solution.py:379
  132.0 0.0 copy-done.8
  132.0 8.4 %partial_product.1.refs_2_.refs_3_ = bf16[2048,256]{1,0:T(8,128)(2,1)S(1)} custom-call(bf16[2048,4096]{1,0:T(8,128)(2,1)} %residual_tile.1.refs_0_.refs_3_.residual_ref, bf16[4096,256]{1,0:T(8,128)(2,1)S(1)} %copy-done.8), custom_call_target="tpu_custom_call" | custom-call | flops 8589934592 | bytes 25165824 | tf_op jit(solution)/shard_map/partial_product/pallas_call | solution.py:252
  140.4 0.9 constant_dynamic-slice_fusion
  141.3 3.4 %collective-permute-start.4 = (bf16[512,256]{1,0:T(8,128)(2,1)S(1)}, bf16[512,256]{1,0:T(8,128)(2,1)S(1)}, u32[]{:S(2)}, u32[]{:S(2)}) collective-permute-start(bf16[512,256]{1,0:T(8,128)(2,1)S(1)} %get-tuple-element.9), channel_id=1, source_target_pairs={{0,1},{1,0},{2,3},{3,2},{4,5},{5,4},{6,7},{7,6},{8,9},{9,8},{10,11... | collective-permute-start | bytes 786440 | tf_op jit(solution)/shard_map/ppermute | solution.py:18
  144.7 0.2 collective-permute-start.5
  145.0 2.1 %collective-permute-start.6 = (bf16[512,256]{1,0:T(8,128)(2,1)S(1)}, bf16[512,256]{1,0:T(8,128)(2,1)S(1)}, u32[]{:S(2)}, u32[]{:S(2)}) collective-permute-start(bf16[512,256]{1,0:T(8,128)(2,1)S(1)} %get-tuple-element.7), channel_id=1, source_target_pairs={{0,3},{1,2},{2,1},{3,0},{4,7},{5,6},{6,5},{7,4},{8,11},{9,10},{10,... | collective-permute-start | bytes 786440 | tf_op jit(solution)/shard_map/ppermute | solution.py:18
  147.1 0.0 copy-done.9
  147.1 13.6 %hessian_rows.2.refs_2_ = bf16[2048,4096]{1,0:T(8,128)(2,1)} custom-call(bf16[1024,1024]{1,0:T(8,128)(2,1)} %bitcast.6.refs_0_, bf16[1024,4096]{1,0:T(8,128)(2,1)} %all-gather.2.cloned.1.call-done.cols_ref.refs_1_, bf16[2048,256]{1,0:T(8,128)(2,1)S(1)} %partial_product.1.refs_2_.refs_3_), custom_call_target="tpu_custom_call" | custom-call | flops 17179869184 | bytes 18874368 | tf_op jit(solution)/shard_map/hessian_rows/pallas_call | solution.py:296
  160.7 0.0 all-to-all-done
  160.7 1.2 copy-done.10
  161.9 13.6 %hessian_rows.3.refs_4_ = bf16[2048,4096]{1,0:T(8,128)(2,1)} custom-call(bf16[1024,1024]{1,0:T(8,128)(2,1)} %bitcast.4.refs_0_, bf16[1024,4096]{1,0:T(8,128)(2,1)} %all-gather.2.cloned.1.call-done.cols_ref.refs_1_, bf16[2048,4096]{1,0:T(8,128)(2,1)} %hessian_rows.2.refs_2_, bf16[2048,256]{1,0:T(8,128)(2,1)S(1)} %copy-done.10), custom_call_target="tpu_custom_call", output_to_operand_aliasing={{}: (2, {})} | custom-call | flops 17179869184 | bytes 18874368 | tf_op jit(solution)/shard_map/hessian_rows/pallas_call | solution.py:296
  175.5 0.0 collective-permute-done.4.refs_1_
  175.5 0.0 collective-permute-done.5.refs_2_
  175.5 0.0 copy-start.14
  175.5 0.0 collective-permute-done.6.refs_3_
  175.5 0.7 copy-done.13
  176.2 0.1 copy-done.14
  176.3 0.1 copy-done.15
  176.4 2.1 %add_pieces.1 = f32[512,256]{1,0:T(8,128)} custom-call(bf16[512,256]{1,0:T(8,128)(2,1)} %get-tuple-element.10.refs_0_, bf16[512,256]{1,0:T(8,128)(2,1)} %copy-done.13, bf16[512,256]{1,0:T(8,128)(2,1)} %copy-done.14, bf16[512,256]{1,0:T(8,128)(2,1)} %copy-done.15, bf16[2048,4096]{1,0:T(8,128)(2,1)} %hessian_rows.3.refs_4_), custom_call_target="tpu_custom_call" | custom-call | bytes 1572864 | tf_op jit(solution)/shard_map/add_pieces/pallas_call | solution.py:321
  (13 shorter events, 0.0 us)
Async XLA Ops:
  7.2 108.0 %all-gather.2.cloned.1.call-start = ((), (), s32[]{:S(2)}) async-start(), calls=%async_computation.2 | async-start | bytes 9437184 | tf_op jit(solution)/shard_map/all_gather | solution.py:349
  13.1 34.1 %collective-permute-start.1 = (bf16[2,128,1152]{2,1,0:T(8,128)(2,1)}, bf16[2,128,1152]{2,1,0:T(8,128)(2,1)S(1)}, u32[]{:S(2)}, u32[]{:S(2)}) collective-permute-start(bf16[2,128,1152]{2,1,0:T(8,128)(2,1)} %take_chunk.2.refs_0_), channel_id=1, source_target_pairs={{0,2},{1,3},{2,0},{3,1},{4,6},{5,7},{6,4},{7,5},{8,10},{9,11},{10,... | collective-permute-start | bytes 1769480 | tf_op jit(solution)/shard_map/ppermute | solution.py:196
  17.1 34.2 %collective-permute-start = (bf16[2,128,1152]{2,1,0:T(8,128)(2,1)}, bf16[2,128,1152]{2,1,0:T(8,128)(2,1)S(1)}, u32[]{:S(2)}, u32[]{:S(2)}) collective-permute-start(bf16[2,128,1152]{2,1,0:T(8,128)(2,1)} %take_chunk.2.refs_0_), channel_id=1, source_target_pairs={{0,1},{1,0},{2,3},{3,2},{4,5},{5,4},{6,7},{7,6},{8,9},{9,8},{10,11... | collective-permute-start | bytes 1769480 | tf_op jit(solution)/shard_map/ppermute | solution.py:196
  18.7 32.6 %collective-permute-start.2 = (bf16[2,128,1152]{2,1,0:T(8,128)(2,1)}, bf16[2,128,1152]{2,1,0:T(8,128)(2,1)S(1)}, u32[]{:S(2)}, u32[]{:S(2)}) collective-permute-start(bf16[2,128,1152]{2,1,0:T(8,128)(2,1)} %take_chunk.2.refs_0_), channel_id=1, source_target_pairs={{1,2},{2,1},{5,6},{6,5},{9,10},{10,9},{13,14},{14,13},{17,18},{18,... | collective-permute-start | bytes 1769480 | tf_op jit(solution)/shard_map/ppermute | solution.py:196
  47.2 19.2 %copy-start.4 = (bf16[2,128,1152]{2,1,0:T(8,128)(2,1)S(1)}, bf16[2,128,1152]{2,1,0:T(8,128)(2,1)}, u32[]{:S(2)}) copy-start(bf16[2,128,1152]{2,1,0:T(8,128)(2,1)} %take_chunk.2.refs_0_) | copy-start | bytes 1769476
  47.2 0.8 copy-start
  50.0 16.4 %collective-permute-start.3 = (bf16[2,128,1152]{2,1,0:T(8,128)(2,1)}, bf16[2,128,1152]{2,1,0:T(8,128)(2,1)S(1)}, u32[]{:S(2)}, u32[]{:S(2)}) collective-permute-start(bf16[2,128,1152]{2,1,0:T(8,128)(2,1)} %relay.1), channel_id=1, source_target_pairs={{2,3},{1,0},{6,7},{5,4},{10,11},{9,8},{14,15},{13,12},{18,19},{17,... | collective-permute-start | bytes 1769480 | tf_op jit(solution)/shard_map/ppermute | solution.py:208
  51.3 22.3 %copy-start.2 = (bf16[2,128,1152]{2,1,0:T(8,128)(2,1)}, bf16[2,128,1152]{2,1,0:T(8,128)(2,1)S(1)}, u32[]{:S(2)}) copy-start(bf16[2,128,1152]{2,1,0:T(8,128)(2,1)S(1)} %collective-permute-done.refs_0_.refs_1_) | copy-start | bytes 1769476
  51.3 22.3 %copy-start.3 = (bf16[2,128,1152]{2,1,0:T(8,128)(2,1)}, bf16[2,128,1152]{2,1,0:T(8,128)(2,1)S(1)}, u32[]{:S(2)}) copy-start(bf16[2,128,1152]{2,1,0:T(8,128)(2,1)S(1)} %collective-permute-done.2.refs_2_.refs_3_) | copy-start | bytes 1769476
  66.4 9.3 %copy-start.6 = (bf16[2,128,1152]{2,1,0:T(8,128)(2,1)}, bf16[2,128,1152]{2,1,0:T(8,128)(2,1)S(1)}, u32[]{:S(2)}) copy-start(bf16[2,128,1152]{2,1,0:T(8,128)(2,1)S(1)} %collective-permute-done.3.refs_4_) | copy-start | bytes 1769476
  66.4 1.3 copy-start.1
  69.2 58.5 %all-to-all-start.1 = ((bf16[8,128,1024]{2,1,0:T(8,128)(2,1)}), bf16[8,128,1024]{2,1,0:T(8,128)(2,1)}, u32[]{:S(2)}, u32[]{:S(2)}) async-start(bf16[8,128,1024]{2,1,0:T(8,128)(2,1)} %bitcast.5), calls=%async_computation.1 | async-start | bytes 4194304 | tf_op jit(solution)/shard_map/all_to_all | solution.py:379
  75.6 26.1 %collective-permute-start.8 = (bf16[2,128,1024]{2,1,0:T(8,128)(2,1)}, bf16[2,128,1024]{2,1,0:T(8,128)(2,1)S(1)}, u32[]{:S(2)}, u32[]{:S(2)}) collective-permute-start(bf16[2,128,1024]{2,1,0:T(8,128)(2,1)} %take_chunk.3.refs_5_.refs_0_), channel_id=1, source_target_pairs={{0,2},{1,3},{2,0},{3,1},{4,6},{5,7},{6,4},{7,5},{8,10},{9,11},{10,... | collective-permute-start | bytes 1572872 | tf_op jit(solution)/shard_map/ppermute | solution.py:196
  75.9 47.0 %collective-permute-start.7 = (bf16[2,128,1024]{2,1,0:T(8,128)(2,1)}, bf16[2,128,1024]{2,1,0:T(8,128)(2,1)S(1)}, u32[]{:S(2)}, u32[]{:S(2)}) collective-permute-start(bf16[2,128,1024]{2,1,0:T(8,128)(2,1)} %take_chunk.3.refs_5_.refs_0_), channel_id=1, source_target_pairs={{0,1},{1,0},{2,3},{3,2},{4,5},{5,4},{6,7},{7,6},{8,9},{9,8},{10,11... | collective-permute-start | bytes 1572872 | tf_op jit(solution)/shard_map/ppermute | solution.py:196
  78.3 45.4 %collective-permute-start.9 = (bf16[2,128,1024]{2,1,0:T(8,128)(2,1)}, bf16[2,128,1024]{2,1,0:T(8,128)(2,1)}, u32[]{:S(2)}, u32[]{:S(2)}) collective-permute-start(bf16[2,128,1024]{2,1,0:T(8,128)(2,1)} %take_chunk.3.refs_5_.refs_0_), channel_id=1, source_target_pairs={{1,2},{2,1},{5,6},{6,5},{9,10},{10,9},{13,14},{14,13},{17,18},{18,... | collective-permute-start | bytes 1572872 | tf_op jit(solution)/shard_map/ppermute | solution.py:196
  101.8 22.0 %collective-permute-start.10 = (bf16[2,128,1024]{2,1,0:T(8,128)(2,1)S(1)}, bf16[2,128,1024]{2,1,0:T(8,128)(2,1)}, u32[]{:S(2)}, u32[]{:S(2)}) collective-permute-start(bf16[2,128,1024]{2,1,0:T(8,128)(2,1)S(1)} %collective-permute-done.8.refs_2_), channel_id=1, source_target_pairs={{2,3},{1,0},{6,7},{5,4},{10,11},{9,8},{14,15},{13,12},{18,19},{17,... | collective-permute-start | bytes 1572872 | tf_op jit(solution)/shard_map/ppermute | solution.py:208
  104.7 19.0 %copy-start.5 = (bf16[2,128,1024]{2,1,0:T(8,128)(2,1)S(1)}, bf16[2,128,1024]{2,1,0:T(8,128)(2,1)}, u32[]{:S(2)}) copy-start(bf16[2,128,1024]{2,1,0:T(8,128)(2,1)} %take_chunk.3.refs_5_.refs_0_) | copy-start | bytes 1572868
  121.6 1.3 copy-start.7
  122.9 0.8 copy-start.11
  123.8 8.2 %copy-start.8 = (bf16[4096,256]{1,0:T(8,128)(2,1)S(1)}, bf16[4096,256]{1,0:T(8,128)(2,1)}, u32[]{:S(2)}) copy-start(bf16[4096,256]{1,0:T(8,128)(2,1)} %copy-done.7) | copy-start | bytes 6291460
  123.8 1.2 copy-start.12
  127.6 33.1 %all-to-all-start = ((bf16[8,128,1024]{2,1,0:T(8,128)(2,1)}), bf16[8,128,1024]{2,1,0:T(8,128)(2,1)}, u32[]{:S(2)}, u32[]{:S(2)}) async-start(bf16[8,128,1024]{2,1,0:T(8,128)(2,1)} %bitcast.3), calls=%async_computation | async-start | bytes 4194304 | tf_op jit(solution)/shard_map/all_to_all | solution.py:379
  140.4 6.7 %copy-start.9 = (bf16[2048,256]{1,0:T(8,128)(2,1)}, bf16[2048,256]{1,0:T(8,128)(2,1)S(1)}, u32[]{:S(2)}) copy-start(bf16[2048,256]{1,0:T(8,128)(2,1)S(1)} %partial_product.1.refs_2_.refs_3_) | copy-start | bytes 3145732
  141.3 34.2 %collective-permute-start.4 = (bf16[512,256]{1,0:T(8,128)(2,1)S(1)}, bf16[512,256]{1,0:T(8,128)(2,1)S(1)}, u32[]{:S(2)}, u32[]{:S(2)}) collective-permute-start(bf16[512,256]{1,0:T(8,128)(2,1)S(1)} %get-tuple-element.9), channel_id=1, source_target_pairs={{0,1},{1,0},{2,3},{3,2},{4,5},{5,4},{6,7},{7,6},{8,9},{9,8},{10,11... | collective-permute-start | bytes 786440 | tf_op jit(solution)/shard_map/ppermute | solution.py:18
  144.7 30.8 %collective-permute-start.5 = (bf16[512,256]{1,0:T(8,128)(2,1)S(1)}, bf16[512,256]{1,0:T(8,128)(2,1)S(1)}, u32[]{:S(2)}, u32[]{:S(2)}) collective-permute-start(bf16[512,256]{1,0:T(8,128)(2,1)S(1)} %get-tuple-element.8), channel_id=1, source_target_pairs={{0,2},{1,3},{2,0},{3,1},{4,6},{5,7},{6,4},{7,5},{8,10},{9,11},{10,... | collective-permute-start | bytes 786440 | tf_op jit(solution)/shard_map/ppermute | solution.py:18
  145.0 30.5 %collective-permute-start.6 = (bf16[512,256]{1,0:T(8,128)(2,1)S(1)}, bf16[512,256]{1,0:T(8,128)(2,1)S(1)}, u32[]{:S(2)}, u32[]{:S(2)}) collective-permute-start(bf16[512,256]{1,0:T(8,128)(2,1)S(1)} %get-tuple-element.7), channel_id=1, source_target_pairs={{0,3},{1,2},{2,1},{3,0},{4,7},{5,6},{6,5},{7,4},{8,11},{9,10},{10,... | collective-permute-start | bytes 786440 | tf_op jit(solution)/shard_map/ppermute | solution.py:18
  160.7 1.2 copy-start.10
  175.5 0.7 copy-start.13
  175.5 0.8 copy-start.14
  175.5 0.9 copy-start.15
Sparse Core Ops, SparseCore 0:
  9.9 57.0 all-gather.1

commit v13 on v12

--- a/solution.py
+++ b/solution.py
@@ -364,7 +364,9 @@
         after = [blocks[near] for near, _ in sources if near] + [residual]
 
     where = narrow_index.reshape(1)
-    product = sum_tails(*chunks[0], where, height, [blocks[0] for blocks, _ in chunks[1:]])
+    later, later_at = chunks[1]
+    direct = [later[near] for near, _ in later_at if near]
+    product = sum_tails(*chunks[0], where, height, [later[0]] + direct[-1:])
     y = lax.all_gather(product, "wide", axis=0, tiled=True)
     y = y.reshape(tokens * wide_count, y.shape[2])
     hr, gram = hr_and_gram(cols, y, scale)
@@ -372,7 +374,7 @@
     row_chunks = []
     placed = []
     for chunk in range(CHUNKS):
-        after = placed[-1:] + [hr] if chunk else []
+        after = placed[-1:] + [hr] if chunk else [product]
         every = place_blocks(*chunks[chunk], where, height, after)
         placed.append(every)
         every = every.reshape(narrow_count * split, tokens, height)

time: 186 us -> 192 us (1.032)
  starting transfers between devices: 27.5 us -> 34.2 us
  local copies, waits for them, and re-layouts: 9.71 us -> 13.2 us
  waiting for transfers between devices: 37.8 us -> 35 us
    ppermute x6, starting transfers between devices: 10.4 us -> 18.5 us  [exchange_blocks(): direct[mask] = lax.ppermute(mine, 'narrow', pairs) if pairs else None]
    ppermute x2, waiting for transfers between devices: 15.1 us -> 10.6 us  [exchange_blocks(): blocks.append(lax.ppermute(onward, 'narrow', pairs))]
    unnamed x33 -> x35, local copies, waits for them, and re-layouts: 8.84 us -> 12.2 us
  transfers between devices with their start and end apart: 14 -> 14, of which waited for: 2 -> 2; matrix products, arithmetic and copies ran while one was open for 3% -> 3% of each run, Pallas kernels for 43% -> 41%
where the time goes in v13:
time: 192 us; the launch traced here: 191 us
  Pallas kernels  81.4 us (42%)
  waiting for transfers between devices  35 us (18%)
  starting transfers between devices  34.2 us (18%)
  between operations  14.2 us (7%)
  local copies, waits for them, and re-layouts  13.2 us (7%)
  blocking collectives  10 us (5%)
  matrix products  3.03 us (2%)
    pallas_call x1, Pallas kernels, residual_tile(): pl.pallas_call(residual_kernel, out_shape=jax.ShapeDtypeStruct((rows, fea...  26.5 us
    pallas_call x2, Pallas kernels, hessian_rows(): pl.pallas_call(kernel, out_shape=jax.ShapeDtypeStruct(shape, BF16), grid=...  26.5 us
    ppermute x6, waiting for transfers between devices, exchange_blocks(): direct[mask] = lax.ppermute(mine, 'narrow', pairs) if pairs else None  23.8 us
    ppermute x6, starting transfers between devices, exchange_blocks(): direct[mask] = lax.ppermute(mine, 'narrow', pairs) if pairs else None  18.5 us
    unnamed x35, local copies, waits for them, and re-layouts  12.2 us
    ppermute x2, waiting for transfers between devices, exchange_blocks(): blocks.append(lax.ppermute(onward, 'narrow', pairs))  10.6 us
    all_gather x1, blocking collectives, body(): y = lax.all_gather(product, 'wide', axis=0, tiled=True)  10 us
    pallas_call x1, Pallas kernels, partial_product(): pl.pallas_call(product_kernel, out_shape=jax.ShapeDtypeStruct((rows, rank...  8.41 us
  transfers between devices with their start and end apart: 14, of which 2 were waited for; matrix products, arithmetic and copies ran while one was open for 3% of the time, Pallas kernels for 41%

profile of v13, /device:TPU:0, one launch (start us, length us, event | category | flops | bytes accessed | tf_op | source)
XLA Modules:
  0.0 191.2 jit_solution(17150501461077584283)
XLA Ops:
  7.2 0.0 all-gather.2.cloned.1.call-start
  7.2 0.7 all-gather.2.cloned.1.call-update
  7.9 3.0 %fusion.2.refs_0_ = f32[128,256]{1,0:T(8,128)} fusion(bf16[128,4096]{1,0:T(8,128)(2,1)} %activations_ref.3, bf16[16384,256]{1,0:T(8,128)(2,1)} %param.9, s32[]{:T(128)S(6)} %select_n.15), kind=kOutput, calls=%fused_computation.2 | convolution fusion | flops 268435456 | bytes 3276804 | tf_op jit(solution)/shard_map/dot_general | solution.py:352
  10.9 2.1 %take_chunk.2.refs_0_ = bf16[2,128,1152]{2,1,0:T(8,128)(2,1)} custom-call(bf16[128,4096]{1,0:T(8,128)(2,1)} %activations_ref.3, f32[128,256]{1,0:T(8,128)} %fusion.2.refs_0_), custom_call_target="tpu_custom_call" | custom-call | bytes 1048576 | tf_op jit(solution)/shard_map/take_chunk/pallas_call | solution.py:117
  13.1 4.0 %collective-permute-start.1 = (bf16[2,128,1152]{2,1,0:T(8,128)(2,1)}, bf16[2,128,1152]{2,1,0:T(8,128)(2,1)S(1)}, u32[]{:S(2)}, u32[]{:S(2)}) collective-permute-start(bf16[2,128,1152]{2,1,0:T(8,128)(2,1)} %take_chunk.2.refs_0_), channel_id=1, source_target_pairs={{0,2},{1,3},{2,0},{3,1},{4,6},{5,7},{6,4},{7,5},{8,10},{9,11},{10,... | collective-permute-start | bytes 1769480 | tf_op jit(solution)/shard_map/ppermute | solution.py:196
  17.1 1.6 collective-permute-start
  18.7 0.7 collective-permute-start.2
  19.4 1.3 copy.11.scales_ref
  20.7 26.5 %residual_tile.1.refs_0_.refs_3_.residual_ref = bf16[2048,4096]{1,0:T(8,128)(2,1)} custom-call(bf16[2048,4096]{1,0:T(8,128)(2,1)} %weight_ref.1, s32[2048,4096]{1,0:T(8,128)} %codes_ref.1, f32[2048,32]{1,0:T(8,128)S(1)} %copy.11.scales_ref), custom_call_target="tpu_custom_call" | custom-call | bytes 92274688 | tf_op jit(solution)/shard_map/residual_tile/pallas_call | solution.py:228
  47.2 0.0 collective-permute-done.1.value_ref.refs_1_.refs_2_
  47.2 0.8 copy-done
  48.1 1.9 %relay.1 = bf16[2,128,1152]{2,1,0:T(8,128)(2,1)} custom-call(bf16[2,128,1152]{2,1,0:T(8,128)(2,1)} %copy-done, bf16[2048,4096]{1,0:T(8,128)(2,1)} %residual_tile.1.refs_0_.refs_3_.residual_ref), custom_call_target="tpu_custom_call" | custom-call | bytes 1179648 | tf_op jit(solution)/shard_map/relay/pallas_call | solution.py:176
  50.0 1.4 collective-permute-start.3
  51.4 0.0 collective-permute-done.refs_0_.refs_1_
  51.4 0.0 copy-start.2
  51.4 0.0 collective-permute-done.2.refs_2_.refs_3_
  51.4 0.8 copy-done.2
  52.2 0.8 copy-done.4
  53.1 2.1 %take_chunk.3.refs_5_.refs_0_ = bf16[2,128,1024]{2,1,0:T(8,128)(2,1)} custom-call(bf16[128,4096]{1,0:T(8,128)(2,1)} %activations_ref.3, bf16[2,128,1152]{2,1,0:T(8,128)(2,1)} %copy-done.2, bf16[2,128,1152]{2,1,0:T(8,128)(2,1)} %copy-done, bf16[2,128,1152]{2,1,0:T(8,128)(2,1)} %copy-done.4, bf16[2048,4096]{1,0:T(8,128)(2,1)} %residual_tile.1.refs_0_.refs_3_.residual_ref), custom_call_target="tpu_custom_call" | custom-call | bytes 1048576 | tf_op jit(solution)/shard_map/take_chunk/pallas_call | solution.py:117
  55.1 0.8 collective-permute-start.4
  55.9 0.0 collective-permute-done.4.refs_6_.refs_3_
  56.0 0.0 copy-start.12
  56.0 10.6 %collective-permute-done.3.refs_4_ = bf16[2,128,1152]{2,1,0:T(8,128)(2,1)S(1)} collective-permute-done((bf16[2,128,1152]{2,1,0:T(8,128)(2,1)}, bf16[2,128,1152]{2,1,0:T(8,128)(2,1)S(1)}, u32[]{:S(2)}, u32[]{:S(2)}) %collective-permute-start.3) | collective-permute-done | bytes 589856 | tf_op jit(solution)/shard_map/ppermute | solution.py:208
  66.5 0.0 copy-done.12
  66.5 0.8 copy-done.8
  67.3 1.7 sum_tails.1.refs_5_
  69.0 0.0 copy-done.1
  69.0 0.0 copy-done.6
  69.0 1.1 copy-done.3
  70.1 1.1 copy-done.5
  71.2 1.1 copy-done.9
  72.2 0.8 copy-done.14
  73.1 1.5 place_blocks.2.refs_5_
  74.5 4.4 %all-to-all-start.1 = ((bf16[8,128,1024]{2,1,0:T(8,128)(2,1)}), bf16[8,128,1024]{2,1,0:T(8,128)(2,1)}, u32[]{:S(2)}, u32[]{:S(2)}) async-start(bf16[8,128,1024]{2,1,0:T(8,128)(2,1)} %bitcast.5), calls=%async_computation.1 | async-start | bytes 4194304 | tf_op jit(solution)/shard_map/all_to_all | solution.py:381
  78.9 0.0 copy-done.7
  78.9 0.0 copy-start.13
  78.9 11.3 %collective-permute-start.9 = (bf16[2,128,1024]{2,1,0:T(8,128)(2,1)S(1)}, bf16[2,128,1024]{2,1,0:T(8,128)(2,1)S(1)}, u32[]{:S(2)}, u32[]{:S(2)}) collective-permute-start(bf16[2,128,1024]{2,1,0:T(8,128)(2,1)S(1)} %copy-done.7), channel_id=1, source_target_pairs={{0,2},{1,3},{2,0},{3,1},{4,6},{5,7},{6,4},{7,5},{8,10},{9,11},{10,... | collective-permute-start | bytes 1572872 | tf_op jit(solution)/shard_map/ppermute | solution.py:196
  90.3 0.0 collective-permute-start.8
  90.3 23.8 %collective-permute-done.9.refs_2_ = bf16[2,128,1024]{2,1,0:T(8,128)(2,1)S(1)} collective-permute-done((bf16[2,128,1024]{2,1,0:T(8,128)(2,1)S(1)}, bf16[2,128,1024]{2,1,0:T(8,128)(2,1)S(1)}, u32[]{:S(2)}, u32[]{:S(2)}) %collective-permute-start.9) | collective-permute-done | bytes 524320 | tf_op jit(solution)/shard_map/ppermute | solution.py:196
  114.0 1.3 collective-permute-start.10
  115.3 0.0 copy-done.15
  115.4 10.0 %all_gather.7 = bf16[8,128,256]{2,1,0:T(8,128)(2,1)S(1)} all-gather(bf16[1,128,256]{2,1,0:T(8,128)(2,1)S(1)} %copy-done.15), channel_id=1, replica_groups=mesh['wide'=8,'narrow'=4] {'wide'}, dimensions={0}, use_global_device_ids=true | all-gather | bytes 589824 | tf_op jit(solution)/shard_map/all_gather | solution.py:370
  125.4 6.4 %hr_and_gram.1 = (bf16[4096,256]{1,0:T(8,128)(2,1)S(1)}, f32[256,256]{1,0:T(8,128)}) custom-call(bf16[1024,4096]{1,0:T(8,128)(2,1)} %all-gather.2.cloned.1.call-done.cols_ref.refs_1_, bf16[1024,256]{1,0:T(8,128)(2,1)S(1)} %bitcast.10), custom_call_target="tpu_custom_call" | custom-call | flops 4294967296 | bytes 16777216 | tf_op jit(solution)/shard_map/hr_and_gram/pallas_call | solution.py:45
  131.8 1.3 copy-done.10
  133.1 0.0 collective-permute-done.8.refs_1_
  133.1 0.0 collective-permute-done.10.refs_4_
  133.1 0.0 copy-done.13
  133.2 2.2 %place_blocks.3 = bf16[4,2,128,1024]{3,2,1,0:T(8,128)(2,1)} custom-call(s32[1]{0:T(128)} %bitcast.where_ref, bf16[2,128,1024]{2,1,0:T(8,128)(2,1)S(1)} %copy-done.7, bf16[2,128,1024]{2,1,0:T(8,128)(2,1)S(1)} %collective-permute-done.8.refs_1_, bf16[2,128,1024]{2,1,0:T(8,128)(2,1)S(1)} %collective-permute-done.9.refs_2_, ...), custom_call_target="tpu_custom_call" | custom-call | bytes 4194304 | tf_op jit(solution)/shard_map/place_blocks/pallas_call | solution.py:90
  135.3 0.0 all-to-all-done.1
  135.3 3.6 %all-to-all-start = ((bf16[8,128,1024]{2,1,0:T(8,128)(2,1)}), bf16[8,128,1024]{2,1,0:T(8,128)(2,1)S(1)}, u32[]{:S(2)}, u32[]{:S(2)}) async-start(bf16[8,128,1024]{2,1,0:T(8,128)(2,1)} %bitcast.3), calls=%async_computation | async-start | bytes 4194304 | tf_op jit(solution)/shard_map/all_to_all | solution.py:381
  139.0 1.6 copy-done.11
  140.6 8.4 %partial_product.1.refs_2_.refs_3_ = bf16[2048,256]{1,0:T(8,128)(2,1)S(1)} custom-call(bf16[2048,4096]{1,0:T(8,128)(2,1)} %residual_tile.1.refs_0_.refs_3_.residual_ref, bf16[4096,256]{1,0:T(8,128)(2,1)S(1)} %copy-done.11), custom_call_target="tpu_custom_call" | custom-call | flops 8589934592 | bytes 25165824 | tf_op jit(solution)/shard_map/partial_product/pallas_call | solution.py:252
  149.0 1.0 constant_dynamic-slice_fusion
  150.0 2.7 %collective-permute-start.5 = (bf16[512,256]{1,0:T(8,128)(2,1)}, bf16[512,256]{1,0:T(8,128)(2,1)S(1)}, u32[]{:S(2)}, u32[]{:S(2)}) collective-permute-start(bf16[512,256]{1,0:T(8,128)(2,1)} %get-tuple-element.9), channel_id=1, source_target_pairs={{0,1},{1,0},{2,3},{3,2},{4,5},{5,4},{6,7},{7,6},{8,9},{9,8},{10,11... | collective-permute-start | bytes 786440 | tf_op jit(solution)/shard_map/ppermute | solution.py:18
  152.7 0.0 collective-permute-start.6
  152.7 2.4 %collective-permute-start.7 = (bf16[512,256]{1,0:T(8,128)(2,1)}, bf16[512,256]{1,0:T(8,128)(2,1)}, u32[]{:S(2)}, u32[]{:S(2)}) collective-permute-start(bf16[512,256]{1,0:T(8,128)(2,1)} %get-tuple-element.7), channel_id=1, source_target_pairs={{0,3},{1,2},{2,1},{3,0},{4,7},{5,6},{6,5},{7,4},{8,11},{9,10},{10,... | collective-permute-start | bytes 786440 | tf_op jit(solution)/shard_map/ppermute | solution.py:18
  155.0 13.6 %hessian_rows.2.refs_2_ = bf16[2048,4096]{1,0:T(8,128)(2,1)} custom-call(bf16[1024,1024]{1,0:T(8,128)(2,1)} %bitcast.6.refs_0_, bf16[1024,4096]{1,0:T(8,128)(2,1)} %all-gather.2.cloned.1.call-done.cols_ref.refs_1_, bf16[2048,256]{1,0:T(8,128)(2,1)S(1)} %partial_product.1.refs_2_.refs_3_), custom_call_target="tpu_custom_call" | custom-call | flops 17179869184 | bytes 18874368 | tf_op jit(solution)/shard_map/hessian_rows/pallas_call | solution.py:296
  168.6 0.0 all-to-all-done
  168.6 12.9 %hessian_rows.3.refs_4_ = bf16[2048,4096]{1,0:T(8,128)(2,1)} custom-call(bf16[1024,1024]{1,0:T(8,128)(2,1)S(1)} %bitcast.9, bf16[1024,4096]{1,0:T(8,128)(2,1)} %all-gather.2.cloned.1.call-done.cols_ref.refs_1_, bf16[2048,4096]{1,0:T(8,128)(2,1)} %hessian_rows.2.refs_2_, ...), custom_call_target="tpu_custom_call", output_to_operand_aliasing={{}: (2, {})} | custom-call | flops 17179869184 | bytes 18874368 | tf_op jit(solution)/shard_map/hessian_rows/pallas_call | solution.py:296
  181.5 0.0 collective-permute-done.5.refs_1_
  181.5 0.0 collective-permute-done.6.refs_2_
  181.5 0.0 collective-permute-done.7.refs_3_
  181.6 0.7 copy-done.16
  182.2 2.1 %add_pieces.1 = f32[512,256]{1,0:T(8,128)} custom-call(bf16[512,256]{1,0:T(8,128)(2,1)} %get-tuple-element.10.refs_0_, bf16[512,256]{1,0:T(8,128)(2,1)} %copy-done.16, bf16[512,256]{1,0:T(8,128)(2,1)} %collective-permute-done.6.refs_2_, bf16[512,256]{1,0:T(8,128)(2,1)} %collective-permute-done.7.refs_3_, bf16[2048,4096]{1,0:T(8,128)(2,1)} %hessian_rows.3.refs_4_), custom_call_target="tpu_custom_call" | custom-call | bytes 1572864 | tf_op jit(solution)/shard_map/add_pieces/pallas_call | solution.py:321
  (15 shorter events, 0.0 us)
Async XLA Ops:
  7.2 118.2 %all-gather.2.cloned.1.call-start = ((), (), s32[]{:S(2)}) async-start(), calls=%async_computation.2 | async-start | bytes 9437184 | tf_op jit(solution)/shard_map/all_gather | solution.py:349
  13.1 34.1 %collective-permute-start.1 = (bf16[2,128,1152]{2,1,0:T(8,128)(2,1)}, bf16[2,128,1152]{2,1,0:T(8,128)(2,1)S(1)}, u32[]{:S(2)}, u32[]{:S(2)}) collective-permute-start(bf16[2,128,1152]{2,1,0:T(8,128)(2,1)} %take_chunk.2.refs_0_), channel_id=1, source_target_pairs={{0,2},{1,3},{2,0},{3,1},{4,6},{5,7},{6,4},{7,5},{8,10},{9,11},{10,... | collective-permute-start | bytes 1769480 | tf_op jit(solution)/shard_map/ppermute | solution.py:196
  17.1 34.3 %collective-permute-start = (bf16[2,128,1152]{2,1,0:T(8,128)(2,1)}, bf16[2,128,1152]{2,1,0:T(8,128)(2,1)S(1)}, u32[]{:S(2)}, u32[]{:S(2)}) collective-permute-start(bf16[2,128,1152]{2,1,0:T(8,128)(2,1)} %take_chunk.2.refs_0_), channel_id=1, source_target_pairs={{0,1},{1,0},{2,3},{3,2},{4,5},{5,4},{6,7},{7,6},{8,9},{9,8},{10,11... | collective-permute-start | bytes 1769480 | tf_op jit(solution)/shard_map/ppermute | solution.py:196
  18.7 32.7 %collective-permute-start.2 = (bf16[2,128,1152]{2,1,0:T(8,128)(2,1)}, bf16[2,128,1152]{2,1,0:T(8,128)(2,1)S(1)}, u32[]{:S(2)}, u32[]{:S(2)}) collective-permute-start(bf16[2,128,1152]{2,1,0:T(8,128)(2,1)} %take_chunk.2.refs_0_), channel_id=1, source_target_pairs={{1,2},{2,1},{5,6},{6,5},{9,10},{10,9},{13,14},{14,13},{17,18},{18,... | collective-permute-start | bytes 1769480 | tf_op jit(solution)/shard_map/ppermute | solution.py:196
  47.2 0.8 copy-start
  50.0 19.0 %copy-start.1 = (bf16[2,128,1152]{2,1,0:T(8,128)(2,1)S(1)}, bf16[2,128,1152]{2,1,0:T(8,128)(2,1)}, u32[]{:S(2)}) copy-start(bf16[2,128,1152]{2,1,0:T(8,128)(2,1)} %copy-done) | copy-start | bytes 1769476
  50.0 19.0 %copy-start.6 = (bf16[2,128,1152]{2,1,0:T(8,128)(2,1)S(1)}, bf16[2,128,1152]{2,1,0:T(8,128)(2,1)}, u32[]{:S(2)}) copy-start(bf16[2,128,1152]{2,1,0:T(8,128)(2,1)} %take_chunk.2.refs_0_) | copy-start | bytes 1769476
  50.0 16.5 %collective-permute-start.3 = (bf16[2,128,1152]{2,1,0:T(8,128)(2,1)}, bf16[2,128,1152]{2,1,0:T(8,128)(2,1)S(1)}, u32[]{:S(2)}, u32[]{:S(2)}) collective-permute-start(bf16[2,128,1152]{2,1,0:T(8,128)(2,1)} %relay.1), channel_id=1, source_target_pairs={{2,3},{1,0},{6,7},{5,4},{10,11},{9,8},{14,15},{13,12},{18,19},{17,... | collective-permute-start | bytes 1769480 | tf_op jit(solution)/shard_map/ppermute | solution.py:208
  51.4 0.8 copy-start.2
  52.2 0.8 copy-start.4
  55.1 23.8 %copy-start.7 = (bf16[2,128,1024]{2,1,0:T(8,128)(2,1)S(1)}, bf16[2,128,1024]{2,1,0:T(8,128)(2,1)}, u32[]{:S(2)}) copy-start(bf16[2,128,1024]{2,1,0:T(8,128)(2,1)} %take_chunk.3.refs_5_.refs_0_) | copy-start | bytes 1572868
  55.1 0.8 collective-permute-start.4
  56.0 10.6 %copy-start.12 = (bf16[2,128,1024]{2,1,0:T(8,128)(2,1)}, bf16[2,128,1024]{2,1,0:T(8,128)(2,1)S(1)}, u32[]{:S(2)}) copy-start(bf16[2,128,1024]{2,1,0:T(8,128)(2,1)S(1)} %collective-permute-done.4.refs_6_.refs_3_) | copy-start | bytes 1572868
  66.5 0.8 copy-start.8
  69.0 1.1 copy-start.3
  70.1 1.1 copy-start.5
  71.2 1.1 copy-start.9
  72.2 0.8 copy-start.14
  73.1 42.3 %copy-start.15 = (bf16[1,128,256]{2,1,0:T(8,128)(2,1)S(1)}, bf16[1,128,256]{2,1,0:T(8,128)(2,1)}, u32[]{:S(2)}) copy-start(bf16[1,128,256]{2,1,0:T(8,128)(2,1)} %sum_tails.1.refs_5_) | copy-start | bytes 196612
  74.5 60.8 %all-to-all-start.1 = ((bf16[8,128,1024]{2,1,0:T(8,128)(2,1)}), bf16[8,128,1024]{2,1,0:T(8,128)(2,1)}, u32[]{:S(2)}, u32[]{:S(2)}) async-start(bf16[8,128,1024]{2,1,0:T(8,128)(2,1)} %bitcast.5), calls=%async_computation.1 | async-start | bytes 4194304 | tf_op jit(solution)/shard_map/all_to_all | solution.py:381
  78.9 54.2 %copy-start.13 = (bf16[2,128,1024]{2,1,0:T(8,128)(2,1)S(1)}, bf16[2,128,1024]{2,1,0:T(8,128)(2,1)}, u32[]{:S(2)}) copy-start(bf16[2,128,1024]{2,1,0:T(8,128)(2,1)} %copy-done.12) | copy-start | bytes 1572868
  78.9 35.1 %collective-permute-start.9 = (bf16[2,128,1024]{2,1,0:T(8,128)(2,1)S(1)}, bf16[2,128,1024]{2,1,0:T(8,128)(2,1)S(1)}, u32[]{:S(2)}, u32[]{:S(2)}) collective-permute-start(bf16[2,128,1024]{2,1,0:T(8,128)(2,1)S(1)} %copy-done.7), channel_id=1, source_target_pairs={{0,2},{1,3},{2,0},{3,1},{4,6},{5,7},{6,4},{7,5},{8,10},{9,11},{10,... | collective-permute-start | bytes 1572872 | tf_op jit(solution)/shard_map/ppermute | solution.py:196
  90.3 42.9 %collective-permute-start.8 = (bf16[2,128,1024]{2,1,0:T(8,128)(2,1)S(1)}, bf16[2,128,1024]{2,1,0:T(8,128)(2,1)S(1)}, u32[]{:S(2)}, u32[]{:S(2)}) collective-permute-start(bf16[2,128,1024]{2,1,0:T(8,128)(2,1)S(1)} %copy-done.7), channel_id=1, source_target_pairs={{0,1},{1,0},{2,3},{3,2},{4,5},{5,4},{6,7},{7,6},{8,9},{9,8},{10,11... | collective-permute-start | bytes 1572872 | tf_op jit(solution)/shard_map/ppermute | solution.py:196
  114.0 19.1 %collective-permute-start.10 = (bf16[2,128,1024]{2,1,0:T(8,128)(2,1)S(1)}, bf16[2,128,1024]{2,1,0:T(8,128)(2,1)S(1)}, u32[]{:S(2)}, u32[]{:S(2)}) collective-permute-start(bf16[2,128,1024]{2,1,0:T(8,128)(2,1)S(1)} %collective-permute-done.9.refs_2_), channel_id=1, source_target_pairs={{2,3},{1,0},{6,7},{5,4},{10,11},{9,8},{14,15},{13,12},{18,19},{17,... | collective-permute-start | bytes 1572872 | tf_op jit(solution)/shard_map/ppermute | solution.py:208
  131.8 1.3 copy-start.10
  135.3 33.3 %all-to-all-start = ((bf16[8,128,1024]{2,1,0:T(8,128)(2,1)}), bf16[8,128,1024]{2,1,0:T(8,128)(2,1)S(1)}, u32[]{:S(2)}, u32[]{:S(2)}) async-start(bf16[8,128,1024]{2,1,0:T(8,128)(2,1)} %bitcast.3), calls=%async_computation | async-start | bytes 4194304 | tf_op jit(solution)/shard_map/all_to_all | solution.py:381
  139.0 1.6 copy-start.11
  150.0 31.6 %collective-permute-start.5 = (bf16[512,256]{1,0:T(8,128)(2,1)}, bf16[512,256]{1,0:T(8,128)(2,1)S(1)}, u32[]{:S(2)}, u32[]{:S(2)}) collective-permute-start(bf16[512,256]{1,0:T(8,128)(2,1)} %get-tuple-element.9), channel_id=1, source_target_pairs={{0,1},{1,0},{2,3},{3,2},{4,5},{5,4},{6,7},{7,6},{8,9},{9,8},{10,11... | collective-permute-start | bytes 786440 | tf_op jit(solution)/shard_map/ppermute | solution.py:18
  152.7 28.9 %collective-permute-start.6 = (bf16[512,256]{1,0:T(8,128)(2,1)}, bf16[512,256]{1,0:T(8,128)(2,1)}, u32[]{:S(2)}, u32[]{:S(2)}) collective-permute-start(bf16[512,256]{1,0:T(8,128)(2,1)} %get-tuple-element.8), channel_id=1, source_target_pairs={{0,2},{1,3},{2,0},{3,1},{4,6},{5,7},{6,4},{7,5},{8,10},{9,11},{10,... | collective-permute-start | bytes 786440 | tf_op jit(solution)/shard_map/ppermute | solution.py:18
  152.7 28.9 %collective-permute-start.7 = (bf16[512,256]{1,0:T(8,128)(2,1)}, bf16[512,256]{1,0:T(8,128)(2,1)}, u32[]{:S(2)}, u32[]{:S(2)}) collective-permute-start(bf16[512,256]{1,0:T(8,128)(2,1)} %get-tuple-element.7), channel_id=1, source_target_pairs={{0,3},{1,2},{2,1},{3,0},{4,7},{5,6},{6,5},{7,4},{8,11},{9,10},{10,... | collective-permute-start | bytes 786440 | tf_op jit(solution)/shard_map/ppermute | solution.py:18
  181.5 0.7 copy-start.16
Sparse Core Ops, SparseCore 0:
  9.9 57.0 all-gather.1

commit v14 on v13

--- a/solution.py
+++ b/solution.py
@@ -365,8 +365,8 @@
 
     where = narrow_index.reshape(1)
     later, later_at = chunks[1]
-    direct = [later[near] for near, _ in later_at if near]
-    product = sum_tails(*chunks[0], where, height, [later[0]] + direct[-1:])
+    halfway = later[later_at[narrow_count // 2][0]]
+    product = sum_tails(*chunks[0], where, height, [later[0], halfway])
     y = lax.all_gather(product, "wide", axis=0, tiled=True)
     y = y.reshape(tokens * wide_count, y.shape[2])
     hr, gram = hr_and_gram(cols, y, scale)

time: 192 us -> 195 us (1.016)
  blocking collectives: 10 us -> 28.8 us
  waiting for transfers between devices: 35 us -> 24.4 us
  starting transfers between devices: 34.2 us -> 28.5 us
    all_gather x1, blocking collectives: 10 us -> 28.8 us  [body(): y = lax.all_gather(product, 'wide', axis=0, tiled=True)]
    ppermute x2, waiting for transfers between devices: 10.6 us -> 0.01 us  [exchange_blocks(): blocks.append(lax.ppermute(onward, 'narrow', pairs))]
    ppermute x6, starting transfers between devices: 18.5 us -> 13.4 us  [exchange_blocks(): direct[mask] = lax.ppermute(mine, 'narrow', pairs) if pairs else None]
  transfers between devices with their start and end apart: 14 -> 14, of which waited for: 2 -> 1; matrix products, arithmetic and copies ran while one was open for 3% -> 3% of each run, Pallas kernels for 41% -> 41%
where the time goes in v14:
time: 195 us; the launch traced here: 194 us
  Pallas kernels  81.4 us (42%)
  blocking collectives  28.8 us (15%)
  starting transfers between devices  28.5 us (15%)
  waiting for transfers between devices  24.4 us (13%)
  between operations  14.2 us (7%)
  local copies, waits for them, and re-layouts  13.4 us (7%)
  matrix products  3.03 us (2%)
    all_gather x1, blocking collectives, body(): y = lax.all_gather(product, 'wide', axis=0, tiled=True)  28.8 us
    pallas_call x1, Pallas kernels, residual_tile(): pl.pallas_call(residual_kernel, out_shape=jax.ShapeDtypeStruct((rows, fea...  26.5 us
    pallas_call x2, Pallas kernels, hessian_rows(): pl.pallas_call(kernel, out_shape=jax.ShapeDtypeStruct(shape, BF16), grid=...  26.5 us
    ppermute x6, waiting for transfers between devices, exchange_blocks(): direct[mask] = lax.ppermute(mine, 'narrow', pairs) if pairs else None  23.7 us
    ppermute x6, starting transfers between devices, exchange_blocks(): direct[mask] = lax.ppermute(mine, 'narrow', pairs) if pairs else None  13.4 us
    unnamed x35, local copies, waits for them, and re-layouts  12.4 us
    pallas_call x1, Pallas kernels, partial_product(): pl.pallas_call(product_kernel, out_shape=jax.ShapeDtypeStruct((rows, rank...  8.41 us
    all_to_all x2, starting transfers between devices, body(): lax.all_to_all(every, 'wide', split_axis=0, concat_axis=0, tiled=True)  7.98 us
  transfers between devices with their start and end apart: 14, of which 1 were waited for; matrix products, arithmetic and copies ran while one was open for 3% of the time, Pallas kernels for 41%

profile of v14, /device:TPU:0, one launch (start us, length us, event | category | flops | bytes accessed | tf_op | source)
XLA Modules:
  0.0 193.8 jit_solution(10596740870166243478)
XLA Ops:
  7.2 0.0 all-gather.2.cloned.1.call-start
  7.2 0.7 all-gather.2.cloned.1.call-update
  7.9 3.0 %fusion.2.refs_0_ = f32[128,256]{1,0:T(8,128)} fusion(bf16[128,4096]{1,0:T(8,128)(2,1)} %activations_ref.3, bf16[16384,256]{1,0:T(8,128)(2,1)} %param.9, s32[]{:T(128)S(6)} %select_n.15), kind=kOutput, calls=%fused_computation.2 | convolution fusion | flops 268435456 | bytes 3276804 | tf_op jit(solution)/shard_map/dot_general | solution.py:352
  10.9 2.1 %take_chunk.2.refs_0_ = bf16[2,128,1152]{2,1,0:T(8,128)(2,1)} custom-call(bf16[128,4096]{1,0:T(8,128)(2,1)} %activations_ref.3, f32[128,256]{1,0:T(8,128)} %fusion.2.refs_0_), custom_call_target="tpu_custom_call" | custom-call | bytes 1048576 | tf_op jit(solution)/shard_map/take_chunk/pallas_call | solution.py:117
  13.1 4.0 %collective-permute-start.1 = (bf16[2,128,1152]{2,1,0:T(8,128)(2,1)}, bf16[2,128,1152]{2,1,0:T(8,128)(2,1)S(1)}, u32[]{:S(2)}, u32[]{:S(2)}) collective-permute-start(bf16[2,128,1152]{2,1,0:T(8,128)(2,1)} %take_chunk.2.refs_0_), channel_id=1, source_target_pairs={{0,2},{1,3},{2,0},{3,1},{4,6},{5,7},{6,4},{7,5},{8,10},{9,11},{10,... | collective-permute-start | bytes 1769480 | tf_op jit(solution)/shard_map/ppermute | solution.py:196
  17.1 1.6 collective-permute-start
  18.7 0.7 collective-permute-start.2
  19.4 1.3 copy.11.scales_ref
  20.7 26.5 %residual_tile.1.refs_0_.refs_3_.residual_ref = bf16[2048,4096]{1,0:T(8,128)(2,1)} custom-call(bf16[2048,4096]{1,0:T(8,128)(2,1)} %weight_ref.1, s32[2048,4096]{1,0:T(8,128)} %codes_ref.1, f32[2048,32]{1,0:T(8,128)S(1)} %copy.11.scales_ref), custom_call_target="tpu_custom_call" | custom-call | bytes 92274688 | tf_op jit(solution)/shard_map/residual_tile/pallas_call | solution.py:228
  47.2 0.0 collective-permute-done.1.value_ref.refs_1_.refs_2_
  47.2 0.0 copy-start
  47.2 0.8 copy-done
  48.1 1.9 relay.1
  50.0 1.4 collective-permute-start.3
  51.4 0.0 collective-permute-done.refs_0_.refs_1_
  51.4 0.0 copy-start.2
  51.4 0.0 collective-permute-done.2.refs_2_.refs_3_
  51.4 0.8 copy-done.2
  52.2 0.8 copy-done.4
  53.1 2.1 %take_chunk.3.refs_5_.refs_0_ = bf16[2,128,1024]{2,1,0:T(8,128)(2,1)} custom-call(bf16[128,4096]{1,0:T(8,128)(2,1)} %activations_ref.3, bf16[2,128,1152]{2,1,0:T(8,128)(2,1)} %copy-done.2, bf16[2,128,1152]{2,1,0:T(8,128)(2,1)} %copy-done, bf16[2,128,1152]{2,1,0:T(8,128)(2,1)} %copy-done.4, bf16[2048,4096]{1,0:T(8,128)(2,1)} %residual_tile.1.refs_0_.refs_3_.residual_ref), custom_call_target="tpu_custom_call" | custom-call | bytes 1048576 | tf_op jit(solution)/shard_map/take_chunk/pallas_call | solution.py:117
  55.1 6.3 %collective-permute-start.4 = (bf16[2,128,1024]{2,1,0:T(8,128)(2,1)}, bf16[2,128,1024]{2,1,0:T(8,128)(2,1)S(1)}, u32[]{:S(2)}, u32[]{:S(2)}) collective-permute-start(bf16[2,128,1024]{2,1,0:T(8,128)(2,1)} %take_chunk.3.refs_5_.refs_0_), channel_id=1, source_target_pairs={{0,2},{1,3},{2,0},{3,1},{4,6},{5,7},{6,4},{7,5},{8,10},{9,11},{10,... | collective-permute-start | bytes 1572872 | tf_op jit(solution)/shard_map/ppermute | solution.py:196
  61.5 23.7 %collective-permute-done.4.refs_6_.refs_2_ = bf16[2,128,1024]{2,1,0:T(8,128)(2,1)S(1)} collective-permute-done((bf16[2,128,1024]{2,1,0:T(8,128)(2,1)}, bf16[2,128,1024]{2,1,0:T(8,128)(2,1)S(1)}, u32[]{:S(2)}, u32[]{:S(2)}) %collective-permute-start.4) | collective-permute-done | bytes 524320 | tf_op jit(solution)/shard_map/ppermute | solution.py:196
  85.2 0.0 collective-permute-done.3.refs_4_
  85.2 0.8 copy-done.12
  86.0 0.2 copy-done.8
  86.2 1.7 sum_tails.1.refs_5_
  87.8 0.0 copy-done.1
  87.8 0.0 copy-done.6
  87.9 1.1 copy-done.3
  88.9 1.1 copy-done.5
  90.0 1.1 copy-done.9
  91.0 0.8 copy-done.14
  91.9 1.5 place_blocks.2.refs_5_
  93.3 4.4 %all-to-all-start.1 = ((bf16[8,128,1024]{2,1,0:T(8,128)(2,1)}), bf16[8,128,1024]{2,1,0:T(8,128)(2,1)}, u32[]{:S(2)}, u32[]{:S(2)}) async-start(bf16[8,128,1024]{2,1,0:T(8,128)(2,1)} %bitcast.5), calls=%async_computation.1 | async-start | bytes 4194304 | tf_op jit(solution)/shard_map/all_to_all | solution.py:381
  97.7 0.0 copy-done.7
  97.7 0.1 collective-permute-start.8
  97.8 0.7 collective-permute-start.9
  98.5 0.0 copy-done.13
  98.5 1.3 collective-permute-start.10
  99.8 0.0 copy-done.15
  99.9 28.8 %all_gather.7 = bf16[8,128,256]{2,1,0:T(8,128)(2,1)S(1)} all-gather(bf16[1,128,256]{2,1,0:T(8,128)(2,1)S(1)} %copy-done.15), channel_id=1, replica_groups=mesh['wide'=8,'narrow'=4] {'wide'}, dimensions={0}, use_global_device_ids=true | all-gather | bytes 589824 | tf_op jit(solution)/shard_map/all_gather | solution.py:370
  128.7 6.4 %hr_and_gram.1 = (bf16[4096,256]{1,0:T(8,128)(2,1)S(1)}, f32[256,256]{1,0:T(8,128)}) custom-call(bf16[1024,4096]{1,0:T(8,128)(2,1)} %all-gather.2.cloned.1.call-done.cols_ref.refs_1_, bf16[1024,256]{1,0:T(8,128)(2,1)S(1)} %bitcast.10), custom_call_target="tpu_custom_call" | custom-call | flops 4294967296 | bytes 16777216 | tf_op jit(solution)/shard_map/hr_and_gram/pallas_call | solution.py:45
  135.1 1.3 copy-done.10
  136.4 0.0 collective-permute-done.8.refs_1_
  136.4 0.0 collective-permute-done.9.refs_3_
  136.4 0.0 collective-permute-done.10.refs_4_
  136.4 2.2 %place_blocks.3 = bf16[4,2,128,1024]{3,2,1,0:T(8,128)(2,1)} custom-call(s32[1]{0:T(128)} %bitcast.where_ref, bf16[2,128,1024]{2,1,0:T(8,128)(2,1)S(1)} %copy-done.7, bf16[2,128,1024]{2,1,0:T(8,128)(2,1)S(1)} %collective-permute-done.8.refs_1_, bf16[2,128,1024]{2,1,0:T(8,128)(2,1)S(1)} %copy-done.13, ...), custom_call_target="tpu_custom_call" | custom-call | bytes 4194304 | tf_op jit(solution)/shard_map/place_blocks/pallas_call | solution.py:90
  138.6 0.0 all-to-all-done.1
  138.6 3.6 %all-to-all-start = ((bf16[8,128,1024]{2,1,0:T(8,128)(2,1)}), bf16[8,128,1024]{2,1,0:T(8,128)(2,1)S(1)}, u32[]{:S(2)}, u32[]{:S(2)}) async-start(bf16[8,128,1024]{2,1,0:T(8,128)(2,1)} %bitcast.3), calls=%async_computation | async-start | bytes 4194304 | tf_op jit(solution)/shard_map/all_to_all | solution.py:381
  142.2 0.0 copy-start.11
  142.2 1.6 copy-done.11
  143.8 8.4 %partial_product.1.refs_2_.refs_3_ = bf16[2048,256]{1,0:T(8,128)(2,1)S(1)} custom-call(bf16[2048,4096]{1,0:T(8,128)(2,1)} %residual_tile.1.refs_0_.refs_3_.residual_ref, bf16[4096,256]{1,0:T(8,128)(2,1)S(1)} %copy-done.11), custom_call_target="tpu_custom_call" | custom-call | flops 8589934592 | bytes 25165824 | tf_op jit(solution)/shard_map/partial_product/pallas_call | solution.py:252
  152.2 1.0 constant_dynamic-slice_fusion
  153.3 0.0 collective-permute-start.5
  153.3 1.1 collective-permute-start.6
  154.3 3.3 %collective-permute-start.7 = (bf16[512,256]{1,0:T(8,128)(2,1)}, bf16[512,256]{1,0:T(8,128)(2,1)}, u32[]{:S(2)}, u32[]{:S(2)}) collective-permute-start(bf16[512,256]{1,0:T(8,128)(2,1)} %get-tuple-element.7), channel_id=1, source_target_pairs={{0,3},{1,2},{2,1},{3,0},{4,7},{5,6},{6,5},{7,4},{8,11},{9,10},{10,... | collective-permute-start | bytes 786440 | tf_op jit(solution)/shard_map/ppermute | solution.py:18
  157.6 13.6 %hessian_rows.2.refs_2_ = bf16[2048,4096]{1,0:T(8,128)(2,1)} custom-call(bf16[1024,1024]{1,0:T(8,128)(2,1)} %bitcast.6.refs_0_, bf16[1024,4096]{1,0:T(8,128)(2,1)} %all-gather.2.cloned.1.call-done.cols_ref.refs_1_, bf16[2048,256]{1,0:T(8,128)(2,1)S(1)} %partial_product.1.refs_2_.refs_3_), custom_call_target="tpu_custom_call" | custom-call | flops 17179869184 | bytes 18874368 | tf_op jit(solution)/shard_map/hessian_rows/pallas_call | solution.py:296
  171.2 0.0 all-to-all-done
  171.2 12.9 %hessian_rows.3.refs_4_ = bf16[2048,4096]{1,0:T(8,128)(2,1)} custom-call(bf16[1024,1024]{1,0:T(8,128)(2,1)S(1)} %bitcast.9, bf16[1024,4096]{1,0:T(8,128)(2,1)} %all-gather.2.cloned.1.call-done.cols_ref.refs_1_, bf16[2048,4096]{1,0:T(8,128)(2,1)} %hessian_rows.2.refs_2_, ...), custom_call_target="tpu_custom_call", output_to_operand_aliasing={{}: (2, {})} | custom-call | flops 17179869184 | bytes 18874368 | tf_op jit(solution)/shard_map/hessian_rows/pallas_call | solution.py:296
  184.2 0.0 collective-permute-done.5.refs_1_
  184.2 0.0 collective-permute-done.6.refs_2_
  184.2 0.0 collective-permute-done.7.refs_3_
  184.2 0.7 copy-done.16
  184.9 2.1 %add_pieces.1 = f32[512,256]{1,0:T(8,128)} custom-call(bf16[512,256]{1,0:T(8,128)(2,1)} %get-tuple-element.10.refs_0_, bf16[512,256]{1,0:T(8,128)(2,1)} %copy-done.16, bf16[512,256]{1,0:T(8,128)(2,1)} %collective-permute-done.6.refs_2_, bf16[512,256]{1,0:T(8,128)(2,1)} %collective-permute-done.7.refs_3_, bf16[2048,4096]{1,0:T(8,128)(2,1)} %hessian_rows.3.refs_4_), custom_call_target="tpu_custom_call" | custom-call | bytes 1572864 | tf_op jit(solution)/shard_map/add_pieces/pallas_call | solution.py:321
  (15 shorter events, 0.0 us)
Async XLA Ops:
  7.2 121.5 %all-gather.2.cloned.1.call-start = ((), (), s32[]{:S(2)}) async-start(), calls=%async_computation.2 | async-start | bytes 9437184 | tf_op jit(solution)/shard_map/all_gather | solution.py:349
  13.1 34.1 %collective-permute-start.1 = (bf16[2,128,1152]{2,1,0:T(8,128)(2,1)}, bf16[2,128,1152]{2,1,0:T(8,128)(2,1)S(1)}, u32[]{:S(2)}, u32[]{:S(2)}) collective-permute-start(bf16[2,128,1152]{2,1,0:T(8,128)(2,1)} %take_chunk.2.refs_0_), channel_id=1, source_target_pairs={{0,2},{1,3},{2,0},{3,1},{4,6},{5,7},{6,4},{7,5},{8,10},{9,11},{10,... | collective-permute-start | bytes 1769480 | tf_op jit(solution)/shard_map/ppermute | solution.py:196
  17.1 34.3 %collective-permute-start = (bf16[2,128,1152]{2,1,0:T(8,128)(2,1)}, bf16[2,128,1152]{2,1,0:T(8,128)(2,1)S(1)}, u32[]{:S(2)}, u32[]{:S(2)}) collective-permute-start(bf16[2,128,1152]{2,1,0:T(8,128)(2,1)} %take_chunk.2.refs_0_), channel_id=1, source_target_pairs={{0,1},{1,0},{2,3},{3,2},{4,5},{5,4},{6,7},{7,6},{8,9},{9,8},{10,11... | collective-permute-start | bytes 1769480 | tf_op jit(solution)/shard_map/ppermute | solution.py:196
  18.7 32.7 %collective-permute-start.2 = (bf16[2,128,1152]{2,1,0:T(8,128)(2,1)}, bf16[2,128,1152]{2,1,0:T(8,128)(2,1)S(1)}, u32[]{:S(2)}, u32[]{:S(2)}) collective-permute-start(bf16[2,128,1152]{2,1,0:T(8,128)(2,1)} %take_chunk.2.refs_0_), channel_id=1, source_target_pairs={{1,2},{2,1},{5,6},{6,5},{9,10},{10,9},{13,14},{14,13},{17,18},{18,... | collective-permute-start | bytes 1769480 | tf_op jit(solution)/shard_map/ppermute | solution.py:196
  47.2 0.8 copy-start
  50.0 37.9 %copy-start.1 = (bf16[2,128,1152]{2,1,0:T(8,128)(2,1)S(1)}, bf16[2,128,1152]{2,1,0:T(8,128)(2,1)}, u32[]{:S(2)}) copy-start(bf16[2,128,1152]{2,1,0:T(8,128)(2,1)} %copy-done) | copy-start | bytes 1769476
  50.0 37.9 %copy-start.6 = (bf16[2,128,1152]{2,1,0:T(8,128)(2,1)S(1)}, bf16[2,128,1152]{2,1,0:T(8,128)(2,1)}, u32[]{:S(2)}) copy-start(bf16[2,128,1152]{2,1,0:T(8,128)(2,1)} %take_chunk.2.refs_0_) | copy-start | bytes 1769476
  50.0 35.2 %collective-permute-start.3 = (bf16[2,128,1152]{2,1,0:T(8,128)(2,1)}, bf16[2,128,1152]{2,1,0:T(8,128)(2,1)S(1)}, u32[]{:S(2)}, u32[]{:S(2)}) collective-permute-start(bf16[2,128,1152]{2,1,0:T(8,128)(2,1)} %relay.1), channel_id=1, source_target_pairs={{2,3},{1,0},{6,7},{5,4},{10,11},{9,8},{14,15},{13,12},{18,19},{17,... | collective-permute-start | bytes 1769480 | tf_op jit(solution)/shard_map/ppermute | solution.py:208
  51.4 0.8 copy-start.2
  52.2 0.8 copy-start.4
  55.1 42.6 %copy-start.7 = (bf16[2,128,1024]{2,1,0:T(8,128)(2,1)S(1)}, bf16[2,128,1024]{2,1,0:T(8,128)(2,1)}, u32[]{:S(2)}) copy-start(bf16[2,128,1024]{2,1,0:T(8,128)(2,1)} %take_chunk.3.refs_5_.refs_0_) | copy-start | bytes 1572868
  55.1 30.0 %collective-permute-start.4 = (bf16[2,128,1024]{2,1,0:T(8,128)(2,1)}, bf16[2,128,1024]{2,1,0:T(8,128)(2,1)S(1)}, u32[]{:S(2)}, u32[]{:S(2)}) collective-permute-start(bf16[2,128,1024]{2,1,0:T(8,128)(2,1)} %take_chunk.3.refs_5_.refs_0_), channel_id=1, source_target_pairs={{0,2},{1,3},{2,0},{3,1},{4,6},{5,7},{6,4},{7,5},{8,10},{9,11},{10,... | collective-permute-start | bytes 1572872 | tf_op jit(solution)/shard_map/ppermute | solution.py:196
  85.2 0.8 copy-start.12
  85.2 1.0 copy-start.8
  87.8 1.1 copy-start.3
  88.9 1.1 copy-start.5
  90.0 1.1 copy-start.9
  91.0 0.8 copy-start.14
  91.9 6.6 %copy-start.13 = (bf16[2,128,1024]{2,1,0:T(8,128)(2,1)S(1)}, bf16[2,128,1024]{2,1,0:T(8,128)(2,1)}, u32[]{:S(2)}) copy-start(bf16[2,128,1024]{2,1,0:T(8,128)(2,1)} %copy-done.12) | copy-start | bytes 1572868
  91.9 8.0 %copy-start.15 = (bf16[1,128,256]{2,1,0:T(8,128)(2,1)S(1)}, bf16[1,128,256]{2,1,0:T(8,128)(2,1)}, u32[]{:S(2)}) copy-start(bf16[1,128,256]{2,1,0:T(8,128)(2,1)} %sum_tails.1.refs_5_) | copy-start | bytes 196612
  93.3 45.3 %all-to-all-start.1 = ((bf16[8,128,1024]{2,1,0:T(8,128)(2,1)}), bf16[8,128,1024]{2,1,0:T(8,128)(2,1)}, u32[]{:S(2)}, u32[]{:S(2)}) async-start(bf16[8,128,1024]{2,1,0:T(8,128)(2,1)} %bitcast.5), calls=%async_computation.1 | async-start | bytes 4194304 | tf_op jit(solution)/shard_map/all_to_all | solution.py:381
  97.7 38.7 %collective-permute-start.8 = (bf16[2,128,1024]{2,1,0:T(8,128)(2,1)S(1)}, bf16[2,128,1024]{2,1,0:T(8,128)(2,1)S(1)}, u32[]{:S(2)}, u32[]{:S(2)}) collective-permute-start(bf16[2,128,1024]{2,1,0:T(8,128)(2,1)S(1)} %copy-done.7), channel_id=1, source_target_pairs={{0,1},{1,0},{2,3},{3,2},{4,5},{5,4},{6,7},{7,6},{8,9},{9,8},{10,11... | collective-permute-start | bytes 1572872 | tf_op jit(solution)/shard_map/ppermute | solution.py:196
  97.8 38.6 %collective-permute-start.9 = (bf16[2,128,1024]{2,1,0:T(8,128)(2,1)S(1)}, bf16[2,128,1024]{2,1,0:T(8,128)(2,1)S(1)}, u32[]{:S(2)}, u32[]{:S(2)}) collective-permute-start(bf16[2,128,1024]{2,1,0:T(8,128)(2,1)S(1)} %copy-done.7), channel_id=1, source_target_pairs={{1,2},{2,1},{5,6},{6,5},{9,10},{10,9},{13,14},{14,13},{17,18},{18,... | collective-permute-start | bytes 1572872 | tf_op jit(solution)/shard_map/ppermute | solution.py:196
  98.5 37.9 %collective-permute-start.10 = (bf16[2,128,1024]{2,1,0:T(8,128)(2,1)S(1)}, bf16[2,128,1024]{2,1,0:T(8,128)(2,1)S(1)}, u32[]{:S(2)}, u32[]{:S(2)}) collective-permute-start(bf16[2,128,1024]{2,1,0:T(8,128)(2,1)S(1)} %copy-done.13), channel_id=1, source_target_pairs={{2,3},{1,0},{6,7},{5,4},{10,11},{9,8},{14,15},{13,12},{18,19},{17,... | collective-permute-start | bytes 1572872 | tf_op jit(solution)/shard_map/ppermute | solution.py:208
  135.1 1.3 copy-start.10
  138.6 32.6 %all-to-all-start = ((bf16[8,128,1024]{2,1,0:T(8,128)(2,1)}), bf16[8,128,1024]{2,1,0:T(8,128)(2,1)S(1)}, u32[]{:S(2)}, u32[]{:S(2)}) async-start(bf16[8,128,1024]{2,1,0:T(8,128)(2,1)} %bitcast.3), calls=%async_computation | async-start | bytes 4194304 | tf_op jit(solution)/shard_map/all_to_all | solution.py:381
  142.2 1.6 copy-start.11
  153.3 30.9 %collective-permute-start.5 = (bf16[512,256]{1,0:T(8,128)(2,1)}, bf16[512,256]{1,0:T(8,128)(2,1)S(1)}, u32[]{:S(2)}, u32[]{:S(2)}) collective-permute-start(bf16[512,256]{1,0:T(8,128)(2,1)} %get-tuple-element.9), channel_id=1, source_target_pairs={{0,1},{1,0},{2,3},{3,2},{4,5},{5,4},{6,7},{7,6},{8,9},{9,8},{10,11... | collective-permute-start | bytes 786440 | tf_op jit(solution)/shard_map/ppermute | solution.py:18
  153.3 30.9 %collective-permute-start.6 = (bf16[512,256]{1,0:T(8,128)(2,1)}, bf16[512,256]{1,0:T(8,128)(2,1)}, u32[]{:S(2)}, u32[]{:S(2)}) collective-permute-start(bf16[512,256]{1,0:T(8,128)(2,1)} %get-tuple-element.8), channel_id=1, source_target_pairs={{0,2},{1,3},{2,0},{3,1},{4,6},{5,7},{6,4},{7,5},{8,10},{9,11},{10,... | collective-permute-start | bytes 786440 | tf_op jit(solution)/shard_map/ppermute | solution.py:18
  154.3 29.9 %collective-permute-start.7 = (bf16[512,256]{1,0:T(8,128)(2,1)}, bf16[512,256]{1,0:T(8,128)(2,1)}, u32[]{:S(2)}, u32[]{:S(2)}) collective-permute-start(bf16[512,256]{1,0:T(8,128)(2,1)} %get-tuple-element.7), channel_id=1, source_target_pairs={{0,3},{1,2},{2,1},{3,0},{4,7},{5,6},{6,5},{7,4},{8,11},{9,10},{10,... | collective-permute-start | bytes 786440 | tf_op jit(solution)/shard_map/ppermute | solution.py:18
  184.2 0.7 copy-start.16
Sparse Core Ops, SparseCore 0:
  9.9 57.0 all-gather.1
